TPU v7x, 256 devices: a whole 4x4x8 slice. The times are simulated.
256 devices in a mesh: section: 4 (over z_lo), ch: 16 (over x, z_hi, core), slab: 4 (over y).
Axes of the slice: x: 4, y: 4, z: 8 (z_hi: 2, z_lo: 4; z = z_hi * 4 + z_lo), core: 2. Of those that a mesh axis runs over, the one named last changes fastest.
Arguments:
- x_in: bfloat16 [4, 384, 32, 128], P(None, 'ch', 'slab'), may hold values from -6 to 6
- cot: bfloat16 [4, 384, 32, 128], P(None, 'ch', 'slab'), may hold values from -0.125 to 0.125
- w1: bfloat16 [4, 9, 384, 384], P('section', None, 'ch'), may hold values from -0.109375 to 0.109375
- gain: float32 [4, 384], P('section'), may hold values from 0.5 to 1.5
Outputs:
- weight_grad: float32 [4, 9, 384, 384], P('section', None, 'ch')
- gain_grad: float32 [4, 384], P('section', 'ch')
All inputs are finite; a program needn't handle non-finite values.
Results may differ from a plain program's by a relative error of at most 0.034.
Values may be sent and summed in bfloat16 or wider, within the bound.
No kernel may reach another device: no remote copies, remote signals or barrier semaphores. Data moves between devices by JAX's collectives and lax.ppermute only.
A program may use at most 128 MiB of HBM per device.

v0:
```python
import jax
import jax.numpy as jnp
from jax import lax
from jax.sharding import PartitionSpec as P

NORM_EPS = 1e-05
SLOPE_SCALE = 0.7978845608028654
CUBIC_COEF = 0.044715


def with_halo(cells, sides, width):
    for axis, dim in sides:
        count = lax.axis_size(axis)
        ends = count - 1
        head = lax.slice_in_dim(cells, 0, width, axis=dim)
        tail = lax.slice_in_dim(cells, cells.shape[dim] - width, cells.shape[dim], axis=dim)
        cells = jnp.concatenate(
            [
                lax.ppermute(tail, axis, [(i, (i + 1) % count) for i in range(ends)]),
                cells,
                lax.ppermute(head, axis, [((i + 1) % count, i) for i in range(ends)]),
            ],
            axis=dim,
        )
    return cells


def passed_along(value, axis, steps):
    count = lax.axis_size(axis)
    initial, last = (max(0, -steps), min(count, count - steps))
    return lax.ppermute(value, axis, [(source, source + steps) for source in range(initial, last)])


def gelu_value(pre_act):
    inner_arg = SLOPE_SCALE * (pre_act + CUBIC_COEF * pre_act * pre_act * pre_act)
    return 0.5 * pre_act * (1.0 + jnp.tanh(inner_arg))


def gelu_slope(pre_act):
    inner_arg = SLOPE_SCALE * (pre_act + CUBIC_COEF * pre_act * pre_act * pre_act)
    tangent = jnp.tanh(inner_arg)
    return 0.5 * (1.0 + tangent) + 0.5 * pre_act * (1.0 - tangent * tangent) * SLOPE_SCALE * (
        1.0 + 3.0 * CUBIC_COEF * pre_act * pre_act
    )


def window(extended, row_start, col_start, row_count, col_count):
    anchor = jnp.int32(0)
    return lax.dynamic_slice(
        extended, (anchor, row_start, col_start), (extended.shape[0], row_count, col_count)
    )


def widen(source, row_count):
    return jnp.pad(source, ((0, 0), (0, 0), (row_count, row_count)))


def normalized(inputs_here, gain_own):
    row_count = inputs_here.shape[1]
    values = inputs_here.astype(jnp.float32)
    sum_values, squares = lax.psum(
        (jnp.sum(values, axis=0), jnp.sum(values * values, axis=0)), "ch"
    )
    all_chans = inputs_here.shape[0] * lax.axis_size("ch")
    pix_mean = sum_values / all_chans
    pix_rstd = lax.rsqrt(squares / all_chans - pix_mean * pix_mean + NORM_EPS)
    normed = ((values - pix_mean) * pix_rstd * gain_own[:, None, None]).astype(jnp.bfloat16)
    rimmed = with_halo(normed, (("slab", 1),), row_count)
    gathered_unit = lax.all_gather(rimmed, "ch", axis=0, tiled=True)
    return (widen(gathered_unit, row_count), pix_mean, pix_rstd)


def convolve(extended, weight, dilation, row_count, col_count):
    all_chans = extended.shape[0]
    own_chans = weight.shape[1]
    running = jnp.zeros((own_chans, row_count * col_count), jnp.float32)
    for tap_index in range(9):
        row_shift = (tap_index // 3 - 1) * dilation
        col_shift = (tap_index % 3 - 1) * dilation
        tap_slab = window(
            extended, row_count + row_shift, row_count + col_shift, row_count, col_count
        )
        running = running + jnp.dot(
            weight[tap_index],
            tap_slab.reshape(all_chans, row_count * col_count),
            preferred_element_type=jnp.float32,
        )
    return running.reshape(own_chans, row_count, col_count)


def weight_terms(extended, slope_grad, dilation, row_count, col_count):
    all_chans = extended.shape[0]
    own_chans = slope_grad.shape[0]
    flat_grad = slope_grad.reshape(own_chans, row_count * col_count)
    tap_terms = []
    for tap_index in range(9):
        row_shift = (tap_index // 3 - 1) * dilation
        col_shift = (tap_index % 3 - 1) * dilation
        tap_slab = window(
            extended, row_count + row_shift, row_count + col_shift, row_count, col_count
        )
        tap_terms.append(
            lax.dot_general(
                flat_grad,
                tap_slab.reshape(all_chans, row_count * col_count),
                (((1,), (1,)), ((), ())),
                preferred_element_type=jnp.float32,
            )
        )
    return jnp.stack(tap_terms)


def place(buffer, new_value, batch_slot, is_live):
    old_value = lax.dynamic_index_in_dim(buffer, batch_slot, 0, keepdims=False)
    return lax.dynamic_update_index_in_dim(
        buffer, jnp.where(is_live, new_value, old_value), batch_slot, 0
    )


def local(x_in, cot, w1, gain):
    batches, own_chans, row_count, col_count = x_in.shape
    all_chans = w1.shape[3]
    pixels = row_count * col_count
    sections = lax.axis_size("section")
    section_index = lax.axis_index("section")
    weight = w1[0]
    gain_all = gain[0]
    gain_own = lax.dynamic_slice_in_dim(gain_all, lax.axis_index("ch") * own_chans, own_chans)
    dilation = jnp.right_shift(jnp.int32(row_count), sections - 1 - section_index)
    tick_count = batches + sections - 1

    def forward_tick(tick_index, state_now):
        incoming, kept_ext, kept_pre, kept_mean, kept_rstd, kept_input = state_now
        batch_index = tick_index - section_index
        is_live = (batch_index >= 0) & (batch_index < batches)
        batch_slot = jnp.clip(batch_index, 0, batches - 1)
        from_data = lax.dynamic_index_in_dim(x_in, batch_slot, 0, keepdims=False)
        inputs_here = jnp.where(section_index == 0, from_data, incoming)
        extended, pix_mean, pix_rstd = normalized(inputs_here, gain_own)
        pre_act = convolve(extended, weight, dilation, row_count, col_count)
        block_out = (inputs_here.astype(jnp.float32) + gelu_value(pre_act)).astype(jnp.bfloat16)
        passed = passed_along(block_out, "section", 1)
        return (
            passed,
            place(kept_ext, extended, batch_slot, is_live),
            place(kept_pre, pre_act, batch_slot, is_live),
            place(kept_mean, pix_mean, batch_slot, is_live),
            place(kept_rstd, pix_rstd, batch_slot, is_live),
            place(kept_input, inputs_here, batch_slot, is_live),
        )

    initial = (
        jnp.zeros((own_chans, row_count, col_count), jnp.bfloat16),
        jnp.zeros((batches, all_chans, 3 * row_count, col_count + 2 * row_count), jnp.bfloat16),
        jnp.zeros((batches, own_chans, row_count, col_count), jnp.float32),
        jnp.zeros((batches, row_count, col_count), jnp.float32),
        jnp.zeros((batches, row_count, col_count), jnp.float32),
        jnp.zeros((batches, own_chans, row_count, col_count), jnp.bfloat16),
    )
    stored = lax.fori_loop(0, tick_count, forward_tick, initial)
    kept_ext, kept_pre, kept_mean, kept_rstd, kept_input = (
        stored[1],
        stored[2],
        stored[3],
        stored[4],
        stored[5],
    )

    def backward_tick(tick_index, state_now):
        incoming, grad_weight, grad_gain = state_now
        batch_index = tick_index - (sections - 1 - section_index)
        is_live = (batch_index >= 0) & (batch_index < batches)
        batch_slot = jnp.clip(batch_index, 0, batches - 1)
        from_data = lax.dynamic_index_in_dim(cot, batch_slot, 0, keepdims=False)
        grad_out = jnp.where(section_index == sections - 1, from_data, incoming)
        extended = lax.dynamic_index_in_dim(kept_ext, batch_slot, 0, keepdims=False)
        pre_act = lax.dynamic_index_in_dim(kept_pre, batch_slot, 0, keepdims=False)
        pix_mean = lax.dynamic_index_in_dim(kept_mean, batch_slot, 0, keepdims=False)
        pix_rstd = lax.dynamic_index_in_dim(kept_rstd, batch_slot, 0, keepdims=False)
        inputs_here = lax.dynamic_index_in_dim(kept_input, batch_slot, 0, keepdims=False)
        slope_grad = (grad_out.astype(jnp.float32) * gelu_slope(pre_act)).astype(jnp.bfloat16)
        weight_step = weight_terms(extended, slope_grad, dilation, row_count, col_count)
        rimmed_grad = with_halo(slope_grad, (("slab", 1),), row_count)
        grad_ext = widen(rimmed_grad, row_count)
        span_rows = own_chans * lax.axis_size("ch")
        running = jnp.zeros((span_rows, pixels), jnp.float32)
        for tap_index in range(9):
            row_shift = (tap_index // 3 - 1) * dilation
            col_shift = (tap_index % 3 - 1) * dilation
            back_slab = window(
                grad_ext, row_count - row_shift, row_count - col_shift, row_count, col_count
            )
            columns = weight[tap_index]
            running = running + lax.dot_general(
                columns,
                back_slab.reshape(own_chans, pixels),
                (((0,), (0,)), ((), ())),
                preferred_element_type=jnp.float32,
            )
        input_grad = lax.psum_scatter(
            running.reshape(span_rows, row_count, col_count).astype(jnp.bfloat16),
            "ch",
            scatter_dimension=0,
            tiled=True,
        ).astype(jnp.float32)
        standard = (inputs_here.astype(jnp.float32) - pix_mean) * pix_rstd
        gain_step = jnp.sum(input_grad * standard, axis=(1, 2))
        scaled = input_grad * gain_own[:, None, None]
        grad_mean, grad_cross = lax.psum(
            (jnp.sum(scaled, axis=0), jnp.sum(scaled * standard, axis=0)), "ch"
        )
        grad_in = (
            grad_out.astype(jnp.float32)
            + pix_rstd * (scaled - grad_mean / all_chans - standard * (grad_cross / all_chans))
        ).astype(jnp.bfloat16)
        passed = passed_along(grad_in, "section", -1)
        return (
            passed,
            jnp.where(is_live, grad_weight + weight_step, grad_weight),
            jnp.where(is_live, grad_gain + gain_step, grad_gain),
        )

    initial_grads = (
        jnp.zeros((own_chans, row_count, col_count), jnp.bfloat16),
        jnp.zeros((9, own_chans, all_chans), jnp.float32),
        jnp.zeros((own_chans,), jnp.float32),
    )
    finished = lax.fori_loop(0, tick_count, backward_tick, initial_grads)
    weight_total, gain_total = (
        lax.psum(finished[1].astype(jnp.bfloat16), "slab").astype(jnp.float32),
        lax.psum(finished[2].astype(jnp.bfloat16), "slab").astype(jnp.float32),
    )
    return (weight_total[None], gain_total[None])


def solution(mesh):
    placed = (
        P(None, "ch", "slab", None),
        P(None, "ch", "slab", None),
        P("section", None, "ch", None),
        P("section", None),
    )
    return jax.shard_map(
        local,
        mesh=mesh,
        in_specs=placed,
        out_specs=(P("section", None, "ch", None), P("section", "ch")),
        check_vma=False,
    )
```

profile of v0, /device:TPU:33, one launch (start us, length us, event | category | flops | bytes accessed | tf_op | source)
XLA Modules:
  0.0 2308.8 jit_solution(15355007884547800855)
XLA Ops:
  15.7 1049.4 %while.47 = (s32[]{:T(128)}, bf16[24,8,128]{2,1,0:T(8,128)(2,1)S(1)}, bf16[4,384,24,144]{1,3,2,0:T(8,128)(2,1)}, f32[4,24,8,128]{3,2,1,0:T(8,128)S(1)}, f32[4,8,...) while((s32[]{:T(128)}, ...), condition=%wide.region_5.6_spmd, body=%wide.region_0.5_spmd.sunk | while | flops 172408832 | bytes 77751360 | solution.py:160
  18.0 44.1 %all-reduce.6 = (f32[8,128]{1,0:T(8,128)S(1)}, f32[8,128]{1,0:T(8,128)S(1)}) all-reduce(f32[8,128]{1,0:T(8,128)S(1)} %get-tuple-element.1489, f32[8,128]{1,0:T(8,128)S(1)} %get-tuple-element.1490), channel_id=1, replica_groups=mesh['section'=4,'ch'=16,'slab'=4] {'ch'}, use_global_device_ids=true, to_apply=%region_4.4 | all-reduce | flops 2048 | bytes 16384 | tf_op jit(solution)/shard_map/while/body/eval_jaxpr/psum | solution.py:61
  77.6 61.9 %all-gather.2.cloned.1.call-done = bf16[384,24,128]{2,1,0:T(8,128)(2,1)} async-done(((bf16[24,24,128]{2,1,0:T(8,128)(2,1)}), bf16[384,24,128]{2,1,0:T(8,128)(2,1)}) %all-gather.2.cloned.1.call-update) | async-done | bytes 2359312 | tf_op jit(solution)/shard_map/while/body/eval_jaxpr/all_gather | solution.py:69
  172.5 43.2 %all-reduce.6 = (f32[8,128]{1,0:T(8,128)S(1)}, f32[8,128]{1,0:T(8,128)S(1)}) all-reduce(f32[8,128]{1,0:T(8,128)S(1)} %get-tuple-element.1489, f32[8,128]{1,0:T(8,128)S(1)} %get-tuple-element.1490), channel_id=1, replica_groups=mesh['section'=4,'ch'=16,'slab'=4] {'ch'}, use_global_device_ids=true, to_apply=%region_4.4 | all-reduce | flops 2048 | bytes 16384 | tf_op jit(solution)/shard_map/while/body/eval_jaxpr/psum | solution.py:61
  231.2 57.4 %all-gather.2.cloned.1.call-done = bf16[384,24,128]{2,1,0:T(8,128)(2,1)} async-done(((bf16[24,24,128]{2,1,0:T(8,128)(2,1)}), bf16[384,24,128]{2,1,0:T(8,128)(2,1)}) %all-gather.2.cloned.1.call-update) | async-done | bytes 2359312 | tf_op jit(solution)/shard_map/while/body/eval_jaxpr/all_gather | solution.py:69
  321.6 43.2 %all-reduce.6 = (f32[8,128]{1,0:T(8,128)S(1)}, f32[8,128]{1,0:T(8,128)S(1)}) all-reduce(f32[8,128]{1,0:T(8,128)S(1)} %get-tuple-element.1489, f32[8,128]{1,0:T(8,128)S(1)} %get-tuple-element.1490), channel_id=1, replica_groups=mesh['section'=4,'ch'=16,'slab'=4] {'ch'}, use_global_device_ids=true, to_apply=%region_4.4 | all-reduce | flops 2048 | bytes 16384 | tf_op jit(solution)/shard_map/while/body/eval_jaxpr/psum | solution.py:61
  380.3 57.4 %all-gather.2.cloned.1.call-done = bf16[384,24,128]{2,1,0:T(8,128)(2,1)} async-done(((bf16[24,24,128]{2,1,0:T(8,128)(2,1)}), bf16[384,24,128]{2,1,0:T(8,128)(2,1)}) %all-gather.2.cloned.1.call-update) | async-done | bytes 2359312 | tf_op jit(solution)/shard_map/while/body/eval_jaxpr/all_gather | solution.py:69
  470.8 43.2 %all-reduce.6 = (f32[8,128]{1,0:T(8,128)S(1)}, f32[8,128]{1,0:T(8,128)S(1)}) all-reduce(f32[8,128]{1,0:T(8,128)S(1)} %get-tuple-element.1489, f32[8,128]{1,0:T(8,128)S(1)} %get-tuple-element.1490), channel_id=1, replica_groups=mesh['section'=4,'ch'=16,'slab'=4] {'ch'}, use_global_device_ids=true, to_apply=%region_4.4 | all-reduce | flops 2048 | bytes 16384 | tf_op jit(solution)/shard_map/while/body/eval_jaxpr/psum | solution.py:61
  529.4 57.4 %all-gather.2.cloned.1.call-done = bf16[384,24,128]{2,1,0:T(8,128)(2,1)} async-done(((bf16[24,24,128]{2,1,0:T(8,128)(2,1)}), bf16[384,24,128]{2,1,0:T(8,128)(2,1)}) %all-gather.2.cloned.1.call-update) | async-done | bytes 2359312 | tf_op jit(solution)/shard_map/while/body/eval_jaxpr/all_gather | solution.py:69
  619.8 43.2 %all-reduce.6 = (f32[8,128]{1,0:T(8,128)S(1)}, f32[8,128]{1,0:T(8,128)S(1)}) all-reduce(f32[8,128]{1,0:T(8,128)S(1)} %get-tuple-element.1489, f32[8,128]{1,0:T(8,128)S(1)} %get-tuple-element.1490), channel_id=1, replica_groups=mesh['section'=4,'ch'=16,'slab'=4] {'ch'}, use_global_device_ids=true, to_apply=%region_4.4 | all-reduce | flops 2048 | bytes 16384 | tf_op jit(solution)/shard_map/while/body/eval_jaxpr/psum | solution.py:61
  678.5 57.4 %all-gather.2.cloned.1.call-done = bf16[384,24,128]{2,1,0:T(8,128)(2,1)} async-done(((bf16[24,24,128]{2,1,0:T(8,128)(2,1)}), bf16[384,24,128]{2,1,0:T(8,128)(2,1)}) %all-gather.2.cloned.1.call-update) | async-done | bytes 2359312 | tf_op jit(solution)/shard_map/while/body/eval_jaxpr/all_gather | solution.py:69
  769.0 43.2 %all-reduce.6 = (f32[8,128]{1,0:T(8,128)S(1)}, f32[8,128]{1,0:T(8,128)S(1)}) all-reduce(f32[8,128]{1,0:T(8,128)S(1)} %get-tuple-element.1489, f32[8,128]{1,0:T(8,128)S(1)} %get-tuple-element.1490), channel_id=1, replica_groups=mesh['section'=4,'ch'=16,'slab'=4] {'ch'}, use_global_device_ids=true, to_apply=%region_4.4 | all-reduce | flops 2048 | bytes 16384 | tf_op jit(solution)/shard_map/while/body/eval_jaxpr/psum | solution.py:61
  827.7 57.4 %all-gather.2.cloned.1.call-done = bf16[384,24,128]{2,1,0:T(8,128)(2,1)} async-done(((bf16[24,24,128]{2,1,0:T(8,128)(2,1)}), bf16[384,24,128]{2,1,0:T(8,128)(2,1)}) %all-gather.2.cloned.1.call-update) | async-done | bytes 2359312 | tf_op jit(solution)/shard_map/while/body/eval_jaxpr/all_gather | solution.py:69
  918.2 43.2 %all-reduce.6 = (f32[8,128]{1,0:T(8,128)S(1)}, f32[8,128]{1,0:T(8,128)S(1)}) all-reduce(f32[8,128]{1,0:T(8,128)S(1)} %get-tuple-element.1489, f32[8,128]{1,0:T(8,128)S(1)} %get-tuple-element.1490), channel_id=1, replica_groups=mesh['section'=4,'ch'=16,'slab'=4] {'ch'}, use_global_device_ids=true, to_apply=%region_4.4 | all-reduce | flops 2048 | bytes 16384 | tf_op jit(solution)/shard_map/while/body/eval_jaxpr/psum | solution.py:61
  976.9 57.4 %all-gather.2.cloned.1.call-done = bf16[384,24,128]{2,1,0:T(8,128)(2,1)} async-done(((bf16[24,24,128]{2,1,0:T(8,128)(2,1)}), bf16[384,24,128]{2,1,0:T(8,128)(2,1)}) %all-gather.2.cloned.1.call-update) | async-done | bytes 2359312 | tf_op jit(solution)/shard_map/while/body/eval_jaxpr/all_gather | solution.py:69
  1065.1 1191.2 %while.48 = (s32[]{:T(128)}, bf16[24,8,128]{2,1,0:T(8,128)(2,1)S(1)}, f32[9,24,384]{2,1,0:T(8,128)}, f32[24]{0:T(128)S(1)}, pred[]{:T(512)}, /*index=5*/s32[]{:T...) while((s32[]{:T(128)}, ...), condition=%wide.region_13.14_spmd.clone, body=%wide.region_6.13_spmd.clone.sunk | while | flops 345605152 | bytes 84956496 | solution.py:228
  1113.1 70.6 %reduce-scatter.2.cloned.1.call-done = bf16[24,8,128]{2,1,0:T(8,128)(2,1)} async-done(((bf16[384,8,128]{2,1,0:T(8,128)(2,1)}), bf16[24,8,128]{2,1,0:T(8,128)(2,1)}) %reduce-scatter.2.cloned.1.call-update) | async-done | bytes 49168 | tf_op jit(solution)/shard_map/while/body/eval_jaxpr/reduce_scatter | solution.py:200
  1184.8 45.1 %all-reduce.7 = (f32[8,128]{1,0:T(8,128)S(1)}, f32[8,128]{1,0:T(8,128)S(1)}) all-reduce(f32[8,128]{1,0:T(8,128)S(1)} %get-tuple-element.1538, f32[8,128]{1,0:T(8,128)S(1)} %get-tuple-element.1539), channel_id=1, replica_groups=mesh['section'=4,'ch'=16,'slab'=4] {'ch'}, use_global_device_ids=true, to_apply=%region_11.11 | all-reduce | flops 2048 | bytes 16384 | tf_op jit(solution)/shard_map/while/body/eval_jaxpr/psum | solution.py:209
  1283.6 70.3 %reduce-scatter.2.cloned.1.call-done = bf16[24,8,128]{2,1,0:T(8,128)(2,1)} async-done(((bf16[384,8,128]{2,1,0:T(8,128)(2,1)}), bf16[24,8,128]{2,1,0:T(8,128)(2,1)}) %reduce-scatter.2.cloned.1.call-update) | async-done | bytes 49168 | tf_op jit(solution)/shard_map/while/body/eval_jaxpr/reduce_scatter | solution.py:200
  1355.0 45.1 %all-reduce.7 = (f32[8,128]{1,0:T(8,128)S(1)}, f32[8,128]{1,0:T(8,128)S(1)}) all-reduce(f32[8,128]{1,0:T(8,128)S(1)} %get-tuple-element.1538, f32[8,128]{1,0:T(8,128)S(1)} %get-tuple-element.1539), channel_id=1, replica_groups=mesh['section'=4,'ch'=16,'slab'=4] {'ch'}, use_global_device_ids=true, to_apply=%region_11.11 | all-reduce | flops 2048 | bytes 16384 | tf_op jit(solution)/shard_map/while/body/eval_jaxpr/psum | solution.py:209
  1453.7 69.9 %reduce-scatter.2.cloned.1.call-done = bf16[24,8,128]{2,1,0:T(8,128)(2,1)} async-done(((bf16[384,8,128]{2,1,0:T(8,128)(2,1)}), bf16[24,8,128]{2,1,0:T(8,128)(2,1)}) %reduce-scatter.2.cloned.1.call-update) | async-done | bytes 49168 | tf_op jit(solution)/shard_map/while/body/eval_jaxpr/reduce_scatter | solution.py:200
  1524.8 45.1 %all-reduce.7 = (f32[8,128]{1,0:T(8,128)S(1)}, f32[8,128]{1,0:T(8,128)S(1)}) all-reduce(f32[8,128]{1,0:T(8,128)S(1)} %get-tuple-element.1538, f32[8,128]{1,0:T(8,128)S(1)} %get-tuple-element.1539), channel_id=1, replica_groups=mesh['section'=4,'ch'=16,'slab'=4] {'ch'}, use_global_device_ids=true, to_apply=%region_11.11 | all-reduce | flops 2048 | bytes 16384 | tf_op jit(solution)/shard_map/while/body/eval_jaxpr/psum | solution.py:209
  1623.2 70.5 %reduce-scatter.2.cloned.1.call-done = bf16[24,8,128]{2,1,0:T(8,128)(2,1)} async-done(((bf16[384,8,128]{2,1,0:T(8,128)(2,1)}), bf16[24,8,128]{2,1,0:T(8,128)(2,1)}) %reduce-scatter.2.cloned.1.call-update) | async-done | bytes 49168 | tf_op jit(solution)/shard_map/while/body/eval_jaxpr/reduce_scatter | solution.py:200
  1694.8 45.1 %all-reduce.7 = (f32[8,128]{1,0:T(8,128)S(1)}, f32[8,128]{1,0:T(8,128)S(1)}) all-reduce(f32[8,128]{1,0:T(8,128)S(1)} %get-tuple-element.1538, f32[8,128]{1,0:T(8,128)S(1)} %get-tuple-element.1539), channel_id=1, replica_groups=mesh['section'=4,'ch'=16,'slab'=4] {'ch'}, use_global_device_ids=true, to_apply=%region_11.11 | all-reduce | flops 2048 | bytes 16384 | tf_op jit(solution)/shard_map/while/body/eval_jaxpr/psum | solution.py:209
  1793.4 70.5 %reduce-scatter.2.cloned.1.call-done = bf16[24,8,128]{2,1,0:T(8,128)(2,1)} async-done(((bf16[384,8,128]{2,1,0:T(8,128)(2,1)}), bf16[24,8,128]{2,1,0:T(8,128)(2,1)}) %reduce-scatter.2.cloned.1.call-update) | async-done | bytes 49168 | tf_op jit(solution)/shard_map/while/body/eval_jaxpr/reduce_scatter | solution.py:200
  1864.9 45.1 %all-reduce.7 = (f32[8,128]{1,0:T(8,128)S(1)}, f32[8,128]{1,0:T(8,128)S(1)}) all-reduce(f32[8,128]{1,0:T(8,128)S(1)} %get-tuple-element.1538, f32[8,128]{1,0:T(8,128)S(1)} %get-tuple-element.1539), channel_id=1, replica_groups=mesh['section'=4,'ch'=16,'slab'=4] {'ch'}, use_global_device_ids=true, to_apply=%region_11.11 | all-reduce | flops 2048 | bytes 16384 | tf_op jit(solution)/shard_map/while/body/eval_jaxpr/psum | solution.py:209
  1963.7 70.4 %reduce-scatter.2.cloned.1.call-done = bf16[24,8,128]{2,1,0:T(8,128)(2,1)} async-done(((bf16[384,8,128]{2,1,0:T(8,128)(2,1)}), bf16[24,8,128]{2,1,0:T(8,128)(2,1)}) %reduce-scatter.2.cloned.1.call-update) | async-done | bytes 49168 | tf_op jit(solution)/shard_map/while/body/eval_jaxpr/reduce_scatter | solution.py:200
  2035.2 45.2 %all-reduce.7 = (f32[8,128]{1,0:T(8,128)S(1)}, f32[8,128]{1,0:T(8,128)S(1)}) all-reduce(f32[8,128]{1,0:T(8,128)S(1)} %get-tuple-element.1538, f32[8,128]{1,0:T(8,128)S(1)} %get-tuple-element.1539), channel_id=1, replica_groups=mesh['section'=4,'ch'=16,'slab'=4] {'ch'}, use_global_device_ids=true, to_apply=%region_11.11 | all-reduce | flops 2048 | bytes 16384 | tf_op jit(solution)/shard_map/while/body/eval_jaxpr/psum | solution.py:209
  2134.0 70.2 %reduce-scatter.2.cloned.1.call-done = bf16[24,8,128]{2,1,0:T(8,128)(2,1)} async-done(((bf16[384,8,128]{2,1,0:T(8,128)(2,1)}), bf16[24,8,128]{2,1,0:T(8,128)(2,1)}) %reduce-scatter.2.cloned.1.call-update) | async-done | bytes 49168 | tf_op jit(solution)/shard_map/while/body/eval_jaxpr/reduce_scatter | solution.py:200
  2205.3 45.2 %all-reduce.7 = (f32[8,128]{1,0:T(8,128)S(1)}, f32[8,128]{1,0:T(8,128)S(1)}) all-reduce(f32[8,128]{1,0:T(8,128)S(1)} %get-tuple-element.1538, f32[8,128]{1,0:T(8,128)S(1)} %get-tuple-element.1539), channel_id=1, replica_groups=mesh['section'=4,'ch'=16,'slab'=4] {'ch'}, use_global_device_ids=true, to_apply=%region_11.11 | all-reduce | flops 2048 | bytes 16384 | tf_op jit(solution)/shard_map/while/body/eval_jaxpr/psum | solution.py:209
  2258.1 8.4 psum.75
  2267.0 33.0 %all-reduce.10.cloned.1.call-done = bf16[1,9,24,384]{3,2,1,0:T(8,128)(2,1)} async-done(((bf16[1,9,24,384]{3,2,1,0:T(8,128)(2,1)}), bf16[1,9,24,384]{3,2,1,0:T(8,128)(2,1)}) %all-reduce.10.cloned.1.call-update) | async-done | bytes 165904 | tf_op jit(solution)/shard_map/psum | solution.py:230
  (685 shorter events, 731.0 us)
Async XLA Ops:
  15.7 123.8 %all-gather.2.cloned.1.call-start = ((), (), s32[]{:S(2)}) async-start(), calls=%async_computation.2 | async-start | bytes 2506752 | tf_op jit(solution)/shard_map/while/body/eval_jaxpr/all_gather | solution.py:69
  170.2 118.4 %all-gather.2.cloned.1.call-start = ((), (), s32[]{:S(2)}) async-start(), calls=%async_computation.2 | async-start | bytes 2506752 | tf_op jit(solution)/shard_map/while/body/eval_jaxpr/all_gather | solution.py:69
  319.3 118.4 %all-gather.2.cloned.1.call-start = ((), (), s32[]{:S(2)}) async-start(), calls=%async_computation.2 | async-start | bytes 2506752 | tf_op jit(solution)/shard_map/while/body/eval_jaxpr/all_gather | solution.py:69
  468.5 118.4 %all-gather.2.cloned.1.call-start = ((), (), s32[]{:S(2)}) async-start(), calls=%async_computation.2 | async-start | bytes 2506752 | tf_op jit(solution)/shard_map/while/body/eval_jaxpr/all_gather | solution.py:69
  617.5 118.4 %all-gather.2.cloned.1.call-start = ((), (), s32[]{:S(2)}) async-start(), calls=%async_computation.2 | async-start | bytes 2506752 | tf_op jit(solution)/shard_map/while/body/eval_jaxpr/all_gather | solution.py:69
  752.6 14.1 collective-permute-start.2
  766.7 118.4 %all-gather.2.cloned.1.call-start = ((), (), s32[]{:S(2)}) async-start(), calls=%async_computation.2 | async-start | bytes 2506752 | tf_op jit(solution)/shard_map/while/body/eval_jaxpr/all_gather | solution.py:69
  901.8 14.1 collective-permute-start.2
  915.9 118.4 %all-gather.2.cloned.1.call-start = ((), (), s32[]{:S(2)}) async-start(), calls=%async_computation.2 | async-start | bytes 2506752 | tf_op jit(solution)/shard_map/while/body/eval_jaxpr/all_gather | solution.py:69
  1051.0 14.1 collective-permute-start.2
  1065.3 118.4 %reduce-scatter.2.cloned.1.call-start = ((), (), s32[]{:S(2)}) async-start(), calls=%async_computation.3 | async-start | bytes 835584 | tf_op jit(solution)/shard_map/while/body/eval_jaxpr/reduce_scatter | solution.py:200
  1066.3 32.3 %collective-permute-start.3 = (bf16[24,8,128]{2,1,0:T(8,128)(2,1)S(1)}, bf16[24,8,128]{2,1,0:T(8,128)(2,1)S(1)}, u32[]{:S(2)}, u32[]{:S(2)}) collective-permute-start(bf16[24,8,128]{2,1,0:T(8,128)(2,1)S(1)} %fusion.302), channel_id=1, source_target_pairs={{1,0},{2,1},{3,2},{5,4},{6,5},{7,6},{9,8},{10,9},{11,10},{13,12},{... | collective-permute-start | bytes 147464 | tf_op jit(solution)/shard_map/while/body/eval_jaxpr/ppermute | solution.py:21
  1067.6 31.0 %collective-permute-start.4 = (bf16[24,8,128]{2,1,0:T(8,128)(2,1)S(1)}, bf16[24,8,128]{2,1,0:T(8,128)(2,1)}, u32[]{:S(2)}, u32[]{:S(2)}) collective-permute-start(bf16[24,8,128]{2,1,0:T(8,128)(2,1)S(1)} %fusion.302), channel_id=1, source_target_pairs={{0,1},{1,2},{2,3},{4,5},{5,6},{6,7},{8,9},{9,10},{10,11},{12,13},{... | collective-permute-start | bytes 147464 | tf_op jit(solution)/shard_map/while/body/eval_jaxpr/ppermute | solution.py:19
  1235.8 118.1 %reduce-scatter.2.cloned.1.call-start = ((), (), s32[]{:S(2)}) async-start(), calls=%async_computation.3 | async-start | bytes 835584 | tf_op jit(solution)/shard_map/while/body/eval_jaxpr/reduce_scatter | solution.py:200
  1236.8 32.3 %collective-permute-start.3 = (bf16[24,8,128]{2,1,0:T(8,128)(2,1)S(1)}, bf16[24,8,128]{2,1,0:T(8,128)(2,1)S(1)}, u32[]{:S(2)}, u32[]{:S(2)}) collective-permute-start(bf16[24,8,128]{2,1,0:T(8,128)(2,1)S(1)} %fusion.302), channel_id=1, source_target_pairs={{1,0},{2,1},{3,2},{5,4},{6,5},{7,6},{9,8},{10,9},{11,10},{13,12},{... | collective-permute-start | bytes 147464 | tf_op jit(solution)/shard_map/while/body/eval_jaxpr/ppermute | solution.py:21
  1238.1 31.0 %collective-permute-start.4 = (bf16[24,8,128]{2,1,0:T(8,128)(2,1)S(1)}, bf16[24,8,128]{2,1,0:T(8,128)(2,1)}, u32[]{:S(2)}, u32[]{:S(2)}) collective-permute-start(bf16[24,8,128]{2,1,0:T(8,128)(2,1)S(1)} %fusion.302), channel_id=1, source_target_pairs={{0,1},{1,2},{2,3},{4,5},{5,6},{6,7},{8,9},{9,10},{10,11},{12,13},{... | collective-permute-start | bytes 147464 | tf_op jit(solution)/shard_map/while/body/eval_jaxpr/ppermute | solution.py:19
  1406.0 117.7 %reduce-scatter.2.cloned.1.call-start = ((), (), s32[]{:S(2)}) async-start(), calls=%async_computation.3 | async-start | bytes 835584 | tf_op jit(solution)/shard_map/while/body/eval_jaxpr/reduce_scatter | solution.py:200
  1407.0 32.3 %collective-permute-start.3 = (bf16[24,8,128]{2,1,0:T(8,128)(2,1)S(1)}, bf16[24,8,128]{2,1,0:T(8,128)(2,1)S(1)}, u32[]{:S(2)}, u32[]{:S(2)}) collective-permute-start(bf16[24,8,128]{2,1,0:T(8,128)(2,1)S(1)} %fusion.302), channel_id=1, source_target_pairs={{1,0},{2,1},{3,2},{5,4},{6,5},{7,6},{9,8},{10,9},{11,10},{13,12},{... | collective-permute-start | bytes 147464 | tf_op jit(solution)/shard_map/while/body/eval_jaxpr/ppermute | solution.py:21
  1408.3 31.0 %collective-permute-start.4 = (bf16[24,8,128]{2,1,0:T(8,128)(2,1)S(1)}, bf16[24,8,128]{2,1,0:T(8,128)(2,1)}, u32[]{:S(2)}, u32[]{:S(2)}) collective-permute-start(bf16[24,8,128]{2,1,0:T(8,128)(2,1)S(1)} %fusion.302), channel_id=1, source_target_pairs={{0,1},{1,2},{2,3},{4,5},{5,6},{6,7},{8,9},{9,10},{10,11},{12,13},{... | collective-permute-start | bytes 147464 | tf_op jit(solution)/shard_map/while/body/eval_jaxpr/ppermute | solution.py:19
  1575.8 117.9 %reduce-scatter.2.cloned.1.call-start = ((), (), s32[]{:S(2)}) async-start(), calls=%async_computation.3 | async-start | bytes 835584 | tf_op jit(solution)/shard_map/while/body/eval_jaxpr/reduce_scatter | solution.py:200
  1576.8 31.9 %collective-permute-start.3 = (bf16[24,8,128]{2,1,0:T(8,128)(2,1)S(1)}, bf16[24,8,128]{2,1,0:T(8,128)(2,1)S(1)}, u32[]{:S(2)}, u32[]{:S(2)}) collective-permute-start(bf16[24,8,128]{2,1,0:T(8,128)(2,1)S(1)} %fusion.302), channel_id=1, source_target_pairs={{1,0},{2,1},{3,2},{5,4},{6,5},{7,6},{9,8},{10,9},{11,10},{13,12},{... | collective-permute-start | bytes 147464 | tf_op jit(solution)/shard_map/while/body/eval_jaxpr/ppermute | solution.py:21
  1578.1 30.7 %collective-permute-start.4 = (bf16[24,8,128]{2,1,0:T(8,128)(2,1)S(1)}, bf16[24,8,128]{2,1,0:T(8,128)(2,1)}, u32[]{:S(2)}, u32[]{:S(2)}) collective-permute-start(bf16[24,8,128]{2,1,0:T(8,128)(2,1)S(1)} %fusion.302), channel_id=1, source_target_pairs={{0,1},{1,2},{2,3},{4,5},{5,6},{6,7},{8,9},{9,10},{10,11},{12,13},{... | collective-permute-start | bytes 147464 | tf_op jit(solution)/shard_map/while/body/eval_jaxpr/ppermute | solution.py:19
  1745.8 118.1 %reduce-scatter.2.cloned.1.call-start = ((), (), s32[]{:S(2)}) async-start(), calls=%async_computation.3 | async-start | bytes 835584 | tf_op jit(solution)/shard_map/while/body/eval_jaxpr/reduce_scatter | solution.py:200
  1746.8 32.1 %collective-permute-start.3 = (bf16[24,8,128]{2,1,0:T(8,128)(2,1)S(1)}, bf16[24,8,128]{2,1,0:T(8,128)(2,1)S(1)}, u32[]{:S(2)}, u32[]{:S(2)}) collective-permute-start(bf16[24,8,128]{2,1,0:T(8,128)(2,1)S(1)} %fusion.302), channel_id=1, source_target_pairs={{1,0},{2,1},{3,2},{5,4},{6,5},{7,6},{9,8},{10,9},{11,10},{13,12},{... | collective-permute-start | bytes 147464 | tf_op jit(solution)/shard_map/while/body/eval_jaxpr/ppermute | solution.py:21
  1748.1 30.8 %collective-permute-start.4 = (bf16[24,8,128]{2,1,0:T(8,128)(2,1)S(1)}, bf16[24,8,128]{2,1,0:T(8,128)(2,1)}, u32[]{:S(2)}, u32[]{:S(2)}) collective-permute-start(bf16[24,8,128]{2,1,0:T(8,128)(2,1)S(1)} %fusion.302), channel_id=1, source_target_pairs={{0,1},{1,2},{2,3},{4,5},{5,6},{6,7},{8,9},{9,10},{10,11},{12,13},{... | collective-permute-start | bytes 147464 | tf_op jit(solution)/shard_map/while/body/eval_jaxpr/ppermute | solution.py:19
  1915.9 118.2 %reduce-scatter.2.cloned.1.call-start = ((), (), s32[]{:S(2)}) async-start(), calls=%async_computation.3 | async-start | bytes 835584 | tf_op jit(solution)/shard_map/while/body/eval_jaxpr/reduce_scatter | solution.py:200
  1916.9 32.3 %collective-permute-start.3 = (bf16[24,8,128]{2,1,0:T(8,128)(2,1)S(1)}, bf16[24,8,128]{2,1,0:T(8,128)(2,1)S(1)}, u32[]{:S(2)}, u32[]{:S(2)}) collective-permute-start(bf16[24,8,128]{2,1,0:T(8,128)(2,1)S(1)} %fusion.302), channel_id=1, source_target_pairs={{1,0},{2,1},{3,2},{5,4},{6,5},{7,6},{9,8},{10,9},{11,10},{13,12},{... | collective-permute-start | bytes 147464 | tf_op jit(solution)/shard_map/while/body/eval_jaxpr/ppermute | solution.py:21
  1918.2 31.0 %collective-permute-start.4 = (bf16[24,8,128]{2,1,0:T(8,128)(2,1)S(1)}, bf16[24,8,128]{2,1,0:T(8,128)(2,1)}, u32[]{:S(2)}, u32[]{:S(2)}) collective-permute-start(bf16[24,8,128]{2,1,0:T(8,128)(2,1)S(1)} %fusion.302), channel_id=1, source_target_pairs={{0,1},{1,2},{2,3},{4,5},{5,6},{6,7},{8,9},{9,10},{10,11},{12,13},{... | collective-permute-start | bytes 147464 | tf_op jit(solution)/shard_map/while/body/eval_jaxpr/ppermute | solution.py:19
  2086.2 118.0 %reduce-scatter.2.cloned.1.call-start = ((), (), s32[]{:S(2)}) async-start(), calls=%async_computation.3 | async-start | bytes 835584 | tf_op jit(solution)/shard_map/while/body/eval_jaxpr/reduce_scatter | solution.py:200
  2087.2 32.3 %collective-permute-start.3 = (bf16[24,8,128]{2,1,0:T(8,128)(2,1)S(1)}, bf16[24,8,128]{2,1,0:T(8,128)(2,1)S(1)}, u32[]{:S(2)}, u32[]{:S(2)}) collective-permute-start(bf16[24,8,128]{2,1,0:T(8,128)(2,1)S(1)} %fusion.302), channel_id=1, source_target_pairs={{1,0},{2,1},{3,2},{5,4},{6,5},{7,6},{9,8},{10,9},{11,10},{13,12},{... | collective-permute-start | bytes 147464 | tf_op jit(solution)/shard_map/while/body/eval_jaxpr/ppermute | solution.py:21
  2088.5 31.0 %collective-permute-start.4 = (bf16[24,8,128]{2,1,0:T(8,128)(2,1)S(1)}, bf16[24,8,128]{2,1,0:T(8,128)(2,1)}, u32[]{:S(2)}, u32[]{:S(2)}) collective-permute-start(bf16[24,8,128]{2,1,0:T(8,128)(2,1)S(1)} %fusion.302), channel_id=1, source_target_pairs={{0,1},{1,2},{2,3},{4,5},{5,6},{6,7},{8,9},{9,10},{10,11},{12,13},{... | collective-permute-start | bytes 147464 | tf_op jit(solution)/shard_map/while/body/eval_jaxpr/ppermute | solution.py:19
  2256.3 43.7 %all-reduce.10.cloned.1.call-start = ((), (), s32[]{:S(2)}) async-start(), calls=%async_computation.1 | async-start | bytes 331776 | tf_op jit(solution)/shard_map/psum | solution.py:230
  (104 other events, 2266.5 us)
Sparse Core Ops, SparseCore 0:
  70.8 68.6 all-gather.1
  224.4 64.1 all-gather.1
  373.5 64.1 all-gather.1
  522.6 64.1 all-gather.1
  671.7 64.1 all-gather.1
  820.9 64.1 all-gather.1
  970.1 64.1 all-gather.1
  1111.0 72.7 reduce-scatter.1
  1281.4 72.3 reduce-scatter.1
  1451.6 72.0 reduce-scatter.1
  1621.1 72.5 reduce-scatter.1
  1791.2 72.5 reduce-scatter.1
  1961.6 72.4 reduce-scatter.1
  2131.8 72.3 reduce-scatter.1
Sparse Core Ops, SparseCore 1:
  2259.1 40.9 all-reduce.9
where the time goes:
time: 2320 us; the launch traced here: 2310 us
  waiting for transfers between devices  951 us (41%)
  blocking collectives  628 us (27%)
  local copies, waits for them, and re-layouts  281 us (12%)
  matrix products  224 us (10%)
  starting transfers between devices  119 us (5%)
  other arithmetic  86.6 us (4%)
    reduce_scatter x7, waiting for transfers between devices, backward_tick(): lax.psum_scatter(running.reshape(span_rows, row_count, col_count).astype(...  492 us
    all_gather x7, waiting for transfers between devices, normalized(): gathered_unit = lax.all_gather(rimmed, 'ch', axis=0, tiled=True)  406 us
    psum x7, blocking collectives, backward_tick(): lax.psum((jnp.sum(scaled, axis=0), jnp.sum(scaled * standard, axis=0)), '...  316 us
    psum x7, blocking collectives, normalized(): lax.psum((jnp.sum(values, axis=0), jnp.sum(values * values, axis=0)), 'ch')  303 us
    dynamic_slice x21, local copies, waits for them, and re-layouts, window(): lax.dynamic_slice(extended, (anchor, row_start, col_start), (extended.sha...  105 us
    dot_general x63, matrix products, backward_tick(): lax.dot_general(columns, back_slab.reshape(own_chans, pixels), (((0,), (0...  81.9 us
    dot_general x63, matrix products, weight_terms(): lax.dot_general(flat_grad, tap_slab.reshape(all_chans, row_count * col_co...  78.9 us
    dot_general x63, matrix products, convolve(): jnp.dot(weight[tap_index], tap_slab.reshape(all_chans, row_count * col_co...  63.6 us
  transfers between devices with their start and end apart: 57, of which 29 were waited for; matrix products, arithmetic and copies ran while one was open for 14% of the time, Pallas kernels for 0%

commit v1 on v0

v1 whole, which is shorter than its diff:
```python
import functools

import jax
import jax.numpy as jnp
import numpy as np
from jax import lax
from jax.experimental import pallas as pl
from jax.experimental.pallas import tpu as pltpu
from jax.sharding import Mesh, PartitionSpec as P

NORM_EPS = 1e-05
SLOPE_SCALE = 0.7978845608028654
CUBIC_COEF = 0.044715
BF = jnp.bfloat16
F32 = jnp.float32

ROWS = 32
CHANS = 384
HALF = 192
TAPS = 9
DIL = (1, 2, 4, 8)
OWN = 16
XWIN = 80
CWIN = 48
PAD = 8
X_WIN = ((0, 80), (0, 80), (0, 80), (8, 64), (16, 48))
S_WIN = ((32, 16), (24, 32), (24, 32), (16, 48))
VMEM_LIMIT = 56 * 1024 * 1024
PARAMS = pltpu.CompilerParams(vmem_limit_bytes=VMEM_LIMIT)
NT = (((1,), (1,)), ((), ()))
NN = (((1,), (0,)), ((), ()))


def dot(a, b, dims):
    return lax.dot_general(a, b, dims, preferred_element_type=F32)


def call(kernel, out_shape, scratch, args, smem=()):
    vm = pl.BlockSpec(memory_space=pltpu.VMEM)
    sm = pl.BlockSpec(memory_space=pltpu.SMEM)
    return pl.pallas_call(
        kernel,
        out_shape=out_shape,
        in_specs=[sm if i in smem else vm for i in range(len(args))],
        out_specs=jax.tree.map(lambda _: vm, out_shape),
        scratch_shapes=scratch,
        compiler_params=PARAMS,
    )(*args)


def shape(dims, dtype):
    return jax.ShapeDtypeStruct(dims, dtype)


def row_loop(body, unroll=4):
    def step(i, carry):
        for k in range(unroll):
            body(i * unroll + k)
        return carry

    lax.fori_loop(0, ROWS // unroll, step, 0)


def in_image(base, first, count, width):
    cols = lax.broadcasted_iota(jnp.int32, (count, HALF), 0) + (base - 32 + first)
    return (cols >= 0) & (cols < width)


def stats(xo, xt):
    mean = (jnp.sum(xo, axis=1, keepdims=True) + jnp.sum(xt, axis=1, keepdims=True)) / CHANS
    square = (
        jnp.sum(xo * xo, axis=1, keepdims=True) + jnp.sum(xt * xt, axis=1, keepdims=True)
    ) / CHANS
    return mean, lax.rsqrt(square - mean * mean + NORM_EPS)


def gelu_parts(pre):
    tangent = jnp.tanh(SLOPE_SCALE * (pre + CUBIC_COEF * pre * pre * pre))
    value = 0.5 * pre * (1.0 + tangent)
    slope = 0.5 * (1.0 + tangent) + 0.5 * pre * (1.0 - tangent * tangent) * SLOPE_SCALE * (
        1.0 + 3.0 * CUBIC_COEF * pre * pre
    )
    return value, slope


def prep_kernel(w_ref, perm_ref, out_ref):
    for t in range(TAPS):
        out_ref[:, t * CHANS : (t + 1) * CHANS] = dot(w_ref[t], perm_ref[...], NN).astype(BF)


def assemble_kernel(slabs, rows, recv_ref, x_ref, cot_ref):
    lanes = XWIN + CWIN
    eye = (
        lax.broadcasted_iota(jnp.int32, (lanes, lanes), 0)
        == lax.broadcasted_iota(jnp.int32, (lanes, lanes), 1)
    ).astype(F32).astype(BF)

    def one(r, carry):
        for y in range(slabs):
            piece = recv_ref[:, y, pl.ds(r, 1)].astype(F32)
            piece = piece.reshape(HALF, lanes).astype(BF)
            flipped = dot(eye, piece, NT).astype(BF)
            x_ref[pl.ds(y * rows + r, 1)] = flipped[:XWIN].reshape(1, XWIN, HALF)
            cot_ref[pl.ds(y * rows + r, 1)] = flipped[XWIN:].reshape(1, CWIN, HALF)
        return carry

    lax.fori_loop(0, rows, one, 0)


def norm_phase(block, xo_ref, xt_ref, gain_ref, nbuf, nk):
    d = DIL[block]
    first_in, width_in = X_WIN[block]
    first_out, width_out = X_WIN[block + 1]
    low = first_out - first_in
    own = 32 - first_in
    for edge in (0, PAD + ROWS):
        nbuf[edge : edge + PAD] = jnp.zeros((PAD, width_out, 3 * CHANS), BF)
        nk[edge : edge + PAD] = jnp.zeros((PAD, OWN, 3 * CHANS), BF)
    gain = gain_ref[...]

    def one(r):
        xo = xo_ref[r].astype(F32)
        xt = xt_ref[r].astype(F32)
        mean, rstd = stats(xo, xt)
        both = jnp.concatenate([(xo - mean) * rstd, (xt - mean) * rstd], axis=1) * gain
        for kx in range(3):
            shift = (-(kx - 1) * d) % width_in
            moved = pltpu.roll(both, shift, 0) if shift else both
            lanes = slice(kx * CHANS, (kx + 1) * CHANS)
            nbuf[PAD + r, :, lanes] = moved[low : low + width_out].astype(BF)
            nk[PAD + r, :, lanes] = moved[own : own + OWN].astype(BF)

    row_loop(one, 2)


def conv_phase(block, nbuf, w_ref, pre):
    d = DIL[block]
    width = X_WIN[block + 1][1]
    step = 8

    def one(i, carry):
        r0 = i * step
        acc = None
        for ky in range(3):
            left = nbuf[pl.ds(PAD + r0 + (ky - 1) * d, step)].reshape(step * width, 3 * CHANS)
            term = dot(left, w_ref[:, ky * 3 * CHANS : (ky + 1) * 3 * CHANS], NT)
            acc = term if acc is None else acc + term
        pre[pl.ds(r0, step)] = acc.reshape(step, width, HALF)
        return carry

    lax.fori_loop(0, ROWS // step, one, 0)


def forward_kernel(block, image, idx_ref, xo_ref, xt_ref, w_ref, gain_ref, y_ref, d_ref, nk, nbuf, pre):
    first_in = X_WIN[block][0]
    first_out, width_out = X_WIN[block + 1]
    first_s, width_s = S_WIN[block]
    norm_phase(block, xo_ref, xt_ref, gain_ref, nbuf, nk)
    conv_phase(block, nbuf, w_ref, pre)
    live = in_image(idx_ref[0], first_out, width_out, image)
    low, at = first_out - first_in, first_s - first_out

    def one(r):
        value, slope = gelu_parts(pre[r])
        out = xo_ref[r].astype(F32)[low : low + width_out] + value
        y_ref[r] = jnp.where(live, out, 0.0).astype(BF)
        d_ref[r] = slope[at : at + width_s]

    row_loop(one, 2)


def scatter_s(block, s, r, sbuf, sown):
    first, width = S_WIN[block]
    sown[r] = s[32 - first : 32 - first + OWN].astype(BF)
    if sbuf is None:
        return
    d = DIL[block]
    first_q, width_q = S_WIN[block - 1]
    low = first_q - first
    gap = jnp.zeros((width_q, 256 - HALF), F32)
    for kx in range(3):
        shift = ((kx - 1) * d) % width
        moved = (pltpu.roll(s, shift, 0) if shift else s)[low : low + width_q]
        sbuf[PAD + r, :, kx * 256 : (kx + 1) * 256] = jnp.concatenate([moved, gap], axis=1).astype(BF)


def q_phase(block, sbuf, w_ref, wq, q_ref):
    d = DIL[block]
    width = S_WIN[block - 1][1]
    for ky in range(3):
        for kx in range(3):
            t = 3 * ky + kx
            wq[ky, kx * 256 : kx * 256 + HALF] = w_ref[:, t * CHANS : (t + 1) * CHANS]
            wq[ky, kx * 256 + HALF : (kx + 1) * 256] = jnp.zeros((256 - HALF, CHANS), BF)
    for edge in (0, PAD + ROWS):
        sbuf[edge : edge + PAD] = jnp.zeros((PAD, width, 768), BF)
    step = 512 // width

    def one(i, carry):
        r0 = i * step
        acc = None
        for ky in range(3):
            left = sbuf[pl.ds(PAD + r0 - (ky - 1) * d, step)].reshape(step * width, 768)
            term = dot(left, wq[ky], NN)
            acc = term if acc is None else acc + term
        q_ref[0, pl.ds(r0, step)] = acc[:, HALF:].reshape(step, width, HALF).astype(BF)
        q_ref[1, pl.ds(r0, step)] = acc[:, :HALF].reshape(step, width, HALF).astype(BF)
        return carry

    lax.fori_loop(0, ROWS // step, one, 0)


def weight_phase(block, dims, idx_ref, sown, nk, w_ref, gain_ref, wg_ref):
    own_chans, share, lines = dims
    d = DIL[block]
    count = (HALF // own_chans) * lines
    bits = lines.bit_length() - 1
    line = lax.broadcasted_iota(jnp.int32, (count, HALF), 0)
    place = jnp.bitwise_and(line, lines - 1)
    want = jnp.right_shift(line, bits) * own_chans + share * idx_ref[1] + place
    pick = (lax.broadcasted_iota(jnp.int32, (count, HALF), 1) == want) & (place < share)
    pick = jnp.where(pick, 1.0, 0.0).astype(BF)
    left = dot(pick, sown[...].reshape(ROWS * OWN, HALF), NT).astype(BF)
    total = jnp.zeros((1, CHANS), F32)
    first = None
    for ky in range(3):
        lanes = slice(ky * 3 * CHANS, (ky + 1) * 3 * CHANS)
        start = PAD + (ky - 1) * d
        right = nk[start : start + ROWS].reshape(ROWS * OWN, 3 * CHANS)
        grads = dot(left, right, NN)
        wg_ref[:, lanes] = grads.astype(BF)
        part = jnp.sum(grads * dot(pick, w_ref[:, lanes], NN), axis=0, keepdims=True)
        for kx in range(3):
            total = total + part[:, kx * CHANS : (kx + 1) * CHANS]
        if ky == 0:
            first = grads[:, :CHANS]
    total = total / gain_ref[...]
    high = total.astype(BF).astype(F32)
    spot = jnp.bitwise_and(lax.broadcasted_iota(jnp.int32, (count, CHANS), 0), lines - 1)
    first = jnp.where(spot == share, high, jnp.where(spot == share + 1, total - high, first))
    wg_ref[:, :CHANS] = first.astype(BF)


def turn_kernel(dims, idx_ref, xo_ref, xt_ref, cot_ref, w_ref, gain_ref, q_ref, wg_ref,
                nbuf, nk, pre, sbuf, sown, wq):
    norm_phase(3, xo_ref, xt_ref, gain_ref, nbuf, nk)
    conv_phase(3, nbuf, w_ref, pre)

    def one(r):
        _, slope = gelu_parts(pre[r])
        s = cot_ref[r].astype(F32) * slope
        scatter_s(3, s.astype(BF).astype(F32), r, sbuf, sown)

    row_loop(one, 2)
    q_phase(3, sbuf, w_ref, wq, q_ref)
    weight_phase(3, dims, idx_ref, sown, nk, w_ref, gain_ref, wg_ref)


def backward_kernel(block, dims, image, first_g, idx_ref, qm_ref, qr_ref, xo_ref, xt_ref, g_ref,
                    gain_up_ref, d_ref, w_ref, nk_ref, gain_ref, *rest):
    if block:
        q_ref, gn_ref, wg_ref, sown, sbuf, wq = rest
    else:
        wg_ref, sown = rest
        q_ref = gn_ref = sbuf = wq = None
    first, width = S_WIN[block]
    at = first - X_WIN[block + 1][0]
    cut = first - first_g
    live = in_image(idx_ref[0], first, width, image)
    gain_own, gain_oth = gain_up_ref[:, :HALF], gain_up_ref[:, HALF:]

    def one(r):
        xo = xo_ref[r].astype(F32)[at : at + width]
        xt = xt_ref[r].astype(F32)[at : at + width]
        mean, rstd = stats(xo, xt)
        uo, ut = (xo - mean) * rstd, (xt - mean) * rstd
        po = (qm_ref[1, r].astype(F32) + qr_ref[0, r].astype(F32)) * gain_own
        pt = (qm_ref[0, r].astype(F32) + qr_ref[1, r].astype(F32)) * gain_oth
        level = (jnp.sum(po, axis=1, keepdims=True) + jnp.sum(pt, axis=1, keepdims=True)) / CHANS
        cross = (
            jnp.sum(po * uo, axis=1, keepdims=True) + jnp.sum(pt * ut, axis=1, keepdims=True)
        ) / CHANS
        g = g_ref[r].astype(F32)[cut : cut + width] + rstd * (po - level - uo * cross)
        g = jnp.where(live, g, 0.0).astype(BF)
        if gn_ref is not None:
            gn_ref[r] = g
        s = (g.astype(F32) * d_ref[r]).astype(BF).astype(F32)
        scatter_s(block, s, r, sbuf, sown)

    row_loop(one, 2)
    if block:
        q_phase(block, sbuf, w_ref, wq, q_ref)
    weight_phase(block, dims, idx_ref, sown, nk_ref, w_ref, gain_ref, wg_ref)


def finish_kernel(dims, slabs, all_ref, perm_ref, out_ref):
    own_chans, share, lines = dims
    bits = lines.bit_length() - 1
    col = lax.broadcasted_iota(jnp.int32, (own_chans, slabs * lines), 1)
    place = jnp.bitwise_and(col, lines - 1)
    row = jnp.right_shift(col, bits) * share + place
    pick = (lax.broadcasted_iota(jnp.int32, (own_chans, slabs * lines), 0) == row) & (place < share)
    pick = jnp.where(pick, 1.0, 0.0).astype(BF)
    for t in range(TAPS):
        grads = dot(pick, all_ref[:, t * CHANS : (t + 1) * CHANS], NN).astype(BF)
        out_ref[t] = dot(grads, perm_ref[...], NT)


def local(sizes, x_in, cot, w1, gain):
    nx, nz, ny, ns = sizes
    own_chans, rows = x_in.shape[1], x_in.shape[2]
    image = x_in.shape[3]
    shards = nx * nz
    share = own_chans // ny
    lines = 8
    while lines < share + 2:
        lines *= 2
    dims = (own_chans, share, lines)
    sec, ax, az = lax.axis_index("section"), lax.axis_index("x"), lax.axis_index("zh")
    core, slab = lax.axis_index("core"), lax.axis_index("slab")
    patch = ax * nz + az
    idx = jnp.stack([patch * OWN, slab]).astype(jnp.int32)

    def other(value):
        return lax.ppermute(value, "core", [(0, 1), (1, 0)])

    order = np.arange(CHANS).reshape(shards, 2, own_chans)
    orders = [np.concatenate([order[:, h].ravel(), order[:, 1 - h].ravel()]) for h in (0, 1)]
    perms = np.stack([np.eye(CHANS, dtype=np.float32)[:, o] for o in orders])
    perm = lax.dynamic_index_in_dim(jnp.asarray(perms, BF), core, 0, keepdims=False)

    packed = call(prep_kernel, shape((own_chans, TAPS * CHANS), BF), [], (w1[0], perm))
    wide = jnp.broadcast_to(packed[None], (ns * nz, own_chans, TAPS * CHANS))
    wide = lax.all_to_all(wide, ("section", "zh"), 0, 0, tiled=True)
    wide = wide.reshape(ns, nz * own_chans, TAPS * CHANS)
    weights = [lax.all_gather(wide[b], "x", axis=0, tiled=True) for b in range(ns)]
    gains = lax.all_gather(gain[0], "section", axis=0)
    gains = gains.reshape(ns, shards, 2, own_chans)
    gains = jnp.concatenate(
        [
            lax.dynamic_index_in_dim(gains, core, 2, keepdims=False).reshape(ns, HALF),
            lax.dynamic_index_in_dim(gains, 1 - core, 2, keepdims=False).reshape(ns, HALF),
        ],
        axis=1,
    )
    gains = [gains[b : b + 1] for b in range(ns)]

    def mine(value, edge):
        value = lax.dynamic_index_in_dim(value, sec, 0, keepdims=False).transpose(1, 0, 2)
        return jnp.pad(value, ((0, 0), (0, 0), (edge, edge)))

    wide_x, wide_c = mine(x_in, 32), mine(cot, 16)
    windows = jnp.stack(
        [
            jnp.concatenate(
                [wide_x[:, :, OWN * p : OWN * p + XWIN], wide_c[:, :, OWN * p : OWN * p + CWIN]], axis=2
            )
            for p in range(shards)
        ]
    )
    windows = jnp.broadcast_to(windows[:, None], (shards, ny) + windows.shape[1:])
    windows = windows.reshape((shards * ny,) + windows.shape[2:])
    recv = lax.all_to_all(windows, ("x", "zh", "slab"), 0, 0, tiled=True)
    recv = recv.reshape(shards, ny, rows, own_chans, XWIN + CWIN)
    x_own, cot_own = call(
        functools.partial(assemble_kernel, ny, rows),
        (shape((ROWS, XWIN, HALF), BF), shape((ROWS, CWIN, HALF), BF)),
        [],
        (recv,),
    )

    taps3 = 3 * CHANS
    nk_shape = (ROWS + 2 * PAD, OWN, taps3)
    halves, slopes, shifted = [(x_own, other(x_own))], [], []
    for b in range(ns - 1):
        width = X_WIN[b + 1][1]
        y, slope, nk = call(
            functools.partial(forward_kernel, b, image),
            (
                shape((ROWS, width, HALF), BF),
                shape((ROWS, S_WIN[b][1], HALF), F32),
                shape(nk_shape, BF),
            ),
            [
                pltpu.VMEM((ROWS + 2 * PAD, width, taps3), BF),
                pltpu.VMEM((ROWS, width, HALF), F32),
            ],
            (idx, *halves[b], weights[b], gains[b]),
            (0,),
        )
        halves.append((y, other(y)))
        slopes.append(slope)
        shifted.append(nk)

    def back_scratch(b):
        width = S_WIN[b - 1][1]
        return [
            pltpu.VMEM((ROWS + 2 * PAD, width, 768), BF),
            pltpu.VMEM((ROWS, OWN, HALF), BF),
            pltpu.VMEM((3, 768, CHANS), BF),
        ]

    count = shards * lines
    wg_shape = shape((count, TAPS * CHANS), BF)
    width = X_WIN[4][1]
    sbuf_s, sown_s, wq_s = back_scratch(3)
    q, grads = call(
        functools.partial(turn_kernel, dims),
        (shape((2, ROWS, S_WIN[2][1], HALF), BF), wg_shape),
        [
            pltpu.VMEM((ROWS + 2 * PAD, width, taps3), BF),
            pltpu.VMEM(nk_shape, BF),
            pltpu.VMEM((ROWS, width, HALF), F32),
            sbuf_s,
            sown_s,
            wq_s,
        ],
        (idx, *halves[3], cot_own, weights[3], gains[3]),
        (0,),
    )
    weight_parts = [None] * 3 + [grads]
    g, first_g = cot_own, S_WIN[3][0]
    for b in (2, 1, 0):
        args = (
            idx, q, other(q), *halves[b + 1], g, gains[b + 1], slopes[b], weights[b], shifted[b], gains[b],
        )
        kernel = functools.partial(backward_kernel, b, dims, image, first_g)
        if b:
            sbuf_s, sown_s, wq_s = back_scratch(b)
            q, g, grads = call(
                kernel,
                (
                    shape((2, ROWS, S_WIN[b - 1][1], HALF), BF),
                    shape((ROWS, S_WIN[b][1], HALF), BF),
                    wg_shape,
                ),
                [sown_s, sbuf_s, wq_s],
                args,
                (0,),
            )
        else:
            (grads,) = call(kernel, (wg_shape,), [pltpu.VMEM((ROWS, OWN, HALF), BF)], args, (0,))
        first_g = S_WIN[b][0]
        weight_parts[b] = grads

    parts = jnp.stack(weight_parts).reshape(ns * shards, lines, TAPS * CHANS)
    parts = lax.all_to_all(parts, ("section", "x", "zh"), 0, 0, tiled=True)
    total = jnp.sum(parts.astype(F32), axis=0)
    gain_sum = total[share, :CHANS] + total[share + 1, :CHANS]
    high = gain_sum.astype(BF)
    low = (gain_sum - high.astype(F32)).astype(BF)
    total = total.astype(BF)
    total = total.at[share, :CHANS].set(high).at[share + 1, :CHANS].set(low)
    every = lax.all_gather(total, "slab", axis=0, tiled=True)
    weight_grad = call(
        functools.partial(finish_kernel, dims, ny),
        shape((TAPS, own_chans, CHANS), F32),
        [],
        (every, perm),
    )
    gain_rows = every.reshape(ny, lines, TAPS * CHANS)[:, share : share + 2, :CHANS]
    gain_all = jnp.sum(gain_rows.astype(F32), axis=(0, 1))
    here = lax.dynamic_slice_in_dim(gain_all, patch * own_chans, own_chans)
    there = lax.dynamic_slice_in_dim(gain_all, HALF + patch * own_chans, own_chans)
    gain_grad = here + other(there)
    return weight_grad[None], gain_grad[None]


def solution(mesh):
    ns, chans, ny = mesh.shape["section"], mesh.shape["ch"], mesh.shape["slab"]
    nz = 2 if chans % 4 == 0 else 1
    nx = chans // (2 * nz)
    axes = ("section", "x", "zh", "core", "slab")
    fine = Mesh(mesh.devices.reshape(ns, nx, nz, 2, ny), axes)
    ch = ("x", "zh", "core")
    return jax.shard_map(
        functools.partial(local, (nx, nz, ny, ns)),
        mesh=fine,
        in_specs=(
            P(None, ch, "slab", None),
            P(None, ch, "slab", None),
            P("section", None, ch, None),
            P("section", None),
        ),
        out_specs=(P("section", None, ch, None), P("section", ch)),
        check_vma=False,
    )
```

time: 2320 us -> 326 us (0.14)
  waiting for transfers between devices: 951 us -> 132 us
  blocking collectives: 628 us -> 18.4 us
  local copies, waits for them, and re-layouts: 281 us -> 16.8 us
  matrix products: 224 us -> 0 us
  Pallas kernels: 0 us -> 108 us
  starting transfers between devices: 119 us -> 30.6 us
  other arithmetic: 86.6 us -> 5.51 us
    psum x15 -> x0, blocking collectives: 628 us -> none  [the longest x7 316 us: backward_tick(): lax.psum((jnp.sum(scaled, axis=0), jnp.sum(scaled * standard, axis=0)), '...]
    reduce_scatter x7 -> x0, waiting for transfers between devices: 492 us -> none  [backward_tick(): lax.psum_scatter(running.reshape(span_rows, row_count, col_count).astype(...]
    all_gather x7 -> x4, waiting for transfers between devices: 406 us -> 0.04 us  [local(): lax.all_gather(wide[b], 'x', axis=0, tiled=True)]
    dot_general x189 -> x0, matrix products: 224 us -> none  [the longest x63 81.9 us: backward_tick(): lax.dot_general(columns, back_slab.reshape(own_chans, pixels), (((0,), (0...]
    dynamic_slice x57 -> x5, local copies, waits for them, and re-layouts: 208 us -> 1.03 us  [the longest x3 0.85 us: mine(): lax.dynamic_index_in_dim(value, sec, 0, keepdims=False).transpose(1, 0, 2)]
    all_to_all x0 -> x3, waiting for transfers between devices: none -> 116 us  [the longest x1 45.1 us: local(): parts = lax.all_to_all(parts, ('section', 'x', 'zh'), 0, 0, tiled=True)]
    ppermute x42 -> x8, starting transfers between devices: 119 us -> 8.45 us  [other(): return lax.ppermute(value, 'core', [(0, 1), (1, 0)])]
    pallas_call x0 -> x10, Pallas kernels: none -> 108 us  [call(): pl.pallas_call(kernel, out_shape=out_shape, in_specs=[sm if i in smem els...]
  transfers between devices with their start and end apart: 57 -> 15, of which waited for: 29 -> 9; matrix products, arithmetic and copies ran while one was open for 14% -> 2% of each run, Pallas kernels for 0% -> 18%
where the time goes in v1:
time: 326 us
  waiting for transfers between devices  132 us (40%)
  Pallas kernels  108 us (33%)
  starting transfers between devices  30.6 us (9%)
  blocking collectives  18.4 us (6%)
  local copies, waits for them, and re-layouts  16.8 us (5%)
  between operations  13.9 us (4%)
  other arithmetic  5.51 us (2%)
    pallas_call x10, Pallas kernels, call(): pl.pallas_call(kernel, out_shape=out_shape, in_specs=[sm if i in smem els...  108 us
    all_to_all x1, waiting for transfers between devices, local(): parts = lax.all_to_all(parts, ('section', 'x', 'zh'), 0, 0, tiled=True)  45.1 us
    all_to_all x1, waiting for transfers between devices, local(): recv = lax.all_to_all(windows, ('x', 'zh', 'slab'), 0, 0, tiled=True)  40.1 us
    all_to_all x1, waiting for transfers between devices, local(): wide = lax.all_to_all(wide, ('section', 'zh'), 0, 0, tiled=True)  30.4 us
    ppermute x8, waiting for transfers between devices, other(): return lax.ppermute(value, 'core', [(0, 1), (1, 0)])  15 us
    all_gather x1, blocking collectives, local(): every = lax.all_gather(total, 'slab', axis=0, tiled=True)  9.75 us
    all_to_all x1, starting transfers between devices, local(): recv = lax.all_to_all(windows, ('x', 'zh', 'slab'), 0, 0, tiled=True)  9.56 us
    all_gather x1, blocking collectives, local(): gains = lax.all_gather(gain[0], 'section', axis=0)  8.63 us
  transfers between devices with their start and end apart: 15, of which 9 were waited for; matrix products, arithmetic and copies ran while one was open for 2% of the time, Pallas kernels for 18%

profile of v1, /device:TPU:33, one launch (start us, length us, event | category | flops | bytes accessed | tf_op | source)
XLA Modules:
  0.0 325.6 jit_solution(16801891302964740718)
XLA Ops:
  7.2 1.7 dynamic-slice_bitcast_fusion.perm_ref
  8.9 2.2 shard_map.69
  11.1 2.1 broadcast_in_dim.9
  13.2 8.0 %all-to-all-start.1 = ((bf16[8,24,3456]{2,1,0:T(8,128)(2,1)}), bf16[8,24,3456]{2,1,0:T(8,128)(2,1)S(1)}, u32[]{:S(2)}, u32[]{:S(2)}) async-start(bf16[8,24,3456]{2,1,0:T(8,128)(2,1)} %broadcast_in_dim.9), calls=%async_computation.1 | async-start | bytes 2654208 | tf_op jit(solution)/shard_map/all_to_all | solution.py:334
  22.1 30.4 %all-to-all-done.1 = bf16[8,24,3456]{2,1,0:T(8,128)(2,1)S(1)} async-done(((bf16[8,24,3456]{2,1,0:T(8,128)(2,1)}), bf16[8,24,3456]{2,1,0:T(8,128)(2,1)S(1)}, u32[]{:S(2)}, u32[]{:S(2)}) %all-to-all-start.1) | async-done | bytes 1327136 | tf_op jit(solution)/shard_map/all_to_all | solution.py:334
  54.7 1.5 broadcast_in_dim.8
  56.2 9.6 %all-to-all-start = ((bf16[32,8,24,128]{3,2,1,0:T(8,128)(2,1)}), bf16[32,8,24,128]{3,2,1,0:T(8,128)(2,1)S(1)}, u32[]{:S(2)}, u32[]{:S(2)}) async-start(bf16[32,8,24,128]{3,2,1,0:T(8,128)(2,1)} %bitcast.16), calls=%async_computation | async-start | bytes 3145728 | tf_op jit(solution)/shard_map/all_to_all | solution.py:363
  67.3 40.1 %all-to-all-done = bf16[32,8,24,128]{3,2,1,0:T(8,128)(2,1)S(1)} async-done(((bf16[32,8,24,128]{3,2,1,0:T(8,128)(2,1)}), bf16[32,8,24,128]{3,2,1,0:T(8,128)(2,1)S(1)}, u32[]{:S(2)}, u32[]{:S(2)}) %all-to-all-start) | async-done | bytes 1572896 | tf_op jit(solution)/shard_map/all_to_all | solution.py:363
  107.4 1.2 copy-done
  108.5 5.0 %shard_map.68 = (bf16[32,80,192]{2,1,0:T(8,128)(2,1)}, bf16[32,48,192]{2,1,0:T(8,128)(2,1)}) custom-call(bf16[8,4,8,24,128]{4,3,2,1,0:T(8,128)(2,1)} %bitcast.63), custom_call_target="tpu_custom_call" | custom-call | tf_op jit(solution)/shard_map/pallas_call | solution.py:41
  113.5 1.9 collective-permute-start
  115.5 8.6 %all-gather = f32[4,1,384]{2,1,0:T(1,128)S(1)} all-gather(f32[1,1,384]{2,1,0:T(1,128)S(1)} %bitcast.77), channel_id=1, replica_groups=mesh['section'=4,'x'=4,'zh'=2,'core'=2,'slab'=4] {'section'}, dimensions={0}, use_global_device_ids=true | all-gather | bytes 7680 | tf_op jit(solution)/shard_map/all_gather | solution.py:337
  126.9 16.9 %shard_map.70 = (bf16[32,80,192]{2,1,0:T(8,128)(2,1)}, f32[32,16,192]{2,1,0:T(8,128)}, bf16[48,16,1152]{2,1,0:T(8,128)(2,1)}) custom-call(s32[2]{0:T(128)} %pad_add_fusion.idx_ref, bf16[32,80,192]{2,1,0:T(8,128)(2,1)} %get-tuple-element.45.xo_ref, bf16[32,80,192]{2,1,0:T(8,128)(2,1)} %copy-done.4, bf16[192,3456]{1,0:T(8,128)(2,1)} %all-gather.6.cloned.1.call-done.w_ref, ...), custom_call_target="tpu_custom_call" | custom-call | tf_op jit(solution)/shard_map/pallas_call | solution.py:41
  143.9 1.8 collective-permute-start.1
  145.7 2.8 collective-permute-done.1.xt_ref
  149.6 17.3 %shard_map.71 = (bf16[32,80,192]{2,1,0:T(8,128)(2,1)}, f32[32,32,192]{2,1,0:T(8,128)}, bf16[48,16,1152]{2,1,0:T(8,128)(2,1)}) custom-call(s32[2]{0:T(128)} %pad_add_fusion.idx_ref, bf16[32,80,192]{2,1,0:T(8,128)(2,1)} %get-tuple-element.46.xo_ref, bf16[32,80,192]{2,1,0:T(8,128)(2,1)} %copy-done.1, bf16[192,3456]{1,0:T(8,128)(2,1)} %all-gather.8.cloned.1.call-done.w_ref, ...), custom_call_target="tpu_custom_call" | custom-call | tf_op jit(solution)/shard_map/pallas_call | solution.py:41
  167.3 2.9 collective-permute-done.2.xt_ref
  171.2 15.8 %shard_map.72 = (bf16[32,64,192]{2,1,0:T(8,128)(2,1)}, f32[32,32,192]{2,1,0:T(8,128)}, bf16[48,16,1152]{2,1,0:T(8,128)(2,1)}) custom-call(s32[2]{0:T(128)} %pad_add_fusion.idx_ref, bf16[32,80,192]{2,1,0:T(8,128)(2,1)} %get-tuple-element.47.xo_ref, bf16[32,80,192]{2,1,0:T(8,128)(2,1)} %copy-done.2, bf16[192,3456]{1,0:T(8,128)(2,1)} %all-gather.10.cloned.1.call-done.w_ref, ...), custom_call_target="tpu_custom_call" | custom-call | tf_op jit(solution)/shard_map/pallas_call | solution.py:41
  187.4 2.5 collective-permute-done.3.xt_ref
  190.9 16.0 %shard_map.73 = (bf16[2,32,32,192]{3,2,1,0:T(8,128)(2,1)}, bf16[64,3456]{1,0:T(8,128)(2,1)}) custom-call(s32[2]{0:T(128)} %pad_add_fusion.idx_ref, bf16[32,64,192]{2,1,0:T(8,128)(2,1)} %get-tuple-element.48.xo_ref, bf16[32,64,192]{2,1,0:T(8,128)(2,1)} %copy-done.3, bf16[32,48,192]{2,1,0:T(8,128)(2,1)} %get-tuple-element.49.cot_ref.g_ref, ...), custom_call_target="tpu_custom_call" | custom-call | tf_op jit(solution)/shard_map/pallas_call | solution.py:41
  207.2 2.5 collective-permute-done.4.qr_ref
  210.8 12.5 %shard_map.74 = (bf16[2,32,32,192]{3,2,1,0:T(8,128)(2,1)}, bf16[32,32,192]{2,1,0:T(8,128)(2,1)}, bf16[64,3456]{1,0:T(8,128)(2,1)}) custom-call(s32[2]{0:T(128)} %pad_add_fusion.idx_ref, bf16[2,32,32,192]{3,2,1,0:T(8,128)(2,1)} %get-tuple-element.50.qm_ref, bf16[2,32,32,192]{3,2,1,0:T(8,128)(2,1)} %copy-done.5, ...), custom_call_target="tpu_custom_call" | custom-call | tf_op jit(solution)/shard_map/pallas_call | solution.py:41
  223.7 2.5 collective-permute-done.5.qr_ref
  227.2 10.7 %shard_map.75 = (bf16[2,32,16,192]{3,2,1,0:T(8,128)(2,1)}, bf16[32,32,192]{2,1,0:T(8,128)(2,1)}, bf16[64,3456]{1,0:T(8,128)(2,1)}) custom-call(s32[2]{0:T(128)} %pad_add_fusion.idx_ref, bf16[2,32,32,192]{3,2,1,0:T(8,128)(2,1)} %get-tuple-element.53.qm_ref, bf16[2,32,32,192]{3,2,1,0:T(8,128)(2,1)} %copy-done.6, ...), custom_call_target="tpu_custom_call" | custom-call | tf_op jit(solution)/shard_map/pallas_call | solution.py:41
  238.3 1.8 collective-permute-done.6.qr_ref
  240.8 8.4 %shard_map.76 = bf16[64,3456]{1,0:T(8,128)(2,1)} custom-call(s32[2]{0:T(128)} %pad_add_fusion.idx_ref, bf16[2,32,16,192]{3,2,1,0:T(8,128)(2,1)} %get-tuple-element.57.qm_ref, bf16[2,32,16,192]{3,2,1,0:T(8,128)(2,1)} %copy-done.8, bf16[32,80,192]{2,1,0:T(8,128)(2,1)} %get-tuple-element.46.xo_ref, bf16[32,80,192]{2,1,0:T(8,128)(2,1)} %copy-done.1, ...), custom_call_target="tpu_custom_call" | custom-call | tf_op jit(solution)/shard_map/pallas_call | solution.py:41
  249.3 2.5 pad_maximum_fusion
  251.8 4.4 %all-to-all-start.2 = ((bf16[32,8,3456]{2,1,0:T(8,128)(2,1)}), bf16[32,8,3456]{2,1,0:T(8,128)(2,1)S(1)}, u32[]{:S(2)}, u32[]{:S(2)}) async-start(bf16[32,8,3456]{2,1,0:T(8,128)(2,1)} %bitcast.29), calls=%async_computation.2 | async-start | bytes 3538944 | tf_op jit(solution)/shard_map/all_to_all | solution.py:447
  256.2 45.1 %all-to-all-done.2 = bf16[32,8,3456]{2,1,0:T(8,128)(2,1)S(1)} async-done(((bf16[32,8,3456]{2,1,0:T(8,128)(2,1)}), bf16[32,8,3456]{2,1,0:T(8,128)(2,1)S(1)}, u32[]{:S(2)}, u32[]{:S(2)}) %all-to-all-start.2) | async-done | bytes 1769504 | tf_op jit(solution)/shard_map/all_to_all | solution.py:447
  302.2 9.7 %all_gather.23.all_ref = bf16[32,3456]{1,0:T(8,128)(2,1)S(1)} all-gather(bf16[8,3456]{1,0:T(8,128)(2,1)S(1)} %scatter.9), channel_id=1, replica_groups=mesh['section'=4,'x'=4,'zh'=2,'core'=2,'slab'=4] {'slab'}, dimensions={0}, use_global_device_ids=true | all-gather | bytes 276480 | tf_op jit(solution)/shard_map/all_gather | solution.py:454
  312.0 3.0 collective-permute-start.7
  315.0 3.4 %shard_map.77 = f32[9,24,384]{2,1,0:T(8,128)} custom-call(bf16[32,3456]{1,0:T(8,128)(2,1)} %copy-done.7, bf16[384,384]{1,0:T(8,128)(2,1)} %dynamic-slice_bitcast_fusion.perm_ref), custom_call_target="tpu_custom_call" | custom-call | tf_op jit(solution)/shard_map/pallas_call | solution.py:41
  (73 shorter events, 16.6 us)
Async XLA Ops:
  13.2 39.2 %all-to-all-start.1 = ((bf16[8,24,3456]{2,1,0:T(8,128)(2,1)}), bf16[8,24,3456]{2,1,0:T(8,128)(2,1)S(1)}, u32[]{:S(2)}, u32[]{:S(2)}) async-start(bf16[8,24,3456]{2,1,0:T(8,128)(2,1)} %broadcast_in_dim.9), calls=%async_computation.1 | async-start | bytes 2654208 | tf_op jit(solution)/shard_map/all_to_all | solution.py:334
  21.2 104.6 %all-gather.6.cloned.1.call-start = ((), (), s32[]{:S(2)}) async-start(), calls=%async_computation.3 | async-start | bytes 1658880 | tf_op jit(solution)/shard_map/all_gather | solution.py:336
  56.2 51.2 %all-to-all-start = ((bf16[32,8,24,128]{3,2,1,0:T(8,128)(2,1)}), bf16[32,8,24,128]{3,2,1,0:T(8,128)(2,1)S(1)}, u32[]{:S(2)}, u32[]{:S(2)}) async-start(bf16[32,8,24,128]{3,2,1,0:T(8,128)(2,1)} %bitcast.16), calls=%async_computation | async-start | bytes 3145728 | tf_op jit(solution)/shard_map/all_to_all | solution.py:363
  65.8 49.7 %copy-start.12 = (f32[1,384]{1,0:T(1,128)S(1)}, f32[1,384]{1,0:T(1,128)}, u32[]{:S(2)}) copy-start(f32[1,384]{1,0:T(1,128)} %param.12) | copy-start | bytes 4612
  65.8 79.9 %all-gather.8.cloned.1.call-start = ((), (), s32[]{:S(2)}) async-start(), calls=%async_computation.4 | async-start | bytes 1658880 | tf_op jit(solution)/shard_map/all_gather | solution.py:336
  66.5 100.7 %all-gather.10.cloned.1.call-start = ((), (), s32[]{:S(2)}) async-start(), calls=%async_computation.5 | async-start | bytes 1658880 | tf_op jit(solution)/shard_map/all_gather | solution.py:336
  67.3 120.1 %all-gather.12.cloned.1.call-start = ((), (), s32[]{:S(2)}) async-start(), calls=%async_computation.6 | async-start | bytes 1658880 | tf_op jit(solution)/shard_map/all_gather | solution.py:336
  107.4 1.2 copy-start
  113.5 12.3 %collective-permute-start = (bf16[32,80,192]{2,1,0:T(8,128)(2,1)}, bf16[32,80,192]{2,1,0:T(8,128)(2,1)S(1)}, u32[]{:S(2)}, u32[]{:S(2)}) collective-permute-start(bf16[32,80,192]{2,1,0:T(8,128)(2,1)} %get-tuple-element.45.xo_ref), channel_id=1, source_target_pairs={{0,4},{4,0},{1,5},{5,1},{2,6},{6,2},{3,7},{7,3},{8,12},{12,8},{9,1... | collective-permute-start | bytes 2949128 | tf_op jit(solution)/shard_map/ppermute | solution.py:325
  125.9 1.1 copy-start.4
  143.9 4.6 %collective-permute-start.1 = (bf16[32,80,192]{2,1,0:T(8,128)(2,1)}, bf16[32,80,192]{2,1,0:T(8,128)(2,1)S(1)}, u32[]{:S(2)}, u32[]{:S(2)}) collective-permute-start(bf16[32,80,192]{2,1,0:T(8,128)(2,1)} %get-tuple-element.46.xo_ref), channel_id=1, source_target_pairs={{0,4},{4,0},{1,5},{5,1},{2,6},{6,2},{3,7},{7,3},{8,12},{12,8},{9,1... | collective-permute-start | bytes 2949128 | tf_op jit(solution)/shard_map/ppermute | solution.py:325
  148.5 1.1 copy-start.1
  166.9 3.2 collective-permute-start.2
  170.2 1.1 copy-start.2
  187.0 2.9 collective-permute-start.3
  189.9 1.0 copy-start.3
  206.9 2.9 collective-permute-start.4
  209.8 1.1 copy-start.5
  223.3 2.9 collective-permute-start.5
  226.2 1.0 copy-start.6
  237.9 2.1 collective-permute-start.6
  240.0 0.8 copy-start.8
  240.8 8.4 %copy-start.9 = (bf16[64,3456]{1,0:T(8,128)(2,1)S(1)}, bf16[64,3456]{1,0:T(8,128)(2,1)}, u32[]{:S(2)}) copy-start(bf16[64,3456]{1,0:T(8,128)(2,1)} %get-tuple-element.63) | copy-start | bytes 1327108
  240.8 8.4 %copy-start.10 = (bf16[64,3456]{1,0:T(8,128)(2,1)S(1)}, bf16[64,3456]{1,0:T(8,128)(2,1)}, u32[]{:S(2)}) copy-start(bf16[64,3456]{1,0:T(8,128)(2,1)} %get-tuple-element.62) | copy-start | bytes 1327108
  240.8 8.4 %copy-start.11 = (bf16[64,3456]{1,0:T(8,128)(2,1)S(1)}, bf16[64,3456]{1,0:T(8,128)(2,1)}, u32[]{:S(2)}) copy-start(bf16[64,3456]{1,0:T(8,128)(2,1)} %get-tuple-element.61) | copy-start | bytes 1327108
  251.8 49.6 %all-to-all-start.2 = ((bf16[32,8,3456]{2,1,0:T(8,128)(2,1)}), bf16[32,8,3456]{2,1,0:T(8,128)(2,1)S(1)}, u32[]{:S(2)}, u32[]{:S(2)}) async-start(bf16[32,8,3456]{2,1,0:T(8,128)(2,1)} %bitcast.29), calls=%async_computation.2 | async-start | bytes 3538944 | tf_op jit(solution)/shard_map/all_to_all | solution.py:447
  311.9 3.1 copy-start.7
  312.0 6.4 %collective-permute-start.7 = (f32[24]{0:T(128)S(1)}, f32[24]{0:T(128)S(1)}, u32[]{:S(2)}, u32[]{:S(2)}) collective-permute-start(f32[24]{0:T(128)S(1)} %dynamic_slice.30), channel_id=1, source_target_pairs={{0,4},{4,0},{1,5},{5,1},{2,6},{6,2},{3,7},{7,3},{8,12},{12,8},{9,1... | collective-permute-start | bytes 296 | tf_op jit(solution)/shard_map/ppermute | solution.py:325
Sparse Core Ops, SparseCore 0:
  53.7 37.9 all-gather.5
  93.4 29.7 all-gather.7
  125.0 28.1 all-gather.9
  155.4 28.1 all-gather.11

commit v2 on v1

--- a/solution.py
+++ b/solution.py
@@ -29,6 +29,9 @@
 PARAMS = pltpu.CompilerParams(vmem_limit_bytes=VMEM_LIMIT)
 NT = (((1,), (1,)), ((), ()))
 NN = (((1,), (0,)), ((), ()))
+LANES = TAPS * CHANS
+CARRY = LANES + 128
+R_NORM, R_EPI, R_BACK = 2, 2, 2
 
 
 def dot(a, b, dims):
@@ -52,40 +55,71 @@
     return jax.ShapeDtypeStruct(dims, dtype)
 
 
-def row_loop(body, unroll=4):
+def row_loop(body, rows, unroll=1):
+    span = rows * unroll
+
     def step(i, carry):
         for k in range(unroll):
-            body(i * unroll + k)
+            body(pl.multiple_of(i * span, span) + k * rows)
         return carry
 
-    lax.fori_loop(0, ROWS // unroll, step, 0)
+    lax.fori_loop(0, ROWS // span, step, 0)
+
+
+def flat(value):
+    return value.reshape(value.shape[0] * value.shape[1], value.shape[2])
 
 
 def in_image(base, first, count, width):
-    cols = lax.broadcasted_iota(jnp.int32, (count, HALF), 0) + (base - 32 + first)
+    cols = lax.broadcasted_iota(jnp.int32, (1, count, HALF), 1) + (base - 32 + first)
     return (cols >= 0) & (cols < width)
 
 
-def stats(xo, xt):
-    mean = (jnp.sum(xo, axis=1, keepdims=True) + jnp.sum(xt, axis=1, keepdims=True)) / CHANS
-    square = (
-        jnp.sum(xo * xo, axis=1, keepdims=True) + jnp.sum(xt * xt, axis=1, keepdims=True)
-    ) / CHANS
-    return mean, lax.rsqrt(square - mean * mean + NORM_EPS)
-
-
-def gelu_parts(pre):
-    tangent = jnp.tanh(SLOPE_SCALE * (pre + CUBIC_COEF * pre * pre * pre))
-    value = 0.5 * pre * (1.0 + tangent)
-    slope = 0.5 * (1.0 + tangent) + 0.5 * pre * (1.0 - tangent * tangent) * SLOPE_SCALE * (
+def widen(own, oth):
+    return jnp.concatenate([own.astype(F32), oth.astype(F32)], axis=1)
+
+
+def chan_mean(value):
+    folded = value[:, :128] + value[:, 128:256] + value[:, 256:]
+    return jnp.sum(folded, axis=1, keepdims=True) / CHANS
+
+
+def unit_of(value):
+    mean = chan_mean(value)
+    rstd = lax.rsqrt(chan_mean(value * value) - mean * mean + NORM_EPS)
+    return (value - mean) * rstd, rstd
+
+
+def read_gain(w_ref):
+    tile = w_ref[0:16, LANES:CARRY].astype(F32)
+    return jnp.concatenate(
+        [(tile[p : p + 1] + tile[3 + p : 4 + p]) + tile[6 + p : 7 + p] for p in range(3)], axis=1
+    )
+
+
+def gelu_inner(pre):
+    return jnp.tanh(SLOPE_SCALE * (pre + CUBIC_COEF * pre * pre * pre))
+
+
+def gelu_slope(pre, tangent):
+    return 0.5 * (1.0 + tangent) + 0.5 * pre * (1.0 - tangent * tangent) * SLOPE_SCALE * (
         1.0 + 3.0 * CUBIC_COEF * pre * pre
     )
-    return value, slope
-
-
-def prep_kernel(w_ref, perm_ref, out_ref):
+
+
+def prep_kernel(w_ref, gain_ref, perm_ref, out_ref):
     for t in range(TAPS):
         out_ref[:, t * CHANS : (t + 1) * CHANS] = dot(w_ref[t], perm_ref[...], NN).astype(BF)
+    rest = jnp.broadcast_to(gain_ref[...], (8, CHANS))
+    row = lax.broadcasted_iota(jnp.int32, (out_ref.shape[0], 128), 0)
+    tile = jnp.zeros((out_ref.shape[0], 128), F32)
+    for k in range(3):
+        piece = rest.astype(BF)
+        rest = rest - piece.astype(F32)
+        moved = dot(piece, perm_ref[...], NN)
+        for p in range(3):
+            tile = jnp.where(row == 3 * k + p, moved[0:1, 128 * p : 128 * p + 128], tile)
+    out_ref[:, LANES:CARRY] = tile.astype(BF)
 
 
 def assemble_kernel(slabs, rows, recv_ref, x_ref, cot_ref):
@@ -107,7 +141,7 @@
     lax.fori_loop(0, rows, one, 0)
 
 
-def norm_phase(block, xo_ref, xt_ref, gain_ref, nbuf, nk):
+def norm_phase(block, xo_ref, xt_ref, gain, nbuf, nk):
     d = DIL[block]
     first_in, width_in = X_WIN[block]
     first_out, width_out = X_WIN[block + 1]
@@ -116,21 +150,20 @@
     for edge in (0, PAD + ROWS):
         nbuf[edge : edge + PAD] = jnp.zeros((PAD, width_out, 3 * CHANS), BF)
         nk[edge : edge + PAD] = jnp.zeros((PAD, OWN, 3 * CHANS), BF)
-    gain = gain_ref[...]
-
-    def one(r):
-        xo = xo_ref[r].astype(F32)
-        xt = xt_ref[r].astype(F32)
-        mean, rstd = stats(xo, xt)
-        both = jnp.concatenate([(xo - mean) * rstd, (xt - mean) * rstd], axis=1) * gain
+    n = R_NORM
+
+    def some(r):
+        unit, _ = unit_of(widen(flat(xo_ref[pl.ds(r, n)]), flat(xt_ref[pl.ds(r, n)])))
+        both = unit * gain
         for kx in range(3):
-            shift = (-(kx - 1) * d) % width_in
+            shift = (-(kx - 1) * d) % (n * width_in)
             moved = pltpu.roll(both, shift, 0) if shift else both
+            moved = moved.reshape(n, width_in, CHANS)
             lanes = slice(kx * CHANS, (kx + 1) * CHANS)
-            nbuf[PAD + r, :, lanes] = moved[low : low + width_out].astype(BF)
-            nk[PAD + r, :, lanes] = moved[own : own + OWN].astype(BF)
-
-    row_loop(one, 2)
+            nbuf[pl.ds(PAD + r, n), :, lanes] = moved[:, low : low + width_out].astype(BF)
+            nk[pl.ds(PAD + r, n), :, lanes] = moved[:, own : own + OWN].astype(BF)
+
+    row_loop(some, n)
 
 
 def conv_phase(block, nbuf, w_ref, pre):
@@ -151,37 +184,44 @@
     lax.fori_loop(0, ROWS // step, one, 0)
 
 
-def forward_kernel(block, image, idx_ref, xo_ref, xt_ref, w_ref, gain_ref, y_ref, d_ref, nk, nbuf, pre):
+def forward_kernel(block, image, idx_ref, xo_ref, xt_ref, w_ref, y_ref, d_ref, nk, gain_ref, nbuf, pre):
     first_in = X_WIN[block][0]
     first_out, width_out = X_WIN[block + 1]
     first_s, width_s = S_WIN[block]
-    norm_phase(block, xo_ref, xt_ref, gain_ref, nbuf, nk)
+    gain = read_gain(w_ref)
+    gain_ref[...] = gain
+    norm_phase(block, xo_ref, xt_ref, gain, nbuf, nk)
     conv_phase(block, nbuf, w_ref, pre)
     live = in_image(idx_ref[0], first_out, width_out, image)
     low, at = first_out - first_in, first_s - first_out
-
-    def one(r):
-        value, slope = gelu_parts(pre[r])
-        out = xo_ref[r].astype(F32)[low : low + width_out] + value
-        y_ref[r] = jnp.where(live, out, 0.0).astype(BF)
-        d_ref[r] = slope[at : at + width_s]
-
-    row_loop(one, 2)
-
-
-def scatter_s(block, s, r, sbuf, sown):
+    n = R_EPI
+
+    def some(r):
+        act = pre[pl.ds(r, n)]
+        tangent = gelu_inner(act)
+        out = xo_ref[pl.ds(r, n)].astype(F32)[:, low : low + width_out] + 0.5 * act * (1.0 + tangent)
+        y_ref[pl.ds(r, n)] = jnp.where(live, out, 0.0).astype(BF)
+        d_ref[pl.ds(r, n)] = gelu_slope(act[:, at : at + width_s], tangent[:, at : at + width_s])
+
+    row_loop(some, n)
+
+
+def scatter_s(block, s, r, n, sbuf, sown):
     first, width = S_WIN[block]
-    sown[r] = s[32 - first : 32 - first + OWN].astype(BF)
+    rows = s.reshape(n, width, HALF)
+    sown[pl.ds(r, n)] = rows[:, 32 - first : 32 - first + OWN].astype(BF)
     if sbuf is None:
         return
     d = DIL[block]
     first_q, width_q = S_WIN[block - 1]
     low = first_q - first
-    gap = jnp.zeros((width_q, 256 - HALF), F32)
+    gap = jnp.zeros((n * width, 256 - HALF), F32)
+    wide = jnp.concatenate([s, gap], axis=1)
     for kx in range(3):
-        shift = ((kx - 1) * d) % width
-        moved = (pltpu.roll(s, shift, 0) if shift else s)[low : low + width_q]
-        sbuf[PAD + r, :, kx * 256 : (kx + 1) * 256] = jnp.concatenate([moved, gap], axis=1).astype(BF)
+        shift = ((kx - 1) * d) % (n * width)
+        moved = pltpu.roll(wide, shift, 0) if shift else wide
+        moved = moved.reshape(n, width, 256)[:, low : low + width_q]
+        sbuf[pl.ds(PAD + r, n), :, kx * 256 : (kx + 1) * 256] = moved.astype(BF)
 
 
 def q_phase(block, sbuf, w_ref, wq, q_ref):
@@ -210,7 +250,7 @@
     lax.fori_loop(0, ROWS // step, one, 0)
 
 
-def weight_phase(block, dims, idx_ref, sown, nk, w_ref, gain_ref, wg_ref):
+def weight_phase(block, dims, idx_ref, sown, nk, w_ref, gain, wg_ref):
     own_chans, share, lines = dims
     d = DIL[block]
     count = (HALF // own_chans) * lines
@@ -234,26 +274,26 @@
             total = total + part[:, kx * CHANS : (kx + 1) * CHANS]
         if ky == 0:
             first = grads[:, :CHANS]
-    total = total / gain_ref[...]
-    high = total.astype(BF).astype(F32)
     spot = jnp.bitwise_and(lax.broadcasted_iota(jnp.int32, (count, CHANS), 0), lines - 1)
-    first = jnp.where(spot == share, high, jnp.where(spot == share + 1, total - high, first))
-    wg_ref[:, :CHANS] = first.astype(BF)
-
-
-def turn_kernel(dims, idx_ref, xo_ref, xt_ref, cot_ref, w_ref, gain_ref, q_ref, wg_ref,
+    wg_ref[:, :CHANS] = jnp.where(spot == share, total / gain, first).astype(BF)
+
+
+def turn_kernel(dims, idx_ref, xo_ref, xt_ref, cot_ref, w_ref, q_ref, wg_ref, gain_ref,
                 nbuf, nk, pre, sbuf, sown, wq):
-    norm_phase(3, xo_ref, xt_ref, gain_ref, nbuf, nk)
+    gain = read_gain(w_ref)
+    gain_ref[...] = gain
+    norm_phase(3, xo_ref, xt_ref, gain, nbuf, nk)
     conv_phase(3, nbuf, w_ref, pre)
-
-    def one(r):
-        _, slope = gelu_parts(pre[r])
-        s = cot_ref[r].astype(F32) * slope
-        scatter_s(3, s.astype(BF).astype(F32), r, sbuf, sown)
-
-    row_loop(one, 2)
+    n = R_BACK
+
+    def some(r):
+        act = flat(pre[pl.ds(r, n)])
+        s = flat(cot_ref[pl.ds(r, n)]).astype(F32) * gelu_slope(act, gelu_inner(act))
+        scatter_s(3, s, r, n, sbuf, sown)
+
+    row_loop(some, n)
     q_phase(3, sbuf, w_ref, wq, q_ref)
-    weight_phase(3, dims, idx_ref, sown, nk, w_ref, gain_ref, wg_ref)
+    weight_phase(3, dims, idx_ref, sown, nk, w_ref, gain, wg_ref)
 
 
 def backward_kernel(block, dims, image, first_g, idx_ref, qm_ref, qr_ref, xo_ref, xt_ref, g_ref,
@@ -267,30 +307,33 @@
     at = first - X_WIN[block + 1][0]
     cut = first - first_g
     live = in_image(idx_ref[0], first, width, image)
-    gain_own, gain_oth = gain_up_ref[:, :HALF], gain_up_ref[:, HALF:]
-
-    def one(r):
-        xo = xo_ref[r].astype(F32)[at : at + width]
-        xt = xt_ref[r].astype(F32)[at : at + width]
-        mean, rstd = stats(xo, xt)
-        uo, ut = (xo - mean) * rstd, (xt - mean) * rstd
-        po = (qm_ref[1, r].astype(F32) + qr_ref[0, r].astype(F32)) * gain_own
-        pt = (qm_ref[0, r].astype(F32) + qr_ref[1, r].astype(F32)) * gain_oth
-        level = (jnp.sum(po, axis=1, keepdims=True) + jnp.sum(pt, axis=1, keepdims=True)) / CHANS
-        cross = (
-            jnp.sum(po * uo, axis=1, keepdims=True) + jnp.sum(pt * ut, axis=1, keepdims=True)
-        ) / CHANS
-        g = g_ref[r].astype(F32)[cut : cut + width] + rstd * (po - level - uo * cross)
-        g = jnp.where(live, g, 0.0).astype(BF)
+    gain_up = gain_up_ref[...]
+    n = R_BACK
+
+    def some(r):
+        rows = pl.ds(r, n)
+        unit, rstd = unit_of(
+            widen(flat(xo_ref[rows, at : at + width]), flat(xt_ref[rows, at : at + width]))
+        )
+        p = gain_up * jnp.concatenate(
+            [
+                flat(qm_ref[1, rows]).astype(F32) + flat(qr_ref[0, rows]).astype(F32),
+                flat(qm_ref[0, rows]).astype(F32) + flat(qr_ref[1, rows]).astype(F32),
+            ],
+            axis=1,
+        )
+        change = p[:, :HALF] - chan_mean(p) - unit[:, :HALF] * chan_mean(p * unit)
+        g = flat(g_ref[rows, cut : cut + width]).astype(F32) + rstd * change
+        g = jnp.where(live, g.reshape(n, width, HALF), 0.0).astype(BF)
         if gn_ref is not None:
-            gn_ref[r] = g
-        s = (g.astype(F32) * d_ref[r]).astype(BF).astype(F32)
-        scatter_s(block, s, r, sbuf, sown)
-
-    row_loop(one, 2)
+            gn_ref[rows] = g
+        s = flat(g.astype(F32) * d_ref[rows])
+        scatter_s(block, s, r, n, sbuf, sown)
+
+    row_loop(some, n)
     if block:
         q_phase(block, sbuf, w_ref, wq, q_ref)
-    weight_phase(block, dims, idx_ref, sown, nk_ref, w_ref, gain_ref, wg_ref)
+    weight_phase(block, dims, idx_ref, sown, nk_ref, w_ref, gain_ref[...], wg_ref)
 
 
 def finish_kernel(dims, slabs, all_ref, perm_ref, out_ref):
@@ -313,7 +356,7 @@
     shards = nx * nz
     share = own_chans // ny
     lines = 8
-    while lines < share + 2:
+    while lines < share + 1:
         lines *= 2
     dims = (own_chans, share, lines)
     sec, ax, az = lax.axis_index("section"), lax.axis_index("x"), lax.axis_index("zh")
@@ -329,21 +372,11 @@
     perms = np.stack([np.eye(CHANS, dtype=np.float32)[:, o] for o in orders])
     perm = lax.dynamic_index_in_dim(jnp.asarray(perms, BF), core, 0, keepdims=False)
 
-    packed = call(prep_kernel, shape((own_chans, TAPS * CHANS), BF), [], (w1[0], perm))
-    wide = jnp.broadcast_to(packed[None], (ns * nz, own_chans, TAPS * CHANS))
+    packed = call(prep_kernel, shape((own_chans, CARRY), BF), [], (w1[0], gain, perm))
+    wide = jnp.broadcast_to(packed[None], (ns * nz, own_chans, CARRY))
     wide = lax.all_to_all(wide, ("section", "zh"), 0, 0, tiled=True)
-    wide = wide.reshape(ns, nz * own_chans, TAPS * CHANS)
+    wide = wide.reshape(ns, nz * own_chans, CARRY)
     weights = [lax.all_gather(wide[b], "x", axis=0, tiled=True) for b in range(ns)]
-    gains = lax.all_gather(gain[0], "section", axis=0)
-    gains = gains.reshape(ns, shards, 2, own_chans)
-    gains = jnp.concatenate(
-        [
-            lax.dynamic_index_in_dim(gains, core, 2, keepdims=False).reshape(ns, HALF),
-            lax.dynamic_index_in_dim(gains, 1 - core, 2, keepdims=False).reshape(ns, HALF),
-        ],
-        axis=1,
-    )
-    gains = [gains[b : b + 1] for b in range(ns)]
 
     def mine(value, edge):
         value = lax.dynamic_index_in_dim(value, sec, 0, keepdims=False).transpose(1, 0, 2)
@@ -360,6 +393,7 @@
     )
     windows = jnp.broadcast_to(windows[:, None], (shards, ny) + windows.shape[1:])
     windows = windows.reshape((shards * ny,) + windows.shape[2:])
+    windows, _ = lax.optimization_barrier((windows, wide))
     recv = lax.all_to_all(windows, ("x", "zh", "slab"), 0, 0, tiled=True)
     recv = recv.reshape(shards, ny, rows, own_chans, XWIN + CWIN)
     x_own, cot_own = call(
@@ -371,26 +405,29 @@
 
     taps3 = 3 * CHANS
     nk_shape = (ROWS + 2 * PAD, OWN, taps3)
-    halves, slopes, shifted = [(x_own, other(x_own))], [], []
+    gain_shape = shape((1, CHANS), F32)
+    halves, slopes, shifted, gains = [(x_own, other(x_own))], [], [], []
     for b in range(ns - 1):
         width = X_WIN[b + 1][1]
-        y, slope, nk = call(
+        y, slope, nk, gain_b = call(
             functools.partial(forward_kernel, b, image),
             (
                 shape((ROWS, width, HALF), BF),
                 shape((ROWS, S_WIN[b][1], HALF), F32),
                 shape(nk_shape, BF),
+                gain_shape,
             ),
             [
                 pltpu.VMEM((ROWS + 2 * PAD, width, taps3), BF),
                 pltpu.VMEM((ROWS, width, HALF), F32),
             ],
-            (idx, *halves[b], weights[b], gains[b]),
+            (idx, *halves[b], weights[b]),
             (0,),
         )
         halves.append((y, other(y)))
         slopes.append(slope)
         shifted.append(nk)
+        gains.append(gain_b)
 
     def back_scratch(b):
         width = S_WIN[b - 1][1]
@@ -404,9 +441,9 @@
     wg_shape = shape((count, TAPS * CHANS), BF)
     width = X_WIN[4][1]
     sbuf_s, sown_s, wq_s = back_scratch(3)
-    q, grads = call(
+    q, grads, gain_b = call(
         functools.partial(turn_kernel, dims),
-        (shape((2, ROWS, S_WIN[2][1], HALF), BF), wg_shape),
+        (shape((2, ROWS, S_WIN[2][1], HALF), BF), wg_shape, gain_shape),
         [
             pltpu.VMEM((ROWS + 2 * PAD, width, taps3), BF),
             pltpu.VMEM(nk_shape, BF),
@@ -415,10 +452,17 @@
             sown_s,
             wq_s,
         ],
-        (idx, *halves[3], cot_own, weights[3], gains[3]),
+        (idx, *halves[3], cot_own, weights[3]),
         (0,),
     )
-    weight_parts = [None] * 3 + [grads]
+    gains.append(gain_b)
+
+    def reduced(value):
+        value = value.reshape(nx, nz * lines, LANES)
+        value = lax.all_to_all(value, "x", 0, 0, tiled=True)
+        return jnp.sum(value.astype(F32), axis=0).astype(BF)
+
+    weight_parts = [None] * 3 + [reduced(grads)]
     g, first_g = cot_own, S_WIN[3][0]
     for b in (2, 1, 0):
         args = (
@@ -441,16 +485,11 @@
         else:
             (grads,) = call(kernel, (wg_shape,), [pltpu.VMEM((ROWS, OWN, HALF), BF)], args, (0,))
         first_g = S_WIN[b][0]
-        weight_parts[b] = grads
-
-    parts = jnp.stack(weight_parts).reshape(ns * shards, lines, TAPS * CHANS)
-    parts = lax.all_to_all(parts, ("section", "x", "zh"), 0, 0, tiled=True)
-    total = jnp.sum(parts.astype(F32), axis=0)
-    gain_sum = total[share, :CHANS] + total[share + 1, :CHANS]
-    high = gain_sum.astype(BF)
-    low = (gain_sum - high.astype(F32)).astype(BF)
-    total = total.astype(BF)
-    total = total.at[share, :CHANS].set(high).at[share + 1, :CHANS].set(low)
+        weight_parts[b] = reduced(grads)
+
+    parts = jnp.stack(weight_parts).reshape(ns * nz, lines, LANES)
+    parts = lax.all_to_all(parts, ("section", "zh"), 0, 0, tiled=True)
+    total = jnp.sum(parts.astype(F32), axis=0).astype(BF)
     every = lax.all_gather(total, "slab", axis=0, tiled=True)
     weight_grad = call(
         functools.partial(finish_kernel, dims, ny),
@@ -458,8 +497,8 @@
         [],
         (every, perm),
     )
-    gain_rows = every.reshape(ny, lines, TAPS * CHANS)[:, share : share + 2, :CHANS]
-    gain_all = jnp.sum(gain_rows.astype(F32), axis=(0, 1))
+    gain_rows = every.reshape(ny, lines, LANES)[:, share, :CHANS]
+    gain_all = jnp.sum(gain_rows.astype(F32), axis=0)
     here = lax.dynamic_slice_in_dim(gain_all, patch * own_chans, own_chans)
     there = lax.dynamic_slice_in_dim(gain_all, HALF + patch * own_chans, own_chans)
     gain_grad = here + other(there)

time: 326 us -> 323 us (level)
  waiting for transfers between devices: 132 us -> 115 us
  starting transfers between devices: 30.6 us -> 46.7 us
    all_to_all x1 -> x4, waiting for transfers between devices: 45.1 us -> 21.3 us  [the longest x1 14 us: local(): parts = lax.all_to_all(parts, ('section', 'zh'), 0, 0, tiled=True)]
    all_to_all x1 -> x4, starting transfers between devices: 4.44 us -> 19.1 us  [the longest x3 12.2 us: reduced(): value = lax.all_to_all(value, 'x', 0, 0, tiled=True)]
    all_to_all x0 -> x1, blocking collectives: none -> 11.2 us  [reduced(): value = lax.all_to_all(value, 'x', 0, 0, tiled=True)]
    all_gather x4, waiting for transfers between devices: 0.04 us -> 9.19 us  [local(): lax.all_gather(wide[b], 'x', axis=0, tiled=True)]
    all_gather x1 -> x0, blocking collectives: 8.63 us -> none  [local(): gains = lax.all_gather(gain[0], 'section', axis=0)]
    ppermute x8, waiting for transfers between devices: 15 us -> 10.4 us  [other(): return lax.ppermute(value, 'core', [(0, 1), (1, 0)])]
    unnamed x26 -> x20, local copies, waits for them, and re-layouts: 8.23 us -> 8.27 us
  transfers between devices with their start and end apart: 15 -> 18, of which waited for: 9 -> 9; matrix products, arithmetic and copies ran while one was open for 2% -> 1% of each run, Pallas kernels for 18% -> 23%
where the time goes in v2:
time: 323 us; the launch traced here: 322 us
  waiting for transfers between devices  115 us (36%)
  Pallas kernels  107 us (33%)
  starting transfers between devices  46.7 us (14%)
  blocking collectives  21.1 us (7%)
  local copies, waits for them, and re-layouts  16 us (5%)
  between operations  13.9 us (4%)
  other arithmetic  3.25 us (1%)
    pallas_call x10, Pallas kernels, call(): pl.pallas_call(kernel, out_shape=out_shape, in_specs=[sm if i in smem els...  107 us
    all_to_all x1, waiting for transfers between devices, local(): recv = lax.all_to_all(windows, ('x', 'zh', 'slab'), 0, 0, tiled=True)  40.1 us
    all_to_all x1, waiting for transfers between devices, local(): wide = lax.all_to_all(wide, ('section', 'zh'), 0, 0, tiled=True)  32.1 us
    all_to_all x1, waiting for transfers between devices, local(): parts = lax.all_to_all(parts, ('section', 'zh'), 0, 0, tiled=True)  14 us
    all_to_all x3, starting transfers between devices, reduced(): value = lax.all_to_all(value, 'x', 0, 0, tiled=True)  12.2 us
    all_to_all x1, blocking collectives, reduced(): value = lax.all_to_all(value, 'x', 0, 0, tiled=True)  11.2 us
    ppermute x8, waiting for transfers between devices, other(): return lax.ppermute(value, 'core', [(0, 1), (1, 0)])  10.4 us
    all_gather x1, blocking collectives, local(): every = lax.all_gather(total, 'slab', axis=0, tiled=True)  9.96 us
  transfers between devices with their start and end apart: 18, of which 9 were waited for; matrix products, arithmetic and copies ran while one was open for 1% of the time, Pallas kernels for 23%

profile of v2, /device:TPU:33, one launch (start us, length us, event | category | flops | bytes accessed | tf_op | source)
XLA Modules:
  0.0 322.4 jit_solution(3289061797936382465)
XLA Ops:
  7.2 1.7 dynamic-slice_bitcast_fusion.perm_ref
  8.9 2.4 shard_map.69
  11.3 2.1 broadcast_in_dim.9
  13.4 8.0 %all-to-all-start.1 = ((bf16[8,24,3584]{2,1,0:T(8,128)(2,1)}), bf16[8,24,3584]{2,1,0:T(8,128)(2,1)S(1)}, u32[]{:S(2)}, u32[]{:S(2)}) async-start(bf16[8,24,3584]{2,1,0:T(8,128)(2,1)} %broadcast_in_dim.9), calls=%async_computation.1 | async-start | bytes 2752512 | tf_op jit(solution)/shard_map/all_to_all | solution.py:377
  21.4 32.1 %all-to-all-done.1 = bf16[8,24,3584]{2,1,0:T(8,128)(2,1)S(1)} async-done(((bf16[8,24,3584]{2,1,0:T(8,128)(2,1)}), bf16[8,24,3584]{2,1,0:T(8,128)(2,1)S(1)}, u32[]{:S(2)}, u32[]{:S(2)}) %all-to-all-start.1) | async-done | bytes 1376288 | tf_op jit(solution)/shard_map/all_to_all | solution.py:377
  56.7 1.5 broadcast_in_dim.8
  58.2 9.7 %all-to-all-start = ((bf16[32,8,24,128]{3,2,1,0:T(8,128)(2,1)}), bf16[32,8,24,128]{3,2,1,0:T(8,128)(2,1)S(1)}, u32[]{:S(2)}, u32[]{:S(2)}) async-start(bf16[32,8,24,128]{3,2,1,0:T(8,128)(2,1)} %bitcast.16), calls=%async_computation | async-start | bytes 3145728 | tf_op jit(solution)/shard_map/all_to_all | solution.py:397
  69.4 40.1 %all-to-all-done = bf16[32,8,24,128]{3,2,1,0:T(8,128)(2,1)S(1)} async-done(((bf16[32,8,24,128]{3,2,1,0:T(8,128)(2,1)}), bf16[32,8,24,128]{3,2,1,0:T(8,128)(2,1)S(1)}, u32[]{:S(2)}, u32[]{:S(2)}) %all-to-all-start) | async-done | bytes 1572896 | tf_op jit(solution)/shard_map/all_to_all | solution.py:397
  110.7 5.0 %shard_map.68 = (bf16[32,80,192]{2,1,0:T(8,128)(2,1)}, bf16[32,48,192]{2,1,0:T(8,128)(2,1)}) custom-call(bf16[8,4,8,24,128]{4,3,2,1,0:T(8,128)(2,1)} %bitcast.66), custom_call_target="tpu_custom_call" | custom-call | tf_op jit(solution)/shard_map/pallas_call | solution.py:44
  115.7 1.9 collective-permute-start
  118.3 2.2 collective-permute-done.xt_ref
  121.6 15.7 %shard_map.70 = (bf16[32,80,192]{2,1,0:T(8,128)(2,1)}, f32[32,16,192]{2,1,0:T(8,128)}, bf16[48,16,1152]{2,1,0:T(8,128)(2,1)}, f32[1,384]{1,0:T(1,128)}) custom-call(s32[2]{0:T(128)} %pad_add_fusion.idx_ref, bf16[32,80,192]{2,1,0:T(8,128)(2,1)} %get-tuple-element.25.xo_ref, bf16[32,80,192]{2,1,0:T(8,128)(2,1)} %copy-done.4, ...), custom_call_target="tpu_custom_call" | custom-call | tf_op jit(solution)/shard_map/pallas_call | solution.py:44
  137.8 2.8 collective-permute-done.1.xt_ref
  141.7 16.2 %shard_map.71 = (bf16[32,80,192]{2,1,0:T(8,128)(2,1)}, f32[32,32,192]{2,1,0:T(8,128)}, bf16[48,16,1152]{2,1,0:T(8,128)(2,1)}, f32[1,384]{1,0:T(1,128)}) custom-call(s32[2]{0:T(128)} %pad_add_fusion.idx_ref, bf16[32,80,192]{2,1,0:T(8,128)(2,1)} %get-tuple-element.26.xo_ref, bf16[32,80,192]{2,1,0:T(8,128)(2,1)} %copy-done.1, ...), custom_call_target="tpu_custom_call" | custom-call | tf_op jit(solution)/shard_map/pallas_call | solution.py:44
  158.3 2.9 collective-permute-done.2.xt_ref
  162.3 14.3 %shard_map.72 = (bf16[32,64,192]{2,1,0:T(8,128)(2,1)}, f32[32,32,192]{2,1,0:T(8,128)}, bf16[48,16,1152]{2,1,0:T(8,128)(2,1)}, f32[1,384]{1,0:T(1,128)}) custom-call(s32[2]{0:T(128)} %pad_add_fusion.idx_ref, bf16[32,80,192]{2,1,0:T(8,128)(2,1)} %get-tuple-element.27.xo_ref, bf16[32,80,192]{2,1,0:T(8,128)(2,1)} %copy-done.2, ...), custom_call_target="tpu_custom_call" | custom-call | tf_op jit(solution)/shard_map/pallas_call | solution.py:44
  176.9 9.2 %all-gather.11.cloned.1.call-done.w_ref = bf16[192,3584]{1,0:T(8,128)(2,1)} async-done(((bf16[48,3584]{1,0:T(8,128)(2,1)}), bf16[192,3584]{1,0:T(8,128)(2,1)}) %all-gather.11.cloned.1.call-update) | async-done | bytes 1376272 | tf_op jit(solution)/shard_map/all_gather | solution.py:379
  187.1 15.8 %shard_map.73 = (bf16[2,32,32,192]{3,2,1,0:T(8,128)(2,1)}, bf16[64,3456]{1,0:T(8,128)(2,1)}, f32[1,384]{1,0:T(1,128)}) custom-call(s32[2]{0:T(128)} %pad_add_fusion.idx_ref, bf16[32,64,192]{2,1,0:T(8,128)(2,1)} %get-tuple-element.28.xo_ref, bf16[32,64,192]{2,1,0:T(8,128)(2,1)} %copy-done.3, bf16[32,48,192]{2,1,0:T(8,128)(2,1)} %get-tuple-element.29.cot_ref.g_ref, ...), custom_call_target="tpu_custom_call" | custom-call | tf_op jit(solution)/shard_map/pallas_call | solution.py:44
  204.3 2.5 collective-permute-done.4.qr_ref
  207.8 13.3 %shard_map.74 = (bf16[2,32,32,192]{3,2,1,0:T(8,128)(2,1)}, bf16[32,32,192]{2,1,0:T(8,128)(2,1)}, bf16[64,3456]{1,0:T(8,128)(2,1)}) custom-call(s32[2]{0:T(128)} %pad_add_fusion.idx_ref, bf16[2,32,32,192]{3,2,1,0:T(8,128)(2,1)} %get-tuple-element.30.qm_ref, bf16[2,32,32,192]{3,2,1,0:T(8,128)(2,1)} %copy-done.6, ...), custom_call_target="tpu_custom_call" | custom-call | tf_op jit(solution)/shard_map/pallas_call | solution.py:44
  221.4 11.2 %all_to_all.35 = bf16[4,16,3456]{2,1,0:T(8,128)(2,1)S(1)} all-to-all(bf16[4,16,3456]{2,1,0:T(8,128)(2,1)S(1)} %bitcast.77), channel_id=1, replica_groups=mesh['section'=4,'x'=4,'zh'=2,'core'=2,'slab'=4] {'x'}, dimensions={0} | all-to-all | bytes 884736 | tf_op jit(solution)/shard_map/all_to_all | solution.py:462
  232.6 3.5 %all-to-all-start.4 = ((bf16[4,16,3456]{2,1,0:T(8,128)(2,1)}), bf16[4,16,3456]{2,1,0:T(8,128)(2,1)S(1)}, u32[]{:S(2)}, u32[]{:S(2)}) async-start(bf16[4,16,3456]{2,1,0:T(8,128)(2,1)} %bitcast.75), calls=%async_computation.4 | async-start | bytes 884736 | tf_op jit(solution)/shard_map/all_to_all | solution.py:462
  237.2 11.5 %shard_map.75 = (bf16[2,32,16,192]{3,2,1,0:T(8,128)(2,1)}, bf16[32,32,192]{2,1,0:T(8,128)(2,1)}, bf16[64,3456]{1,0:T(8,128)(2,1)}) custom-call(s32[2]{0:T(128)} %pad_add_fusion.idx_ref, bf16[2,32,32,192]{3,2,1,0:T(8,128)(2,1)} %get-tuple-element.35.qm_ref, bf16[2,32,32,192]{3,2,1,0:T(8,128)(2,1)} %copy-done.5, ...), custom_call_target="tpu_custom_call" | custom-call | tf_op jit(solution)/shard_map/pallas_call | solution.py:44
  250.1 4.5 %all-to-all-start.3 = ((bf16[4,16,3456]{2,1,0:T(8,128)(2,1)}), bf16[4,16,3456]{2,1,0:T(8,128)(2,1)S(1)}, u32[]{:S(2)}, u32[]{:S(2)}) async-start(bf16[4,16,3456]{2,1,0:T(8,128)(2,1)} %bitcast.76), calls=%async_computation.3 | async-start | bytes 884736 | tf_op jit(solution)/shard_map/all_to_all | solution.py:462
  255.3 9.3 %shard_map.76 = bf16[64,3456]{1,0:T(8,128)(2,1)} custom-call(s32[2]{0:T(128)} %pad_add_fusion.idx_ref, bf16[2,32,16,192]{3,2,1,0:T(8,128)(2,1)} %get-tuple-element.40.qm_ref, bf16[2,32,16,192]{3,2,1,0:T(8,128)(2,1)} %copy-done.8, bf16[32,80,192]{2,1,0:T(8,128)(2,1)} %get-tuple-element.26.xo_ref, bf16[32,80,192]{2,1,0:T(8,128)(2,1)} %copy-done.1, ...), custom_call_target="tpu_custom_call" | custom-call | tf_op jit(solution)/shard_map/pallas_call | solution.py:44
  264.6 4.2 %all-to-all-start.2 = ((bf16[4,16,3456]{2,1,0:T(8,128)(2,1)}), bf16[4,16,3456]{2,1,0:T(8,128)(2,1)S(1)}, u32[]{:S(2)}, u32[]{:S(2)}) async-start(bf16[4,16,3456]{2,1,0:T(8,128)(2,1)} %bitcast.69), calls=%async_computation.2 | async-start | bytes 884736 | tf_op jit(solution)/shard_map/all_to_all | solution.py:462
  269.1 7.3 %all-to-all-done.2 = bf16[4,16,3456]{2,1,0:T(8,128)(2,1)S(1)} async-done(((bf16[4,16,3456]{2,1,0:T(8,128)(2,1)}), bf16[4,16,3456]{2,1,0:T(8,128)(2,1)S(1)}, u32[]{:S(2)}, u32[]{:S(2)}) %all-to-all-start.2) | async-done | bytes 442400 | tf_op jit(solution)/shard_map/all_to_all | solution.py:462
  277.3 6.9 %all-to-all-start.6 = ((bf16[8,8,3456]{2,1,0:T(8,128)(2,1)}), bf16[8,8,3456]{2,1,0:T(8,128)(2,1)S(1)}, u32[]{:S(2)}, u32[]{:S(2)}) async-start(bf16[8,8,3456]{2,1,0:T(8,128)(2,1)} %bitcast.32), calls=%async_computation.6 | async-start | bytes 884736 | tf_op jit(solution)/shard_map/all_to_all | solution.py:491
  284.2 14.0 %all-to-all-done.6 = bf16[8,8,3456]{2,1,0:T(8,128)(2,1)S(1)} async-done(((bf16[8,8,3456]{2,1,0:T(8,128)(2,1)}), bf16[8,8,3456]{2,1,0:T(8,128)(2,1)S(1)}, u32[]{:S(2)}, u32[]{:S(2)}) %all-to-all-start.6) | async-done | bytes 442400 | tf_op jit(solution)/shard_map/all_to_all | solution.py:491
  298.3 10.0 %all_gather.19.all_ref = bf16[32,3456]{1,0:T(8,128)(2,1)S(1)} all-gather(bf16[8,3456]{1,0:T(8,128)(2,1)S(1)} %reduce_sum.73), channel_id=1, replica_groups=mesh['section'=4,'x'=4,'zh'=2,'core'=2,'slab'=4] {'slab'}, dimensions={0}, use_global_device_ids=true | all-gather | bytes 276480 | tf_op jit(solution)/shard_map/all_gather | solution.py:493
  308.4 3.5 %collective-permute-start.7 = (f32[24]{0:T(128)S(1)}, f32[24]{0:T(128)S(1)}, u32[]{:S(2)}, u32[]{:S(2)}) collective-permute-start(f32[24]{0:T(128)S(1)} %dynamic_slice.21), channel_id=1, source_target_pairs={{0,4},{4,0},{1,5},{5,1},{2,6},{6,2},{3,7},{7,3},{8,12},{12,8},{9,1... | collective-permute-start | bytes 296 | tf_op jit(solution)/shard_map/ppermute | solution.py:368
  311.9 3.4 %shard_map.77 = f32[9,24,384]{2,1,0:T(8,128)} custom-call(bf16[32,3456]{1,0:T(8,128)(2,1)} %copy-done.7, bf16[384,384]{1,0:T(8,128)(2,1)} %dynamic-slice_bitcast_fusion.perm_ref), custom_call_target="tpu_custom_call" | custom-call | tf_op jit(solution)/shard_map/pallas_call | solution.py:44
  (67 shorter events, 19.9 us)
Async XLA Ops:
  13.4 40.1 %all-to-all-start.1 = ((bf16[8,24,3584]{2,1,0:T(8,128)(2,1)}), bf16[8,24,3584]{2,1,0:T(8,128)(2,1)S(1)}, u32[]{:S(2)}, u32[]{:S(2)}) async-start(bf16[8,24,3584]{2,1,0:T(8,128)(2,1)} %broadcast_in_dim.9), calls=%async_computation.1 | async-start | bytes 2752512 | tf_op jit(solution)/shard_map/all_to_all | solution.py:377
  21.4 99.1 %all-gather.5.cloned.1.call-start = ((), (), s32[]{:S(2)}) async-start(), calls=%async_computation.7 | async-start | bytes 1720320 | tf_op jit(solution)/shard_map/all_gather | solution.py:379
  58.2 51.3 %all-to-all-start = ((bf16[32,8,24,128]{3,2,1,0:T(8,128)(2,1)}), bf16[32,8,24,128]{3,2,1,0:T(8,128)(2,1)S(1)}, u32[]{:S(2)}, u32[]{:S(2)}) async-start(bf16[32,8,24,128]{3,2,1,0:T(8,128)(2,1)} %bitcast.16), calls=%async_computation | async-start | bytes 3145728 | tf_op jit(solution)/shard_map/all_to_all | solution.py:397
  67.9 69.9 %all-gather.7.cloned.1.call-start = ((), (), s32[]{:S(2)}) async-start(), calls=%async_computation.8 | async-start | bytes 1720320 | tf_op jit(solution)/shard_map/all_gather | solution.py:379
  68.7 89.6 %all-gather.9.cloned.1.call-start = ((), (), s32[]{:S(2)}) async-start(), calls=%async_computation.9 | async-start | bytes 1720320 | tf_op jit(solution)/shard_map/all_gather | solution.py:379
  69.4 116.7 %all-gather.11.cloned.1.call-start = ((), (), s32[]{:S(2)}) async-start(), calls=%async_computation.10 | async-start | bytes 1720320 | tf_op jit(solution)/shard_map/all_gather | solution.py:379
  109.5 1.2 copy-start
  115.7 4.8 %collective-permute-start = (bf16[32,80,192]{2,1,0:T(8,128)(2,1)}, bf16[32,80,192]{2,1,0:T(8,128)(2,1)S(1)}, u32[]{:S(2)}, u32[]{:S(2)}) collective-permute-start(bf16[32,80,192]{2,1,0:T(8,128)(2,1)} %get-tuple-element.25.xo_ref), channel_id=1, source_target_pairs={{0,4},{4,0},{1,5},{5,1},{2,6},{6,2},{3,7},{7,3},{8,12},{12,8},{9,1... | collective-permute-start | bytes 2949128 | tf_op jit(solution)/shard_map/ppermute | solution.py:368
  120.5 1.1 copy-start.4
  137.3 3.3 %collective-permute-start.1 = (bf16[32,80,192]{2,1,0:T(8,128)(2,1)}, bf16[32,80,192]{2,1,0:T(8,128)(2,1)S(1)}, u32[]{:S(2)}, u32[]{:S(2)}) collective-permute-start(bf16[32,80,192]{2,1,0:T(8,128)(2,1)} %get-tuple-element.26.xo_ref), channel_id=1, source_target_pairs={{0,4},{4,0},{1,5},{5,1},{2,6},{6,2},{3,7},{7,3},{8,12},{12,8},{9,1... | collective-permute-start | bytes 2949128 | tf_op jit(solution)/shard_map/ppermute | solution.py:368
  140.6 1.1 copy-start.1
  157.9 3.3 %collective-permute-start.2 = (bf16[32,80,192]{2,1,0:T(8,128)(2,1)}, bf16[32,80,192]{2,1,0:T(8,128)(2,1)S(1)}, u32[]{:S(2)}, u32[]{:S(2)}) collective-permute-start(bf16[32,80,192]{2,1,0:T(8,128)(2,1)} %get-tuple-element.27.xo_ref), channel_id=1, source_target_pairs={{0,4},{4,0},{1,5},{5,1},{2,6},{6,2},{3,7},{7,3},{8,12},{12,8},{9,1... | collective-permute-start | bytes 2949128 | tf_op jit(solution)/shard_map/ppermute | solution.py:368
  161.2 1.1 copy-start.2
  176.6 9.5 %collective-permute-start.3 = (bf16[32,64,192]{2,1,0:T(8,128)(2,1)}, bf16[32,64,192]{2,1,0:T(8,128)(2,1)S(1)}, u32[]{:S(2)}, u32[]{:S(2)}) collective-permute-start(bf16[32,64,192]{2,1,0:T(8,128)(2,1)} %get-tuple-element.28.xo_ref), channel_id=1, source_target_pairs={{0,4},{4,0},{1,5},{5,1},{2,6},{6,2},{3,7},{7,3},{8,12},{12,8},{9,1... | collective-permute-start | bytes 2359304 | tf_op jit(solution)/shard_map/ppermute | solution.py:368
  186.1 1.0 copy-start.3
  202.9 3.9 %collective-permute-start.4 = (bf16[2,32,32,192]{3,2,1,0:T(8,128)(2,1)}, bf16[2,32,32,192]{3,2,1,0:T(8,128)(2,1)S(1)}, u32[]{:S(2)}, u32[]{:S(2)}) collective-permute-start(bf16[2,32,32,192]{3,2,1,0:T(8,128)(2,1)} %get-tuple-element.30.qm_ref), channel_id=1, source_target_pairs={{0,4},{4,0},{1,5},{5,1},{2,6},{6,2},{3,7},{7,3},{8,12},{12,8},{9,1... | collective-permute-start | bytes 2359304 | tf_op jit(solution)/shard_map/ppermute | solution.py:368
  206.8 1.0 copy-start.6
  207.8 13.7 %copy-start.9 = (bf16[64,3456]{1,0:T(8,128)(2,1)S(1)}, bf16[64,3456]{1,0:T(8,128)(2,1)}, u32[]{:S(2)}) copy-start(bf16[64,3456]{1,0:T(8,128)(2,1)} %get-tuple-element.47) | copy-start | bytes 1327108
  221.1 15.0 %collective-permute-start.5 = (bf16[2,32,32,192]{3,2,1,0:T(8,128)(2,1)}, bf16[2,32,32,192]{3,2,1,0:T(8,128)(2,1)S(1)}, u32[]{:S(2)}, u32[]{:S(2)}) collective-permute-start(bf16[2,32,32,192]{3,2,1,0:T(8,128)(2,1)} %get-tuple-element.35.qm_ref), channel_id=1, source_target_pairs={{0,4},{4,0},{1,5},{5,1},{2,6},{6,2},{3,7},{7,3},{8,12},{12,8},{9,1... | collective-permute-start | bytes 2359304 | tf_op jit(solution)/shard_map/ppermute | solution.py:368
  232.6 17.5 %all-to-all-start.4 = ((bf16[4,16,3456]{2,1,0:T(8,128)(2,1)}), bf16[4,16,3456]{2,1,0:T(8,128)(2,1)S(1)}, u32[]{:S(2)}, u32[]{:S(2)}) async-start(bf16[4,16,3456]{2,1,0:T(8,128)(2,1)} %bitcast.75), calls=%async_computation.4 | async-start | bytes 884736 | tf_op jit(solution)/shard_map/all_to_all | solution.py:462
  236.1 1.1 copy-start.5
  248.6 5.9 %collective-permute-start.6 = (bf16[2,32,16,192]{3,2,1,0:T(8,128)(2,1)}, bf16[2,32,16,192]{3,2,1,0:T(8,128)(2,1)S(1)}, u32[]{:S(2)}, u32[]{:S(2)}) collective-permute-start(bf16[2,32,16,192]{3,2,1,0:T(8,128)(2,1)} %get-tuple-element.40.qm_ref), channel_id=1, source_target_pairs={{0,4},{4,0},{1,5},{5,1},{2,6},{6,2},{3,7},{7,3},{8,12},{12,8},{9,1... | collective-permute-start | bytes 1179656 | tf_op jit(solution)/shard_map/ppermute | solution.py:368
  250.1 14.6 %all-to-all-start.3 = ((bf16[4,16,3456]{2,1,0:T(8,128)(2,1)}), bf16[4,16,3456]{2,1,0:T(8,128)(2,1)S(1)}, u32[]{:S(2)}, u32[]{:S(2)}) async-start(bf16[4,16,3456]{2,1,0:T(8,128)(2,1)} %bitcast.76), calls=%async_computation.3 | async-start | bytes 884736 | tf_op jit(solution)/shard_map/all_to_all | solution.py:462
  254.5 0.8 copy-start.8
  264.6 11.7 %all-to-all-start.2 = ((bf16[4,16,3456]{2,1,0:T(8,128)(2,1)}), bf16[4,16,3456]{2,1,0:T(8,128)(2,1)S(1)}, u32[]{:S(2)}, u32[]{:S(2)}) async-start(bf16[4,16,3456]{2,1,0:T(8,128)(2,1)} %bitcast.69), calls=%async_computation.2 | async-start | bytes 884736 | tf_op jit(solution)/shard_map/all_to_all | solution.py:462
  277.3 21.0 %all-to-all-start.6 = ((bf16[8,8,3456]{2,1,0:T(8,128)(2,1)}), bf16[8,8,3456]{2,1,0:T(8,128)(2,1)S(1)}, u32[]{:S(2)}, u32[]{:S(2)}) async-start(bf16[8,8,3456]{2,1,0:T(8,128)(2,1)} %bitcast.32), calls=%async_computation.6 | async-start | bytes 884736 | tf_op jit(solution)/shard_map/all_to_all | solution.py:491
  308.3 3.6 %copy-start.7 = (bf16[32,3456]{1,0:T(8,128)(2,1)}, bf16[32,3456]{1,0:T(8,128)(2,1)S(1)}, u32[]{:S(2)}) copy-start(bf16[32,3456]{1,0:T(8,128)(2,1)S(1)} %all_gather.19.all_ref) | copy-start | bytes 663556
  308.4 6.9 %collective-permute-start.7 = (f32[24]{0:T(128)S(1)}, f32[24]{0:T(128)S(1)}, u32[]{:S(2)}, u32[]{:S(2)}) collective-permute-start(f32[24]{0:T(128)S(1)} %dynamic_slice.21), channel_id=1, source_target_pairs={{0,4},{4,0},{1,5},{5,1},{2,6},{6,2},{3,7},{7,3},{8,12},{12,8},{9,1... | collective-permute-start | bytes 296 | tf_op jit(solution)/shard_map/ppermute | solution.py:368
Sparse Core Ops, SparseCore 0:
  54.8 38.6 all-gather.4
  95.2 30.6 all-gather.6
  127.8 28.2 all-gather.8
  157.8 28.3 all-gather.10

commit v3 on v2

--- a/solution.py
+++ b/solution.py
@@ -25,13 +25,13 @@
 PAD = 8
 X_WIN = ((0, 80), (0, 80), (0, 80), (8, 64), (16, 48))
 S_WIN = ((32, 16), (24, 32), (24, 32), (16, 48))
-VMEM_LIMIT = 56 * 1024 * 1024
+VMEM_LIMIT = 26 * 1024 * 1024
 PARAMS = pltpu.CompilerParams(vmem_limit_bytes=VMEM_LIMIT)
 NT = (((1,), (1,)), ((), ()))
 NN = (((1,), (0,)), ((), ()))
 LANES = TAPS * CHANS
 CARRY = LANES + 128
-R_NORM, R_EPI, R_BACK = 2, 2, 2
+R_NORM, R_EPI, R_TURN, R_BACK = 4, 2, 2, 8
 
 
 def dot(a, b, dims):
@@ -131,7 +131,7 @@
 
     def one(r, carry):
         for y in range(slabs):
-            piece = recv_ref[:, y, pl.ds(r, 1)].astype(F32)
+            piece = recv_ref[y, :, pl.ds(r, 1)].astype(F32)
             piece = piece.reshape(HALF, lanes).astype(BF)
             flipped = dot(eye, piece, NT).astype(BF)
             x_ref[pl.ds(y * rows + r, 1)] = flipped[:XWIN].reshape(1, XWIN, HALF)
@@ -184,7 +184,17 @@
     lax.fori_loop(0, ROWS // step, one, 0)
 
 
-def forward_kernel(block, image, idx_ref, xo_ref, xt_ref, w_ref, y_ref, d_ref, nk, gain_ref, nbuf, pre):
+def forward_kernel(block, image, pieces, idx_ref, xo_ref, xt_ref, *rest):
+    w_refs, rest = rest[:pieces], rest[pieces:]
+    y_ref, d_ref, nk, gain_ref, *rest = rest
+    w_ref = w_refs[0]
+    if pieces > 1:
+        w_ref, *rest = rest
+        lines = HALF // pieces
+        for j in range(pieces):
+            place = lax.rem(idx_ref[2] + j, pieces) * lines
+            w_ref[pl.ds(pl.multiple_of(place, lines), lines)] = w_refs[j][...]
+    nbuf, pre = rest
     first_in = X_WIN[block][0]
     first_out, width_out = X_WIN[block + 1]
     first_s, width_s = S_WIN[block]
@@ -284,7 +294,7 @@
     gain_ref[...] = gain
     norm_phase(3, xo_ref, xt_ref, gain, nbuf, nk)
     conv_phase(3, nbuf, w_ref, pre)
-    n = R_BACK
+    n = R_TURN
 
     def some(r):
         act = flat(pre[pl.ds(r, n)])
@@ -362,7 +372,7 @@
     sec, ax, az = lax.axis_index("section"), lax.axis_index("x"), lax.axis_index("zh")
     core, slab = lax.axis_index("core"), lax.axis_index("slab")
     patch = ax * nz + az
-    idx = jnp.stack([patch * OWN, slab]).astype(jnp.int32)
+    idx = jnp.stack([patch * OWN, slab, ax]).astype(jnp.int32)
 
     def other(value):
         return lax.ppermute(value, "core", [(0, 1), (1, 0)])
@@ -371,12 +381,6 @@
     orders = [np.concatenate([order[:, h].ravel(), order[:, 1 - h].ravel()]) for h in (0, 1)]
     perms = np.stack([np.eye(CHANS, dtype=np.float32)[:, o] for o in orders])
     perm = lax.dynamic_index_in_dim(jnp.asarray(perms, BF), core, 0, keepdims=False)
-
-    packed = call(prep_kernel, shape((own_chans, CARRY), BF), [], (w1[0], gain, perm))
-    wide = jnp.broadcast_to(packed[None], (ns * nz, own_chans, CARRY))
-    wide = lax.all_to_all(wide, ("section", "zh"), 0, 0, tiled=True)
-    wide = wide.reshape(ns, nz * own_chans, CARRY)
-    weights = [lax.all_gather(wide[b], "x", axis=0, tiled=True) for b in range(ns)]
 
     def mine(value, edge):
         value = lax.dynamic_index_in_dim(value, sec, 0, keepdims=False).transpose(1, 0, 2)
@@ -391,16 +395,30 @@
             for p in range(shards)
         ]
     )
-    windows = jnp.broadcast_to(windows[:, None], (shards, ny) + windows.shape[1:])
-    windows = windows.reshape((shards * ny,) + windows.shape[2:])
-    windows, _ = lax.optimization_barrier((windows, wide))
-    recv = lax.all_to_all(windows, ("x", "zh", "slab"), 0, 0, tiled=True)
-    recv = recv.reshape(shards, ny, rows, own_chans, XWIN + CWIN)
+    recv = lax.all_to_all(windows, ("x", "zh"), 0, 0, tiled=True)
+
+    packed = call(prep_kernel, shape((own_chans, CARRY), BF), [], (w1[0], gain, perm))
+    wide = jnp.broadcast_to(packed[None], (ns * nz, own_chans, CARRY))
+    wide, recv = lax.optimization_barrier((wide, recv))
+    wide = lax.all_to_all(wide, ("section", "zh"), 0, 0, tiled=True)
+    wide = wide.reshape(ns, nz * own_chans, CARRY)
+
+
+    def from_chips(value):
+        moves = [[(i, (i - j) % nx) for i in range(nx)] for j in range(1, nx)]
+        return [value] + [lax.ppermute(value, "x", move) for move in moves]
+
+    weights = [
+        from_chips(wide[b]) if b < 2 else [lax.all_gather(wide[b], "x", axis=0, tiled=True)]
+        for b in range(ns)
+    ]
+
+    every_row = lax.all_gather(recv, "slab", axis=0)
     x_own, cot_own = call(
         functools.partial(assemble_kernel, ny, rows),
         (shape((ROWS, XWIN, HALF), BF), shape((ROWS, CWIN, HALF), BF)),
         [],
-        (recv,),
+        (every_row,),
     )
 
     taps3 = 3 * CHANS
@@ -409,25 +427,28 @@
     halves, slopes, shifted, gains = [(x_own, other(x_own))], [], [], []
     for b in range(ns - 1):
         width = X_WIN[b + 1][1]
-        y, slope, nk, gain_b = call(
-            functools.partial(forward_kernel, b, image),
+        pieces = len(weights[b])
+        y, slope, nk, gain_b, *whole = call(
+            functools.partial(forward_kernel, b, image, pieces),
             (
                 shape((ROWS, width, HALF), BF),
                 shape((ROWS, S_WIN[b][1], HALF), F32),
                 shape(nk_shape, BF),
                 gain_shape,
-            ),
+            )
+            + (shape((HALF, CARRY), BF),) * (pieces > 1),
             [
                 pltpu.VMEM((ROWS + 2 * PAD, width, taps3), BF),
                 pltpu.VMEM((ROWS, width, HALF), F32),
             ],
-            (idx, *halves[b], weights[b]),
+            (idx, *halves[b], *weights[b]),
             (0,),
         )
         halves.append((y, other(y)))
         slopes.append(slope)
         shifted.append(nk)
         gains.append(gain_b)
+        weights[b] = whole[0] if whole else weights[b][0]
 
     def back_scratch(b):
         width = S_WIN[b - 1][1]
@@ -452,17 +473,19 @@
             sown_s,
             wq_s,
         ],
-        (idx, *halves[3], cot_own, weights[3]),
+        (idx, *halves[3], cot_own, weights[3][0]),
         (0,),
     )
     gains.append(gain_b)
 
-    def reduced(value):
+    def reduced(b, value):
+        if b > 1:
+            return lax.psum_scatter(value, "x", scatter_dimension=0, tiled=True)
         value = value.reshape(nx, nz * lines, LANES)
         value = lax.all_to_all(value, "x", 0, 0, tiled=True)
         return jnp.sum(value.astype(F32), axis=0).astype(BF)
 
-    weight_parts = [None] * 3 + [reduced(grads)]
+    weight_parts = [None] * 3 + [reduced(3, grads)]
     g, first_g = cot_own, S_WIN[3][0]
     for b in (2, 1, 0):
         args = (
@@ -485,7 +508,7 @@
         else:
             (grads,) = call(kernel, (wg_shape,), [pltpu.VMEM((ROWS, OWN, HALF), BF)], args, (0,))
         first_g = S_WIN[b][0]
-        weight_parts[b] = reduced(grads)
+        weight_parts[b] = reduced(b, grads)
 
     parts = jnp.stack(weight_parts).reshape(ns * nz, lines, LANES)
     parts = lax.all_to_all(parts, ("section", "zh"), 0, 0, tiled=True)

time: 323 us -> 316 us (0.978)
  Pallas kernels: 107 us -> 73.5 us
  local copies, waits for them, and re-layouts: 16 us -> 42.8 us
  blocking collectives: 21.1 us -> 9.3 us
  waiting for transfers between devices: 115 us -> 125 us
  starting transfers between devices: 46.7 us -> 40.6 us
  other arithmetic: 3.25 us -> 9.35 us
    ppermute x0 -> x6, waiting for transfers between devices: none -> 45.3 us  [from_chips(): return [value] + [lax.ppermute(value, 'x', move) for move in moves]]
    pallas_call x10, Pallas kernels: 107 us -> 73.5 us  [call(): pl.pallas_call(kernel, out_shape=out_shape, in_specs=[sm if i in smem els...]
    unnamed x20 -> x86, local copies, waits for them, and re-layouts: 8.27 us -> 38.4 us
    all_to_all x1, waiting for transfers between devices: 40.1 us -> 14.9 us  [local(): recv = lax.all_to_all(windows, ('x', 'zh'), 0, 0, tiled=True)]
    all_to_all x1 -> x0, blocking collectives: 11.2 us -> none  [reduced(): value = lax.all_to_all(value, 'x', 0, 0, tiled=True)]
    all_gather x4 -> x2, waiting for transfers between devices: 9.19 us -> 0.01 us  [local(): lax.all_gather(wide[b], 'x', axis=0, tiled=True)]
    ppermute x0 -> x6, starting transfers between devices: none -> 4.94 us  [from_chips(): return [value] + [lax.ppermute(value, 'x', move) for move in moves]]
    all_to_all x1, starting transfers between devices: 8.01 us -> 3.52 us  [local(): wide = lax.all_to_all(wide, ('section', 'zh'), 0, 0, tiled=True)]
  transfers between devices with their start and end apart: 18 -> 24, of which waited for: 9 -> 15; matrix products, arithmetic and copies ran while one was open for 1% -> 1% of each run, Pallas kernels for 23% -> 19%
where the time goes in v3:
time: 316 us; the launch traced here: 315 us
  waiting for transfers between devices  125 us (40%)
  Pallas kernels  73.5 us (23%)
  local copies, waits for them, and re-layouts  42.8 us (14%)
  starting transfers between devices  40.6 us (13%)
  between operations  14 us (4%)
  other arithmetic  9.35 us (3%)
  blocking collectives  9.3 us (3%)
    pallas_call x10, Pallas kernels, call(): pl.pallas_call(kernel, out_shape=out_shape, in_specs=[sm if i in smem els...  73.5 us
    ppermute x6, waiting for transfers between devices, from_chips(): return [value] + [lax.ppermute(value, 'x', move) for move in moves]  45.3 us
    unnamed x86, local copies, waits for them, and re-layouts  38.4 us
    all_to_all x1, waiting for transfers between devices, local(): wide = lax.all_to_all(wide, ('section', 'zh'), 0, 0, tiled=True)  30.8 us
    all_to_all x1, waiting for transfers between devices, local(): recv = lax.all_to_all(windows, ('x', 'zh'), 0, 0, tiled=True)  14.9 us
    all_to_all x1, waiting for transfers between devices, local(): parts = lax.all_to_all(parts, ('section', 'zh'), 0, 0, tiled=True)  14.4 us
    ppermute x8, waiting for transfers between devices, other(): return lax.ppermute(value, 'core', [(0, 1), (1, 0)])  10.4 us
    all_to_all x1, starting transfers between devices, local(): recv = lax.all_to_all(windows, ('x', 'zh'), 0, 0, tiled=True)  9.75 us
  transfers between devices with their start and end apart: 24, of which 15 were waited for; matrix products, arithmetic and copies ran while one was open for 1% of the time, Pallas kernels for 19%

profile of v3, /device:TPU:33, one launch (start us, length us, event | category | flops | bytes accessed | tf_op | source)
XLA Modules:
  0.0 314.6 jit_solution(14163184959703801076)
XLA Ops:
  14.0 9.7 %all-to-all-start = ((bf16[8,8,24,128]{3,1,2,0:T(8,128)(2,1)}), bf16[8,8,24,128]{3,1,2,0:T(8,128)(2,1)S(1)}, u32[]{:S(2)}, u32[]{:S(2)}) async-start(bf16[8,8,24,128]{3,1,2,0:T(8,128)(2,1)} %fusion.7), calls=%async_computation | async-start | bytes 786432 | tf_op jit(solution)/shard_map/all_to_all | solution.py:398
  25.2 14.9 %all-to-all-done = bf16[8,8,24,128]{3,1,2,0:T(8,128)(2,1)S(1)} async-done(((bf16[8,8,24,128]{3,1,2,0:T(8,128)(2,1)}), bf16[8,8,24,128]{3,1,2,0:T(8,128)(2,1)S(1)}, u32[]{:S(2)}, u32[]{:S(2)}) %all-to-all-start) | async-done | bytes 393248 | tf_op jit(solution)/shard_map/all_to_all | solution.py:398
  41.2 3.5 %all-to-all-start.1 = ((bf16[8,24,3584]{2,1,0:T(8,128)(2,1)}), bf16[8,24,3584]{2,1,0:T(8,128)(2,1)S(1)}, u32[]{:S(2)}, u32[]{:S(2)}) async-start(bf16[8,24,3584]{2,1,0:T(8,128)(2,1)} %broadcast_in_dim.12), calls=%async_computation.1 | async-start | bytes 2752512 | tf_op jit(solution)/shard_map/all_to_all | solution.py:403
  45.7 30.8 %all-to-all-done.1 = bf16[8,24,3584]{2,1,0:T(8,128)(2,1)S(1)} async-done(((bf16[8,24,3584]{2,1,0:T(8,128)(2,1)}), bf16[8,24,3584]{2,1,0:T(8,128)(2,1)S(1)}, u32[]{:S(2)}, u32[]{:S(2)}) %all-to-all-start.1) | async-done | bytes 1376288 | tf_op jit(solution)/shard_map/all_to_all | solution.py:403
  79.0 2.2 shard_map.69
  85.7 7.3 %collective-permute-done.1.rest_1_ = bf16[48,3584]{1,0:T(8,128)(2,1)S(1)} collective-permute-done((bf16[48,3584]{1,0:T(8,128)(2,1)S(1)}, bf16[48,3584]{1,0:T(8,128)(2,1)S(1)}, u32[]{:S(2)}, u32[]{:S(2)}) %collective-permute-start.1) | collective-permute-done | bytes 344096 | tf_op jit(solution)/shard_map/ppermute | solution.py:409
  93.1 2.4 collective-permute-done.2.rest_2_
  95.5 15.2 %collective-permute-done.3.rest_3_ = bf16[48,3584]{1,0:T(8,128)(2,1)S(1)} collective-permute-done((bf16[48,3584]{1,0:T(8,128)(2,1)S(1)}, bf16[48,3584]{1,0:T(8,128)(2,1)S(1)}, u32[]{:S(2)}, u32[]{:S(2)}) %collective-permute-start.3) | collective-permute-done | bytes 344096 | tf_op jit(solution)/shard_map/ppermute | solution.py:409
  112.0 11.8 %shard_map.70 = (bf16[32,80,192]{2,1,0:T(8,128)(2,1)S(1)}, f32[32,16,192]{2,1,0:T(8,128)S(1)}, bf16[48,16,1152]{2,1,0:T(8,128)(2,1)S(1)}, f32[1,384]{1,0:T(1,128)S(1)}, bf16[192,3584]{1,0:T(8,128)(2,1)S(1)}) custom-call(s32[3]{0:T(128)S(1)} %pad_add_fusion.idx_ref, bf16[32,80,192]{2,1,0:T(8,128)(2,1)S(1)} %copy-done.24, ...), custom_call_target="tpu_custom_call" | custom-call | tf_op jit(solution)/shard_map/pallas_call | solution.py:44
  127.4 1.9 collective-permute-start.5
  130.1 7.3 %collective-permute-done.5.rest_1_ = bf16[48,3584]{1,0:T(8,128)(2,1)} collective-permute-done((bf16[48,3584]{1,0:T(8,128)(2,1)}, bf16[48,3584]{1,0:T(8,128)(2,1)}, u32[]{:S(2)}, u32[]{:S(2)}) %collective-permute-start.5) | collective-permute-done | bytes 344096 | tf_op jit(solution)/shard_map/ppermute | solution.py:409
  137.4 3.2 %collective-permute-done.6.rest_2_ = bf16[48,3584]{1,0:T(8,128)(2,1)} collective-permute-done((bf16[48,3584]{1,0:T(8,128)(2,1)}, bf16[48,3584]{1,0:T(8,128)(2,1)}, u32[]{:S(2)}, u32[]{:S(2)}) %collective-permute-start.6) | collective-permute-done | bytes 344096 | tf_op jit(solution)/shard_map/ppermute | solution.py:409
  140.6 9.9 %collective-permute-done.7.rest_3_ = bf16[48,3584]{1,0:T(8,128)(2,1)} collective-permute-done((bf16[48,3584]{1,0:T(8,128)(2,1)}, bf16[48,3584]{1,0:T(8,128)(2,1)}, u32[]{:S(2)}, u32[]{:S(2)}) %collective-permute-start.7) | collective-permute-done | bytes 344096 | tf_op jit(solution)/shard_map/ppermute | solution.py:409
  150.5 13.5 %shard_map.71 = (bf16[32,80,192]{2,1,0:T(8,128)(2,1)}, f32[32,32,192]{2,1,0:T(8,128)S(1)}, bf16[48,16,1152]{2,1,0:T(8,128)(2,1)S(1)}, f32[1,384]{1,0:T(1,128)S(1)}, bf16[192,3584]{1,0:T(8,128)(2,1)S(1)}) custom-call(s32[3]{0:T(128)S(1)} %pad_add_fusion.idx_ref, bf16[32,80,192]{2,1,0:T(8,128)(2,1)S(1)} %get-tuple-element.32.xo_ref, ...), custom_call_target="tpu_custom_call" | custom-call | tf_op jit(solution)/shard_map/pallas_call | solution.py:44
  168.0 2.9 collective-permute-done.8.xt_ref
  172.2 11.7 %shard_map.72 = (bf16[32,64,192]{2,1,0:T(8,128)(2,1)}, f32[32,32,192]{2,1,0:T(8,128)S(1)}, bf16[48,16,1152]{2,1,0:T(8,128)(2,1)S(1)}, f32[1,384]{1,0:T(1,128)S(1)}) custom-call(s32[3]{0:T(128)S(1)} %pad_add_fusion.idx_ref, bf16[32,80,192]{2,1,0:T(8,128)(2,1)} %get-tuple-element.33.xo_ref, bf16[32,80,192]{2,1,0:T(8,128)(2,1)S(1)} %collective-permute-done.8.xt_ref, ...), custom_call_target="tpu_custom_call" | custom-call | tf_op jit(solution)/shard_map/pallas_call | solution.py:44
  186.5 2.5 collective-permute-done.9.xt_ref
  192.6 12.7 %shard_map.73 = (bf16[2,32,32,192]{3,2,1,0:T(8,128)(2,1)}, bf16[64,3456]{1,0:T(8,128)(2,1)S(1)}, f32[1,384]{1,0:T(1,128)S(1)}) custom-call(s32[3]{0:T(128)S(1)} %pad_add_fusion.idx_ref, bf16[32,64,192]{2,1,0:T(8,128)(2,1)} %get-tuple-element.34.xo_ref, bf16[32,64,192]{2,1,0:T(8,128)(2,1)S(1)} %copy-done.7, ...), custom_call_target="tpu_custom_call" | custom-call | tf_op jit(solution)/shard_map/pallas_call | solution.py:44
  206.4 2.6 collective-permute-done.10.qr_ref
  212.9 8.0 %shard_map.74 = (bf16[2,32,32,192]{3,2,1,0:T(8,128)(2,1)}, bf16[32,32,192]{2,1,0:T(8,128)(2,1)S(1)}, bf16[64,3456]{1,0:T(8,128)(2,1)S(1)}) custom-call(s32[3]{0:T(128)S(1)} %pad_add_fusion.idx_ref, bf16[2,32,32,192]{3,2,1,0:T(8,128)(2,1)} %get-tuple-element.36.qm_ref, bf16[2,32,32,192]{3,2,1,0:T(8,128)(2,1)} %collective-permute-done.10.qr_ref, ...), custom_call_target="tpu_custom_call" | custom-call | tf_op jit(solution)/shard_map/pallas_call | solution.py:44
  223.0 2.5 collective-permute-done.11.qr_ref
  234.1 6.2 %shard_map.75 = (bf16[2,32,16,192]{3,2,1,0:T(8,128)(2,1)}, bf16[32,32,192]{2,1,0:T(8,128)(2,1)S(1)}, bf16[64,3456]{1,0:T(8,128)(2,1)S(1)}) custom-call(s32[3]{0:T(128)S(1)} %pad_add_fusion.idx_ref, bf16[2,32,32,192]{3,2,1,0:T(8,128)(2,1)} %get-tuple-element.41.qm_ref, bf16[2,32,32,192]{3,2,1,0:T(8,128)(2,1)S(1)} %copy-done.30, ...), custom_call_target="tpu_custom_call" | custom-call | tf_op jit(solution)/shard_map/pallas_call | solution.py:44
  242.2 4.3 %all-to-all-start.3 = ((bf16[4,16,3456]{2,1,0:T(8,128)(2,1)}), bf16[4,16,3456]{2,1,0:T(8,128)(2,1)}, u32[]{:S(2)}, u32[]{:S(2)}) async-start(bf16[4,16,3456]{2,1,0:T(8,128)(2,1)} %bitcast.68), calls=%async_computation.3 | async-start | bytes 884736 | tf_op jit(solution)/shard_map/all_to_all | solution.py:485
  250.5 4.5 %shard_map.76 = bf16[64,3456]{1,0:T(8,128)(2,1)} custom-call(s32[3]{0:T(128)S(1)} %pad_add_fusion.idx_ref, bf16[2,32,16,192]{3,2,1,0:T(8,128)(2,1)} %get-tuple-element.47.qm_ref, bf16[2,32,16,192]{3,2,1,0:T(8,128)(2,1)} %collective-permute-done.12.qr_ref, bf16[32,80,192]{2,1,0:T(8,128)(2,1)S(1)} %get-tuple-element.32.xo_ref, ...), custom_call_target="tpu_custom_call" | custom-call | tf_op jit(solution)/shard_map/pallas_call | solution.py:44
  255.0 2.3 all-to-all-done.3
  257.3 3.5 %all-to-all-start.2 = ((bf16[4,16,3456]{2,1,0:T(8,128)(2,1)}), bf16[4,16,3456]{2,1,0:T(8,128)(2,1)S(1)}, u32[]{:S(2)}, u32[]{:S(2)}) async-start(bf16[4,16,3456]{2,1,0:T(8,128)(2,1)} %bitcast.24), calls=%async_computation.2 | async-start | bytes 884736 | tf_op jit(solution)/shard_map/all_to_all | solution.py:485
  261.9 6.9 %all-to-all-done.2 = bf16[4,16,3456]{2,1,0:T(8,128)(2,1)S(1)} async-done(((bf16[4,16,3456]{2,1,0:T(8,128)(2,1)}), bf16[4,16,3456]{2,1,0:T(8,128)(2,1)S(1)}, u32[]{:S(2)}, u32[]{:S(2)}) %all-to-all-start.2) | async-done | bytes 442400 | tf_op jit(solution)/shard_map/all_to_all | solution.py:485
  270.7 7.1 %all-to-all-start.4 = ((bf16[8,8,3456]{2,1,0:T(8,128)(2,1)}), bf16[8,8,3456]{2,1,0:T(8,128)(2,1)S(1)}, u32[]{:S(2)}, u32[]{:S(2)}) async-start(bf16[8,8,3456]{2,1,0:T(8,128)(2,1)} %bitcast.30), calls=%async_computation.6 | async-start | bytes 884736 | tf_op jit(solution)/shard_map/all_to_all | solution.py:514
  277.8 14.4 %all-to-all-done.4 = bf16[8,8,3456]{2,1,0:T(8,128)(2,1)S(1)} async-done(((bf16[8,8,3456]{2,1,0:T(8,128)(2,1)}), bf16[8,8,3456]{2,1,0:T(8,128)(2,1)S(1)}, u32[]{:S(2)}, u32[]{:S(2)}) %all-to-all-start.4) | async-done | bytes 442400 | tf_op jit(solution)/shard_map/all_to_all | solution.py:514
  292.3 9.3 %all_gather.19.all_ref = bf16[32,3456]{1,0:T(8,128)(2,1)S(1)} all-gather(bf16[8,3456]{1,0:T(8,128)(2,1)S(1)} %reduce_sum.47), channel_id=1, replica_groups=mesh['section'=4,'x'=4,'zh'=2,'core'=2,'slab'=4] {'slab'}, dimensions={0}, use_global_device_ids=true | all-gather | bytes 276480 | tf_op jit(solution)/shard_map/all_gather | solution.py:516
  301.7 3.4 %collective-permute-start.13 = (f32[24]{0:T(128)S(1)}, f32[24]{0:T(128)S(1)}, u32[]{:S(2)}, u32[]{:S(2)}) collective-permute-start(f32[24]{0:T(128)S(1)} %dynamic_slice.21), channel_id=1, source_target_pairs={{0,4},{4,0},{1,5},{5,1},{2,6},{6,2},{3,7},{7,3},{8,12},{12,8},{9,1... | collective-permute-start | bytes 296 | tf_op jit(solution)/shard_map/ppermute | solution.py:378
  305.1 2.4 shard_map.77
  (141 shorter events, 59.9 us)
Async XLA Ops:
  8.2 15.6 %copy-start.42 = (bf16[2,384,384]{2,1,0:T(8,128)(2,1)S(1)}, bf16[2,384,384]{2,1,0:T(8,128)(2,1)}, u32[]{:S(2)}) copy-start(bf16[2,384,384]{2,1,0:T(8,128)(2,1)} %constant.54.clone) | copy-start | bytes 1769476
  8.3 15.5 %copy-start.40 = (bf16[1,9,24,384]{3,2,1,0:T(8,128)(2,1)S(1)}, bf16[1,9,24,384]{3,2,1,0:T(8,128)(2,1)}, u32[]{:S(2)}) copy-start(bf16[1,9,24,384]{3,2,1,0:T(8,128)(2,1)} %param.7) | copy-start | bytes 497668
  8.4 15.5 %copy-start.41 = (f32[1,384]{1,0:T(1,128)S(1)}, f32[1,384]{1,0:T(1,128)}, u32[]{:S(2)}) copy-start(f32[1,384]{1,0:T(1,128)} %gain_ref.1) | copy-start | bytes 4612
  14.0 26.0 %all-to-all-start = ((bf16[8,8,24,128]{3,1,2,0:T(8,128)(2,1)}), bf16[8,8,24,128]{3,1,2,0:T(8,128)(2,1)S(1)}, u32[]{:S(2)}, u32[]{:S(2)}) async-start(bf16[8,8,24,128]{3,1,2,0:T(8,128)(2,1)} %fusion.7), calls=%async_computation | async-start | bytes 786432 | tf_op jit(solution)/shard_map/all_to_all | solution.py:398
  41.2 35.3 %all-to-all-start.1 = ((bf16[8,24,3584]{2,1,0:T(8,128)(2,1)}), bf16[8,24,3584]{2,1,0:T(8,128)(2,1)S(1)}, u32[]{:S(2)}, u32[]{:S(2)}) async-start(bf16[8,24,3584]{2,1,0:T(8,128)(2,1)} %broadcast_in_dim.12), calls=%async_computation.1 | async-start | bytes 2752512 | tf_op jit(solution)/shard_map/all_to_all | solution.py:403
  44.7 32.9 %all-gather.9.cloned.1.call-start = ((), (), s32[]{:S(2)}) async-start(), calls=%async_computation.11 | async-start | bytes 1966080 | tf_op jit(solution)/shard_map/all_gather | solution.py:416
  45.6 122.3 %all-gather.5.cloned.1.call-start = ((), (), s32[]{:S(2)}) async-start(), calls=%async_computation.7 | async-start | bytes 1720320 | tf_op jit(solution)/shard_map/all_gather | solution.py:412
  77.6 108.9 %all-gather.7.cloned.1.call-start = ((), (), s32[]{:S(2)}) async-start(), calls=%async_computation.8 | async-start | bytes 1720320 | tf_op jit(solution)/shard_map/all_gather | solution.py:412
  81.2 29.4 %collective-permute-start = (bf16[32,80,192]{2,1,0:T(8,128)(2,1)S(1)}, bf16[32,80,192]{2,1,0:T(8,128)(2,1)}, u32[]{:S(2)}, u32[]{:S(2)}) collective-permute-start(bf16[32,80,192]{2,1,0:T(8,128)(2,1)S(1)} %get-tuple-element.30.xo_ref), channel_id=1, source_target_pairs={{0,4},{4,0},{1,5},{5,1},{2,6},{6,2},{3,7},{7,3},{8,12},{12,8},{9,1... | collective-permute-start | bytes 2949128 | tf_op jit(solution)/shard_map/ppermute | solution.py:378
  83.4 9.7 %collective-permute-start.1 = (bf16[48,3584]{1,0:T(8,128)(2,1)S(1)}, bf16[48,3584]{1,0:T(8,128)(2,1)S(1)}, u32[]{:S(2)}, u32[]{:S(2)}) collective-permute-start(bf16[48,3584]{1,0:T(8,128)(2,1)S(1)} %bitcast.63), channel_id=1, source_target_pairs={{0,48},{16,0},{32,16},{48,32},{1,49},{17,1},{33,17},{49,33},{2,50}... | collective-permute-start | bytes 1032200 | tf_op jit(solution)/shard_map/ppermute | solution.py:409
  84.5 11.0 %collective-permute-start.2 = (bf16[48,3584]{1,0:T(8,128)(2,1)S(1)}, bf16[48,3584]{1,0:T(8,128)(2,1)S(1)}, u32[]{:S(2)}, u32[]{:S(2)}) collective-permute-start(bf16[48,3584]{1,0:T(8,128)(2,1)S(1)} %bitcast.64), channel_id=1, source_target_pairs={{0,32},{16,48},{32,0},{48,16},{1,33},{17,49},{33,1},{49,17},{2,34}... | collective-permute-start | bytes 1032200 | tf_op jit(solution)/shard_map/ppermute | solution.py:409
  85.1 25.5 %collective-permute-start.3 = (bf16[48,3584]{1,0:T(8,128)(2,1)S(1)}, bf16[48,3584]{1,0:T(8,128)(2,1)S(1)}, u32[]{:S(2)}, u32[]{:S(2)}) collective-permute-start(bf16[48,3584]{1,0:T(8,128)(2,1)S(1)} %bitcast.65), channel_id=1, source_target_pairs={{0,16},{16,32},{32,48},{48,0},{1,17},{17,33},{33,49},{49,1},{2,18}... | collective-permute-start | bytes 1032200 | tf_op jit(solution)/shard_map/ppermute | solution.py:409
  126.8 23.7 %collective-permute-start.4 = (bf16[32,80,192]{2,1,0:T(8,128)(2,1)S(1)}, bf16[32,80,192]{2,1,0:T(8,128)(2,1)S(1)}, u32[]{:S(2)}, u32[]{:S(2)}) collective-permute-start(bf16[32,80,192]{2,1,0:T(8,128)(2,1)S(1)} %get-tuple-element.32.xo_ref), channel_id=1, source_target_pairs={{0,4},{4,0},{1,5},{5,1},{2,6},{6,2},{3,7},{7,3},{8,12},{12,8},{9,1... | collective-permute-start | bytes 2949128 | tf_op jit(solution)/shard_map/ppermute | solution.py:378
  127.4 10.0 %collective-permute-start.5 = (bf16[48,3584]{1,0:T(8,128)(2,1)}, bf16[48,3584]{1,0:T(8,128)(2,1)}, u32[]{:S(2)}, u32[]{:S(2)}) collective-permute-start(bf16[48,3584]{1,0:T(8,128)(2,1)} %bitcast.21.rest_0_), channel_id=1, source_target_pairs={{0,48},{16,0},{32,16},{48,32},{1,49},{17,1},{33,17},{49,33},{2,50}... | collective-permute-start | bytes 1032200 | tf_op jit(solution)/shard_map/ppermute | solution.py:409
  129.4 11.2 %collective-permute-start.6 = (bf16[48,3584]{1,0:T(8,128)(2,1)}, bf16[48,3584]{1,0:T(8,128)(2,1)}, u32[]{:S(2)}, u32[]{:S(2)}) collective-permute-start(bf16[48,3584]{1,0:T(8,128)(2,1)} %bitcast.21.rest_0_), channel_id=1, source_target_pairs={{0,32},{16,48},{32,0},{48,16},{1,33},{17,49},{33,1},{49,17},{2,34}... | collective-permute-start | bytes 1032200 | tf_op jit(solution)/shard_map/ppermute | solution.py:409
  130.1 20.5 %collective-permute-start.7 = (bf16[48,3584]{1,0:T(8,128)(2,1)}, bf16[48,3584]{1,0:T(8,128)(2,1)}, u32[]{:S(2)}, u32[]{:S(2)}) collective-permute-start(bf16[48,3584]{1,0:T(8,128)(2,1)} %bitcast.21.rest_0_), channel_id=1, source_target_pairs={{0,16},{16,32},{32,48},{48,0},{1,17},{17,33},{33,49},{49,1},{2,18}... | collective-permute-start | bytes 1032200 | tf_op jit(solution)/shard_map/ppermute | solution.py:409
  130.1 138.8 %reduce-scatter.5.cloned.1.call-start = ((), (), s32[]{:S(2)}) async-start(), calls=%async_computation.10 | async-start | bytes 552960 | tf_op jit(solution)/shard_map/reduce_scatter | solution.py:483
  150.5 13.5 %copy-start.2 = (bf16[32,80,192]{2,1,0:T(8,128)(2,1)}, bf16[32,80,192]{2,1,0:T(8,128)(2,1)S(1)}, u32[]{:S(2)}) copy-start(bf16[32,80,192]{2,1,0:T(8,128)(2,1)S(1)} %collective-permute-done.4.xt_ref) | copy-start | bytes 2949124
  167.3 3.6 %collective-permute-start.8 = (bf16[32,80,192]{2,1,0:T(8,128)(2,1)}, bf16[32,80,192]{2,1,0:T(8,128)(2,1)S(1)}, u32[]{:S(2)}, u32[]{:S(2)}) collective-permute-start(bf16[32,80,192]{2,1,0:T(8,128)(2,1)} %get-tuple-element.33.xo_ref), channel_id=1, source_target_pairs={{0,4},{4,0},{1,5},{5,1},{2,6},{6,2},{3,7},{7,3},{8,12},{12,8},{9,1... | collective-permute-start | bytes 2949128 | tf_op jit(solution)/shard_map/ppermute | solution.py:378
  186.1 2.9 collective-permute-start.9
  192.6 16.5 %copy-start.1 = (bf16[192,3584]{1,0:T(8,128)(2,1)S(1)}, bf16[192,3584]{1,0:T(8,128)(2,1)}, u32[]{:S(2)}) copy-start(bf16[192,3584]{1,0:T(8,128)(2,1)} %all-gather.5.cloned.1.call-done.rest_0_.w_ref) | copy-start | bytes 4128772
  206.0 3.0 collective-permute-start.10
  206.4 62.5 %reduce-scatter.3.cloned.1.call-start = ((), (), s32[]{:S(2)}) async-start(), calls=%async_computation.9 | async-start | bytes 552960 | tf_op jit(solution)/shard_map/reduce_scatter | solution.py:483
  222.6 2.9 collective-permute-start.11
  234.1 12.5 %copy-start.3 = (bf16[32,80,192]{2,1,0:T(8,128)(2,1)S(1)}, bf16[32,80,192]{2,1,0:T(8,128)(2,1)}, u32[]{:S(2)}) copy-start(bf16[32,80,192]{2,1,0:T(8,128)(2,1)} %copy-done.2) | copy-start | bytes 2949124
  234.1 12.5 %copy-start.32 = (f32[32,16,192]{2,1,0:T(8,128)S(1)}, f32[32,16,192]{2,1,0:T(8,128)}, u32[]{:S(2)}) copy-start(f32[32,16,192]{2,1,0:T(8,128)} %copy-done.31) | copy-start | bytes 1179652
  241.8 4.7 %collective-permute-start.12 = (bf16[2,32,16,192]{3,2,1,0:T(8,128)(2,1)}, bf16[2,32,16,192]{3,2,1,0:T(8,128)(2,1)}, u32[]{:S(2)}, u32[]{:S(2)}) collective-permute-start(bf16[2,32,16,192]{3,2,1,0:T(8,128)(2,1)} %get-tuple-element.47.qm_ref), channel_id=1, source_target_pairs={{0,4},{4,0},{1,5},{5,1},{2,6},{6,2},{3,7},{7,3},{8,12},{12,8},{9,1... | collective-permute-start | bytes 1179656 | tf_op jit(solution)/shard_map/ppermute | solution.py:378
  242.2 15.1 %all-to-all-start.3 = ((bf16[4,16,3456]{2,1,0:T(8,128)(2,1)}), bf16[4,16,3456]{2,1,0:T(8,128)(2,1)}, u32[]{:S(2)}, u32[]{:S(2)}) async-start(bf16[4,16,3456]{2,1,0:T(8,128)(2,1)} %bitcast.68), calls=%async_computation.3 | async-start | bytes 884736 | tf_op jit(solution)/shard_map/all_to_all | solution.py:485
  257.3 11.4 %all-to-all-start.2 = ((bf16[4,16,3456]{2,1,0:T(8,128)(2,1)}), bf16[4,16,3456]{2,1,0:T(8,128)(2,1)S(1)}, u32[]{:S(2)}, u32[]{:S(2)}) async-start(bf16[4,16,3456]{2,1,0:T(8,128)(2,1)} %bitcast.24), calls=%async_computation.2 | async-start | bytes 884736 | tf_op jit(solution)/shard_map/all_to_all | solution.py:485
  268.8 36.3 %copy-start.10 = (bf16[384,384]{1,0:T(8,128)(2,1)S(1)}, bf16[384,384]{1,0:T(8,128)(2,1)}, u32[]{:S(2)}) copy-start(bf16[384,384]{1,0:T(8,128)(2,1)} %copy-done.9) | copy-start | bytes 884740
  270.7 21.5 %all-to-all-start.4 = ((bf16[8,8,3456]{2,1,0:T(8,128)(2,1)}), bf16[8,8,3456]{2,1,0:T(8,128)(2,1)S(1)}, u32[]{:S(2)}, u32[]{:S(2)}) async-start(bf16[8,8,3456]{2,1,0:T(8,128)(2,1)} %bitcast.30), calls=%async_computation.6 | async-start | bytes 884736 | tf_op jit(solution)/shard_map/all_to_all | solution.py:514
  301.7 5.8 %collective-permute-start.13 = (f32[24]{0:T(128)S(1)}, f32[24]{0:T(128)S(1)}, u32[]{:S(2)}, u32[]{:S(2)}) collective-permute-start(f32[24]{0:T(128)S(1)} %dynamic_slice.21), channel_id=1, source_target_pairs={{0,4},{4,0},{1,5},{5,1},{2,6},{6,2},{3,7},{7,3},{8,12},{12,8},{9,1... | collective-permute-start | bytes 296 | tf_op jit(solution)/shard_map/ppermute | solution.py:378
  (35 other events, 50.1 us)
Sparse Core Ops, SparseCore 0:
  47.4 29.2 all-gather.8
  78.5 36.3 all-gather.4
  130.2 29.3 all-gather.6
  206.5 22.1 reduce-scatter.4
  231.3 24.4 reduce-scatter.2

commit v4 on v3

--- a/solution.py
+++ b/solution.py
@@ -25,7 +25,7 @@
 PAD = 8
 X_WIN = ((0, 80), (0, 80), (0, 80), (8, 64), (16, 48))
 S_WIN = ((32, 16), (24, 32), (24, 32), (16, 48))
-VMEM_LIMIT = 26 * 1024 * 1024
+VMEM_LIMIT = 56 * 1024 * 1024
 PARAMS = pltpu.CompilerParams(vmem_limit_bytes=VMEM_LIMIT)
 NT = (((1,), (1,)), ((), ()))
 NN = (((1,), (0,)), ((), ()))
@@ -38,14 +38,19 @@
     return lax.dot_general(a, b, dims, preferred_element_type=F32)
 
 
-def call(kernel, out_shape, scratch, args, smem=()):
+def call(kernel, out_shape, scratch, args, smem=(), far=(), far_out=()):
     vm = pl.BlockSpec(memory_space=pltpu.VMEM)
     sm = pl.BlockSpec(memory_space=pltpu.SMEM)
+    hb = pl.BlockSpec(memory_space=pltpu.HBM)
+    if isinstance(out_shape, tuple):
+        out_specs = tuple(hb if i in far_out else vm for i in range(len(out_shape)))
+    else:
+        out_specs = vm
     return pl.pallas_call(
         kernel,
         out_shape=out_shape,
-        in_specs=[sm if i in smem else vm for i in range(len(args))],
-        out_specs=jax.tree.map(lambda _: vm, out_shape),
+        in_specs=[sm if i in smem else hb if i in far else vm for i in range(len(args))],
+        out_specs=out_specs,
         scratch_shapes=scratch,
         compiler_params=PARAMS,
     )(*args)
@@ -122,6 +127,28 @@
     out_ref[:, LANES:CARRY] = tile.astype(BF)
 
 
+def window_kernel(idx_ref, x_ref, cot_ref, out_ref):
+    shards, rows, chans, lanes = out_ref.shape
+    image = x_ref.shape[3]
+    x = x_ref[idx_ref[3]].astype(F32)
+    cot = cot_ref[idx_ref[3]].astype(F32)
+    lane = lax.broadcasted_iota(jnp.int32, (chans, lanes), 1)
+    room = jnp.zeros((chans, lanes - image), F32)
+    for r in range(rows):
+        from_x, from_cot = x[:, r, :], cot[:, r, :]
+        if image < lanes:
+            from_x = jnp.concatenate([from_x, room], axis=1)
+            from_cot = jnp.concatenate([from_cot, room], axis=1)
+        for p in range(shards):
+            here = None
+            for value, start in ((from_x, OWN * p - 32), (from_cot, OWN * p - 16 - XWIN)):
+                shift = (-start) % lanes
+                moved = pltpu.roll(value, shift, 1) if shift else value
+                moved = jnp.where((lane + start >= 0) & (lane + start < image), moved, 0.0)
+                here = moved if here is None else jnp.where(lane < XWIN, here, moved)
+            out_ref[p, r] = here.astype(BF)
+
+
 def assemble_kernel(slabs, rows, recv_ref, x_ref, cot_ref):
     lanes = XWIN + CWIN
     eye = (
@@ -184,23 +211,29 @@
     lax.fori_loop(0, ROWS // step, one, 0)
 
 
-def forward_kernel(block, image, pieces, idx_ref, xo_ref, xt_ref, *rest):
+def forward_kernel(block, image, pieces, spin, idx_ref, xo_ref, xt_ref, *rest):
     w_refs, rest = rest[:pieces], rest[pieces:]
-    y_ref, d_ref, nk, gain_ref, *rest = rest
+    y_ref, d_ref, gain_ref, nk_far, *rest = rest
     w_ref = w_refs[0]
+    whole = None
     if pieces > 1:
-        w_ref, *rest = rest
+        whole_far, nk, nbuf, pre, sem, w_ref = rest
         lines = HALF // pieces
         for j in range(pieces):
-            place = lax.rem(idx_ref[2] + j, pieces) * lines
+            place = lax.rem(idx_ref[spin] + j, pieces) * lines
             w_ref[pl.ds(pl.multiple_of(place, lines), lines)] = w_refs[j][...]
-    nbuf, pre = rest
+        whole = pltpu.make_async_copy(w_ref, whole_far, sem.at[1])
+        whole.start()
+    else:
+        nk, nbuf, pre, sem = rest
     first_in = X_WIN[block][0]
     first_out, width_out = X_WIN[block + 1]
     first_s, width_s = S_WIN[block]
     gain = read_gain(w_ref)
     gain_ref[...] = gain
     norm_phase(block, xo_ref, xt_ref, gain, nbuf, nk)
+    kept = pltpu.make_async_copy(nk, nk_far, sem.at[0])
+    kept.start()
     conv_phase(block, nbuf, w_ref, pre)
     live = in_image(idx_ref[0], first_out, width_out, image)
     low, at = first_out - first_in, first_s - first_out
@@ -214,6 +247,9 @@
         d_ref[pl.ds(r, n)] = gelu_slope(act[:, at : at + width_s], tangent[:, at : at + width_s])
 
     row_loop(some, n)
+    kept.wait()
+    if whole is not None:
+        whole.wait()
 
 
 def scatter_s(block, s, r, n, sbuf, sown):
@@ -307,12 +343,16 @@
 
 
 def backward_kernel(block, dims, image, first_g, idx_ref, qm_ref, qr_ref, xo_ref, xt_ref, g_ref,
-                    gain_up_ref, d_ref, w_ref, nk_ref, gain_ref, *rest):
+                    gain_up_ref, d_ref, w_far, nk_far, gain_ref, *rest):
     if block:
-        q_ref, gn_ref, wg_ref, sown, sbuf, wq = rest
+        q_ref, gn_ref, wg_ref, w_ref, nk_ref, sem, sown, sbuf, wq = rest
     else:
-        wg_ref, sown = rest
+        wg_ref, w_ref, nk_ref, sem, sown = rest
         q_ref = gn_ref = sbuf = wq = None
+    weights_in = pltpu.make_async_copy(w_far, w_ref, sem.at[0])
+    kept_in = pltpu.make_async_copy(nk_far, nk_ref, sem.at[1])
+    weights_in.start()
+    kept_in.start()
     first, width = S_WIN[block]
     at = first - X_WIN[block + 1][0]
     cut = first - first_g
@@ -341,8 +381,10 @@
         scatter_s(block, s, r, n, sbuf, sown)
 
     row_loop(some, n)
+    weights_in.wait()
     if block:
         q_phase(block, sbuf, w_ref, wq, q_ref)
+    kept_in.wait()
     weight_phase(block, dims, idx_ref, sown, nk_ref, w_ref, gain_ref[...], wg_ref)
 
 
@@ -372,7 +414,7 @@
     sec, ax, az = lax.axis_index("section"), lax.axis_index("x"), lax.axis_index("zh")
     core, slab = lax.axis_index("core"), lax.axis_index("slab")
     patch = ax * nz + az
-    idx = jnp.stack([patch * OWN, slab, ax]).astype(jnp.int32)
+    idx = jnp.stack([patch * OWN, slab, ax, sec]).astype(jnp.int32)
 
     def other(value):
         return lax.ppermute(value, "core", [(0, 1), (1, 0)])
@@ -382,34 +424,31 @@
     perms = np.stack([np.eye(CHANS, dtype=np.float32)[:, o] for o in orders])
     perm = lax.dynamic_index_in_dim(jnp.asarray(perms, BF), core, 0, keepdims=False)
 
-    def mine(value, edge):
-        value = lax.dynamic_index_in_dim(value, sec, 0, keepdims=False).transpose(1, 0, 2)
-        return jnp.pad(value, ((0, 0), (0, 0), (edge, edge)))
-
-    wide_x, wide_c = mine(x_in, 32), mine(cot, 16)
-    windows = jnp.stack(
-        [
-            jnp.concatenate(
-                [wide_x[:, :, OWN * p : OWN * p + XWIN], wide_c[:, :, OWN * p : OWN * p + CWIN]], axis=2
-            )
-            for p in range(shards)
-        ]
+    windows = call(
+        window_kernel, shape((shards, rows, own_chans, XWIN + CWIN), BF), [], (idx, x_in, cot), (0,)
     )
     recv = lax.all_to_all(windows, ("x", "zh"), 0, 0, tiled=True)
 
     packed = call(prep_kernel, shape((own_chans, CARRY), BF), [], (w1[0], gain, perm))
+    if nx == ny:
+        turn = []
+        for n in range(ns * nx * ny):
+            b, i, j = n // (nx * ny), n // ny % nx, n % ny
+            turn.append((n, (b * nx + j) * ny + i if b % 2 else n))
+        packed = lax.ppermute(packed, ("section", "x", "slab"), turn)
     wide = jnp.broadcast_to(packed[None], (ns * nz, own_chans, CARRY))
     wide, recv = lax.optimization_barrier((wide, recv))
     wide = lax.all_to_all(wide, ("section", "zh"), 0, 0, tiled=True)
     wide = wide.reshape(ns, nz * own_chans, CARRY)
 
 
-    def from_chips(value):
-        moves = [[(i, (i - j) % nx) for i in range(nx)] for j in range(1, nx)]
-        return [value] + [lax.ppermute(value, "x", move) for move in moves]
-
+    def from_chips(value, axis, size):
+        moves = [[(i, (i - j) % size) for i in range(size)] for j in range(1, size)]
+        return [value] + [lax.ppermute(value, axis, move) for move in moves]
+
+    along = [("slab" if b % 2 and nx == ny else "x") for b in range(ns)]
     weights = [
-        from_chips(wide[b]) if b < 2 else [lax.all_gather(wide[b], "x", axis=0, tiled=True)]
+        [lax.all_gather(wide[b], along[b], axis=0, tiled=True)] if b % 2 else from_chips(wide[b], "x", nx)
         for b in range(ns)
     ]
 
@@ -428,21 +467,28 @@
     for b in range(ns - 1):
         width = X_WIN[b + 1][1]
         pieces = len(weights[b])
-        y, slope, nk, gain_b, *whole = call(
-            functools.partial(forward_kernel, b, image, pieces),
+        many = pieces > 1
+        whole_shape = shape((HALF, CARRY), BF)
+        y, slope, gain_b, nk, *whole = call(
+            functools.partial(forward_kernel, b, image, pieces, 2),
             (
                 shape((ROWS, width, HALF), BF),
                 shape((ROWS, S_WIN[b][1], HALF), F32),
+                gain_shape,
                 shape(nk_shape, BF),
-                gain_shape,
             )
-            + (shape((HALF, CARRY), BF),) * (pieces > 1),
+            + (whole_shape,) * many,
             [
+                pltpu.VMEM(nk_shape, BF),
                 pltpu.VMEM((ROWS + 2 * PAD, width, taps3), BF),
                 pltpu.VMEM((ROWS, width, HALF), F32),
-            ],
+                pltpu.SemaphoreType.DMA((2,)),
+            ]
+            + [pltpu.VMEM((HALF, CARRY), BF)] * many,
             (idx, *halves[b], *weights[b]),
             (0,),
+            (),
+            (3, 4),
         )
         halves.append((y, other(y)))
         slopes.append(slope)
@@ -492,6 +538,11 @@
             idx, q, other(q), *halves[b + 1], g, gains[b + 1], slopes[b], weights[b], shifted[b], gains[b],
         )
         kernel = functools.partial(backward_kernel, b, dims, image, first_g)
+        fetched = [
+            pltpu.VMEM((HALF, CARRY), BF),
+            pltpu.VMEM(nk_shape, BF),
+            pltpu.SemaphoreType.DMA((2,)),
+        ]
         if b:
             sbuf_s, sown_s, wq_s = back_scratch(b)
             q, g, grads = call(
@@ -501,12 +552,14 @@
                     shape((ROWS, S_WIN[b][1], HALF), BF),
                     wg_shape,
                 ),
-                [sown_s, sbuf_s, wq_s],
+                fetched + [sown_s, sbuf_s, wq_s],
                 args,
                 (0,),
+                (8, 9),
             )
         else:
-            (grads,) = call(kernel, (wg_shape,), [pltpu.VMEM((ROWS, OWN, HALF), BF)], args, (0,))
+            own_s = pltpu.VMEM((ROWS, OWN, HALF), BF)
+            (grads,) = call(kernel, (wg_shape,), fetched + [own_s], args, (0,), (8, 9))
         first_g = S_WIN[b][0]
         weight_parts[b] = reduced(b, grads)
 

time: 316 us -> 289 us (0.915)
  local copies, waits for them, and re-layouts: 42.8 us -> 11.6 us
  Pallas kernels: 73.5 us -> 91.8 us
  waiting for transfers between devices: 125 us -> 115 us
  other arithmetic: 9.35 us -> 3.29 us
    unnamed x86 -> x36, local copies, waits for them, and re-layouts: 38.4 us -> 8.58 us
    pallas_call x10 -> x11, Pallas kernels: 73.5 us -> 91.8 us  [call(): pl.pallas_call(kernel, out_shape=out_shape, in_specs=[sm if i in smem els...]
    ppermute x6 -> x7, waiting for transfers between devices: 45.3 us -> 35.8 us  [the longest x6 35.8 us: from_chips(): return [value] + [lax.ppermute(value, axis, move) for move in moves]]
    unnamed x7 -> x0, other arithmetic: 4.93 us -> none
    all_gather x1, waiting for transfers between devices: 0.02 us -> 4.45 us  [local(): every_row = lax.all_gather(recv, 'slab', axis=0)]
    ppermute x6 -> x7, starting transfers between devices: 4.94 us -> 7.26 us  [the longest x6 5.69 us: from_chips(): return [value] + [lax.ppermute(value, axis, move) for move in moves]]
  transfers between devices with their start and end apart: 24 -> 25, of which waited for: 15 -> 15; matrix products, arithmetic and copies ran while one was open for 1% -> 1% of each run, Pallas kernels for 19% -> 26%
where the time goes in v4:
time: 289 us; the launch traced here: 288 us
  waiting for transfers between devices  115 us (40%)
  Pallas kernels  91.8 us (32%)
  starting transfers between devices  41.5 us (14%)
  between operations  14 us (5%)
  local copies, waits for them, and re-layouts  11.6 us (4%)
  blocking collectives  10.4 us (4%)
  other arithmetic  3.29 us (1%)
    pallas_call x11, Pallas kernels, call(): pl.pallas_call(kernel, out_shape=out_shape, in_specs=[sm if i in smem els...  91.8 us
    ppermute x6, waiting for transfers between devices, from_chips(): return [value] + [lax.ppermute(value, axis, move) for move in moves]  35.8 us
    all_to_all x1, waiting for transfers between devices, local(): wide = lax.all_to_all(wide, ('section', 'zh'), 0, 0, tiled=True)  30.6 us
    all_to_all x1, waiting for transfers between devices, local(): parts = lax.all_to_all(parts, ('section', 'zh'), 0, 0, tiled=True)  13.5 us
    all_to_all x1, waiting for transfers between devices, local(): recv = lax.all_to_all(windows, ('x', 'zh'), 0, 0, tiled=True)  11.8 us
    all_gather x1, blocking collectives, local(): every = lax.all_gather(total, 'slab', axis=0, tiled=True)  10.4 us
    ppermute x8, waiting for transfers between devices, other(): return lax.ppermute(value, 'core', [(0, 1), (1, 0)])  10.2 us
    all_to_all x1, starting transfers between devices, local(): recv = lax.all_to_all(windows, ('x', 'zh'), 0, 0, tiled=True)  9.75 us
  transfers between devices with their start and end apart: 25, of which 15 were waited for; matrix products, arithmetic and copies ran while one was open for 1% of the time, Pallas kernels for 26%

profile of v4, /device:TPU:33, one launch (start us, length us, event | category | flops | bytes accessed | tf_op | source)
XLA Modules:
  0.0 288.1 jit_solution(2291346032942464373)
XLA Ops:
  7.8 2.1 shard_map.69
  9.9 9.7 %all-to-all-start = ((bf16[8,8,24,128]{3,2,1,0:T(8,128)(2,1)}), bf16[8,8,24,128]{3,2,1,0:T(8,128)(2,1)S(1)}, u32[]{:S(2)}, u32[]{:S(2)}) async-start(bf16[8,8,24,128]{3,2,1,0:T(8,128)(2,1)} %shard_map.69), calls=%async_computation | async-start | bytes 786432 | tf_op jit(solution)/shard_map/all_to_all | solution.py:430
  20.4 2.4 shard_map.68
  24.3 11.8 %all-to-all-done = bf16[8,8,24,128]{3,2,1,0:T(8,128)(2,1)S(1)} async-done(((bf16[8,8,24,128]{3,2,1,0:T(8,128)(2,1)}), bf16[8,8,24,128]{3,2,1,0:T(8,128)(2,1)S(1)}, u32[]{:S(2)}, u32[]{:S(2)}) %all-to-all-start) | async-done | bytes 393248 | tf_op jit(solution)/shard_map/all_to_all | solution.py:430
  37.4 3.5 %all-to-all-start.1 = ((bf16[8,24,3584]{2,1,0:T(8,128)(2,1)}), bf16[8,24,3584]{2,1,0:T(8,128)(2,1)S(1)}, u32[]{:S(2)}, u32[]{:S(2)}) async-start(bf16[8,24,3584]{2,1,0:T(8,128)(2,1)} %broadcast_in_dim.12), calls=%async_computation.1 | async-start | bytes 2752512 | tf_op jit(solution)/shard_map/all_to_all | solution.py:441
  41.7 30.6 %all-to-all-done.1 = bf16[8,24,3584]{2,1,0:T(8,128)(2,1)S(1)} async-done(((bf16[8,24,3584]{2,1,0:T(8,128)(2,1)}), bf16[8,24,3584]{2,1,0:T(8,128)(2,1)S(1)}, u32[]{:S(2)}, u32[]{:S(2)}) %all-to-all-start.1) | async-done | bytes 1376288 | tf_op jit(solution)/shard_map/all_to_all | solution.py:441
  73.3 4.5 %all-gather.9.cloned.1.call-done = bf16[32,8,24,128]{3,2,1,0:T(8,128)(2,1)} async-done(((bf16[8,8,24,128]{3,2,1,0:T(8,128)(2,1)}), bf16[32,8,24,128]{3,2,1,0:T(8,128)(2,1)}) %all-gather.9.cloned.1.call-update) | async-done | bytes 1572880 | tf_op jit(solution)/shard_map/all_gather | solution.py:455
  77.8 5.0 %shard_map.70 = (bf16[32,80,192]{2,1,0:T(8,128)(2,1)}, bf16[32,48,192]{2,1,0:T(8,128)(2,1)}) custom-call(bf16[4,8,8,24,128]{4,3,2,1,0:T(8,128)(2,1)} %bitcast.24), custom_call_target="tpu_custom_call" | custom-call | tf_op jit(solution)/shard_map/pallas_call | solution.py:49
  83.4 3.6 %collective-permute-start.2 = (bf16[48,3584]{1,0:T(8,128)(2,1)S(1)}, bf16[48,3584]{1,0:T(8,128)(2,1)S(1)}, u32[]{:S(2)}, u32[]{:S(2)}) collective-permute-start(bf16[48,3584]{1,0:T(8,128)(2,1)S(1)} %bitcast.31), channel_id=1, source_target_pairs={{0,48},{16,0},{32,16},{48,32},{1,49},{17,1},{33,17},{49,33},{2,50}... | collective-permute-start | bytes 1032200 | tf_op jit(solution)/shard_map/ppermute | solution.py:447
  87.6 14.3 %collective-permute-done.2.rest_1_ = bf16[48,3584]{1,0:T(8,128)(2,1)S(1)} collective-permute-done((bf16[48,3584]{1,0:T(8,128)(2,1)S(1)}, bf16[48,3584]{1,0:T(8,128)(2,1)S(1)}, u32[]{:S(2)}, u32[]{:S(2)}) %collective-permute-start.2) | collective-permute-done | bytes 344096 | tf_op jit(solution)/shard_map/ppermute | solution.py:447
  101.9 3.5 %collective-permute-done.4.rest_3_ = bf16[48,3584]{1,0:T(8,128)(2,1)S(1)} collective-permute-done((bf16[48,3584]{1,0:T(8,128)(2,1)S(1)}, bf16[48,3584]{1,0:T(8,128)(2,1)S(1)}, u32[]{:S(2)}, u32[]{:S(2)}) %collective-permute-start.4) | collective-permute-done | bytes 344096 | tf_op jit(solution)/shard_map/ppermute | solution.py:447
  107.3 13.8 %shard_map.71 = (bf16[32,80,192]{2,1,0:T(8,128)(2,1)}, f32[32,16,192]{2,1,0:T(8,128)}, f32[1,384]{1,0:T(1,128)}, bf16[48,16,1152]{2,1,0:T(8,128)(2,1)}, bf16[192,3584]{1,0:T(8,128)(2,1)}) custom-call(s32[4]{0:T(128)} %pad_add_fusion.idx_ref, bf16[32,80,192]{2,1,0:T(8,128)(2,1)} %get-tuple-element.30.xo_ref, bf16[32,80,192]{2,1,0:T(8,128)(2,1)} %copy-done.6, ...), custom_call_target="tpu_custom_call" | custom-call | tf_op jit(solution)/shard_map/pallas_call | solution.py:49
  121.9 2.8 collective-permute-done.5.xt_ref
  125.9 14.2 %shard_map.72 = (bf16[32,80,192]{2,1,0:T(8,128)(2,1)}, f32[32,32,192]{2,1,0:T(8,128)}, f32[1,384]{1,0:T(1,128)}, bf16[48,16,1152]{2,1,0:T(8,128)(2,1)}) custom-call(s32[4]{0:T(128)} %pad_add_fusion.idx_ref, bf16[32,80,192]{2,1,0:T(8,128)(2,1)} %get-tuple-element.32.xo_ref, bf16[32,80,192]{2,1,0:T(8,128)(2,1)} %copy-done, ...), custom_call_target="tpu_custom_call" | custom-call | tf_op jit(solution)/shard_map/pallas_call | solution.py:49
  142.0 8.1 %collective-permute-done.7.rest_1_ = bf16[48,3584]{1,0:T(8,128)(2,1)S(1)} collective-permute-done((bf16[48,3584]{1,0:T(8,128)(2,1)S(1)}, bf16[48,3584]{1,0:T(8,128)(2,1)S(1)}, u32[]{:S(2)}, u32[]{:S(2)}) %collective-permute-start.7) | collective-permute-done | bytes 344096 | tf_op jit(solution)/shard_map/ppermute | solution.py:447
  151.9 8.1 %collective-permute-done.9.rest_3_ = bf16[48,3584]{1,0:T(8,128)(2,1)S(1)} collective-permute-done((bf16[48,3584]{1,0:T(8,128)(2,1)S(1)}, bf16[48,3584]{1,0:T(8,128)(2,1)S(1)}, u32[]{:S(2)}, u32[]{:S(2)}) %collective-permute-start.9) | collective-permute-done | bytes 344096 | tf_op jit(solution)/shard_map/ppermute | solution.py:447
  161.8 12.4 %shard_map.73 = (bf16[32,64,192]{2,1,0:T(8,128)(2,1)}, f32[32,32,192]{2,1,0:T(8,128)}, f32[1,384]{1,0:T(1,128)}, bf16[48,16,1152]{2,1,0:T(8,128)(2,1)}, bf16[192,3584]{1,0:T(8,128)(2,1)}) custom-call(s32[4]{0:T(128)} %pad_add_fusion.idx_ref, bf16[32,80,192]{2,1,0:T(8,128)(2,1)} %get-tuple-element.33.xo_ref, bf16[32,80,192]{2,1,0:T(8,128)(2,1)} %copy-done.1, ...), custom_call_target="tpu_custom_call" | custom-call | tf_op jit(solution)/shard_map/pallas_call | solution.py:49
  174.9 2.5 collective-permute-done.10.xt_ref
  178.3 14.3 %shard_map.74 = (bf16[2,32,32,192]{3,2,1,0:T(8,128)(2,1)}, bf16[64,3456]{1,0:T(8,128)(2,1)}, f32[1,384]{1,0:T(1,128)}) custom-call(s32[4]{0:T(128)} %pad_add_fusion.idx_ref, bf16[32,64,192]{2,1,0:T(8,128)(2,1)} %get-tuple-element.34.xo_ref, bf16[32,64,192]{2,1,0:T(8,128)(2,1)} %copy-done.2, bf16[32,48,192]{2,1,0:T(8,128)(2,1)} %get-tuple-element.35.cot_ref.g_ref, ...), custom_call_target="tpu_custom_call" | custom-call | tf_op jit(solution)/shard_map/pallas_call | solution.py:49
  193.1 2.4 collective-permute-done.11.qr_ref
  196.6 9.8 %shard_map.75 = (bf16[2,32,32,192]{3,2,1,0:T(8,128)(2,1)}, bf16[32,32,192]{2,1,0:T(8,128)(2,1)}, bf16[64,3456]{1,0:T(8,128)(2,1)}) custom-call(s32[4]{0:T(128)} %pad_add_fusion.idx_ref, bf16[2,32,32,192]{3,2,1,0:T(8,128)(2,1)} %get-tuple-element.36.qm_ref, bf16[2,32,32,192]{3,2,1,0:T(8,128)(2,1)} %copy-done.7, ...), custom_call_target="tpu_custom_call" | custom-call | tf_op jit(solution)/shard_map/pallas_call | solution.py:49
  206.8 2.5 collective-permute-done.12.qr_ref
  210.3 8.3 %shard_map.76 = (bf16[2,32,16,192]{3,2,1,0:T(8,128)(2,1)}, bf16[32,32,192]{2,1,0:T(8,128)(2,1)}, bf16[64,3456]{1,0:T(8,128)(2,1)}) custom-call(s32[4]{0:T(128)} %pad_add_fusion.idx_ref, bf16[2,32,32,192]{3,2,1,0:T(8,128)(2,1)} %get-tuple-element.42.qm_ref, bf16[2,32,32,192]{3,2,1,0:T(8,128)(2,1)} %copy-done.8, ...), custom_call_target="tpu_custom_call" | custom-call | tf_op jit(solution)/shard_map/pallas_call | solution.py:49
  219.0 3.7 %all-to-all-start.3 = ((bf16[4,16,3456]{2,1,0:T(8,128)(2,1)}), bf16[4,16,3456]{2,1,0:T(8,128)(2,1)S(1)}, u32[]{:S(2)}, u32[]{:S(2)}) async-start(bf16[4,16,3456]{2,1,0:T(8,128)(2,1)} %bitcast.36), calls=%async_computation.3 | async-start | bytes 884736 | tf_op jit(solution)/shard_map/all_to_all | solution.py:531
  223.5 6.1 %shard_map.77 = bf16[64,3456]{1,0:T(8,128)(2,1)} custom-call(s32[4]{0:T(128)} %pad_add_fusion.idx_ref, bf16[2,32,16,192]{3,2,1,0:T(8,128)(2,1)} %get-tuple-element.47.qm_ref, bf16[2,32,16,192]{3,2,1,0:T(8,128)(2,1)} %copy-done.10, bf16[32,80,192]{2,1,0:T(8,128)(2,1)} %get-tuple-element.32.xo_ref, bf16[32,80,192]{2,1,0:T(8,128)(2,1)} %copy-done, ...), custom_call_target="tpu_custom_call" | custom-call | tf_op jit(solution)/shard_map/pallas_call | solution.py:49
  231.5 3.5 %all-to-all-start.2 = ((bf16[4,16,3456]{2,1,0:T(8,128)(2,1)}), bf16[4,16,3456]{2,1,0:T(8,128)(2,1)S(1)}, u32[]{:S(2)}, u32[]{:S(2)}) async-start(bf16[4,16,3456]{2,1,0:T(8,128)(2,1)} %bitcast.23), calls=%async_computation.2 | async-start | bytes 884736 | tf_op jit(solution)/shard_map/all_to_all | solution.py:531
  235.0 6.5 %all-to-all-done.2 = bf16[4,16,3456]{2,1,0:T(8,128)(2,1)S(1)} async-done(((bf16[4,16,3456]{2,1,0:T(8,128)(2,1)}), bf16[4,16,3456]{2,1,0:T(8,128)(2,1)S(1)}, u32[]{:S(2)}, u32[]{:S(2)}) %all-to-all-start.2) | async-done | bytes 442400 | tf_op jit(solution)/shard_map/all_to_all | solution.py:531
  243.5 6.5 %all-to-all-start.4 = ((bf16[8,8,3456]{2,1,0:T(8,128)(2,1)}), bf16[8,8,3456]{2,1,0:T(8,128)(2,1)S(1)}, u32[]{:S(2)}, u32[]{:S(2)}) async-start(bf16[8,8,3456]{2,1,0:T(8,128)(2,1)} %bitcast.17), calls=%async_computation.6 | async-start | bytes 884736 | tf_op jit(solution)/shard_map/all_to_all | solution.py:567
  250.1 13.5 %all-to-all-done.4 = bf16[8,8,3456]{2,1,0:T(8,128)(2,1)S(1)} async-done(((bf16[8,8,3456]{2,1,0:T(8,128)(2,1)}), bf16[8,8,3456]{2,1,0:T(8,128)(2,1)S(1)}, u32[]{:S(2)}, u32[]{:S(2)}) %all-to-all-start.4) | async-done | bytes 442400 | tf_op jit(solution)/shard_map/all_to_all | solution.py:567
  263.6 10.4 %all_gather.19.all_ref = bf16[32,3456]{1,0:T(8,128)(2,1)S(1)} all-gather(bf16[8,3456]{1,0:T(8,128)(2,1)S(1)} %reduce_sum.47), channel_id=1, replica_groups=mesh['section'=4,'x'=4,'zh'=2,'core'=2,'slab'=4] {'slab'}, dimensions={0}, use_global_device_ids=true | all-gather | bytes 276480 | tf_op jit(solution)/shard_map/all_gather | solution.py:569
  274.2 3.3 %collective-permute-start.14 = (f32[24]{0:T(128)S(1)}, f32[24]{0:T(128)S(1)}, u32[]{:S(2)}, u32[]{:S(2)}) collective-permute-start(f32[24]{0:T(128)S(1)} %dynamic_slice.12), channel_id=1, source_target_pairs={{0,4},{4,0},{1,5},{5,1},{2,6},{6,2},{3,7},{7,3},{8,12},{12,8},{9,1... | collective-permute-start | bytes 296 | tf_op jit(solution)/shard_map/ppermute | solution.py:420
  277.5 3.4 %shard_map.78 = f32[9,24,384]{2,1,0:T(8,128)} custom-call(bf16[32,3456]{1,0:T(8,128)(2,1)} %copy-done.9, bf16[384,384]{1,0:T(8,128)(2,1)} %dynamic-slice_bitcast_fusion.perm_ref), custom_call_target="tpu_custom_call" | custom-call | tf_op jit(solution)/shard_map/pallas_call | solution.py:49
  (82 shorter events, 26.9 us)
Async XLA Ops:
  7.2 12.5 %copy-start.17 = (bf16[2,384,384]{2,1,0:T(8,128)(2,1)S(1)}, bf16[2,384,384]{2,1,0:T(8,128)(2,1)}, u32[]{:S(2)}) copy-start(bf16[2,384,384]{2,1,0:T(8,128)(2,1)} %constant.46.clone) | copy-start | bytes 1769476
  9.9 26.2 %all-to-all-start = ((bf16[8,8,24,128]{3,2,1,0:T(8,128)(2,1)}), bf16[8,8,24,128]{3,2,1,0:T(8,128)(2,1)S(1)}, u32[]{:S(2)}, u32[]{:S(2)}) async-start(bf16[8,8,24,128]{3,2,1,0:T(8,128)(2,1)} %shard_map.69), calls=%async_computation | async-start | bytes 786432 | tf_op jit(solution)/shard_map/all_to_all | solution.py:430
  22.8 1.6 collective-permute-start
  37.4 34.9 %all-to-all-start.1 = ((bf16[8,24,3584]{2,1,0:T(8,128)(2,1)}), bf16[8,24,3584]{2,1,0:T(8,128)(2,1)S(1)}, u32[]{:S(2)}, u32[]{:S(2)}) async-start(bf16[8,24,3584]{2,1,0:T(8,128)(2,1)} %broadcast_in_dim.12), calls=%async_computation.1 | async-start | bytes 2752512 | tf_op jit(solution)/shard_map/all_to_all | solution.py:441
  40.9 36.8 %all-gather.9.cloned.1.call-start = ((), (), s32[]{:S(2)}) async-start(), calls=%async_computation.11 | async-start | bytes 1966080 | tf_op jit(solution)/shard_map/all_gather | solution.py:455
  41.7 83.1 %all-gather.5.cloned.1.call-start = ((), (), s32[]{:S(2)}) async-start(), calls=%async_computation.7 | async-start | bytes 1720320 | tf_op jit(solution)/shard_map/all_gather | solution.py:451
  73.2 32.3 %copy-start.5 = (bf16[2,24,3584]{2,1,0:T(8,128)(2,1)}, bf16[2,24,3584]{2,1,0:T(8,128)(2,1)S(1)}, u32[]{:S(2)}) copy-start(bf16[2,24,3584]{2,1,0:T(8,128)(2,1)S(1)} %get-tuple-element.59) | copy-start | bytes 1032196
  73.2 67.9 %copy-start.4 = (bf16[2,24,3584]{2,1,0:T(8,128)(2,1)}, bf16[2,24,3584]{2,1,0:T(8,128)(2,1)S(1)}, u32[]{:S(2)}) copy-start(bf16[2,24,3584]{2,1,0:T(8,128)(2,1)S(1)} %get-tuple-element.57) | copy-start | bytes 1032196
  73.2 101.6 %all-gather.7.cloned.1.call-start = ((), (), s32[]{:S(2)}) async-start(), calls=%async_computation.8 | async-start | bytes 1720320 | tf_op jit(solution)/shard_map/all_gather | solution.py:451
  82.7 22.7 %collective-permute-start.1 = (bf16[32,80,192]{2,1,0:T(8,128)(2,1)}, bf16[32,80,192]{2,1,0:T(8,128)(2,1)S(1)}, u32[]{:S(2)}, u32[]{:S(2)}) collective-permute-start(bf16[32,80,192]{2,1,0:T(8,128)(2,1)} %get-tuple-element.30.xo_ref), channel_id=1, source_target_pairs={{0,4},{4,0},{1,5},{5,1},{2,6},{6,2},{3,7},{7,3},{8,12},{12,8},{9,1... | collective-permute-start | bytes 2949128 | tf_op jit(solution)/shard_map/ppermute | solution.py:420
  83.4 18.5 %collective-permute-start.2 = (bf16[48,3584]{1,0:T(8,128)(2,1)S(1)}, bf16[48,3584]{1,0:T(8,128)(2,1)S(1)}, u32[]{:S(2)}, u32[]{:S(2)}) collective-permute-start(bf16[48,3584]{1,0:T(8,128)(2,1)S(1)} %bitcast.31), channel_id=1, source_target_pairs={{0,48},{16,0},{32,16},{48,32},{1,49},{17,1},{33,17},{49,33},{2,50}... | collective-permute-start | bytes 1032200 | tf_op jit(solution)/shard_map/ppermute | solution.py:447
  87.0 14.9 %collective-permute-start.3 = (bf16[48,3584]{1,0:T(8,128)(2,1)S(1)}, bf16[48,3584]{1,0:T(8,128)(2,1)S(1)}, u32[]{:S(2)}, u32[]{:S(2)}) collective-permute-start(bf16[48,3584]{1,0:T(8,128)(2,1)S(1)} %bitcast.32), channel_id=1, source_target_pairs={{0,32},{16,48},{32,0},{48,16},{1,33},{17,49},{33,1},{49,17},{2,34}... | collective-permute-start | bytes 1032200 | tf_op jit(solution)/shard_map/ppermute | solution.py:447
  87.0 18.4 %collective-permute-start.4 = (bf16[48,3584]{1,0:T(8,128)(2,1)S(1)}, bf16[48,3584]{1,0:T(8,128)(2,1)S(1)}, u32[]{:S(2)}, u32[]{:S(2)}) collective-permute-start(bf16[48,3584]{1,0:T(8,128)(2,1)S(1)} %bitcast.33), channel_id=1, source_target_pairs={{0,16},{16,32},{32,48},{48,0},{1,17},{17,33},{33,49},{49,1},{2,18}... | collective-permute-start | bytes 1032200 | tf_op jit(solution)/shard_map/ppermute | solution.py:447
  101.9 3.6 %copy-start.11 = (bf16[48,3584]{1,0:T(8,128)(2,1)}, bf16[48,3584]{1,0:T(8,128)(2,1)S(1)}, u32[]{:S(2)}) copy-start(bf16[48,3584]{1,0:T(8,128)(2,1)S(1)} %collective-permute-done.2.rest_1_) | copy-start | bytes 1032196
  101.9 3.6 %copy-start.13 = (bf16[48,3584]{1,0:T(8,128)(2,1)}, bf16[48,3584]{1,0:T(8,128)(2,1)S(1)}, u32[]{:S(2)}) copy-start(bf16[48,3584]{1,0:T(8,128)(2,1)S(1)} %collective-permute-done.3.rest_2_) | copy-start | bytes 1032196
  121.1 3.6 %collective-permute-start.5 = (bf16[32,80,192]{2,1,0:T(8,128)(2,1)}, bf16[32,80,192]{2,1,0:T(8,128)(2,1)S(1)}, u32[]{:S(2)}, u32[]{:S(2)}) collective-permute-start(bf16[32,80,192]{2,1,0:T(8,128)(2,1)} %get-tuple-element.32.xo_ref), channel_id=1, source_target_pairs={{0,4},{4,0},{1,5},{5,1},{2,6},{6,2},{3,7},{7,3},{8,12},{12,8},{9,1... | collective-permute-start | bytes 2949128 | tf_op jit(solution)/shard_map/ppermute | solution.py:420
  121.9 119.8 %reduce-scatter.5.cloned.1.call-start = ((), (), s32[]{:S(2)}) async-start(), calls=%async_computation.10 | async-start | bytes 552960 | tf_op jit(solution)/shard_map/reduce_scatter | solution.py:529
  140.1 20.0 %collective-permute-start.6 = (bf16[32,80,192]{2,1,0:T(8,128)(2,1)}, bf16[32,80,192]{2,1,0:T(8,128)(2,1)S(1)}, u32[]{:S(2)}, u32[]{:S(2)}) collective-permute-start(bf16[32,80,192]{2,1,0:T(8,128)(2,1)} %get-tuple-element.33.xo_ref), channel_id=1, source_target_pairs={{0,4},{4,0},{1,5},{5,1},{2,6},{6,2},{3,7},{7,3},{8,12},{12,8},{9,1... | collective-permute-start | bytes 2949128 | tf_op jit(solution)/shard_map/ppermute | solution.py:420
  140.5 9.5 %collective-permute-start.7 = (bf16[48,3584]{1,0:T(8,128)(2,1)S(1)}, bf16[48,3584]{1,0:T(8,128)(2,1)S(1)}, u32[]{:S(2)}, u32[]{:S(2)}) collective-permute-start(bf16[48,3584]{1,0:T(8,128)(2,1)S(1)} %bitcast.27), channel_id=1, source_target_pairs={{0,48},{16,0},{32,16},{48,32},{1,49},{17,1},{33,17},{49,33},{2,50}... | collective-permute-start | bytes 1032200 | tf_op jit(solution)/shard_map/ppermute | solution.py:447
  141.1 10.8 %collective-permute-start.8 = (bf16[48,3584]{1,0:T(8,128)(2,1)S(1)}, bf16[48,3584]{1,0:T(8,128)(2,1)S(1)}, u32[]{:S(2)}, u32[]{:S(2)}) collective-permute-start(bf16[48,3584]{1,0:T(8,128)(2,1)S(1)} %bitcast.28), channel_id=1, source_target_pairs={{0,32},{16,48},{32,0},{48,16},{1,33},{17,49},{33,1},{49,17},{2,34}... | collective-permute-start | bytes 1032200 | tf_op jit(solution)/shard_map/ppermute | solution.py:447
  141.2 18.9 %collective-permute-start.9 = (bf16[48,3584]{1,0:T(8,128)(2,1)S(1)}, bf16[48,3584]{1,0:T(8,128)(2,1)S(1)}, u32[]{:S(2)}, u32[]{:S(2)}) collective-permute-start(bf16[48,3584]{1,0:T(8,128)(2,1)S(1)} %bitcast.29), channel_id=1, source_target_pairs={{0,16},{16,32},{32,48},{48,0},{1,17},{17,33},{33,49},{49,1},{2,18}... | collective-permute-start | bytes 1032200 | tf_op jit(solution)/shard_map/ppermute | solution.py:447
  150.1 10.0 %copy-start.12 = (bf16[48,3584]{1,0:T(8,128)(2,1)}, bf16[48,3584]{1,0:T(8,128)(2,1)S(1)}, u32[]{:S(2)}) copy-start(bf16[48,3584]{1,0:T(8,128)(2,1)S(1)} %collective-permute-done.7.rest_1_) | copy-start | bytes 1032196
  151.9 8.1 %copy-start.14 = (bf16[48,3584]{1,0:T(8,128)(2,1)}, bf16[48,3584]{1,0:T(8,128)(2,1)S(1)}, u32[]{:S(2)}) copy-start(bf16[48,3584]{1,0:T(8,128)(2,1)S(1)} %collective-permute-done.8.rest_2_) | copy-start | bytes 1032196
  174.3 3.1 %collective-permute-start.10 = (bf16[32,64,192]{2,1,0:T(8,128)(2,1)}, bf16[32,64,192]{2,1,0:T(8,128)(2,1)S(1)}, u32[]{:S(2)}, u32[]{:S(2)}) collective-permute-start(bf16[32,64,192]{2,1,0:T(8,128)(2,1)} %get-tuple-element.34.xo_ref), channel_id=1, source_target_pairs={{0,4},{4,0},{1,5},{5,1},{2,6},{6,2},{3,7},{7,3},{8,12},{12,8},{9,1... | collective-permute-start | bytes 2359304 | tf_op jit(solution)/shard_map/ppermute | solution.py:420
  192.7 2.9 collective-permute-start.11
  193.1 48.6 %reduce-scatter.3.cloned.1.call-start = ((), (), s32[]{:S(2)}) async-start(), calls=%async_computation.9 | async-start | bytes 552960 | tf_op jit(solution)/shard_map/reduce_scatter | solution.py:529
  206.4 3.0 %collective-permute-start.12 = (bf16[2,32,32,192]{3,2,1,0:T(8,128)(2,1)}, bf16[2,32,32,192]{3,2,1,0:T(8,128)(2,1)S(1)}, u32[]{:S(2)}, u32[]{:S(2)}) collective-permute-start(bf16[2,32,32,192]{3,2,1,0:T(8,128)(2,1)} %get-tuple-element.42.qm_ref), channel_id=1, source_target_pairs={{0,4},{4,0},{1,5},{5,1},{2,6},{6,2},{3,7},{7,3},{8,12},{12,8},{9,1... | collective-permute-start | bytes 2359304 | tf_op jit(solution)/shard_map/ppermute | solution.py:420
  218.6 4.1 %collective-permute-start.13 = (bf16[2,32,16,192]{3,2,1,0:T(8,128)(2,1)}, bf16[2,32,16,192]{3,2,1,0:T(8,128)(2,1)S(1)}, u32[]{:S(2)}, u32[]{:S(2)}) collective-permute-start(bf16[2,32,16,192]{3,2,1,0:T(8,128)(2,1)} %get-tuple-element.47.qm_ref), channel_id=1, source_target_pairs={{0,4},{4,0},{1,5},{5,1},{2,6},{6,2},{3,7},{7,3},{8,12},{12,8},{9,1... | collective-permute-start | bytes 1179656 | tf_op jit(solution)/shard_map/ppermute | solution.py:420
  219.0 12.5 %all-to-all-start.3 = ((bf16[4,16,3456]{2,1,0:T(8,128)(2,1)}), bf16[4,16,3456]{2,1,0:T(8,128)(2,1)S(1)}, u32[]{:S(2)}, u32[]{:S(2)}) async-start(bf16[4,16,3456]{2,1,0:T(8,128)(2,1)} %bitcast.36), calls=%async_computation.3 | async-start | bytes 884736 | tf_op jit(solution)/shard_map/all_to_all | solution.py:531
  231.5 10.1 %all-to-all-start.2 = ((bf16[4,16,3456]{2,1,0:T(8,128)(2,1)}), bf16[4,16,3456]{2,1,0:T(8,128)(2,1)S(1)}, u32[]{:S(2)}, u32[]{:S(2)}) async-start(bf16[4,16,3456]{2,1,0:T(8,128)(2,1)} %bitcast.23), calls=%async_computation.2 | async-start | bytes 884736 | tf_op jit(solution)/shard_map/all_to_all | solution.py:531
  243.5 20.1 %all-to-all-start.4 = ((bf16[8,8,3456]{2,1,0:T(8,128)(2,1)}), bf16[8,8,3456]{2,1,0:T(8,128)(2,1)S(1)}, u32[]{:S(2)}, u32[]{:S(2)}) async-start(bf16[8,8,3456]{2,1,0:T(8,128)(2,1)} %bitcast.17), calls=%async_computation.6 | async-start | bytes 884736 | tf_op jit(solution)/shard_map/all_to_all | solution.py:567
  274.2 6.8 %collective-permute-start.14 = (f32[24]{0:T(128)S(1)}, f32[24]{0:T(128)S(1)}, u32[]{:S(2)}, u32[]{:S(2)}) collective-permute-start(f32[24]{0:T(128)S(1)} %dynamic_slice.12), channel_id=1, source_target_pairs={{0,4},{4,0},{1,5},{5,1},{2,6},{6,2},{3,7},{7,3},{8,12},{12,8},{9,1... | collective-permute-start | bytes 296 | tf_op jit(solution)/shard_map/ppermute | solution.py:420
  (11 other events, 13.3 us)
Sparse Core Ops, SparseCore 0:
  43.6 34.1 all-gather.8
  79.6 27.0 all-gather.4
  122.0 23.7 all-gather.6
  193.2 18.4 reduce-scatter.4
  214.2 24.9 reduce-scatter.2

commit v5 on v4

--- a/solution.py
+++ b/solution.py
@@ -38,7 +38,7 @@
     return lax.dot_general(a, b, dims, preferred_element_type=F32)
 
 
-def call(kernel, out_shape, scratch, args, smem=(), far=(), far_out=()):
+def call(kernel, out_shape, scratch, args, smem=(), far=(), far_out=(), micros=2):
     vm = pl.BlockSpec(memory_space=pltpu.VMEM)
     sm = pl.BlockSpec(memory_space=pltpu.SMEM)
     hb = pl.BlockSpec(memory_space=pltpu.HBM)
@@ -53,6 +53,7 @@
         out_specs=out_specs,
         scratch_shapes=scratch,
         compiler_params=PARAMS,
+        cost_estimate=pl.CostEstimate(flops=micros * 10**9, bytes_accessed=micros * 10**6, transcendentals=0),
     )(*args)
 
 
@@ -430,12 +431,6 @@
     recv = lax.all_to_all(windows, ("x", "zh"), 0, 0, tiled=True)
 
     packed = call(prep_kernel, shape((own_chans, CARRY), BF), [], (w1[0], gain, perm))
-    if nx == ny:
-        turn = []
-        for n in range(ns * nx * ny):
-            b, i, j = n // (nx * ny), n // ny % nx, n % ny
-            turn.append((n, (b * nx + j) * ny + i if b % 2 else n))
-        packed = lax.ppermute(packed, ("section", "x", "slab"), turn)
     wide = jnp.broadcast_to(packed[None], (ns * nz, own_chans, CARRY))
     wide, recv = lax.optimization_barrier((wide, recv))
     wide = lax.all_to_all(wide, ("section", "zh"), 0, 0, tiled=True)
@@ -446,9 +441,8 @@
         moves = [[(i, (i - j) % size) for i in range(size)] for j in range(1, size)]
         return [value] + [lax.ppermute(value, axis, move) for move in moves]
 
-    along = [("slab" if b % 2 and nx == ny else "x") for b in range(ns)]
     weights = [
-        [lax.all_gather(wide[b], along[b], axis=0, tiled=True)] if b % 2 else from_chips(wide[b], "x", nx)
+        from_chips(wide[b], "x", nx) if b < 1 else [lax.all_gather(wide[b], "x", axis=0, tiled=True)]
         for b in range(ns)
     ]
 
@@ -489,6 +483,7 @@
             (0,),
             (),
             (3, 4),
+            30,
         )
         halves.append((y, other(y)))
         slopes.append(slope)
@@ -521,6 +516,7 @@
         ],
         (idx, *halves[3], cot_own, weights[3][0]),
         (0,),
+        micros=12,
     )
     gains.append(gain_b)
 
@@ -556,6 +552,7 @@
                 args,
                 (0,),
                 (8, 9),
+                micros=8,
             )
         else:
             own_s = pltpu.VMEM((ROWS, OWN, HALF), BF)

time: 289 us -> 296 us (1.024)
  waiting for transfers between devices: 115 us -> 124 us
    all_to_all x1, waiting for transfers between devices: 30.6 us -> 3.88 us  [local(): wide = lax.all_to_all(wide, ('section', 'zh'), 0, 0, tiled=True)]
    all_gather x2 -> x3, waiting for transfers between devices: 0.01 us -> 21.9 us  [local(): lax.all_gather(wide[b], 'x', axis=0, tiled=True)]
    ppermute x6 -> x3, waiting for transfers between devices: 35.8 us -> 17.9 us  [from_chips(): return [value] + [lax.ppermute(value, axis, move) for move in moves]]
    all_gather x1, waiting for transfers between devices: 4.45 us -> 22.2 us  [local(): every_row = lax.all_gather(recv, 'slab', axis=0)]
    reduce_scatter x2, waiting for transfers between devices: 0.04 us -> 14.2 us  [reduced(): return lax.psum_scatter(value, 'x', scatter_dimension=0, tiled=True)]
    ppermute x6 -> x3, starting transfers between devices: 5.69 us -> 1.47 us  [from_chips(): return [value] + [lax.ppermute(value, axis, move) for move in moves]]
    ppermute x8, starting transfers between devices: 7.03 us -> 10.3 us  [other(): return lax.ppermute(value, 'core', [(0, 1), (1, 0)])]
    unnamed x36 -> x28, local copies, waits for them, and re-layouts: 8.58 us -> 7.81 us
  transfers between devices with their start and end apart: 25 -> 22, of which waited for: 15 -> 15; matrix products, arithmetic and copies ran while one was open for 1% -> 1% of each run, Pallas kernels for 26% -> 22%
where the time goes in v5:
time: 296 us; the launch traced here: 295 us
  waiting for transfers between devices  124 us (42%)
  Pallas kernels  91.7 us (31%)
  starting transfers between devices  39.1 us (13%)
  between operations  15.9 us (5%)
  local copies, waits for them, and re-layouts  11.9 us (4%)
  blocking collectives  9.62 us (3%)
  other arithmetic  3.23 us (1%)
    pallas_call x11, Pallas kernels, call(): pl.pallas_call(kernel, out_shape=out_shape, in_specs=[sm if i in smem els...  91.7 us
    all_gather x1, waiting for transfers between devices, local(): every_row = lax.all_gather(recv, 'slab', axis=0)  22.2 us
    all_gather x3, waiting for transfers between devices, local(): lax.all_gather(wide[b], 'x', axis=0, tiled=True)  21.9 us
    ppermute x3, waiting for transfers between devices, from_chips(): return [value] + [lax.ppermute(value, axis, move) for move in moves]  17.9 us
    reduce_scatter x2, waiting for transfers between devices, reduced(): return lax.psum_scatter(value, 'x', scatter_dimension=0, tiled=True)  14.2 us
    all_to_all x1, waiting for transfers between devices, local(): parts = lax.all_to_all(parts, ('section', 'zh'), 0, 0, tiled=True)  13.1 us
    all_to_all x1, waiting for transfers between devices, local(): recv = lax.all_to_all(windows, ('x', 'zh'), 0, 0, tiled=True)  13.1 us
    ppermute x8, starting transfers between devices, other(): return lax.ppermute(value, 'core', [(0, 1), (1, 0)])  10.3 us
  transfers between devices with their start and end apart: 22, of which 15 were waited for; matrix products, arithmetic and copies ran while one was open for 1% of the time, Pallas kernels for 22%

profile of v5, /device:TPU:33, one launch (start us, length us, event | category | flops | bytes accessed | tf_op | source)
XLA Modules:
  0.0 295.2 jit_solution(8057883037665897123)
XLA Ops:
  10.7 9.7 %all-to-all-start = ((bf16[8,8,24,128]{3,2,1,0:T(8,128)(2,1)}), bf16[8,8,24,128]{3,2,1,0:T(8,128)(2,1)S(1)}, u32[]{:S(2)}, u32[]{:S(2)}) async-start(bf16[8,8,24,128]{3,2,1,0:T(8,128)(2,1)} %shard_map.69), calls=%async_computation | async-start | bytes 786432 | tf_op jit(solution)/shard_map/all_to_all | solution.py:431
  21.3 2.4 shard_map.68
  23.7 13.1 %all-to-all-done = bf16[8,8,24,128]{3,2,1,0:T(8,128)(2,1)S(1)} async-done(((bf16[8,8,24,128]{3,2,1,0:T(8,128)(2,1)}), bf16[8,8,24,128]{3,2,1,0:T(8,128)(2,1)S(1)}, u32[]{:S(2)}, u32[]{:S(2)}) %all-to-all-start) | async-done | bytes 393248 | tf_op jit(solution)/shard_map/all_to_all | solution.py:431
  36.8 2.3 broadcast_in_dim.12
  39.1 3.5 %all-to-all-start.1 = ((bf16[8,24,3584]{2,1,0:T(8,128)(2,1)}), bf16[8,24,3584]{2,1,0:T(8,128)(2,1)S(1)}, u32[]{:S(2)}, u32[]{:S(2)}) async-start(bf16[8,24,3584]{2,1,0:T(8,128)(2,1)} %broadcast_in_dim.12), calls=%async_computation.1 | async-start | bytes 2752512 | tf_op jit(solution)/shard_map/all_to_all | solution.py:436
  42.7 22.2 %all-gather.12.cloned.1.call-done = bf16[32,8,24,128]{3,2,1,0:T(8,128)(2,1)} async-done(((bf16[8,8,24,128]{3,2,1,0:T(8,128)(2,1)}), bf16[32,8,24,128]{3,2,1,0:T(8,128)(2,1)}) %all-gather.12.cloned.1.call-update) | async-done | bytes 1572880 | tf_op jit(solution)/shard_map/all_gather | solution.py:449
  64.8 5.0 %shard_map.70 = (bf16[32,80,192]{2,1,0:T(8,128)(2,1)}, bf16[32,48,192]{2,1,0:T(8,128)(2,1)}) custom-call(bf16[4,8,8,24,128]{4,3,2,1,0:T(8,128)(2,1)} %bitcast.37), custom_call_target="tpu_custom_call" | custom-call | flops 2000000000 | bytes 2000000 | tf_op jit(solution)/shard_map/pallas_call | solution.py:49
  70.5 3.9 %all-to-all-done.1 = bf16[8,24,3584]{2,1,0:T(8,128)(2,1)S(1)} async-done(((bf16[8,24,3584]{2,1,0:T(8,128)(2,1)}), bf16[8,24,3584]{2,1,0:T(8,128)(2,1)S(1)}, u32[]{:S(2)}, u32[]{:S(2)}) %all-to-all-start.1) | async-done | bytes 1376288 | tf_op jit(solution)/shard_map/all_to_all | solution.py:436
  76.9 7.0 %collective-permute-done.1.rest_1_ = bf16[48,3584]{1,0:T(8,128)(2,1)S(1)} collective-permute-done((bf16[48,3584]{1,0:T(8,128)(2,1)S(1)}, bf16[48,3584]{1,0:T(8,128)(2,1)S(1)}, u32[]{:S(2)}, u32[]{:S(2)}) %collective-permute-start.1) | collective-permute-done | bytes 344096 | tf_op jit(solution)/shard_map/ppermute | solution.py:442
  85.7 9.0 %collective-permute-done.3.rest_3_ = bf16[48,3584]{1,0:T(8,128)(2,1)S(1)} collective-permute-done((bf16[48,3584]{1,0:T(8,128)(2,1)S(1)}, bf16[48,3584]{1,0:T(8,128)(2,1)S(1)}, u32[]{:S(2)}, u32[]{:S(2)}) %collective-permute-start.3) | collective-permute-done | bytes 344096 | tf_op jit(solution)/shard_map/ppermute | solution.py:442
  96.6 13.8 %shard_map.71 = (bf16[32,80,192]{2,1,0:T(8,128)(2,1)}, f32[32,16,192]{2,1,0:T(8,128)}, f32[1,384]{1,0:T(1,128)}, bf16[48,16,1152]{2,1,0:T(8,128)(2,1)}, bf16[192,3584]{1,0:T(8,128)(2,1)}) custom-call(s32[4]{0:T(128)} %pad_add_fusion.idx_ref, bf16[32,80,192]{2,1,0:T(8,128)(2,1)} %get-tuple-element.29.xo_ref, bf16[32,80,192]{2,1,0:T(8,128)(2,1)} %copy-done.7, ...), custom_call_target="tpu_custom_call" | custom-call | flops 30000001024 | bytes 30000000 | tf_op jit(solution)/shard_map/pallas_call | solution.py:49
  111.1 2.8 collective-permute-done.4.xt_ref
  115.0 14.2 %shard_map.72 = (bf16[32,80,192]{2,1,0:T(8,128)(2,1)}, f32[32,32,192]{2,1,0:T(8,128)}, f32[1,384]{1,0:T(1,128)}, bf16[48,16,1152]{2,1,0:T(8,128)(2,1)}) custom-call(s32[4]{0:T(128)} %pad_add_fusion.idx_ref, bf16[32,80,192]{2,1,0:T(8,128)(2,1)} %get-tuple-element.31.xo_ref, bf16[32,80,192]{2,1,0:T(8,128)(2,1)} %copy-done.1, ...), custom_call_target="tpu_custom_call" | custom-call | flops 30000001024 | bytes 30000000 | tf_op jit(solution)/shard_map/pallas_call | solution.py:49
  129.7 7.1 %all-gather.8.cloned.1.call-done.rest_0_.w_far = bf16[192,3584]{1,0:T(8,128)(2,1)} async-done(((bf16[48,3584]{1,0:T(8,128)(2,1)}), bf16[192,3584]{1,0:T(8,128)(2,1)}) %all-gather.8.cloned.1.call-update) | async-done | bytes 1376272 | tf_op jit(solution)/shard_map/all_gather | solution.py:445
  137.9 12.4 %shard_map.73 = (bf16[32,64,192]{2,1,0:T(8,128)(2,1)}, f32[32,32,192]{2,1,0:T(8,128)}, f32[1,384]{1,0:T(1,128)}, bf16[48,16,1152]{2,1,0:T(8,128)(2,1)}) custom-call(s32[4]{0:T(128)} %pad_add_fusion.idx_ref, bf16[32,80,192]{2,1,0:T(8,128)(2,1)} %get-tuple-element.32.xo_ref, bf16[32,80,192]{2,1,0:T(8,128)(2,1)} %copy-done.6, ...), custom_call_target="tpu_custom_call" | custom-call | flops 30000001024 | bytes 30000000 | tf_op jit(solution)/shard_map/pallas_call | solution.py:49
  151.8 14.8 %all-gather.10.cloned.1.call-done.w_ref = bf16[192,3584]{1,0:T(8,128)(2,1)} async-done(((bf16[48,3584]{1,0:T(8,128)(2,1)}), bf16[192,3584]{1,0:T(8,128)(2,1)}) %all-gather.10.cloned.1.call-update) | async-done | bytes 1376272 | tf_op jit(solution)/shard_map/all_gather | solution.py:445
  167.6 14.3 %shard_map.74 = (bf16[2,32,32,192]{3,2,1,0:T(8,128)(2,1)}, bf16[64,3456]{1,0:T(8,128)(2,1)}, f32[1,384]{1,0:T(1,128)}) custom-call(s32[4]{0:T(128)} %pad_add_fusion.idx_ref, bf16[32,64,192]{2,1,0:T(8,128)(2,1)} %get-tuple-element.33.xo_ref, bf16[32,64,192]{2,1,0:T(8,128)(2,1)} %copy-done.8, bf16[32,48,192]{2,1,0:T(8,128)(2,1)} %get-tuple-element.34.cot_ref.g_ref, ...), custom_call_target="tpu_custom_call" | custom-call | flops 12000000000 | bytes 12000000 | tf_op jit(solution)/shard_map/pallas_call | solution.py:49
  183.1 2.5 collective-permute-done.7.qr_ref
  186.7 9.7 %shard_map.75 = (bf16[2,32,32,192]{3,2,1,0:T(8,128)(2,1)}, bf16[32,32,192]{2,1,0:T(8,128)(2,1)}, bf16[64,3456]{1,0:T(8,128)(2,1)}) custom-call(s32[4]{0:T(128)} %pad_add_fusion.idx_ref, bf16[2,32,32,192]{3,2,1,0:T(8,128)(2,1)} %get-tuple-element.35.qm_ref, bf16[2,32,32,192]{3,2,1,0:T(8,128)(2,1)} %copy-done.10, ...), custom_call_target="tpu_custom_call" | custom-call | flops 8000000000 | bytes 8000000 | tf_op jit(solution)/shard_map/pallas_call | solution.py:49
  196.9 2.4 collective-permute-done.8.qr_ref
  200.3 8.2 %shard_map.76 = (bf16[2,32,16,192]{3,2,1,0:T(8,128)(2,1)}, bf16[32,32,192]{2,1,0:T(8,128)(2,1)}, bf16[64,3456]{1,0:T(8,128)(2,1)}) custom-call(s32[4]{0:T(128)} %pad_add_fusion.idx_ref, bf16[2,32,32,192]{3,2,1,0:T(8,128)(2,1)} %get-tuple-element.40.qm_ref, bf16[2,32,32,192]{3,2,1,0:T(8,128)(2,1)} %copy-done.9, ...), custom_call_target="tpu_custom_call" | custom-call | flops 8000000000 | bytes 8000000 | tf_op jit(solution)/shard_map/pallas_call | solution.py:49
  209.1 3.5 %all-to-all-start.3 = ((bf16[4,16,3456]{2,1,0:T(8,128)(2,1)}), bf16[4,16,3456]{2,1,0:T(8,128)(2,1)S(1)}, u32[]{:S(2)}, u32[]{:S(2)}) async-start(bf16[4,16,3456]{2,1,0:T(8,128)(2,1)} %bitcast.27), calls=%async_computation.3 | async-start | bytes 884736 | tf_op jit(solution)/shard_map/all_to_all | solution.py:527
  213.4 6.1 %shard_map.77 = bf16[64,3456]{1,0:T(8,128)(2,1)} custom-call(s32[4]{0:T(128)} %pad_add_fusion.idx_ref, bf16[2,32,16,192]{3,2,1,0:T(8,128)(2,1)} %get-tuple-element.45.qm_ref, bf16[2,32,16,192]{3,2,1,0:T(8,128)(2,1)} %copy-done.2, bf16[32,80,192]{2,1,0:T(8,128)(2,1)} %get-tuple-element.31.xo_ref, bf16[32,80,192]{2,1,0:T(8,128)(2,1)} %copy-done.1, ...), custom_call_target="tpu_custom_call" | custom-call | flops 2000000000 | bytes 2000000 | tf_op jit(solution)/shard_map/pallas_call | solution.py:49
  219.5 2.4 all-to-all-done.3
  221.9 3.5 %all-to-all-start.2 = ((bf16[4,16,3456]{2,1,0:T(8,128)(2,1)}), bf16[4,16,3456]{2,1,0:T(8,128)(2,1)S(1)}, u32[]{:S(2)}, u32[]{:S(2)}) async-start(bf16[4,16,3456]{2,1,0:T(8,128)(2,1)} %bitcast.23), calls=%async_computation.2 | async-start | bytes 884736 | tf_op jit(solution)/shard_map/all_to_all | solution.py:527
  225.4 7.2 %all-to-all-done.2 = bf16[4,16,3456]{2,1,0:T(8,128)(2,1)S(1)} async-done(((bf16[4,16,3456]{2,1,0:T(8,128)(2,1)}), bf16[4,16,3456]{2,1,0:T(8,128)(2,1)S(1)}, u32[]{:S(2)}, u32[]{:S(2)}) %all-to-all-start.2) | async-done | bytes 442400 | tf_op jit(solution)/shard_map/all_to_all | solution.py:527
  232.7 14.2 %reduce-scatter.3.cloned.1.call-done = bf16[16,3456]{1,0:T(8,128)(2,1)} async-done(((bf16[64,3456]{1,0:T(8,128)(2,1)}), bf16[16,3456]{1,0:T(8,128)(2,1)}) %reduce-scatter.3.cloned.1.call-update) | async-done | bytes 110608 | tf_op jit(solution)/shard_map/reduce_scatter | solution.py:525
  248.7 6.9 %all-to-all-start.4 = ((bf16[8,8,3456]{2,1,0:T(8,128)(2,1)}), bf16[8,8,3456]{2,1,0:T(8,128)(2,1)S(1)}, u32[]{:S(2)}, u32[]{:S(2)}) async-start(bf16[8,8,3456]{2,1,0:T(8,128)(2,1)} %bitcast.17), calls=%async_computation.6 | async-start | bytes 884736 | tf_op jit(solution)/shard_map/all_to_all | solution.py:564
  255.7 13.1 %all-to-all-done.4 = bf16[8,8,3456]{2,1,0:T(8,128)(2,1)S(1)} async-done(((bf16[8,8,3456]{2,1,0:T(8,128)(2,1)}), bf16[8,8,3456]{2,1,0:T(8,128)(2,1)S(1)}, u32[]{:S(2)}, u32[]{:S(2)}) %all-to-all-start.4) | async-done | bytes 442400 | tf_op jit(solution)/shard_map/all_to_all | solution.py:564
  268.9 9.6 %all_gather.23.all_ref = bf16[32,3456]{1,0:T(8,128)(2,1)S(1)} all-gather(bf16[8,3456]{1,0:T(8,128)(2,1)S(1)} %reduce_sum.47), channel_id=1, replica_groups=mesh['section'=4,'x'=4,'zh'=2,'core'=2,'slab'=4] {'slab'}, dimensions={0}, use_global_device_ids=true | all-gather | bytes 276480 | tf_op jit(solution)/shard_map/all_gather | solution.py:566
  278.6 5.0 %collective-permute-start.10 = (f32[24]{0:T(128)S(1)}, f32[24]{0:T(128)S(1)}, u32[]{:S(2)}, u32[]{:S(2)}) collective-permute-start(f32[24]{0:T(128)S(1)} %dynamic_slice.12), channel_id=1, source_target_pairs={{0,4},{4,0},{1,5},{5,1},{2,6},{6,2},{3,7},{7,3},{8,12},{12,8},{9,1... | collective-permute-start | bytes 296 | tf_op jit(solution)/shard_map/ppermute | solution.py:421
  283.6 3.4 %shard_map.78 = f32[9,24,384]{2,1,0:T(8,128)} custom-call(bf16[32,3456]{1,0:T(8,128)(2,1)} %copy-done.4, bf16[384,384]{1,0:T(8,128)(2,1)} %dynamic-slice_bitcast_fusion.perm_ref), custom_call_target="tpu_custom_call" | custom-call | flops 2000000000 | bytes 2000000 | tf_op jit(solution)/shard_map/pallas_call | solution.py:49
  (69 shorter events, 24.0 us)
Async XLA Ops:
  8.6 11.9 %copy-start.5 = (bf16[2,384,384]{2,1,0:T(8,128)(2,1)S(1)}, bf16[2,384,384]{2,1,0:T(8,128)(2,1)}, u32[]{:S(2)}) copy-start(bf16[2,384,384]{2,1,0:T(8,128)(2,1)} %constant.46.clone) | copy-start | bytes 1769476
  10.7 26.0 %all-to-all-start = ((bf16[8,8,24,128]{3,2,1,0:T(8,128)(2,1)}), bf16[8,8,24,128]{3,2,1,0:T(8,128)(2,1)S(1)}, u32[]{:S(2)}, u32[]{:S(2)}) async-start(bf16[8,8,24,128]{3,2,1,0:T(8,128)(2,1)} %shard_map.69), calls=%async_computation | async-start | bytes 786432 | tf_op jit(solution)/shard_map/all_to_all | solution.py:431
  20.5 44.4 %all-gather.12.cloned.1.call-start = ((), (), s32[]{:S(2)}) async-start(), calls=%async_computation.12 | async-start | bytes 1966080 | tf_op jit(solution)/shard_map/all_gather | solution.py:449
  36.8 2.3 copy-start
  39.1 35.3 %all-to-all-start.1 = ((bf16[8,24,3584]{2,1,0:T(8,128)(2,1)}), bf16[8,24,3584]{2,1,0:T(8,128)(2,1)S(1)}, u32[]{:S(2)}, u32[]{:S(2)}) async-start(bf16[8,24,3584]{2,1,0:T(8,128)(2,1)} %broadcast_in_dim.12), calls=%async_computation.1 | async-start | bytes 2752512 | tf_op jit(solution)/shard_map/all_to_all | solution.py:436
  42.6 71.3 %all-gather.6.cloned.1.call-start = ((), (), s32[]{:S(2)}) async-start(), calls=%async_computation.7 | async-start | bytes 1720320 | tf_op jit(solution)/shard_map/all_gather | solution.py:445
  69.8 25.0 %collective-permute-start = (bf16[32,80,192]{2,1,0:T(8,128)(2,1)}, bf16[32,80,192]{2,1,0:T(8,128)(2,1)S(1)}, u32[]{:S(2)}, u32[]{:S(2)}) collective-permute-start(bf16[32,80,192]{2,1,0:T(8,128)(2,1)} %get-tuple-element.29.xo_ref), channel_id=1, source_target_pairs={{0,4},{4,0},{1,5},{5,1},{2,6},{6,2},{3,7},{7,3},{8,12},{12,8},{9,1... | collective-permute-start | bytes 2949128 | tf_op jit(solution)/shard_map/ppermute | solution.py:421
  75.3 19.4 %copy-start.3 = (bf16[2,24,3584]{2,1,0:T(8,128)(2,1)}, bf16[2,24,3584]{2,1,0:T(8,128)(2,1)S(1)}, u32[]{:S(2)}) copy-start(bf16[2,24,3584]{2,1,0:T(8,128)(2,1)S(1)} %get-tuple-element.57) | copy-start | bytes 1032196
  75.3 8.6 %collective-permute-start.1 = (bf16[48,3584]{1,0:T(8,128)(2,1)S(1)}, bf16[48,3584]{1,0:T(8,128)(2,1)S(1)}, u32[]{:S(2)}, u32[]{:S(2)}) collective-permute-start(bf16[48,3584]{1,0:T(8,128)(2,1)S(1)} %bitcast.30), channel_id=1, source_target_pairs={{0,48},{16,0},{32,16},{48,32},{1,49},{17,1},{33,17},{49,33},{2,50}... | collective-permute-start | bytes 1032200 | tf_op jit(solution)/shard_map/ppermute | solution.py:442
  75.9 9.8 %collective-permute-start.2 = (bf16[48,3584]{1,0:T(8,128)(2,1)S(1)}, bf16[48,3584]{1,0:T(8,128)(2,1)S(1)}, u32[]{:S(2)}, u32[]{:S(2)}) collective-permute-start(bf16[48,3584]{1,0:T(8,128)(2,1)S(1)} %bitcast.31), channel_id=1, source_target_pairs={{0,32},{16,48},{32,0},{48,16},{1,33},{17,49},{33,1},{49,17},{2,34}... | collective-permute-start | bytes 1032200 | tf_op jit(solution)/shard_map/ppermute | solution.py:442
  76.4 18.3 %collective-permute-start.3 = (bf16[48,3584]{1,0:T(8,128)(2,1)S(1)}, bf16[48,3584]{1,0:T(8,128)(2,1)S(1)}, u32[]{:S(2)}, u32[]{:S(2)}) collective-permute-start(bf16[48,3584]{1,0:T(8,128)(2,1)S(1)} %bitcast.32), channel_id=1, source_target_pairs={{0,16},{16,32},{32,48},{48,0},{1,17},{17,33},{33,49},{49,1},{2,18}... | collective-permute-start | bytes 1032200 | tf_op jit(solution)/shard_map/ppermute | solution.py:442
  76.8 60.0 %all-gather.8.cloned.1.call-start = ((), (), s32[]{:S(2)}) async-start(), calls=%async_computation.8 | async-start | bytes 1720320 | tf_op jit(solution)/shard_map/all_gather | solution.py:445
  83.9 10.9 %copy-start.11 = (bf16[48,3584]{1,0:T(8,128)(2,1)}, bf16[48,3584]{1,0:T(8,128)(2,1)S(1)}, u32[]{:S(2)}) copy-start(bf16[48,3584]{1,0:T(8,128)(2,1)S(1)} %collective-permute-done.1.rest_1_) | copy-start | bytes 1032196
  85.7 9.1 %copy-start.12 = (bf16[48,3584]{1,0:T(8,128)(2,1)}, bf16[48,3584]{1,0:T(8,128)(2,1)S(1)}, u32[]{:S(2)}) copy-start(bf16[48,3584]{1,0:T(8,128)(2,1)S(1)} %collective-permute-done.2.rest_2_) | copy-start | bytes 1032196
  95.5 1.1 copy-start.7
  110.4 3.5 %collective-permute-start.4 = (bf16[32,80,192]{2,1,0:T(8,128)(2,1)}, bf16[32,80,192]{2,1,0:T(8,128)(2,1)S(1)}, u32[]{:S(2)}, u32[]{:S(2)}) collective-permute-start(bf16[32,80,192]{2,1,0:T(8,128)(2,1)} %get-tuple-element.31.xo_ref), channel_id=1, source_target_pairs={{0,4},{4,0},{1,5},{5,1},{2,6},{6,2},{3,7},{7,3},{8,12},{12,8},{9,1... | collective-permute-start | bytes 2949128 | tf_op jit(solution)/shard_map/ppermute | solution.py:421
  111.1 55.5 %all-gather.10.cloned.1.call-start = ((), (), s32[]{:S(2)}) async-start(), calls=%async_computation.9 | async-start | bytes 1720320 | tf_op jit(solution)/shard_map/all_gather | solution.py:445
  113.9 1.1 copy-start.1
  129.2 7.6 %collective-permute-start.5 = (bf16[32,80,192]{2,1,0:T(8,128)(2,1)}, bf16[32,80,192]{2,1,0:T(8,128)(2,1)S(1)}, u32[]{:S(2)}, u32[]{:S(2)}) collective-permute-start(bf16[32,80,192]{2,1,0:T(8,128)(2,1)} %get-tuple-element.32.xo_ref), channel_id=1, source_target_pairs={{0,4},{4,0},{1,5},{5,1},{2,6},{6,2},{3,7},{7,3},{8,12},{12,8},{9,1... | collective-permute-start | bytes 2949128 | tf_op jit(solution)/shard_map/ppermute | solution.py:421
  129.7 103.0 %reduce-scatter.5.cloned.1.call-start = ((), (), s32[]{:S(2)}) async-start(), calls=%async_computation.11 | async-start | bytes 552960 | tf_op jit(solution)/shard_map/reduce_scatter | solution.py:525
  136.8 1.1 copy-start.6
  150.3 16.3 %collective-permute-start.6 = (bf16[32,64,192]{2,1,0:T(8,128)(2,1)}, bf16[32,64,192]{2,1,0:T(8,128)(2,1)S(1)}, u32[]{:S(2)}, u32[]{:S(2)}) collective-permute-start(bf16[32,64,192]{2,1,0:T(8,128)(2,1)} %get-tuple-element.33.xo_ref), channel_id=1, source_target_pairs={{0,4},{4,0},{1,5},{5,1},{2,6},{6,2},{3,7},{7,3},{8,12},{12,8},{9,1... | collective-permute-start | bytes 2359304 | tf_op jit(solution)/shard_map/ppermute | solution.py:421
  181.9 3.7 %collective-permute-start.7 = (bf16[2,32,32,192]{3,2,1,0:T(8,128)(2,1)}, bf16[2,32,32,192]{3,2,1,0:T(8,128)(2,1)S(1)}, u32[]{:S(2)}, u32[]{:S(2)}) collective-permute-start(bf16[2,32,32,192]{3,2,1,0:T(8,128)(2,1)} %get-tuple-element.35.qm_ref), channel_id=1, source_target_pairs={{0,4},{4,0},{1,5},{5,1},{2,6},{6,2},{3,7},{7,3},{8,12},{12,8},{9,1... | collective-permute-start | bytes 2359304 | tf_op jit(solution)/shard_map/ppermute | solution.py:421
  185.6 1.1 copy-start.10
  196.4 3.0 %collective-permute-start.8 = (bf16[2,32,32,192]{3,2,1,0:T(8,128)(2,1)}, bf16[2,32,32,192]{3,2,1,0:T(8,128)(2,1)S(1)}, u32[]{:S(2)}, u32[]{:S(2)}) collective-permute-start(bf16[2,32,32,192]{3,2,1,0:T(8,128)(2,1)} %get-tuple-element.40.qm_ref), channel_id=1, source_target_pairs={{0,4},{4,0},{1,5},{5,1},{2,6},{6,2},{3,7},{7,3},{8,12},{12,8},{9,1... | collective-permute-start | bytes 2359304 | tf_op jit(solution)/shard_map/ppermute | solution.py:421
  196.9 50.0 %reduce-scatter.3.cloned.1.call-start = ((), (), s32[]{:S(2)}) async-start(), calls=%async_computation.10 | async-start | bytes 552960 | tf_op jit(solution)/shard_map/reduce_scatter | solution.py:525
  208.6 4.0 %collective-permute-start.9 = (bf16[2,32,16,192]{3,2,1,0:T(8,128)(2,1)}, bf16[2,32,16,192]{3,2,1,0:T(8,128)(2,1)S(1)}, u32[]{:S(2)}, u32[]{:S(2)}) collective-permute-start(bf16[2,32,16,192]{3,2,1,0:T(8,128)(2,1)} %get-tuple-element.45.qm_ref), channel_id=1, source_target_pairs={{0,4},{4,0},{1,5},{5,1},{2,6},{6,2},{3,7},{7,3},{8,12},{12,8},{9,1... | collective-permute-start | bytes 1179656 | tf_op jit(solution)/shard_map/ppermute | solution.py:421
  209.1 12.8 %all-to-all-start.3 = ((bf16[4,16,3456]{2,1,0:T(8,128)(2,1)}), bf16[4,16,3456]{2,1,0:T(8,128)(2,1)S(1)}, u32[]{:S(2)}, u32[]{:S(2)}) async-start(bf16[4,16,3456]{2,1,0:T(8,128)(2,1)} %bitcast.27), calls=%async_computation.3 | async-start | bytes 884736 | tf_op jit(solution)/shard_map/all_to_all | solution.py:527
  221.9 10.7 %all-to-all-start.2 = ((bf16[4,16,3456]{2,1,0:T(8,128)(2,1)}), bf16[4,16,3456]{2,1,0:T(8,128)(2,1)S(1)}, u32[]{:S(2)}, u32[]{:S(2)}) async-start(bf16[4,16,3456]{2,1,0:T(8,128)(2,1)} %bitcast.23), calls=%async_computation.2 | async-start | bytes 884736 | tf_op jit(solution)/shard_map/all_to_all | solution.py:527
  248.7 20.0 %all-to-all-start.4 = ((bf16[8,8,3456]{2,1,0:T(8,128)(2,1)}), bf16[8,8,3456]{2,1,0:T(8,128)(2,1)S(1)}, u32[]{:S(2)}, u32[]{:S(2)}) async-start(bf16[8,8,3456]{2,1,0:T(8,128)(2,1)} %bitcast.17), calls=%async_computation.6 | async-start | bytes 884736 | tf_op jit(solution)/shard_map/all_to_all | solution.py:564
  278.5 5.1 %copy-start.4 = (bf16[32,3456]{1,0:T(8,128)(2,1)}, bf16[32,3456]{1,0:T(8,128)(2,1)S(1)}, u32[]{:S(2)}) copy-start(bf16[32,3456]{1,0:T(8,128)(2,1)S(1)} %all_gather.23.all_ref) | copy-start | bytes 663556
  278.6 8.4 %collective-permute-start.10 = (f32[24]{0:T(128)S(1)}, f32[24]{0:T(128)S(1)}, u32[]{:S(2)}, u32[]{:S(2)}) collective-permute-start(f32[24]{0:T(128)S(1)} %dynamic_slice.12), channel_id=1, source_target_pairs={{0,4},{4,0},{1,5},{5,1},{2,6},{6,2},{3,7},{7,3},{8,12},{12,8},{9,1... | collective-permute-start | bytes 296 | tf_op jit(solution)/shard_map/ppermute | solution.py:421
  (4 other events, 3.5 us)
Sparse Core Ops, SparseCore 0:
  39.2 25.5 all-gather.11
Sparse Core Ops, SparseCore 1:
  76.9 28.7 all-gather.5
  111.1 25.6 all-gather.7
  138.5 28.0 all-gather.9
  197.0 22.1 reduce-scatter.4
  221.8 25.0 reduce-scatter.2

commit v6 on v5

--- a/solution.py
+++ b/solution.py
@@ -441,10 +441,10 @@
         moves = [[(i, (i - j) % size) for i in range(size)] for j in range(1, size)]
         return [value] + [lax.ppermute(value, axis, move) for move in moves]
 
-    weights = [
-        from_chips(wide[b], "x", nx) if b < 1 else [lax.all_gather(wide[b], "x", axis=0, tiled=True)]
-        for b in range(ns)
-    ]
+    first = from_chips(wide[0], "x", nx)
+    pair = lax.all_gather(wide[1:3], "x", axis=1, tiled=True)
+    last = lax.all_gather(wide[3], "x", axis=0, tiled=True)
+    weights = [first, [pair[0]], [pair[1]], [last]]
 
     every_row = lax.all_gather(recv, "slab", axis=0)
     x_own, cot_own = call(
@@ -520,14 +520,12 @@
     )
     gains.append(gain_b)
 
-    def reduced(b, value):
-        if b > 1:
-            return lax.psum_scatter(value, "x", scatter_dimension=0, tiled=True)
-        value = value.reshape(nx, nz * lines, LANES)
+    def reduced(*values):
+        value = jnp.stack([v.reshape(nx, nz * lines, LANES) for v in values], axis=1)
         value = lax.all_to_all(value, "x", 0, 0, tiled=True)
         return jnp.sum(value.astype(F32), axis=0).astype(BF)
 
-    weight_parts = [None] * 3 + [reduced(3, grads)]
+    weight_parts = [None] * 3 + [grads]
     g, first_g = cot_own, S_WIN[3][0]
     for b in (2, 1, 0):
         args = (
@@ -558,9 +556,11 @@
             own_s = pltpu.VMEM((ROWS, OWN, HALF), BF)
             (grads,) = call(kernel, (wg_shape,), fetched + [own_s], args, (0,), (8, 9))
         first_g = S_WIN[b][0]
-        weight_parts[b] = reduced(b, grads)
-
-    parts = jnp.stack(weight_parts).reshape(ns * nz, lines, LANES)
+        weight_parts[b] = grads
+        if b == 2:
+            late = reduced(*weight_parts[2:])
+
+    parts = jnp.concatenate([reduced(*weight_parts[:2]), late]).reshape(ns * nz, lines, LANES)
     parts = lax.all_to_all(parts, ("section", "zh"), 0, 0, tiled=True)
     total = jnp.sum(parts.astype(F32), axis=0).astype(BF)
     every = lax.all_gather(total, "slab", axis=0, tiled=True)

time: 296 us -> 294 us (level)
  waiting for transfers between devices: 124 us -> 118 us
  local copies, waits for them, and re-layouts: 11.9 us -> 16.2 us
    all_to_all x1, waiting for transfers between devices: 3.88 us -> 30.9 us  [local(): wide = lax.all_to_all(wide, ('section', 'zh'), 0, 0, tiled=True)]
    all_gather x1, waiting for transfers between devices: 22.2 us -> 0.02 us  [local(): every_row = lax.all_gather(recv, 'slab', axis=0)]
    reduce_scatter x2 -> x0, waiting for transfers between devices: 14.2 us -> none  [reduced(): return lax.psum_scatter(value, 'x', scatter_dimension=0, tiled=True)]
    all_gather x3 -> x2, waiting for transfers between devices: 21.9 us -> 9.74 us  [the longest x1 9.74 us: local(): last = lax.all_gather(wide[3], 'x', axis=0, tiled=True)]
    ppermute x3, waiting for transfers between devices: 17.9 us -> 25 us  [from_chips(): return [value] + [lax.ppermute(value, axis, move) for move in moves]]
    all_to_all x2, waiting for transfers between devices: 9.58 us -> 16.2 us  [reduced(): value = lax.all_to_all(value, 'x', 0, 0, tiled=True)]
    squeeze x0 -> x1, local copies, waits for them, and re-layouts: none -> 3.56 us  [local(): weights = [first, [pair[0]], [pair[1]], [last]]]
    unnamed x28 -> x34, local copies, waits for them, and re-layouts: 7.81 us -> 7.87 us
  transfers between devices with their start and end apart: 22 -> 19, of which waited for: 15 -> 12; matrix products, arithmetic and copies ran while one was open for 1% -> 3% of each run, Pallas kernels for 22% -> 15%
where the time goes in v6:
time: 294 us; the launch traced here: 293 us
  waiting for transfers between devices  118 us (40%)
  Pallas kernels  91.7 us (31%)
  starting transfers between devices  37.8 us (13%)
  local copies, waits for them, and re-layouts  16.2 us (6%)
  between operations  13.9 us (5%)
  blocking collectives  9.75 us (3%)
  other arithmetic  5.65 us (2%)
    pallas_call x11, Pallas kernels, call(): pl.pallas_call(kernel, out_shape=out_shape, in_specs=[sm if i in smem els...  91.7 us
    all_to_all x1, waiting for transfers between devices, local(): wide = lax.all_to_all(wide, ('section', 'zh'), 0, 0, tiled=True)  30.9 us
    ppermute x3, waiting for transfers between devices, from_chips(): return [value] + [lax.ppermute(value, axis, move) for move in moves]  25 us
    all_to_all x2, waiting for transfers between devices, reduced(): value = lax.all_to_all(value, 'x', 0, 0, tiled=True)  16.2 us
    all_to_all x1, waiting for transfers between devices, local(): parts = lax.all_to_all(parts, ('section', 'zh'), 0, 0, tiled=True)  14.2 us
    all_to_all x1, waiting for transfers between devices, local(): recv = lax.all_to_all(windows, ('x', 'zh'), 0, 0, tiled=True)  13.2 us
    all_gather x1, blocking collectives, local(): every = lax.all_gather(total, 'slab', axis=0, tiled=True)  9.75 us
    all_to_all x1, starting transfers between devices, local(): recv = lax.all_to_all(windows, ('x', 'zh'), 0, 0, tiled=True)  9.75 us
  transfers between devices with their start and end apart: 19, of which 12 were waited for; matrix products, arithmetic and copies ran while one was open for 3% of the time, Pallas kernels for 15%

profile of v6, /device:TPU:33, one launch (start us, length us, event | category | flops | bytes accessed | tf_op | source)
XLA Modules:
  0.0 293.3 jit_solution(15744825561068157757)
XLA Ops:
  7.8 2.1 shard_map.69
  10.0 9.7 %all-to-all-start = ((bf16[8,8,24,128]{3,2,1,0:T(8,128)(2,1)}), bf16[8,8,24,128]{3,2,1,0:T(8,128)(2,1)S(1)}, u32[]{:S(2)}, u32[]{:S(2)}) async-start(bf16[8,8,24,128]{3,2,1,0:T(8,128)(2,1)} %shard_map.69), calls=%async_computation | async-start | bytes 786432 | tf_op jit(solution)/shard_map/all_to_all | solution.py:431
  20.5 2.4 shard_map.68
  22.8 13.2 %all-to-all-done = bf16[8,8,24,128]{3,2,1,0:T(8,128)(2,1)S(1)} async-done(((bf16[8,8,24,128]{3,2,1,0:T(8,128)(2,1)}), bf16[8,8,24,128]{3,2,1,0:T(8,128)(2,1)S(1)}, u32[]{:S(2)}, u32[]{:S(2)}) %all-to-all-start) | async-done | bytes 393248 | tf_op jit(solution)/shard_map/all_to_all | solution.py:431
  36.0 2.2 broadcast_in_dim.12
  38.2 3.5 %all-to-all-start.1 = ((bf16[8,24,3584]{2,1,0:T(8,128)(2,1)}), bf16[8,24,3584]{2,1,0:T(8,128)(2,1)S(1)}, u32[]{:S(2)}, u32[]{:S(2)}) async-start(bf16[8,24,3584]{2,1,0:T(8,128)(2,1)} %broadcast_in_dim.12), calls=%async_computation.1 | async-start | bytes 2752512 | tf_op jit(solution)/shard_map/all_to_all | solution.py:436
  42.6 30.9 %all-to-all-done.1 = bf16[8,24,3584]{2,1,0:T(8,128)(2,1)S(1)} async-done(((bf16[8,24,3584]{2,1,0:T(8,128)(2,1)}), bf16[8,24,3584]{2,1,0:T(8,128)(2,1)S(1)}, u32[]{:S(2)}, u32[]{:S(2)}) %all-to-all-start.1) | async-done | bytes 1376288 | tf_op jit(solution)/shard_map/all_to_all | solution.py:436
  74.5 4.9 %shard_map.70 = (bf16[32,80,192]{2,1,0:T(8,128)(2,1)}, bf16[32,48,192]{2,1,0:T(8,128)(2,1)}) custom-call(bf16[4,8,8,24,128]{4,3,2,1,0:T(8,128)(2,1)} %bitcast.43), custom_call_target="tpu_custom_call" | custom-call | flops 2000000000 | bytes 2000000 | tf_op jit(solution)/shard_map/pallas_call | solution.py:49
  83.6 7.3 %collective-permute-done.1.rest_1_ = bf16[48,3584]{1,0:T(8,128)(2,1)S(1)} collective-permute-done((bf16[48,3584]{1,0:T(8,128)(2,1)S(1)}, bf16[48,3584]{1,0:T(8,128)(2,1)S(1)}, u32[]{:S(2)}, u32[]{:S(2)}) %collective-permute-start.1) | collective-permute-done | bytes 344096 | tf_op jit(solution)/shard_map/ppermute | solution.py:442
  91.0 3.3 %collective-permute-done.2.rest_2_ = bf16[48,3584]{1,0:T(8,128)(2,1)S(1)} collective-permute-done((bf16[48,3584]{1,0:T(8,128)(2,1)S(1)}, bf16[48,3584]{1,0:T(8,128)(2,1)S(1)}, u32[]{:S(2)}, u32[]{:S(2)}) %collective-permute-start.2) | collective-permute-done | bytes 344096 | tf_op jit(solution)/shard_map/ppermute | solution.py:442
  94.2 14.4 %collective-permute-done.3.rest_3_ = bf16[48,3584]{1,0:T(8,128)(2,1)S(1)} collective-permute-done((bf16[48,3584]{1,0:T(8,128)(2,1)S(1)}, bf16[48,3584]{1,0:T(8,128)(2,1)S(1)}, u32[]{:S(2)}, u32[]{:S(2)}) %collective-permute-start.3) | collective-permute-done | bytes 344096 | tf_op jit(solution)/shard_map/ppermute | solution.py:442
  110.5 13.8 %shard_map.71 = (bf16[32,80,192]{2,1,0:T(8,128)(2,1)}, f32[32,16,192]{2,1,0:T(8,128)}, f32[1,384]{1,0:T(1,128)}, bf16[48,16,1152]{2,1,0:T(8,128)(2,1)}, bf16[192,3584]{1,0:T(8,128)(2,1)}) custom-call(s32[4]{0:T(128)} %pad_add_fusion.idx_ref, bf16[32,80,192]{2,1,0:T(8,128)(2,1)} %get-tuple-element.29.xo_ref, bf16[32,80,192]{2,1,0:T(8,128)(2,1)} %copy-done.10, ...), custom_call_target="tpu_custom_call" | custom-call | flops 30000001024 | bytes 30000000 | tf_op jit(solution)/shard_map/pallas_call | solution.py:49
  125.0 3.6 %slice_bitcast_fusion = (bf16[192,3584]{1,0:T(8,128)(2,1)}, bf16[192,3584]{1,0:T(8,128)(2,1)}) fusion(bf16[2,192,3584]{2,1,0:T(8,128)(2,1)} %all-gather.5.cloned.1.call-done), kind=kLoop, calls=%fused_computation | loop fusion | bytes 5505024 | tf_op jit(solution)/shard_map/squeeze | solution.py:447
  129.7 14.2 %shard_map.72 = (bf16[32,80,192]{2,1,0:T(8,128)(2,1)}, f32[32,32,192]{2,1,0:T(8,128)}, f32[1,384]{1,0:T(1,128)}, bf16[48,16,1152]{2,1,0:T(8,128)(2,1)}) custom-call(s32[4]{0:T(128)} %pad_add_fusion.idx_ref, bf16[32,80,192]{2,1,0:T(8,128)(2,1)} %get-tuple-element.31.xo_ref, bf16[32,80,192]{2,1,0:T(8,128)(2,1)} %copy-done.1, ...), custom_call_target="tpu_custom_call" | custom-call | flops 30000001024 | bytes 30000000 | tf_op jit(solution)/shard_map/pallas_call | solution.py:49
  144.1 3.2 %collective-permute-done.5.xt_ref = bf16[32,80,192]{2,1,0:T(8,128)(2,1)S(1)} collective-permute-done((bf16[32,80,192]{2,1,0:T(8,128)(2,1)}, bf16[32,80,192]{2,1,0:T(8,128)(2,1)S(1)}, u32[]{:S(2)}, u32[]{:S(2)}) %collective-permute-start.5) | collective-permute-done | bytes 983072 | tf_op jit(solution)/shard_map/ppermute | solution.py:421
  148.3 12.4 %shard_map.73 = (bf16[32,64,192]{2,1,0:T(8,128)(2,1)}, f32[32,32,192]{2,1,0:T(8,128)}, f32[1,384]{1,0:T(1,128)}, bf16[48,16,1152]{2,1,0:T(8,128)(2,1)}) custom-call(s32[4]{0:T(128)} %pad_add_fusion.idx_ref, bf16[32,80,192]{2,1,0:T(8,128)(2,1)} %get-tuple-element.32.xo_ref, bf16[32,80,192]{2,1,0:T(8,128)(2,1)} %copy-done.9, ...), custom_call_target="tpu_custom_call" | custom-call | flops 30000001024 | bytes 30000000 | tf_op jit(solution)/shard_map/pallas_call | solution.py:49
  161.1 9.7 %all-gather.7.cloned.1.call-done.w_ref = bf16[192,3584]{1,0:T(8,128)(2,1)} async-done(((bf16[48,3584]{1,0:T(8,128)(2,1)}), bf16[192,3584]{1,0:T(8,128)(2,1)}) %all-gather.7.cloned.1.call-update) | async-done | bytes 1376272 | tf_op jit(solution)/shard_map/all_gather | solution.py:446
  171.9 14.3 %shard_map.74 = (bf16[2,32,32,192]{3,2,1,0:T(8,128)(2,1)}, bf16[64,3456]{1,0:T(8,128)(2,1)}, f32[1,384]{1,0:T(1,128)}) custom-call(s32[4]{0:T(128)} %pad_add_fusion.idx_ref, bf16[32,64,192]{2,1,0:T(8,128)(2,1)} %get-tuple-element.33.xo_ref, bf16[32,64,192]{2,1,0:T(8,128)(2,1)} %copy-done.11, bf16[32,48,192]{2,1,0:T(8,128)(2,1)} %get-tuple-element.34.cot_ref.g_ref, ...), custom_call_target="tpu_custom_call" | custom-call | flops 12000000000 | bytes 12000000 | tf_op jit(solution)/shard_map/pallas_call | solution.py:49
  187.6 2.5 collective-permute-done.7.qr_ref
  191.2 9.7 %shard_map.75 = (bf16[2,32,32,192]{3,2,1,0:T(8,128)(2,1)}, bf16[32,32,192]{2,1,0:T(8,128)(2,1)}, bf16[64,3456]{1,0:T(8,128)(2,1)}) custom-call(s32[4]{0:T(128)} %pad_add_fusion.idx_ref, bf16[2,32,32,192]{3,2,1,0:T(8,128)(2,1)} %get-tuple-element.35.qm_ref, bf16[2,32,32,192]{3,2,1,0:T(8,128)(2,1)} %copy-done.12, ...), custom_call_target="tpu_custom_call" | custom-call | flops 8000000000 | bytes 8000000 | tf_op jit(solution)/shard_map/pallas_call | solution.py:49
  201.4 2.5 collective-permute-done.8.qr_ref
  204.8 8.2 %shard_map.76 = (bf16[2,32,16,192]{3,2,1,0:T(8,128)(2,1)}, bf16[32,32,192]{2,1,0:T(8,128)(2,1)}, bf16[64,3456]{1,0:T(8,128)(2,1)}) custom-call(s32[4]{0:T(128)} %pad_add_fusion.idx_ref, bf16[2,32,32,192]{3,2,1,0:T(8,128)(2,1)} %get-tuple-element.40.qm_ref, bf16[2,32,32,192]{3,2,1,0:T(8,128)(2,1)} %copy-done.13, ...), custom_call_target="tpu_custom_call" | custom-call | flops 8000000000 | bytes 8000000 | tf_op jit(solution)/shard_map/pallas_call | solution.py:49
  214.6 3.5 %all-to-all-start.3 = ((bf16[4,2,16,3456]{3,2,1,0:T(8,128)(2,1)}), bf16[4,2,16,3456]{3,2,1,0:T(8,128)(2,1)S(1)}, u32[]{:S(2)}, u32[]{:S(2)}) async-start(bf16[4,2,16,3456]{3,2,1,0:T(8,128)(2,1)} %pad_maximum_fusion.1), calls=%async_computation.3 | async-start | bytes 1769472 | tf_op jit(solution)/shard_map/all_to_all | solution.py:525
  219.0 6.1 %shard_map.77 = bf16[64,3456]{1,0:T(8,128)(2,1)} custom-call(s32[4]{0:T(128)} %pad_add_fusion.idx_ref, bf16[2,32,16,192]{3,2,1,0:T(8,128)(2,1)} %get-tuple-element.45.qm_ref, bf16[2,32,16,192]{3,2,1,0:T(8,128)(2,1)} %copy-done.2, bf16[32,80,192]{2,1,0:T(8,128)(2,1)} %get-tuple-element.31.xo_ref, bf16[32,80,192]{2,1,0:T(8,128)(2,1)} %copy-done.1, ...), custom_call_target="tpu_custom_call" | custom-call | flops 2000000000 | bytes 2000000 | tf_op jit(solution)/shard_map/pallas_call | solution.py:49
  227.2 4.1 %all-to-all-done.3 = bf16[4,2,16,3456]{3,2,1,0:T(8,128)(2,1)S(1)} async-done(((bf16[4,2,16,3456]{3,2,1,0:T(8,128)(2,1)}), bf16[4,2,16,3456]{3,2,1,0:T(8,128)(2,1)S(1)}, u32[]{:S(2)}, u32[]{:S(2)}) %all-to-all-start.3) | async-done | bytes 884768 | tf_op jit(solution)/shard_map/all_to_all | solution.py:525
  231.3 3.5 %all-to-all-start.2 = ((bf16[4,2,16,3456]{3,2,1,0:T(8,128)(2,1)}), bf16[4,2,16,3456]{3,2,1,0:T(8,128)(2,1)S(1)}, u32[]{:S(2)}, u32[]{:S(2)}) async-start(bf16[4,2,16,3456]{3,2,1,0:T(8,128)(2,1)} %pad_maximum_fusion), calls=%async_computation.2 | async-start | bytes 1769472 | tf_op jit(solution)/shard_map/all_to_all | solution.py:525
  235.0 12.1 %all-to-all-done.2 = bf16[4,2,16,3456]{3,2,1,0:T(8,128)(2,1)S(1)} async-done(((bf16[4,2,16,3456]{3,2,1,0:T(8,128)(2,1)}), bf16[4,2,16,3456]{3,2,1,0:T(8,128)(2,1)S(1)}, u32[]{:S(2)}, u32[]{:S(2)}) %all-to-all-start.2) | async-done | bytes 884768 | tf_op jit(solution)/shard_map/all_to_all | solution.py:525
  248.1 6.9 %all-to-all-start.4 = ((bf16[8,8,3456]{2,1,0:T(8,128)(2,1)}), bf16[8,8,3456]{2,1,0:T(8,128)(2,1)S(1)}, u32[]{:S(2)}, u32[]{:S(2)}) async-start(bf16[8,8,3456]{2,1,0:T(8,128)(2,1)} %bitcast.20), calls=%async_computation.4 | async-start | bytes 884736 | tf_op jit(solution)/shard_map/all_to_all | solution.py:564
  255.1 14.2 %all-to-all-done.4 = bf16[8,8,3456]{2,1,0:T(8,128)(2,1)S(1)} async-done(((bf16[8,8,3456]{2,1,0:T(8,128)(2,1)}), bf16[8,8,3456]{2,1,0:T(8,128)(2,1)S(1)}, u32[]{:S(2)}, u32[]{:S(2)}) %all-to-all-start.4) | async-done | bytes 442400 | tf_op jit(solution)/shard_map/all_to_all | solution.py:564
  269.3 9.8 %all_gather.19.all_ref = bf16[32,3456]{1,0:T(8,128)(2,1)S(1)} all-gather(bf16[8,3456]{1,0:T(8,128)(2,1)S(1)} %reduce_sum.47), channel_id=1, replica_groups=mesh['section'=4,'x'=4,'zh'=2,'core'=2,'slab'=4] {'slab'}, dimensions={0}, use_global_device_ids=true | all-gather | bytes 276480 | tf_op jit(solution)/shard_map/all_gather | solution.py:566
  279.2 3.5 %collective-permute-start.10 = (f32[24]{0:T(128)S(1)}, f32[24]{0:T(128)S(1)}, u32[]{:S(2)}, u32[]{:S(2)}) collective-permute-start(f32[24]{0:T(128)S(1)} %dynamic_slice.12), channel_id=1, source_target_pairs={{0,4},{4,0},{1,5},{5,1},{2,6},{6,2},{3,7},{7,3},{8,12},{12,8},{9,1... | collective-permute-start | bytes 296 | tf_op jit(solution)/shard_map/ppermute | solution.py:421
  282.7 3.4 %shard_map.78 = f32[9,24,384]{2,1,0:T(8,128)} custom-call(bf16[32,3456]{1,0:T(8,128)(2,1)} %copy-done.7, bf16[384,384]{1,0:T(8,128)(2,1)} %dynamic-slice_bitcast_fusion.perm_ref), custom_call_target="tpu_custom_call" | custom-call | flops 2000000000 | bytes 2000000 | tf_op jit(solution)/shard_map/pallas_call | solution.py:49
  (70 shorter events, 23.9 us)
Async XLA Ops:
  7.8 11.9 %copy-start.8 = (bf16[2,384,384]{2,1,0:T(8,128)(2,1)S(1)}, bf16[2,384,384]{2,1,0:T(8,128)(2,1)}, u32[]{:S(2)}) copy-start(bf16[2,384,384]{2,1,0:T(8,128)(2,1)} %constant.46.clone) | copy-start | bytes 1769476
  10.0 26.0 %all-to-all-start = ((bf16[8,8,24,128]{3,2,1,0:T(8,128)(2,1)}), bf16[8,8,24,128]{3,2,1,0:T(8,128)(2,1)S(1)}, u32[]{:S(2)}, u32[]{:S(2)}) async-start(bf16[8,8,24,128]{3,2,1,0:T(8,128)(2,1)} %shard_map.69), calls=%async_computation | async-start | bytes 786432 | tf_op jit(solution)/shard_map/all_to_all | solution.py:431
  36.0 2.2 copy-start
  38.2 35.3 %all-to-all-start.1 = ((bf16[8,24,3584]{2,1,0:T(8,128)(2,1)}), bf16[8,24,3584]{2,1,0:T(8,128)(2,1)S(1)}, u32[]{:S(2)}, u32[]{:S(2)}) async-start(bf16[8,24,3584]{2,1,0:T(8,128)(2,1)} %broadcast_in_dim.12), calls=%async_computation.1 | async-start | bytes 2752512 | tf_op jit(solution)/shard_map/all_to_all | solution.py:436
  41.8 32.7 %all-gather.9.cloned.1.call-start = ((), (), s32[]{:S(2)}) async-start(), calls=%async_computation.7 | async-start | bytes 1966080 | tf_op jit(solution)/shard_map/all_gather | solution.py:449
  42.5 82.5 %all-gather.5.cloned.1.call-start = ((), (), s32[]{:S(2)}) async-start(), calls=%async_computation.5 | async-start | bytes 3440640 | tf_op jit(solution)/shard_map/all_gather | solution.py:445
  74.4 96.4 %all-gather.7.cloned.1.call-start = ((), (), s32[]{:S(2)}) async-start(), calls=%async_computation.6 | async-start | bytes 1720320 | tf_op jit(solution)/shard_map/all_gather | solution.py:446
  79.4 29.2 %collective-permute-start = (bf16[32,80,192]{2,1,0:T(8,128)(2,1)}, bf16[32,80,192]{2,1,0:T(8,128)(2,1)S(1)}, u32[]{:S(2)}, u32[]{:S(2)}) collective-permute-start(bf16[32,80,192]{2,1,0:T(8,128)(2,1)} %get-tuple-element.29.xo_ref), channel_id=1, source_target_pairs={{0,4},{4,0},{1,5},{5,1},{2,6},{6,2},{3,7},{7,3},{8,12},{12,8},{9,1... | collective-permute-start | bytes 2949128 | tf_op jit(solution)/shard_map/ppermute | solution.py:421
  81.3 27.4 %copy-start.6 = (bf16[2,24,3584]{2,1,0:T(8,128)(2,1)}, bf16[2,24,3584]{2,1,0:T(8,128)(2,1)S(1)}, u32[]{:S(2)}) copy-start(bf16[2,24,3584]{2,1,0:T(8,128)(2,1)S(1)} %get-tuple-element.57) | copy-start | bytes 1032196
  81.3 9.7 %collective-permute-start.1 = (bf16[48,3584]{1,0:T(8,128)(2,1)S(1)}, bf16[48,3584]{1,0:T(8,128)(2,1)S(1)}, u32[]{:S(2)}, u32[]{:S(2)}) collective-permute-start(bf16[48,3584]{1,0:T(8,128)(2,1)S(1)} %bitcast.38), channel_id=1, source_target_pairs={{0,48},{16,0},{32,16},{48,32},{1,49},{17,1},{33,17},{49,33},{2,50}... | collective-permute-start | bytes 1032200 | tf_op jit(solution)/shard_map/ppermute | solution.py:442
  82.5 11.7 %collective-permute-start.2 = (bf16[48,3584]{1,0:T(8,128)(2,1)S(1)}, bf16[48,3584]{1,0:T(8,128)(2,1)S(1)}, u32[]{:S(2)}, u32[]{:S(2)}) collective-permute-start(bf16[48,3584]{1,0:T(8,128)(2,1)S(1)} %bitcast.39), channel_id=1, source_target_pairs={{0,32},{16,48},{32,0},{48,16},{1,33},{17,49},{33,1},{49,17},{2,34}... | collective-permute-start | bytes 1032200 | tf_op jit(solution)/shard_map/ppermute | solution.py:442
  83.1 25.5 %collective-permute-start.3 = (bf16[48,3584]{1,0:T(8,128)(2,1)S(1)}, bf16[48,3584]{1,0:T(8,128)(2,1)S(1)}, u32[]{:S(2)}, u32[]{:S(2)}) collective-permute-start(bf16[48,3584]{1,0:T(8,128)(2,1)S(1)} %bitcast.40), channel_id=1, source_target_pairs={{0,16},{16,32},{32,48},{48,0},{1,17},{17,33},{33,49},{49,1},{2,18}... | collective-permute-start | bytes 1032200 | tf_op jit(solution)/shard_map/ppermute | solution.py:442
  91.0 17.7 %copy-start.14 = (bf16[48,3584]{1,0:T(8,128)(2,1)}, bf16[48,3584]{1,0:T(8,128)(2,1)S(1)}, u32[]{:S(2)}) copy-start(bf16[48,3584]{1,0:T(8,128)(2,1)S(1)} %collective-permute-done.1.rest_1_) | copy-start | bytes 1032196
  94.2 14.4 %copy-start.15 = (bf16[48,3584]{1,0:T(8,128)(2,1)}, bf16[48,3584]{1,0:T(8,128)(2,1)S(1)}, u32[]{:S(2)}) copy-start(bf16[48,3584]{1,0:T(8,128)(2,1)S(1)} %collective-permute-done.2.rest_2_) | copy-start | bytes 1032196
  109.4 1.1 copy-start.10
  124.4 4.2 %collective-permute-start.4 = (bf16[32,80,192]{2,1,0:T(8,128)(2,1)}, bf16[32,80,192]{2,1,0:T(8,128)(2,1)S(1)}, u32[]{:S(2)}, u32[]{:S(2)}) collective-permute-start(bf16[32,80,192]{2,1,0:T(8,128)(2,1)} %get-tuple-element.31.xo_ref), channel_id=1, source_target_pairs={{0,4},{4,0},{1,5},{5,1},{2,6},{6,2},{3,7},{7,3},{8,12},{12,8},{9,1... | collective-permute-start | bytes 2949128 | tf_op jit(solution)/shard_map/ppermute | solution.py:421
  128.6 1.1 copy-start.1
  143.9 3.3 %collective-permute-start.5 = (bf16[32,80,192]{2,1,0:T(8,128)(2,1)}, bf16[32,80,192]{2,1,0:T(8,128)(2,1)S(1)}, u32[]{:S(2)}, u32[]{:S(2)}) collective-permute-start(bf16[32,80,192]{2,1,0:T(8,128)(2,1)} %get-tuple-element.32.xo_ref), channel_id=1, source_target_pairs={{0,4},{4,0},{1,5},{5,1},{2,6},{6,2},{3,7},{7,3},{8,12},{12,8},{9,1... | collective-permute-start | bytes 2949128 | tf_op jit(solution)/shard_map/ppermute | solution.py:421
  147.2 1.1 copy-start.9
  160.7 10.2 %collective-permute-start.6 = (bf16[32,64,192]{2,1,0:T(8,128)(2,1)}, bf16[32,64,192]{2,1,0:T(8,128)(2,1)S(1)}, u32[]{:S(2)}, u32[]{:S(2)}) collective-permute-start(bf16[32,64,192]{2,1,0:T(8,128)(2,1)} %get-tuple-element.33.xo_ref), channel_id=1, source_target_pairs={{0,4},{4,0},{1,5},{5,1},{2,6},{6,2},{3,7},{7,3},{8,12},{12,8},{9,1... | collective-permute-start | bytes 2359304 | tf_op jit(solution)/shard_map/ppermute | solution.py:421
  186.2 3.9 %collective-permute-start.7 = (bf16[2,32,32,192]{3,2,1,0:T(8,128)(2,1)}, bf16[2,32,32,192]{3,2,1,0:T(8,128)(2,1)S(1)}, u32[]{:S(2)}, u32[]{:S(2)}) collective-permute-start(bf16[2,32,32,192]{3,2,1,0:T(8,128)(2,1)} %get-tuple-element.35.qm_ref), channel_id=1, source_target_pairs={{0,4},{4,0},{1,5},{5,1},{2,6},{6,2},{3,7},{7,3},{8,12},{12,8},{9,1... | collective-permute-start | bytes 2359304 | tf_op jit(solution)/shard_map/ppermute | solution.py:421
  190.1 1.0 copy-start.12
  200.9 3.0 %collective-permute-start.8 = (bf16[2,32,32,192]{3,2,1,0:T(8,128)(2,1)}, bf16[2,32,32,192]{3,2,1,0:T(8,128)(2,1)S(1)}, u32[]{:S(2)}, u32[]{:S(2)}) collective-permute-start(bf16[2,32,32,192]{3,2,1,0:T(8,128)(2,1)} %get-tuple-element.40.qm_ref), channel_id=1, source_target_pairs={{0,4},{4,0},{1,5},{5,1},{2,6},{6,2},{3,7},{7,3},{8,12},{12,8},{9,1... | collective-permute-start | bytes 2359304 | tf_op jit(solution)/shard_map/ppermute | solution.py:421
  204.8 8.7 %copy-start.3 = (bf16[64,3456]{1,0:T(8,128)(2,1)S(1)}, bf16[64,3456]{1,0:T(8,128)(2,1)}, u32[]{:S(2)}) copy-start(bf16[64,3456]{1,0:T(8,128)(2,1)} %get-tuple-element.53) | copy-start | bytes 1327108
  204.8 8.7 %copy-start.5 = (bf16[64,3456]{1,0:T(8,128)(2,1)S(1)}, bf16[64,3456]{1,0:T(8,128)(2,1)}, u32[]{:S(2)}) copy-start(bf16[64,3456]{1,0:T(8,128)(2,1)} %get-tuple-element.52) | copy-start | bytes 1327108
  213.1 5.1 %collective-permute-start.9 = (bf16[2,32,16,192]{3,2,1,0:T(8,128)(2,1)}, bf16[2,32,16,192]{3,2,1,0:T(8,128)(2,1)S(1)}, u32[]{:S(2)}, u32[]{:S(2)}) collective-permute-start(bf16[2,32,16,192]{3,2,1,0:T(8,128)(2,1)} %get-tuple-element.45.qm_ref), channel_id=1, source_target_pairs={{0,4},{4,0},{1,5},{5,1},{2,6},{6,2},{3,7},{7,3},{8,12},{12,8},{9,1... | collective-permute-start | bytes 1179656 | tf_op jit(solution)/shard_map/ppermute | solution.py:421
  214.6 16.7 %all-to-all-start.3 = ((bf16[4,2,16,3456]{3,2,1,0:T(8,128)(2,1)}), bf16[4,2,16,3456]{3,2,1,0:T(8,128)(2,1)S(1)}, u32[]{:S(2)}, u32[]{:S(2)}) async-start(bf16[4,2,16,3456]{3,2,1,0:T(8,128)(2,1)} %pad_maximum_fusion.1), calls=%async_computation.3 | async-start | bytes 1769472 | tf_op jit(solution)/shard_map/all_to_all | solution.py:525
  219.0 6.2 %copy-start.4 = (bf16[64,3456]{1,0:T(8,128)(2,1)S(1)}, bf16[64,3456]{1,0:T(8,128)(2,1)}, u32[]{:S(2)}) copy-start(bf16[64,3456]{1,0:T(8,128)(2,1)} %get-tuple-element.51) | copy-start | bytes 1327108
  231.3 15.8 %all-to-all-start.2 = ((bf16[4,2,16,3456]{3,2,1,0:T(8,128)(2,1)}), bf16[4,2,16,3456]{3,2,1,0:T(8,128)(2,1)S(1)}, u32[]{:S(2)}, u32[]{:S(2)}) async-start(bf16[4,2,16,3456]{3,2,1,0:T(8,128)(2,1)} %pad_maximum_fusion), calls=%async_computation.2 | async-start | bytes 1769472 | tf_op jit(solution)/shard_map/all_to_all | solution.py:525
  248.1 21.1 %all-to-all-start.4 = ((bf16[8,8,3456]{2,1,0:T(8,128)(2,1)}), bf16[8,8,3456]{2,1,0:T(8,128)(2,1)S(1)}, u32[]{:S(2)}, u32[]{:S(2)}) async-start(bf16[8,8,3456]{2,1,0:T(8,128)(2,1)} %bitcast.20), calls=%async_computation.4 | async-start | bytes 884736 | tf_op jit(solution)/shard_map/all_to_all | solution.py:564
  279.1 3.6 %copy-start.7 = (bf16[32,3456]{1,0:T(8,128)(2,1)}, bf16[32,3456]{1,0:T(8,128)(2,1)S(1)}, u32[]{:S(2)}) copy-start(bf16[32,3456]{1,0:T(8,128)(2,1)S(1)} %all_gather.19.all_ref) | copy-start | bytes 663556
  279.2 7.0 %collective-permute-start.10 = (f32[24]{0:T(128)S(1)}, f32[24]{0:T(128)S(1)}, u32[]{:S(2)}, u32[]{:S(2)}) collective-permute-start(f32[24]{0:T(128)S(1)} %dynamic_slice.12), channel_id=1, source_target_pairs={{0,4},{4,0},{1,5},{5,1},{2,6},{6,2},{3,7},{7,3},{8,12},{12,8},{9,1... | collective-permute-start | bytes 296 | tf_op jit(solution)/shard_map/ppermute | solution.py:421
  (4 other events, 3.5 us)
Sparse Core Ops, SparseCore 0:
  44.4 29.2 all-gather.8
  75.5 48.3 all-gather.4
  144.2 26.6 all-gather.6

commit v7 on v6

--- a/solution.py
+++ b/solution.py
@@ -150,7 +150,8 @@
             out_ref[p, r] = here.astype(BF)
 
 
-def assemble_kernel(slabs, rows, recv_ref, x_ref, cot_ref):
+def assemble_kernel(slabs, rows, idx_ref, *refs):
+    pieces, (x_ref, cot_ref) = refs[:slabs], refs[slabs:]
     lanes = XWIN + CWIN
     eye = (
         lax.broadcasted_iota(jnp.int32, (lanes, lanes), 0)
@@ -159,11 +160,12 @@
 
     def one(r, carry):
         for y in range(slabs):
-            piece = recv_ref[y, :, pl.ds(r, 1)].astype(F32)
+            piece = pieces[y][:, pl.ds(r, 1)].astype(F32)
             piece = piece.reshape(HALF, lanes).astype(BF)
             flipped = dot(eye, piece, NT).astype(BF)
-            x_ref[pl.ds(y * rows + r, 1)] = flipped[:XWIN].reshape(1, XWIN, HALF)
-            cot_ref[pl.ds(y * rows + r, 1)] = flipped[XWIN:].reshape(1, CWIN, HALF)
+            place = lax.rem(idx_ref[1] + y, slabs) * rows + r
+            x_ref[pl.ds(place, 1)] = flipped[:XWIN].reshape(1, XWIN, HALF)
+            cot_ref[pl.ds(place, 1)] = flipped[XWIN:].reshape(1, CWIN, HALF)
         return carry
 
     lax.fori_loop(0, rows, one, 0)
@@ -212,21 +214,24 @@
     lax.fori_loop(0, ROWS // step, one, 0)
 
 
-def forward_kernel(block, image, pieces, spin, idx_ref, xo_ref, xt_ref, *rest):
+def forward_kernel(block, image, pieces, index, idx_ref, xo_ref, xt_ref, *rest):
     w_refs, rest = rest[:pieces], rest[pieces:]
     y_ref, d_ref, gain_ref, nk_far, *rest = rest
-    w_ref = w_refs[0]
     whole = None
     if pieces > 1:
         whole_far, nk, nbuf, pre, sem, w_ref = rest
         lines = HALF // pieces
         for j in range(pieces):
-            place = lax.rem(idx_ref[spin] + j, pieces) * lines
+            place = lax.rem(idx_ref[2] + j, pieces) * lines
             w_ref[pl.ds(pl.multiple_of(place, lines), lines)] = w_refs[j][...]
         whole = pltpu.make_async_copy(w_ref, whole_far, sem.at[1])
         whole.start()
     else:
-        nk, nbuf, pre, sem = rest
+        nk, nbuf, pre, sem, w_ref = rest
+        source = w_refs[0] if index is None else w_refs[0].at[index]
+        coming = pltpu.make_async_copy(source, w_ref, sem.at[1])
+        coming.start()
+        coming.wait()
     first_in = X_WIN[block][0]
     first_out, width_out = X_WIN[block + 1]
     first_s, width_s = S_WIN[block]
@@ -343,13 +348,14 @@
     weight_phase(3, dims, idx_ref, sown, nk, w_ref, gain, wg_ref)
 
 
-def backward_kernel(block, dims, image, first_g, idx_ref, qm_ref, qr_ref, xo_ref, xt_ref, g_ref,
+def backward_kernel(block, dims, image, first_g, index, idx_ref, qm_ref, qr_ref, xo_ref, xt_ref, g_ref,
                     gain_up_ref, d_ref, w_far, nk_far, gain_ref, *rest):
     if block:
         q_ref, gn_ref, wg_ref, w_ref, nk_ref, sem, sown, sbuf, wq = rest
     else:
         wg_ref, w_ref, nk_ref, sem, sown = rest
         q_ref = gn_ref = sbuf = wq = None
+    w_far = w_far if index is None else w_far.at[index]
     weights_in = pltpu.make_async_copy(w_far, w_ref, sem.at[0])
     kept_in = pltpu.make_async_copy(nk_far, nk_ref, sem.at[1])
     weights_in.start()
@@ -428,30 +434,32 @@
     windows = call(
         window_kernel, shape((shards, rows, own_chans, XWIN + CWIN), BF), [], (idx, x_in, cot), (0,)
     )
-    recv = lax.all_to_all(windows, ("x", "zh"), 0, 0, tiled=True)
-
-    packed = call(prep_kernel, shape((own_chans, CARRY), BF), [], (w1[0], gain, perm))
-    wide = jnp.broadcast_to(packed[None], (ns * nz, own_chans, CARRY))
-    wide, recv = lax.optimization_barrier((wide, recv))
-    wide = lax.all_to_all(wide, ("section", "zh"), 0, 0, tiled=True)
-    wide = wide.reshape(ns, nz * own_chans, CARRY)
-
 
     def from_chips(value, axis, size):
         moves = [[(i, (i - j) % size) for i in range(size)] for j in range(1, size)]
         return [value] + [lax.ppermute(value, axis, move) for move in moves]
 
+    packed = call(prep_kernel, shape((own_chans, CARRY), BF), [], (w1[0], gain, perm))
+    wide = jnp.broadcast_to(packed[None], (ns * nz, own_chans, CARRY))
+    wide = lax.all_to_all(wide, ("section", "zh"), 0, 0, tiled=True)
+    wide = wide.reshape(ns, nz * own_chans, CARRY)
+
+
     first = from_chips(wide[0], "x", nx)
     pair = lax.all_gather(wide[1:3], "x", axis=1, tiled=True)
     last = lax.all_gather(wide[3], "x", axis=0, tiled=True)
-    weights = [first, [pair[0]], [pair[1]], [last]]
-
-    every_row = lax.all_gather(recv, "slab", axis=0)
+
+    windows, wide = lax.optimization_barrier((windows, wide))
+    recv = lax.all_to_all(windows, ("x", "zh"), 0, 0, tiled=True)
+    recv, first = lax.optimization_barrier((recv, first))
+    weights, index = [first, [pair], [pair], [last]], [None, 0, 1, None]
+    row_pieces = from_chips(recv, "slab", ny)
     x_own, cot_own = call(
         functools.partial(assemble_kernel, ny, rows),
         (shape((ROWS, XWIN, HALF), BF), shape((ROWS, CWIN, HALF), BF)),
         [],
-        (every_row,),
+        (idx, *row_pieces),
+        (0,),
     )
 
     taps3 = 3 * CHANS
@@ -464,7 +472,7 @@
         many = pieces > 1
         whole_shape = shape((HALF, CARRY), BF)
         y, slope, gain_b, nk, *whole = call(
-            functools.partial(forward_kernel, b, image, pieces, 2),
+            functools.partial(forward_kernel, b, image, pieces, index[b]),
             (
                 shape((ROWS, width, HALF), BF),
                 shape((ROWS, S_WIN[b][1], HALF), F32),
@@ -478,12 +486,12 @@
                 pltpu.VMEM((ROWS, width, HALF), F32),
                 pltpu.SemaphoreType.DMA((2,)),
             ]
-            + [pltpu.VMEM((HALF, CARRY), BF)] * many,
+            + [pltpu.VMEM((HALF, CARRY), BF)],
             (idx, *halves[b], *weights[b]),
             (0,),
-            (),
+            () if many else (3,),
             (3, 4),
-            30,
+            0,
         )
         halves.append((y, other(y)))
         slopes.append(slope)
@@ -531,7 +539,7 @@
         args = (
             idx, q, other(q), *halves[b + 1], g, gains[b + 1], slopes[b], weights[b], shifted[b], gains[b],
         )
-        kernel = functools.partial(backward_kernel, b, dims, image, first_g)
+        kernel = functools.partial(backward_kernel, b, dims, image, first_g, index[b])
         fetched = [
             pltpu.VMEM((HALF, CARRY), BF),
             pltpu.VMEM(nk_shape, BF),

time: 294 us -> 310 us (1.054)
  blocking collectives: 9.75 us -> 51.8 us
  waiting for transfers between devices: 118 us -> 94.2 us
  local copies, waits for them, and re-layouts: 16.2 us -> 12.4 us
    all_to_all x0 -> x1, blocking collectives: none -> 42.5 us  [local(): wide = lax.all_to_all(wide, ('section', 'zh'), 0, 0, tiled=True)]
    all_to_all x1 -> x0, waiting for transfers between devices: 30.9 us -> none  [local(): wide = lax.all_to_all(wide, ('section', 'zh'), 0, 0, tiled=True)]
    ppermute x3 -> x6, waiting for transfers between devices: 25 us -> 36 us  [from_chips(): return [value] + [lax.ppermute(value, axis, move) for move in moves]]
    all_gather x1, waiting for transfers between devices: 9.74 us -> 0.01 us  [local(): last = lax.all_gather(wide[3], 'x', axis=0, tiled=True)]
    ppermute x8, waiting for transfers between devices: 8.19 us -> 16.2 us  [other(): return lax.ppermute(value, 'core', [(0, 1), (1, 0)])]
    all_to_all x1, starting transfers between devices: 9.75 us -> 4.51 us  [local(): recv = lax.all_to_all(windows, ('x', 'zh'), 0, 0, tiled=True)]
    ppermute x3 -> x6, starting transfers between devices: 2.36 us -> 7.53 us  [from_chips(): return [value] + [lax.ppermute(value, axis, move) for move in moves]]
    squeeze x1 -> x0, local copies, waits for them, and re-layouts: 3.56 us -> none  [local(): weights = [first, [pair[0]], [pair[1]], [last]]]
  transfers between devices with their start and end apart: 19 -> 20, of which waited for: 12 -> 16; matrix products, arithmetic and copies ran while one was open for 3% -> 1% of each run, Pallas kernels for 15% -> 19%
where the time goes in v7:
time: 310 us
  waiting for transfers between devices  94.2 us (30%)
  Pallas kernels  93.6 us (30%)
  blocking collectives  51.8 us (17%)
  starting transfers between devices  37.9 us (12%)
  between operations  14.2 us (5%)
  local copies, waits for them, and re-layouts  12.4 us (4%)
  other arithmetic  5.5 us (2%)
    pallas_call x11, Pallas kernels, call(): pl.pallas_call(kernel, out_shape=out_shape, in_specs=[sm if i in smem els...  93.6 us
    all_to_all x1, blocking collectives, local(): wide = lax.all_to_all(wide, ('section', 'zh'), 0, 0, tiled=True)  42.5 us
    ppermute x6, waiting for transfers between devices, from_chips(): return [value] + [lax.ppermute(value, axis, move) for move in moves]  36 us
    ppermute x8, waiting for transfers between devices, other(): return lax.ppermute(value, 'core', [(0, 1), (1, 0)])  16.2 us
    all_to_all x2, waiting for transfers between devices, reduced(): value = lax.all_to_all(value, 'x', 0, 0, tiled=True)  15.9 us
    all_to_all x1, waiting for transfers between devices, local(): parts = lax.all_to_all(parts, ('section', 'zh'), 0, 0, tiled=True)  13.9 us
    all_to_all x1, waiting for transfers between devices, local(): recv = lax.all_to_all(windows, ('x', 'zh'), 0, 0, tiled=True)  12.2 us
    all_to_all x2, starting transfers between devices, reduced(): value = lax.all_to_all(value, 'x', 0, 0, tiled=True)  10.2 us
  transfers between devices with their start and end apart: 20, of which 16 were waited for; matrix products, arithmetic and copies ran while one was open for 1% of the time, Pallas kernels for 19%

profile of v7, /device:TPU:33, one launch (start us, length us, event | category | flops | bytes accessed | tf_op | source)
XLA Modules:
  0.0 309.6 jit_solution(8316662964823960599)
XLA Ops:
  12.3 42.5 %all_to_all.25 = bf16[8,24,3584]{2,1,0:T(8,128)(2,1)S(1)} all-to-all(bf16[8,24,3584]{2,1,0:T(8,128)(2,1)S(1)} %broadcast_in_dim.12), channel_id=1, replica_groups=mesh['section'=4,'x'=4,'zh'=2,'core'=2,'slab'=4] {'section','zh'}, dimensions={0} | all-to-all | bytes 2752512 | tf_op jit(solution)/shard_map/all_to_all | solution.py:444
  58.4 4.5 %all-to-all-start = ((bf16[8,8,24,128]{3,2,1,0:T(8,128)(2,1)}), bf16[8,8,24,128]{3,2,1,0:T(8,128)(2,1)S(1)}, u32[]{:S(2)}, u32[]{:S(2)}) async-start(bf16[8,8,24,128]{3,2,1,0:T(8,128)(2,1)} %shard_map.68), calls=%async_computation | async-start | bytes 786432 | tf_op jit(solution)/shard_map/all_to_all | solution.py:453
  63.8 2.6 collective-permute-start
  67.5 12.2 %all-to-all-done.refs_0_ = bf16[8,8,24,128]{3,2,1,0:T(8,128)(2,1)S(1)} async-done(((bf16[8,8,24,128]{3,2,1,0:T(8,128)(2,1)}), bf16[8,8,24,128]{3,2,1,0:T(8,128)(2,1)S(1)}, u32[]{:S(2)}, u32[]{:S(2)}) %all-to-all-start) | async-done | bytes 393248 | tf_op jit(solution)/shard_map/all_to_all | solution.py:453
  79.8 3.6 %collective-permute-done.rest_1_ = bf16[48,3584]{1,0:T(8,128)(2,1)S(1)} collective-permute-done((bf16[48,3584]{1,0:T(8,128)(2,1)S(1)}, bf16[48,3584]{1,0:T(8,128)(2,1)S(1)}, u32[]{:S(2)}, u32[]{:S(2)}) %collective-permute-start) | collective-permute-done | bytes 344096 | tf_op jit(solution)/shard_map/ppermute | solution.py:440
  83.4 2.9 collective-permute-done.1.rest_2_
  86.3 9.8 %collective-permute-done.2.rest_3_ = bf16[48,3584]{1,0:T(8,128)(2,1)S(1)} collective-permute-done((bf16[48,3584]{1,0:T(8,128)(2,1)S(1)}, bf16[48,3584]{1,0:T(8,128)(2,1)S(1)}, u32[]{:S(2)}, u32[]{:S(2)}) %collective-permute-start.2) | collective-permute-done | bytes 344096 | tf_op jit(solution)/shard_map/ppermute | solution.py:440
  96.1 2.9 collective-permute-start.3
  99.9 6.5 %collective-permute-done.3.refs_1_ = bf16[8,8,24,128]{3,2,1,0:T(8,128)(2,1)S(1)} collective-permute-done((bf16[8,8,24,128]{3,2,1,0:T(8,128)(2,1)S(1)}, bf16[8,8,24,128]{3,2,1,0:T(8,128)(2,1)S(1)}, u32[]{:S(2)}, u32[]{:S(2)}) %collective-permute-start.3) | collective-permute-done | bytes 393248 | tf_op jit(solution)/shard_map/ppermute | solution.py:440
  107.7 11.8 %collective-permute-done.5.refs_3_ = bf16[8,8,24,128]{3,2,1,0:T(8,128)(2,1)S(1)} collective-permute-done((bf16[8,8,24,128]{3,2,1,0:T(8,128)(2,1)S(1)}, bf16[8,8,24,128]{3,2,1,0:T(8,128)(2,1)S(1)}, u32[]{:S(2)}, u32[]{:S(2)}) %collective-permute-start.5) | collective-permute-done | bytes 393248 | tf_op jit(solution)/shard_map/ppermute | solution.py:440
  120.3 4.9 %shard_map.70 = (bf16[32,80,192]{2,1,0:T(8,128)(2,1)}, bf16[32,48,192]{2,1,0:T(8,128)(2,1)}) custom-call(s32[4]{0:T(128)} %pad_add_fusion.idx_ref, bf16[8,8,24,128]{3,2,1,0:T(8,128)(2,1)} %copy-done.8, bf16[8,8,24,128]{3,2,1,0:T(8,128)(2,1)} %copy-done.16, bf16[8,8,24,128]{3,2,1,0:T(8,128)(2,1)} %copy-done.17, bf16[8,8,24,128]{3,2,1,0:T(8,128)(2,1)} %copy-done.18), custom_call_target="tpu_custom_call" | custom-call | flops 2000000000 | bytes 2000000 | tf_op jit(solution)/shard_map/pallas_call | solution.py:49
  126.1 2.9 collective-permute-done.6.xt_ref
  130.1 13.9 %shard_map.71 = (bf16[32,80,192]{2,1,0:T(8,128)(2,1)}, f32[32,16,192]{2,1,0:T(8,128)}, f32[1,384]{1,0:T(1,128)}, bf16[48,16,1152]{2,1,0:T(8,128)(2,1)}, bf16[192,3584]{1,0:T(8,128)(2,1)}) custom-call(s32[4]{0:T(128)} %pad_add_fusion.idx_ref, bf16[32,80,192]{2,1,0:T(8,128)(2,1)} %get-tuple-element.32.xo_ref, bf16[32,80,192]{2,1,0:T(8,128)(2,1)} %copy-done.2, ...), custom_call_target="tpu_custom_call" | custom-call | tf_op jit(solution)/shard_map/pallas_call | solution.py:49
  144.4 2.8 collective-permute-done.7.xt_ref
  148.4 15.0 %shard_map.72 = (bf16[32,80,192]{2,1,0:T(8,128)(2,1)}, f32[32,32,192]{2,1,0:T(8,128)}, f32[1,384]{1,0:T(1,128)}, bf16[48,16,1152]{2,1,0:T(8,128)(2,1)}) custom-call(s32[4]{0:T(128)} %pad_add_fusion.idx_ref, bf16[32,80,192]{2,1,0:T(8,128)(2,1)} %get-tuple-element.37.xo_ref, bf16[32,80,192]{2,1,0:T(8,128)(2,1)} %copy-done, ...), custom_call_target="tpu_custom_call" | custom-call | tf_op jit(solution)/shard_map/pallas_call | solution.py:49
  164.0 2.9 collective-permute-done.8.xt_ref
  168.0 13.4 %shard_map.73 = (bf16[32,64,192]{2,1,0:T(8,128)(2,1)}, f32[32,32,192]{2,1,0:T(8,128)}, f32[1,384]{1,0:T(1,128)}, bf16[48,16,1152]{2,1,0:T(8,128)(2,1)}) custom-call(s32[4]{0:T(128)} %pad_add_fusion.idx_ref, bf16[32,80,192]{2,1,0:T(8,128)(2,1)} %get-tuple-element.38.xo_ref, bf16[32,80,192]{2,1,0:T(8,128)(2,1)} %copy-done.3, ...), custom_call_target="tpu_custom_call" | custom-call | tf_op jit(solution)/shard_map/pallas_call | solution.py:49
  181.9 2.5 collective-permute-done.9.xt_ref
  185.4 14.4 %shard_map.74 = (bf16[2,32,32,192]{3,2,1,0:T(8,128)(2,1)}, bf16[64,3456]{1,0:T(8,128)(2,1)}, f32[1,384]{1,0:T(1,128)}) custom-call(s32[4]{0:T(128)} %pad_add_fusion.idx_ref, bf16[32,64,192]{2,1,0:T(8,128)(2,1)} %get-tuple-element.39.xo_ref, bf16[32,64,192]{2,1,0:T(8,128)(2,1)} %copy-done.13, bf16[32,48,192]{2,1,0:T(8,128)(2,1)} %get-tuple-element.40.cot_ref.g_ref, ...), custom_call_target="tpu_custom_call" | custom-call | flops 12000000000 | bytes 12000000 | tf_op jit(solution)/shard_map/pallas_call | solution.py:49
  200.1 2.5 collective-permute-done.10.qr_ref
  203.6 9.7 %shard_map.75 = (bf16[2,32,32,192]{3,2,1,0:T(8,128)(2,1)}, bf16[32,32,192]{2,1,0:T(8,128)(2,1)}, bf16[64,3456]{1,0:T(8,128)(2,1)}) custom-call(s32[4]{0:T(128)} %pad_add_fusion.idx_ref, bf16[2,32,32,192]{3,2,1,0:T(8,128)(2,1)} %get-tuple-element.41.qm_ref, bf16[2,32,32,192]{3,2,1,0:T(8,128)(2,1)} %copy-done.15, ...), custom_call_target="tpu_custom_call" | custom-call | flops 8000000000 | bytes 8000000 | tf_op jit(solution)/shard_map/pallas_call | solution.py:49
  217.3 8.3 %shard_map.76 = (bf16[2,32,16,192]{3,2,1,0:T(8,128)(2,1)}, bf16[32,32,192]{2,1,0:T(8,128)(2,1)}, bf16[64,3456]{1,0:T(8,128)(2,1)}) custom-call(s32[4]{0:T(128)} %pad_add_fusion.idx_ref, bf16[2,32,32,192]{3,2,1,0:T(8,128)(2,1)} %get-tuple-element.46.qm_ref, bf16[2,32,32,192]{3,2,1,0:T(8,128)(2,1)} %copy-done.14, ...), custom_call_target="tpu_custom_call" | custom-call | flops 8000000000 | bytes 8000000 | tf_op jit(solution)/shard_map/pallas_call | solution.py:49
  227.1 6.7 %all-to-all-start.3 = ((bf16[4,2,16,3456]{3,2,1,0:T(8,128)(2,1)}), bf16[4,2,16,3456]{3,2,1,0:T(8,128)(2,1)S(1)}, u32[]{:S(2)}, u32[]{:S(2)}) async-start(bf16[4,2,16,3456]{3,2,1,0:T(8,128)(2,1)} %pad_maximum_fusion.1), calls=%async_computation.3 | async-start | bytes 1769472 | tf_op jit(solution)/shard_map/all_to_all | solution.py:533
  234.6 6.1 %shard_map.77 = bf16[64,3456]{1,0:T(8,128)(2,1)} custom-call(s32[4]{0:T(128)} %pad_add_fusion.idx_ref, bf16[2,32,16,192]{3,2,1,0:T(8,128)(2,1)} %get-tuple-element.51.qm_ref, bf16[2,32,16,192]{3,2,1,0:T(8,128)(2,1)} %copy-done.4, bf16[32,80,192]{2,1,0:T(8,128)(2,1)} %get-tuple-element.37.xo_ref, bf16[32,80,192]{2,1,0:T(8,128)(2,1)} %copy-done, ...), custom_call_target="tpu_custom_call" | custom-call | flops 2000000000 | bytes 2000000 | tf_op jit(solution)/shard_map/pallas_call | solution.py:49
  242.8 4.0 %all-to-all-done.3 = bf16[4,2,16,3456]{3,2,1,0:T(8,128)(2,1)S(1)} async-done(((bf16[4,2,16,3456]{3,2,1,0:T(8,128)(2,1)}), bf16[4,2,16,3456]{3,2,1,0:T(8,128)(2,1)S(1)}, u32[]{:S(2)}, u32[]{:S(2)}) %all-to-all-start.3) | async-done | bytes 884768 | tf_op jit(solution)/shard_map/all_to_all | solution.py:533
  246.9 3.5 %all-to-all-start.2 = ((bf16[4,2,16,3456]{3,2,1,0:T(8,128)(2,1)}), bf16[4,2,16,3456]{3,2,1,0:T(8,128)(2,1)S(1)}, u32[]{:S(2)}, u32[]{:S(2)}) async-start(bf16[4,2,16,3456]{3,2,1,0:T(8,128)(2,1)} %pad_maximum_fusion), calls=%async_computation.2 | async-start | bytes 1769472 | tf_op jit(solution)/shard_map/all_to_all | solution.py:533
  250.5 11.9 %all-to-all-done.2 = bf16[4,2,16,3456]{3,2,1,0:T(8,128)(2,1)S(1)} async-done(((bf16[4,2,16,3456]{3,2,1,0:T(8,128)(2,1)}), bf16[4,2,16,3456]{3,2,1,0:T(8,128)(2,1)S(1)}, u32[]{:S(2)}, u32[]{:S(2)}) %all-to-all-start.2) | async-done | bytes 884768 | tf_op jit(solution)/shard_map/all_to_all | solution.py:533
  263.4 7.8 %all-to-all-start.4 = ((bf16[8,8,3456]{2,1,0:T(8,128)(2,1)}), bf16[8,8,3456]{2,1,0:T(8,128)(2,1)S(1)}, u32[]{:S(2)}, u32[]{:S(2)}) async-start(bf16[8,8,3456]{2,1,0:T(8,128)(2,1)} %bitcast.17), calls=%async_computation.4 | async-start | bytes 884736 | tf_op jit(solution)/shard_map/all_to_all | solution.py:572
  271.2 13.9 %all-to-all-done.4 = bf16[8,8,3456]{2,1,0:T(8,128)(2,1)S(1)} async-done(((bf16[8,8,3456]{2,1,0:T(8,128)(2,1)}), bf16[8,8,3456]{2,1,0:T(8,128)(2,1)S(1)}, u32[]{:S(2)}, u32[]{:S(2)}) %all-to-all-start.4) | async-done | bytes 442400 | tf_op jit(solution)/shard_map/all_to_all | solution.py:572
  285.2 9.3 %all_gather.11.all_ref = bf16[32,3456]{1,0:T(8,128)(2,1)S(1)} all-gather(bf16[8,3456]{1,0:T(8,128)(2,1)S(1)} %reduce_sum.47), channel_id=1, replica_groups=mesh['section'=4,'x'=4,'zh'=2,'core'=2,'slab'=4] {'slab'}, dimensions={0}, use_global_device_ids=true | all-gather | bytes 276480 | tf_op jit(solution)/shard_map/all_gather | solution.py:574
  294.6 4.1 %collective-permute-start.13 = (f32[24]{0:T(128)S(1)}, f32[24]{0:T(128)S(1)}, u32[]{:S(2)}, u32[]{:S(2)}) collective-permute-start(f32[24]{0:T(128)S(1)} %dynamic_slice.12), channel_id=1, source_target_pairs={{0,4},{4,0},{1,5},{5,1},{2,6},{6,2},{3,7},{7,3},{8,12},{12,8},{9,1... | collective-permute-start | bytes 296 | tf_op jit(solution)/shard_map/ppermute | solution.py:427
  298.7 3.4 %shard_map.78 = f32[9,24,384]{2,1,0:T(8,128)} custom-call(bf16[32,3456]{1,0:T(8,128)(2,1)} %copy-done.12, bf16[384,384]{1,0:T(8,128)(2,1)} %dynamic-slice_bitcast_fusion.perm_ref), custom_call_target="tpu_custom_call" | custom-call | flops 2000000000 | bytes 2000000 | tf_op jit(solution)/shard_map/pallas_call | solution.py:49
  (75 shorter events, 31.8 us)
Async XLA Ops:
  7.2 140.1 %all-gather.3.cloned.1.call-start = ((), (), s32[]{:S(2)}) async-start(), calls=%async_computation.5 | async-start | bytes 3440640 | tf_op jit(solution)/shard_map/all_gather | solution.py:449
  58.4 21.4 %all-to-all-start = ((bf16[8,8,24,128]{3,2,1,0:T(8,128)(2,1)}), bf16[8,8,24,128]{3,2,1,0:T(8,128)(2,1)S(1)}, u32[]{:S(2)}, u32[]{:S(2)}) async-start(bf16[8,8,24,128]{3,2,1,0:T(8,128)(2,1)} %shard_map.68), calls=%async_computation | async-start | bytes 786432 | tf_op jit(solution)/shard_map/all_to_all | solution.py:453
  62.9 118.9 %all-gather.5.cloned.1.call-start = ((), (), s32[]{:S(2)}) async-start(), calls=%async_computation.6 | async-start | bytes 1720320 | tf_op jit(solution)/shard_map/all_gather | solution.py:450
  63.8 61.5 %copy-start.1 = (bf16[2,24,3584]{2,1,0:T(8,128)(2,1)}, bf16[2,24,3584]{2,1,0:T(8,128)(2,1)S(1)}, u32[]{:S(2)}) copy-start(bf16[2,24,3584]{2,1,0:T(8,128)(2,1)S(1)} %get-tuple-element.61) | copy-start | bytes 1032196
  63.8 19.7 %collective-permute-start = (bf16[48,3584]{1,0:T(8,128)(2,1)S(1)}, bf16[48,3584]{1,0:T(8,128)(2,1)S(1)}, u32[]{:S(2)}, u32[]{:S(2)}) collective-permute-start(bf16[48,3584]{1,0:T(8,128)(2,1)S(1)} %bitcast.30), channel_id=1, source_target_pairs={{0,48},{16,0},{32,16},{48,32},{1,49},{17,1},{33,17},{49,33},{2,50}... | collective-permute-start | bytes 1032200 | tf_op jit(solution)/shard_map/ppermute | solution.py:440
  66.4 20.0 %collective-permute-start.1 = (bf16[48,3584]{1,0:T(8,128)(2,1)S(1)}, bf16[48,3584]{1,0:T(8,128)(2,1)S(1)}, u32[]{:S(2)}, u32[]{:S(2)}) collective-permute-start(bf16[48,3584]{1,0:T(8,128)(2,1)S(1)} %bitcast.31), channel_id=1, source_target_pairs={{0,32},{16,48},{32,0},{48,16},{1,33},{17,49},{33,1},{49,17},{2,34}... | collective-permute-start | bytes 1032200 | tf_op jit(solution)/shard_map/ppermute | solution.py:440
  67.0 29.2 %collective-permute-start.2 = (bf16[48,3584]{1,0:T(8,128)(2,1)S(1)}, bf16[48,3584]{1,0:T(8,128)(2,1)S(1)}, u32[]{:S(2)}, u32[]{:S(2)}) collective-permute-start(bf16[48,3584]{1,0:T(8,128)(2,1)S(1)} %bitcast.32), channel_id=1, source_target_pairs={{0,16},{16,32},{32,48},{48,0},{1,17},{17,33},{33,49},{49,1},{2,18}... | collective-permute-start | bytes 1032200 | tf_op jit(solution)/shard_map/ppermute | solution.py:440
  79.8 39.8 %copy-start.8 = (bf16[8,8,24,128]{3,2,1,0:T(8,128)(2,1)}, bf16[8,8,24,128]{3,2,1,0:T(8,128)(2,1)S(1)}, u32[]{:S(2)}) copy-start(bf16[8,8,24,128]{3,2,1,0:T(8,128)(2,1)S(1)} %all-to-all-done.refs_0_) | copy-start | bytes 1179652
  83.4 41.9 %copy-start.9 = (bf16[48,3584]{1,0:T(8,128)(2,1)}, bf16[48,3584]{1,0:T(8,128)(2,1)S(1)}, u32[]{:S(2)}) copy-start(bf16[48,3584]{1,0:T(8,128)(2,1)S(1)} %collective-permute-done.rest_1_) | copy-start | bytes 1032196
  86.3 38.9 %copy-start.10 = (bf16[48,3584]{1,0:T(8,128)(2,1)}, bf16[48,3584]{1,0:T(8,128)(2,1)S(1)}, u32[]{:S(2)}) copy-start(bf16[48,3584]{1,0:T(8,128)(2,1)S(1)} %collective-permute-done.1.rest_2_) | copy-start | bytes 1032196
  96.1 29.1 %copy-start.11 = (bf16[48,3584]{1,0:T(8,128)(2,1)}, bf16[48,3584]{1,0:T(8,128)(2,1)S(1)}, u32[]{:S(2)}) copy-start(bf16[48,3584]{1,0:T(8,128)(2,1)S(1)} %collective-permute-done.2.rest_3_) | copy-start | bytes 1032196
  96.1 10.3 %collective-permute-start.3 = (bf16[8,8,24,128]{3,2,1,0:T(8,128)(2,1)S(1)}, bf16[8,8,24,128]{3,2,1,0:T(8,128)(2,1)S(1)}, u32[]{:S(2)}, u32[]{:S(2)}) collective-permute-start(bf16[8,8,24,128]{3,2,1,0:T(8,128)(2,1)S(1)} %all-to-all-done.refs_0_), channel_id=1, source_target_pairs={{0,3},{1,0},{2,1},{3,2},{4,7},{5,4},{6,5},{7,6},{8,11},{9,8},{10,9... | collective-permute-start | bytes 1179656 | tf_op jit(solution)/shard_map/ppermute | solution.py:440
  99.1 8.7 %collective-permute-start.4 = (bf16[8,8,24,128]{3,2,1,0:T(8,128)(2,1)S(1)}, bf16[8,8,24,128]{3,2,1,0:T(8,128)(2,1)S(1)}, u32[]{:S(2)}, u32[]{:S(2)}) collective-permute-start(bf16[8,8,24,128]{3,2,1,0:T(8,128)(2,1)S(1)} %all-to-all-done.refs_0_), channel_id=1, source_target_pairs={{0,2},{1,3},{2,0},{3,1},{4,6},{5,7},{6,4},{7,5},{8,10},{9,11},{10,... | collective-permute-start | bytes 1179656 | tf_op jit(solution)/shard_map/ppermute | solution.py:440
  99.1 20.4 %collective-permute-start.5 = (bf16[8,8,24,128]{3,2,1,0:T(8,128)(2,1)S(1)}, bf16[8,8,24,128]{3,2,1,0:T(8,128)(2,1)S(1)}, u32[]{:S(2)}, u32[]{:S(2)}) collective-permute-start(bf16[8,8,24,128]{3,2,1,0:T(8,128)(2,1)S(1)} %all-to-all-done.refs_0_), channel_id=1, source_target_pairs={{0,1},{1,2},{2,3},{3,0},{4,5},{5,6},{6,7},{7,4},{8,9},{9,10},{10,1... | collective-permute-start | bytes 1179656 | tf_op jit(solution)/shard_map/ppermute | solution.py:440
  106.4 13.1 %copy-start.16 = (bf16[8,8,24,128]{3,2,1,0:T(8,128)(2,1)}, bf16[8,8,24,128]{3,2,1,0:T(8,128)(2,1)S(1)}, u32[]{:S(2)}) copy-start(bf16[8,8,24,128]{3,2,1,0:T(8,128)(2,1)S(1)} %collective-permute-done.3.refs_1_) | copy-start | bytes 1179652
  107.7 11.8 %copy-start.17 = (bf16[8,8,24,128]{3,2,1,0:T(8,128)(2,1)}, bf16[8,8,24,128]{3,2,1,0:T(8,128)(2,1)S(1)}, u32[]{:S(2)}) copy-start(bf16[8,8,24,128]{3,2,1,0:T(8,128)(2,1)S(1)} %collective-permute-done.4.refs_2_) | copy-start | bytes 1179652
  125.3 3.7 %collective-permute-start.6 = (bf16[32,80,192]{2,1,0:T(8,128)(2,1)}, bf16[32,80,192]{2,1,0:T(8,128)(2,1)S(1)}, u32[]{:S(2)}, u32[]{:S(2)}) collective-permute-start(bf16[32,80,192]{2,1,0:T(8,128)(2,1)} %get-tuple-element.32.xo_ref), channel_id=1, source_target_pairs={{0,4},{4,0},{1,5},{5,1},{2,6},{6,2},{3,7},{7,3},{8,12},{12,8},{9,1... | collective-permute-start | bytes 2949128 | tf_op jit(solution)/shard_map/ppermute | solution.py:427
  143.9 3.3 %collective-permute-start.7 = (bf16[32,80,192]{2,1,0:T(8,128)(2,1)}, bf16[32,80,192]{2,1,0:T(8,128)(2,1)S(1)}, u32[]{:S(2)}, u32[]{:S(2)}) collective-permute-start(bf16[32,80,192]{2,1,0:T(8,128)(2,1)} %get-tuple-element.37.xo_ref), channel_id=1, source_target_pairs={{0,4},{4,0},{1,5},{5,1},{2,6},{6,2},{3,7},{7,3},{8,12},{12,8},{9,1... | collective-permute-start | bytes 2949128 | tf_op jit(solution)/shard_map/ppermute | solution.py:427
  147.3 1.1 copy-start
  163.4 3.5 %collective-permute-start.8 = (bf16[32,80,192]{2,1,0:T(8,128)(2,1)}, bf16[32,80,192]{2,1,0:T(8,128)(2,1)S(1)}, u32[]{:S(2)}, u32[]{:S(2)}) collective-permute-start(bf16[32,80,192]{2,1,0:T(8,128)(2,1)} %get-tuple-element.38.xo_ref), channel_id=1, source_target_pairs={{0,4},{4,0},{1,5},{5,1},{2,6},{6,2},{3,7},{7,3},{8,12},{12,8},{9,1... | collective-permute-start | bytes 2949128 | tf_op jit(solution)/shard_map/ppermute | solution.py:427
  181.4 3.0 collective-permute-start.9
  199.7 2.9 collective-permute-start.10
  213.4 3.0 collective-permute-start.11
  217.3 8.7 %copy-start.5 = (bf16[64,3456]{1,0:T(8,128)(2,1)S(1)}, bf16[64,3456]{1,0:T(8,128)(2,1)}, u32[]{:S(2)}) copy-start(bf16[64,3456]{1,0:T(8,128)(2,1)} %get-tuple-element.59) | copy-start | bytes 1327108
  217.3 8.7 %copy-start.7 = (bf16[64,3456]{1,0:T(8,128)(2,1)S(1)}, bf16[64,3456]{1,0:T(8,128)(2,1)}, u32[]{:S(2)}) copy-start(bf16[64,3456]{1,0:T(8,128)(2,1)} %get-tuple-element.58) | copy-start | bytes 1327108
  225.6 8.2 %collective-permute-start.12 = (bf16[2,32,16,192]{3,2,1,0:T(8,128)(2,1)}, bf16[2,32,16,192]{3,2,1,0:T(8,128)(2,1)S(1)}, u32[]{:S(2)}, u32[]{:S(2)}) collective-permute-start(bf16[2,32,16,192]{3,2,1,0:T(8,128)(2,1)} %get-tuple-element.51.qm_ref), channel_id=1, source_target_pairs={{0,4},{4,0},{1,5},{5,1},{2,6},{6,2},{3,7},{7,3},{8,12},{12,8},{9,1... | collective-permute-start | bytes 1179656 | tf_op jit(solution)/shard_map/ppermute | solution.py:427
  227.1 19.8 %all-to-all-start.3 = ((bf16[4,2,16,3456]{3,2,1,0:T(8,128)(2,1)}), bf16[4,2,16,3456]{3,2,1,0:T(8,128)(2,1)S(1)}, u32[]{:S(2)}, u32[]{:S(2)}) async-start(bf16[4,2,16,3456]{3,2,1,0:T(8,128)(2,1)} %pad_maximum_fusion.1), calls=%async_computation.3 | async-start | bytes 1769472 | tf_op jit(solution)/shard_map/all_to_all | solution.py:533
  234.6 6.1 %copy-start.6 = (bf16[64,3456]{1,0:T(8,128)(2,1)S(1)}, bf16[64,3456]{1,0:T(8,128)(2,1)}, u32[]{:S(2)}) copy-start(bf16[64,3456]{1,0:T(8,128)(2,1)} %get-tuple-element.57) | copy-start | bytes 1327108
  246.9 15.6 %all-to-all-start.2 = ((bf16[4,2,16,3456]{3,2,1,0:T(8,128)(2,1)}), bf16[4,2,16,3456]{3,2,1,0:T(8,128)(2,1)S(1)}, u32[]{:S(2)}, u32[]{:S(2)}) async-start(bf16[4,2,16,3456]{3,2,1,0:T(8,128)(2,1)} %pad_maximum_fusion), calls=%async_computation.2 | async-start | bytes 1769472 | tf_op jit(solution)/shard_map/all_to_all | solution.py:533
  263.4 21.7 %all-to-all-start.4 = ((bf16[8,8,3456]{2,1,0:T(8,128)(2,1)}), bf16[8,8,3456]{2,1,0:T(8,128)(2,1)S(1)}, u32[]{:S(2)}, u32[]{:S(2)}) async-start(bf16[8,8,3456]{2,1,0:T(8,128)(2,1)} %bitcast.17), calls=%async_computation.4 | async-start | bytes 884736 | tf_op jit(solution)/shard_map/all_to_all | solution.py:572
  294.5 4.2 %copy-start.12 = (bf16[32,3456]{1,0:T(8,128)(2,1)}, bf16[32,3456]{1,0:T(8,128)(2,1)S(1)}, u32[]{:S(2)}) copy-start(bf16[32,3456]{1,0:T(8,128)(2,1)S(1)} %all_gather.11.all_ref) | copy-start | bytes 663556
  294.6 7.6 %collective-permute-start.13 = (f32[24]{0:T(128)S(1)}, f32[24]{0:T(128)S(1)}, u32[]{:S(2)}, u32[]{:S(2)}) collective-permute-start(f32[24]{0:T(128)S(1)} %dynamic_slice.12), channel_id=1, source_target_pairs={{0,4},{4,0},{1,5},{5,1},{2,6},{6,2},{3,7},{7,3},{8,12},{12,8},{9,1... | collective-permute-start | bytes 296 | tf_op jit(solution)/shard_map/ppermute | solution.py:427
  (7 other events, 6.8 us)
Sparse Core Ops, SparseCore 0:
  55.9 53.8 all-gather.2
  144.5 29.2 all-gather.4

commit v8 on v7

--- a/solution.py
+++ b/solution.py
@@ -446,12 +446,12 @@
 
 
     first = from_chips(wide[0], "x", nx)
-    pair = lax.all_gather(wide[1:3], "x", axis=1, tiled=True)
-    last = lax.all_gather(wide[3], "x", axis=0, tiled=True)
 
     windows, wide = lax.optimization_barrier((windows, wide))
     recv = lax.all_to_all(windows, ("x", "zh"), 0, 0, tiled=True)
-    recv, first = lax.optimization_barrier((recv, first))
+    rest, first, recv = lax.optimization_barrier((wide[1:], first, recv))
+    pair = lax.all_gather(rest[:2], "x", axis=1, tiled=True)
+    last = lax.all_gather(rest[2], "x", axis=0, tiled=True)
     weights, index = [first, [pair], [pair], [last]], [None, 0, 1, None]
     row_pieces = from_chips(recv, "slab", ny)
     x_own, cot_own = call(
@@ -566,9 +566,11 @@
         first_g = S_WIN[b][0]
         weight_parts[b] = grads
         if b == 2:
-            late = reduced(*weight_parts[2:])
-
-    parts = jnp.concatenate([reduced(*weight_parts[:2]), late]).reshape(ns * nz, lines, LANES)
+            late = [reduced(*weight_parts[2:])]
+        else:
+            late.insert(0, reduced(grads))
+
+    parts = jnp.concatenate(late).reshape(ns * nz, lines, LANES)
     parts = lax.all_to_all(parts, ("section", "zh"), 0, 0, tiled=True)
     total = jnp.sum(parts.astype(F32), axis=0).astype(BF)
     every = lax.all_gather(total, "slab", axis=0, tiled=True)

time: 310 us -> 289 us (0.932)
  blocking collectives: 51.8 us -> 9.81 us
  waiting for transfers between devices: 94.2 us -> 105 us
  starting transfers between devices: 37.9 us -> 46.6 us
    all_to_all x1 -> x0, blocking collectives: 42.5 us -> none  [local(): wide = lax.all_to_all(wide, ('section', 'zh'), 0, 0, tiled=True)]
    all_to_all x0 -> x1, waiting for transfers between devices: none -> 29.4 us  [local(): wide = lax.all_to_all(wide, ('section', 'zh'), 0, 0, tiled=True)]
    all_to_all x1, waiting for transfers between devices: 12.2 us -> 0.01 us  [local(): recv = lax.all_to_all(windows, ('x', 'zh'), 0, 0, tiled=True)]
    all_to_all x0 -> x1, starting transfers between devices: none -> 8.01 us  [local(): wide = lax.all_to_all(wide, ('section', 'zh'), 0, 0, tiled=True)]
    all_to_all x2 -> x3, waiting for transfers between devices: 15.9 us -> 10.4 us  [reduced(): value = lax.all_to_all(value, 'x', 0, 0, tiled=True)]
    ppermute x6, waiting for transfers between devices: 36 us -> 39.6 us  [from_chips(): return [value] + [lax.ppermute(value, axis, move) for move in moves]]
    ppermute x8, waiting for transfers between devices: 16.2 us -> 12.9 us  [other(): return lax.ppermute(value, 'core', [(0, 1), (1, 0)])]
    unnamed x38 -> x32, local copies, waits for them, and re-layouts: 7.88 us -> 8.67 us
  transfers between devices with their start and end apart: 20 -> 22, of which waited for: 16 -> 16; matrix products, arithmetic and copies ran while one was open for 1% -> 1% of each run, Pallas kernels for 19% -> 23%
where the time goes in v8:
time: 289 us; the launch traced here: 288 us
  waiting for transfers between devices  105 us (36%)
  Pallas kernels  93.4 us (32%)
  starting transfers between devices  46.6 us (16%)
  local copies, waits for them, and re-layouts  14.4 us (5%)
  between operations  14.2 us (5%)
  blocking collectives  9.81 us (3%)
  other arithmetic  4.45 us (2%)
    pallas_call x11, Pallas kernels, call(): pl.pallas_call(kernel, out_shape=out_shape, in_specs=[sm if i in smem els...  93.4 us
    ppermute x6, waiting for transfers between devices, from_chips(): return [value] + [lax.ppermute(value, axis, move) for move in moves]  39.6 us
    all_to_all x1, waiting for transfers between devices, local(): wide = lax.all_to_all(wide, ('section', 'zh'), 0, 0, tiled=True)  29.4 us
    all_to_all x1, waiting for transfers between devices, local(): parts = lax.all_to_all(parts, ('section', 'zh'), 0, 0, tiled=True)  13.1 us
    ppermute x8, waiting for transfers between devices, other(): return lax.ppermute(value, 'core', [(0, 1), (1, 0)])  12.9 us
    all_to_all x3, starting transfers between devices, reduced(): value = lax.all_to_all(value, 'x', 0, 0, tiled=True)  10.9 us
    all_to_all x3, waiting for transfers between devices, reduced(): value = lax.all_to_all(value, 'x', 0, 0, tiled=True)  10.4 us
    all_gather x1, blocking collectives, local(): every = lax.all_gather(total, 'slab', axis=0, tiled=True)  9.81 us
  transfers between devices with their start and end apart: 22, of which 16 were waited for; matrix products, arithmetic and copies ran while one was open for 1% of the time, Pallas kernels for 23%

profile of v8, /device:TPU:33, one launch (start us, length us, event | category | flops | bytes accessed | tf_op | source)
XLA Modules:
  0.0 288.2 jit_solution(2784924208979258406)
XLA Ops:
  13.4 8.0 %all-to-all-start = ((bf16[8,24,3584]{2,1,0:T(8,128)(2,1)}), bf16[8,24,3584]{2,1,0:T(8,128)(2,1)S(1)}, u32[]{:S(2)}, u32[]{:S(2)}) async-start(bf16[8,24,3584]{2,1,0:T(8,128)(2,1)} %broadcast_in_dim.12), calls=%async_computation | async-start | bytes 2752512 | tf_op jit(solution)/shard_map/all_to_all | solution.py:444
  24.1 29.4 %all-to-all-done = bf16[8,24,3584]{2,1,0:T(8,128)(2,1)S(1)} async-done(((bf16[8,24,3584]{2,1,0:T(8,128)(2,1)}), bf16[8,24,3584]{2,1,0:T(8,128)(2,1)S(1)}, u32[]{:S(2)}, u32[]{:S(2)}) %all-to-all-start) | async-done | bytes 1376288 | tf_op jit(solution)/shard_map/all_to_all | solution.py:444
  53.5 6.7 %all-to-all-start.1 = ((bf16[8,8,24,128]{3,2,1,0:T(8,128)(2,1)}), bf16[8,8,24,128]{3,2,1,0:T(8,128)(2,1)S(1)}, u32[]{:S(2)}, u32[]{:S(2)}) async-start(bf16[8,8,24,128]{3,2,1,0:T(8,128)(2,1)} %shard_map.68), calls=%async_computation.1 | async-start | bytes 786432 | tf_op jit(solution)/shard_map/all_to_all | solution.py:451
  60.2 2.7 collective-permute-start
  64.2 6.5 %collective-permute-done.rest_1_ = bf16[48,3584]{1,0:T(8,128)(2,1)S(1)} collective-permute-done((bf16[48,3584]{1,0:T(8,128)(2,1)S(1)}, bf16[48,3584]{1,0:T(8,128)(2,1)S(1)}, u32[]{:S(2)}, u32[]{:S(2)}) %collective-permute-start) | collective-permute-done | bytes 344096 | tf_op jit(solution)/shard_map/ppermute | solution.py:440
  70.7 3.2 %collective-permute-done.1.rest_2_ = bf16[48,3584]{1,0:T(8,128)(2,1)S(1)} collective-permute-done((bf16[48,3584]{1,0:T(8,128)(2,1)S(1)}, bf16[48,3584]{1,0:T(8,128)(2,1)S(1)}, u32[]{:S(2)}, u32[]{:S(2)}) %collective-permute-start.1) | collective-permute-done | bytes 344096 | tf_op jit(solution)/shard_map/ppermute | solution.py:440
  74.6 9.9 %collective-permute-done.2.rest_3_ = bf16[48,3584]{1,0:T(8,128)(2,1)} collective-permute-done((bf16[48,3584]{1,0:T(8,128)(2,1)S(1)}, bf16[48,3584]{1,0:T(8,128)(2,1)}, u32[]{:S(2)}, u32[]{:S(2)}) %collective-permute-start.2) | collective-permute-done | bytes 344096 | tf_op jit(solution)/shard_map/ppermute | solution.py:440
  85.5 2.8 collective-permute-start.3
  89.4 7.8 %collective-permute-done.3.refs_1_ = bf16[8,8,24,128]{3,2,1,0:T(8,128)(2,1)S(1)} collective-permute-done((bf16[8,8,24,128]{3,2,1,0:T(8,128)(2,1)S(1)}, bf16[8,8,24,128]{3,2,1,0:T(8,128)(2,1)S(1)}, u32[]{:S(2)}, u32[]{:S(2)}) %collective-permute-start.3) | collective-permute-done | bytes 393248 | tf_op jit(solution)/shard_map/ppermute | solution.py:440
  99.5 9.9 %collective-permute-done.5.refs_3_ = bf16[8,8,24,128]{3,2,1,0:T(8,128)(2,1)S(1)} collective-permute-done((bf16[8,8,24,128]{3,2,1,0:T(8,128)(2,1)S(1)}, bf16[8,8,24,128]{3,2,1,0:T(8,128)(2,1)S(1)}, u32[]{:S(2)}, u32[]{:S(2)}) %collective-permute-start.5) | collective-permute-done | bytes 393248 | tf_op jit(solution)/shard_map/ppermute | solution.py:440
  110.1 4.9 %shard_map.70 = (bf16[32,80,192]{2,1,0:T(8,128)(2,1)}, bf16[32,48,192]{2,1,0:T(8,128)(2,1)}) custom-call(s32[4]{0:T(128)} %pad_add_fusion.idx_ref, bf16[8,8,24,128]{3,2,1,0:T(8,128)(2,1)} %copy-done.6, bf16[8,8,24,128]{3,2,1,0:T(8,128)(2,1)} %copy-done.13, bf16[8,8,24,128]{3,2,1,0:T(8,128)(2,1)} %copy-done.14, bf16[8,8,24,128]{3,2,1,0:T(8,128)(2,1)} %copy-done.15), custom_call_target="tpu_custom_call" | custom-call | flops 2000000000 | bytes 2000000 | tf_op jit(solution)/shard_map/pallas_call | solution.py:49
  115.5 2.9 collective-permute-done.6.xt_ref
  119.4 13.8 %shard_map.71 = (bf16[32,80,192]{2,1,0:T(8,128)(2,1)}, f32[32,16,192]{2,1,0:T(8,128)}, f32[1,384]{1,0:T(1,128)}, bf16[48,16,1152]{2,1,0:T(8,128)(2,1)}, bf16[192,3584]{1,0:T(8,128)(2,1)}) custom-call(s32[4]{0:T(128)} %pad_add_fusion.idx_ref, bf16[32,80,192]{2,1,0:T(8,128)(2,1)} %get-tuple-element.37.xo_ref, bf16[32,80,192]{2,1,0:T(8,128)(2,1)} %copy-done.2, ...), custom_call_target="tpu_custom_call" | custom-call | tf_op jit(solution)/shard_map/pallas_call | solution.py:49
  137.7 15.1 %shard_map.72 = (bf16[32,80,192]{2,1,0:T(8,128)(2,1)}, f32[32,32,192]{2,1,0:T(8,128)}, f32[1,384]{1,0:T(1,128)}, bf16[48,16,1152]{2,1,0:T(8,128)(2,1)}) custom-call(s32[4]{0:T(128)} %pad_add_fusion.idx_ref, bf16[32,80,192]{2,1,0:T(8,128)(2,1)} %get-tuple-element.42.xo_ref, bf16[32,80,192]{2,1,0:T(8,128)(2,1)} %copy-done, ...), custom_call_target="tpu_custom_call" | custom-call | tf_op jit(solution)/shard_map/pallas_call | solution.py:49
  153.4 2.9 %collective-permute-done.8.xt_ref = bf16[32,80,192]{2,1,0:T(8,128)(2,1)S(1)} collective-permute-done((bf16[32,80,192]{2,1,0:T(8,128)(2,1)}, bf16[32,80,192]{2,1,0:T(8,128)(2,1)S(1)}, u32[]{:S(2)}, u32[]{:S(2)}) %collective-permute-start.8) | collective-permute-done | bytes 983072 | tf_op jit(solution)/shard_map/ppermute | solution.py:427
  157.4 13.3 %shard_map.73 = (bf16[32,64,192]{2,1,0:T(8,128)(2,1)}, f32[32,32,192]{2,1,0:T(8,128)}, f32[1,384]{1,0:T(1,128)}, bf16[48,16,1152]{2,1,0:T(8,128)(2,1)}) custom-call(s32[4]{0:T(128)} %pad_add_fusion.idx_ref, bf16[32,80,192]{2,1,0:T(8,128)(2,1)} %get-tuple-element.44.xo_ref, bf16[32,80,192]{2,1,0:T(8,128)(2,1)} %copy-done.3, ...), custom_call_target="tpu_custom_call" | custom-call | tf_op jit(solution)/shard_map/pallas_call | solution.py:49
  171.2 2.5 collective-permute-done.9.xt_ref
  174.7 14.3 %shard_map.74 = (bf16[2,32,32,192]{3,2,1,0:T(8,128)(2,1)}, bf16[64,3456]{1,0:T(8,128)(2,1)}, f32[1,384]{1,0:T(1,128)}) custom-call(s32[4]{0:T(128)} %pad_add_fusion.idx_ref, bf16[32,64,192]{2,1,0:T(8,128)(2,1)} %get-tuple-element.45.xo_ref, bf16[32,64,192]{2,1,0:T(8,128)(2,1)} %copy-done.10, bf16[32,48,192]{2,1,0:T(8,128)(2,1)} %get-tuple-element.46.cot_ref.g_ref, ...), custom_call_target="tpu_custom_call" | custom-call | flops 12000000000 | bytes 12000000 | tf_op jit(solution)/shard_map/pallas_call | solution.py:49
  189.4 2.5 collective-permute-done.10.qr_ref
  193.0 9.8 %shard_map.75 = (bf16[2,32,32,192]{3,2,1,0:T(8,128)(2,1)}, bf16[32,32,192]{2,1,0:T(8,128)(2,1)}, bf16[64,3456]{1,0:T(8,128)(2,1)}) custom-call(s32[4]{0:T(128)} %pad_add_fusion.idx_ref, bf16[2,32,32,192]{3,2,1,0:T(8,128)(2,1)} %get-tuple-element.47.qm_ref, bf16[2,32,32,192]{3,2,1,0:T(8,128)(2,1)} %copy-done.12, ...), custom_call_target="tpu_custom_call" | custom-call | flops 8000000000 | bytes 8000000 | tf_op jit(solution)/shard_map/pallas_call | solution.py:49
  205.2 3.5 %all-to-all-start.4 = ((bf16[4,2,16,3456]{3,2,1,0:T(8,128)(2,1)}), bf16[4,2,16,3456]{3,2,1,0:T(8,128)(2,1)S(1)}, u32[]{:S(2)}, u32[]{:S(2)}) async-start(bf16[4,2,16,3456]{3,2,1,0:T(8,128)(2,1)} %pad_maximum_fusion), calls=%async_computation.4 | async-start | bytes 1769472 | tf_op jit(solution)/shard_map/all_to_all | solution.py:533
  209.7 8.2 %shard_map.76 = (bf16[2,32,16,192]{3,2,1,0:T(8,128)(2,1)}, bf16[32,32,192]{2,1,0:T(8,128)(2,1)}, bf16[64,3456]{1,0:T(8,128)(2,1)}) custom-call(s32[4]{0:T(128)} %pad_add_fusion.idx_ref, bf16[2,32,32,192]{3,2,1,0:T(8,128)(2,1)} %get-tuple-element.52.qm_ref, bf16[2,32,32,192]{3,2,1,0:T(8,128)(2,1)} %copy-done.11, ...), custom_call_target="tpu_custom_call" | custom-call | flops 8000000000 | bytes 8000000 | tf_op jit(solution)/shard_map/pallas_call | solution.py:49
  218.2 3.9 %all-to-all-done.4 = bf16[4,2,16,3456]{3,2,1,0:T(8,128)(2,1)S(1)} async-done(((bf16[4,2,16,3456]{3,2,1,0:T(8,128)(2,1)}), bf16[4,2,16,3456]{3,2,1,0:T(8,128)(2,1)S(1)}, u32[]{:S(2)}, u32[]{:S(2)}) %all-to-all-start.4) | async-done | bytes 884768 | tf_op jit(solution)/shard_map/all_to_all | solution.py:533
  222.0 3.7 %all-to-all-start.3 = ((bf16[4,1,16,3456]{3,2,1,0:T(8,128)(2,1)}), bf16[4,1,16,3456]{3,2,1,0:T(8,128)(2,1)S(1)}, u32[]{:S(2)}, u32[]{:S(2)}) async-start(bf16[4,1,16,3456]{3,2,1,0:T(8,128)(2,1)} %bitcast.37), calls=%async_computation.3 | async-start | bytes 884736 | tf_op jit(solution)/shard_map/all_to_all | solution.py:533
  226.5 6.1 %shard_map.77 = bf16[64,3456]{1,0:T(8,128)(2,1)} custom-call(s32[4]{0:T(128)} %pad_add_fusion.idx_ref, bf16[2,32,16,192]{3,2,1,0:T(8,128)(2,1)} %get-tuple-element.57.qm_ref, bf16[2,32,16,192]{3,2,1,0:T(8,128)(2,1)} %copy-done.4, bf16[32,80,192]{2,1,0:T(8,128)(2,1)} %get-tuple-element.42.xo_ref, bf16[32,80,192]{2,1,0:T(8,128)(2,1)} %copy-done, ...), custom_call_target="tpu_custom_call" | custom-call | flops 2000000000 | bytes 2000000 | tf_op jit(solution)/shard_map/pallas_call | solution.py:49
  232.8 3.8 %all-to-all-start.2 = ((bf16[4,1,16,3456]{3,2,1,0:T(8,128)(2,1)}), bf16[4,1,16,3456]{3,2,1,0:T(8,128)(2,1)S(1)}, u32[]{:S(2)}, u32[]{:S(2)}) async-start(bf16[4,1,16,3456]{3,2,1,0:T(8,128)(2,1)} %bitcast.30), calls=%async_computation.2 | async-start | bytes 884736 | tf_op jit(solution)/shard_map/all_to_all | solution.py:533
  236.9 6.3 %all-to-all-done.2 = bf16[4,1,16,3456]{3,2,1,0:T(8,128)(2,1)S(1)} async-done(((bf16[4,1,16,3456]{3,2,1,0:T(8,128)(2,1)}), bf16[4,1,16,3456]{3,2,1,0:T(8,128)(2,1)S(1)}, u32[]{:S(2)}, u32[]{:S(2)}) %all-to-all-start.2) | async-done | bytes 442400 | tf_op jit(solution)/shard_map/all_to_all | solution.py:533
  244.0 6.0 %all-to-all-start.5 = ((bf16[8,8,3456]{2,1,0:T(8,128)(2,1)}), bf16[8,8,3456]{2,1,0:T(8,128)(2,1)S(1)}, u32[]{:S(2)}, u32[]{:S(2)}) async-start(bf16[8,8,3456]{2,1,0:T(8,128)(2,1)} %bitcast.19), calls=%async_computation.5 | async-start | bytes 884736 | tf_op jit(solution)/shard_map/all_to_all | solution.py:574
  250.0 13.1 %all-to-all-done.5 = bf16[8,8,3456]{2,1,0:T(8,128)(2,1)S(1)} async-done(((bf16[8,8,3456]{2,1,0:T(8,128)(2,1)}), bf16[8,8,3456]{2,1,0:T(8,128)(2,1)S(1)}, u32[]{:S(2)}, u32[]{:S(2)}) %all-to-all-start.5) | async-done | bytes 442400 | tf_op jit(solution)/shard_map/all_to_all | solution.py:574
  263.2 9.8 %all_gather.11.all_ref = bf16[32,3456]{1,0:T(8,128)(2,1)S(1)} all-gather(bf16[8,3456]{1,0:T(8,128)(2,1)S(1)} %reduce_sum.66), channel_id=1, replica_groups=mesh['section'=4,'x'=4,'zh'=2,'core'=2,'slab'=4] {'slab'}, dimensions={0}, use_global_device_ids=true | all-gather | bytes 276480 | tf_op jit(solution)/shard_map/all_gather | solution.py:576
  273.1 4.3 %collective-permute-start.13 = (f32[24]{0:T(128)S(1)}, f32[24]{0:T(128)S(1)}, u32[]{:S(2)}, u32[]{:S(2)}) collective-permute-start(f32[24]{0:T(128)S(1)} %dynamic_slice.12), channel_id=1, source_target_pairs={{0,4},{4,0},{1,5},{5,1},{2,6},{6,2},{3,7},{7,3},{8,12},{12,8},{9,1... | collective-permute-start | bytes 296 | tf_op jit(solution)/shard_map/ppermute | solution.py:427
  277.4 3.4 %shard_map.78 = f32[9,24,384]{2,1,0:T(8,128)} custom-call(bf16[32,3456]{1,0:T(8,128)(2,1)} %copy-done.9, bf16[384,384]{1,0:T(8,128)(2,1)} %dynamic-slice_bitcast_fusion.perm_ref), custom_call_target="tpu_custom_call" | custom-call | flops 2000000000 | bytes 2000000 | tf_op jit(solution)/shard_map/pallas_call | solution.py:49
  (74 shorter events, 33.3 us)
Async XLA Ops:
  13.4 40.1 %all-to-all-start = ((bf16[8,24,3584]{2,1,0:T(8,128)(2,1)}), bf16[8,24,3584]{2,1,0:T(8,128)(2,1)S(1)}, u32[]{:S(2)}, u32[]{:S(2)}) async-start(bf16[8,24,3584]{2,1,0:T(8,128)(2,1)} %broadcast_in_dim.12), calls=%async_computation | async-start | bytes 2752512 | tf_op jit(solution)/shard_map/all_to_all | solution.py:444
  53.5 31.0 %all-to-all-start.1 = ((bf16[8,8,24,128]{3,2,1,0:T(8,128)(2,1)}), bf16[8,8,24,128]{3,2,1,0:T(8,128)(2,1)S(1)}, u32[]{:S(2)}, u32[]{:S(2)}) async-start(bf16[8,8,24,128]{3,2,1,0:T(8,128)(2,1)} %shard_map.68), calls=%async_computation.1 | async-start | bytes 786432 | tf_op jit(solution)/shard_map/all_to_all | solution.py:451
  60.2 76.4 %all-gather.4.cloned.1.call-start = ((), (), s32[]{:S(2)}) async-start(), calls=%async_computation.6 | async-start | bytes 3440640 | tf_op jit(solution)/shard_map/all_gather | solution.py:453
  60.2 25.2 %copy-start.1 = (bf16[2,24,3584]{2,1,0:T(8,128)(2,1)}, bf16[2,24,3584]{2,1,0:T(8,128)(2,1)S(1)}, u32[]{:S(2)}) copy-start(bf16[2,24,3584]{2,1,0:T(8,128)(2,1)S(1)} %slice.21) | copy-start | bytes 1032196
  60.2 10.5 %collective-permute-start = (bf16[48,3584]{1,0:T(8,128)(2,1)S(1)}, bf16[48,3584]{1,0:T(8,128)(2,1)S(1)}, u32[]{:S(2)}, u32[]{:S(2)}) collective-permute-start(bf16[48,3584]{1,0:T(8,128)(2,1)S(1)} %bitcast.31), channel_id=1, source_target_pairs={{0,48},{16,0},{32,16},{48,32},{1,49},{17,1},{33,17},{49,33},{2,50}... | collective-permute-start | bytes 1032200 | tf_op jit(solution)/shard_map/ppermute | solution.py:440
  62.9 10.9 %collective-permute-start.1 = (bf16[48,3584]{1,0:T(8,128)(2,1)S(1)}, bf16[48,3584]{1,0:T(8,128)(2,1)S(1)}, u32[]{:S(2)}, u32[]{:S(2)}) collective-permute-start(bf16[48,3584]{1,0:T(8,128)(2,1)S(1)} %bitcast.32), channel_id=1, source_target_pairs={{0,32},{16,48},{32,0},{48,16},{1,33},{17,49},{33,1},{49,17},{2,34}... | collective-permute-start | bytes 1032200 | tf_op jit(solution)/shard_map/ppermute | solution.py:440
  63.5 21.0 %collective-permute-start.2 = (bf16[48,3584]{1,0:T(8,128)(2,1)S(1)}, bf16[48,3584]{1,0:T(8,128)(2,1)}, u32[]{:S(2)}, u32[]{:S(2)}) collective-permute-start(bf16[48,3584]{1,0:T(8,128)(2,1)S(1)} %bitcast.33), channel_id=1, source_target_pairs={{0,16},{16,32},{32,48},{48,0},{1,17},{17,33},{33,49},{49,1},{2,18}... | collective-permute-start | bytes 1032200 | tf_op jit(solution)/shard_map/ppermute | solution.py:440
  70.7 44.4 %copy-start.7 = (bf16[48,3584]{1,0:T(8,128)(2,1)}, bf16[48,3584]{1,0:T(8,128)(2,1)S(1)}, u32[]{:S(2)}) copy-start(bf16[48,3584]{1,0:T(8,128)(2,1)S(1)} %collective-permute-done.rest_1_) | copy-start | bytes 1032196
  84.5 24.9 %copy-start.6 = (bf16[8,8,24,128]{3,2,1,0:T(8,128)(2,1)}, bf16[8,8,24,128]{3,2,1,0:T(8,128)(2,1)S(1)}, u32[]{:S(2)}) copy-start(bf16[8,8,24,128]{3,2,1,0:T(8,128)(2,1)S(1)} %all-to-all-done.1.refs_0_) | copy-start | bytes 1179652
  85.5 85.7 %all-gather.6.cloned.1.call-start = ((), (), s32[]{:S(2)}) async-start(), calls=%async_computation.7 | async-start | bytes 1720320 | tf_op jit(solution)/shard_map/all_gather | solution.py:454
  85.5 11.6 %collective-permute-start.3 = (bf16[8,8,24,128]{3,2,1,0:T(8,128)(2,1)S(1)}, bf16[8,8,24,128]{3,2,1,0:T(8,128)(2,1)S(1)}, u32[]{:S(2)}, u32[]{:S(2)}) collective-permute-start(bf16[8,8,24,128]{3,2,1,0:T(8,128)(2,1)S(1)} %all-to-all-done.1.refs_0_), channel_id=1, source_target_pairs={{0,3},{1,0},{2,1},{3,2},{4,7},{5,4},{6,5},{7,6},{8,11},{9,8},{10,9... | collective-permute-start | bytes 1179656 | tf_op jit(solution)/shard_map/ppermute | solution.py:440
  88.3 11.2 %collective-permute-start.4 = (bf16[8,8,24,128]{3,2,1,0:T(8,128)(2,1)S(1)}, bf16[8,8,24,128]{3,2,1,0:T(8,128)(2,1)S(1)}, u32[]{:S(2)}, u32[]{:S(2)}) collective-permute-start(bf16[8,8,24,128]{3,2,1,0:T(8,128)(2,1)S(1)} %all-to-all-done.1.refs_0_), channel_id=1, source_target_pairs={{0,2},{1,3},{2,0},{3,1},{4,6},{5,7},{6,4},{7,5},{8,10},{9,11},{10,... | collective-permute-start | bytes 1179656 | tf_op jit(solution)/shard_map/ppermute | solution.py:440
  88.7 20.7 %collective-permute-start.5 = (bf16[8,8,24,128]{3,2,1,0:T(8,128)(2,1)S(1)}, bf16[8,8,24,128]{3,2,1,0:T(8,128)(2,1)S(1)}, u32[]{:S(2)}, u32[]{:S(2)}) collective-permute-start(bf16[8,8,24,128]{3,2,1,0:T(8,128)(2,1)S(1)} %all-to-all-done.1.refs_0_), channel_id=1, source_target_pairs={{0,1},{1,2},{2,3},{3,0},{4,5},{5,6},{6,7},{7,4},{8,9},{9,10},{10,1... | collective-permute-start | bytes 1179656 | tf_op jit(solution)/shard_map/ppermute | solution.py:440
  97.1 12.3 %copy-start.13 = (bf16[8,8,24,128]{3,2,1,0:T(8,128)(2,1)}, bf16[8,8,24,128]{3,2,1,0:T(8,128)(2,1)S(1)}, u32[]{:S(2)}) copy-start(bf16[8,8,24,128]{3,2,1,0:T(8,128)(2,1)S(1)} %collective-permute-done.3.refs_1_) | copy-start | bytes 1179652
  99.5 9.9 %copy-start.14 = (bf16[8,8,24,128]{3,2,1,0:T(8,128)(2,1)}, bf16[8,8,24,128]{3,2,1,0:T(8,128)(2,1)S(1)}, u32[]{:S(2)}) copy-start(bf16[8,8,24,128]{3,2,1,0:T(8,128)(2,1)S(1)} %collective-permute-done.4.refs_2_) | copy-start | bytes 1179652
  115.1 3.3 %collective-permute-start.6 = (bf16[32,80,192]{2,1,0:T(8,128)(2,1)}, bf16[32,80,192]{2,1,0:T(8,128)(2,1)S(1)}, u32[]{:S(2)}, u32[]{:S(2)}) collective-permute-start(bf16[32,80,192]{2,1,0:T(8,128)(2,1)} %get-tuple-element.37.xo_ref), channel_id=1, source_target_pairs={{0,4},{4,0},{1,5},{5,1},{2,6},{6,2},{3,7},{7,3},{8,12},{12,8},{9,1... | collective-permute-start | bytes 2949128 | tf_op jit(solution)/shard_map/ppermute | solution.py:427
  133.2 3.3 %collective-permute-start.7 = (bf16[32,80,192]{2,1,0:T(8,128)(2,1)}, bf16[32,80,192]{2,1,0:T(8,128)(2,1)S(1)}, u32[]{:S(2)}, u32[]{:S(2)}) collective-permute-start(bf16[32,80,192]{2,1,0:T(8,128)(2,1)} %get-tuple-element.42.xo_ref), channel_id=1, source_target_pairs={{0,4},{4,0},{1,5},{5,1},{2,6},{6,2},{3,7},{7,3},{8,12},{12,8},{9,1... | collective-permute-start | bytes 2949128 | tf_op jit(solution)/shard_map/ppermute | solution.py:427
  136.5 1.2 copy-start
  152.8 3.5 %collective-permute-start.8 = (bf16[32,80,192]{2,1,0:T(8,128)(2,1)}, bf16[32,80,192]{2,1,0:T(8,128)(2,1)S(1)}, u32[]{:S(2)}, u32[]{:S(2)}) collective-permute-start(bf16[32,80,192]{2,1,0:T(8,128)(2,1)} %get-tuple-element.44.xo_ref), channel_id=1, source_target_pairs={{0,4},{4,0},{1,5},{5,1},{2,6},{6,2},{3,7},{7,3},{8,12},{12,8},{9,1... | collective-permute-start | bytes 2949128 | tf_op jit(solution)/shard_map/ppermute | solution.py:427
  156.3 1.1 copy-start.3
  170.7 3.0 %collective-permute-start.9 = (bf16[32,64,192]{2,1,0:T(8,128)(2,1)}, bf16[32,64,192]{2,1,0:T(8,128)(2,1)S(1)}, u32[]{:S(2)}, u32[]{:S(2)}) collective-permute-start(bf16[32,64,192]{2,1,0:T(8,128)(2,1)} %get-tuple-element.45.xo_ref), channel_id=1, source_target_pairs={{0,4},{4,0},{1,5},{5,1},{2,6},{6,2},{3,7},{7,3},{8,12},{12,8},{9,1... | collective-permute-start | bytes 2359304 | tf_op jit(solution)/shard_map/ppermute | solution.py:427
  189.0 2.9 collective-permute-start.10
  191.9 1.1 copy-start.12
  193.0 10.2 %copy-start.5 = (bf16[64,3456]{1,0:T(8,128)(2,1)S(1)}, bf16[64,3456]{1,0:T(8,128)(2,1)}, u32[]{:S(2)}) copy-start(bf16[64,3456]{1,0:T(8,128)(2,1)} %get-tuple-element.65) | copy-start | bytes 1327108
  202.7 6.0 %collective-permute-start.11 = (bf16[2,32,32,192]{3,2,1,0:T(8,128)(2,1)}, bf16[2,32,32,192]{3,2,1,0:T(8,128)(2,1)S(1)}, u32[]{:S(2)}, u32[]{:S(2)}) collective-permute-start(bf16[2,32,32,192]{3,2,1,0:T(8,128)(2,1)} %get-tuple-element.52.qm_ref), channel_id=1, source_target_pairs={{0,4},{4,0},{1,5},{5,1},{2,6},{6,2},{3,7},{7,3},{8,12},{12,8},{9,1... | collective-permute-start | bytes 2359304 | tf_op jit(solution)/shard_map/ppermute | solution.py:427
  205.2 16.8 %all-to-all-start.4 = ((bf16[4,2,16,3456]{3,2,1,0:T(8,128)(2,1)}), bf16[4,2,16,3456]{3,2,1,0:T(8,128)(2,1)S(1)}, u32[]{:S(2)}, u32[]{:S(2)}) async-start(bf16[4,2,16,3456]{3,2,1,0:T(8,128)(2,1)} %pad_maximum_fusion), calls=%async_computation.4 | async-start | bytes 1769472 | tf_op jit(solution)/shard_map/all_to_all | solution.py:533
  217.9 7.8 %collective-permute-start.12 = (bf16[2,32,16,192]{3,2,1,0:T(8,128)(2,1)}, bf16[2,32,16,192]{3,2,1,0:T(8,128)(2,1)S(1)}, u32[]{:S(2)}, u32[]{:S(2)}) collective-permute-start(bf16[2,32,16,192]{3,2,1,0:T(8,128)(2,1)} %get-tuple-element.57.qm_ref), channel_id=1, source_target_pairs={{0,4},{4,0},{1,5},{5,1},{2,6},{6,2},{3,7},{7,3},{8,12},{12,8},{9,1... | collective-permute-start | bytes 1179656 | tf_op jit(solution)/shard_map/ppermute | solution.py:427
  222.0 10.8 %all-to-all-start.3 = ((bf16[4,1,16,3456]{3,2,1,0:T(8,128)(2,1)}), bf16[4,1,16,3456]{3,2,1,0:T(8,128)(2,1)S(1)}, u32[]{:S(2)}, u32[]{:S(2)}) async-start(bf16[4,1,16,3456]{3,2,1,0:T(8,128)(2,1)} %bitcast.37), calls=%async_computation.3 | async-start | bytes 884736 | tf_op jit(solution)/shard_map/all_to_all | solution.py:533
  232.8 10.3 %all-to-all-start.2 = ((bf16[4,1,16,3456]{3,2,1,0:T(8,128)(2,1)}), bf16[4,1,16,3456]{3,2,1,0:T(8,128)(2,1)S(1)}, u32[]{:S(2)}, u32[]{:S(2)}) async-start(bf16[4,1,16,3456]{3,2,1,0:T(8,128)(2,1)} %bitcast.30), calls=%async_computation.2 | async-start | bytes 884736 | tf_op jit(solution)/shard_map/all_to_all | solution.py:533
  244.0 19.1 %all-to-all-start.5 = ((bf16[8,8,3456]{2,1,0:T(8,128)(2,1)}), bf16[8,8,3456]{2,1,0:T(8,128)(2,1)S(1)}, u32[]{:S(2)}, u32[]{:S(2)}) async-start(bf16[8,8,3456]{2,1,0:T(8,128)(2,1)} %bitcast.19), calls=%async_computation.5 | async-start | bytes 884736 | tf_op jit(solution)/shard_map/all_to_all | solution.py:574
  273.0 4.4 %copy-start.9 = (bf16[32,3456]{1,0:T(8,128)(2,1)}, bf16[32,3456]{1,0:T(8,128)(2,1)S(1)}, u32[]{:S(2)}) copy-start(bf16[32,3456]{1,0:T(8,128)(2,1)S(1)} %all_gather.11.all_ref) | copy-start | bytes 663556
  273.1 7.7 %collective-permute-start.13 = (f32[24]{0:T(128)S(1)}, f32[24]{0:T(128)S(1)}, u32[]{:S(2)}, u32[]{:S(2)}) collective-permute-start(f32[24]{0:T(128)S(1)} %dynamic_slice.12), channel_id=1, source_target_pairs={{0,4},{4,0},{1,5},{5,1},{2,6},{6,2},{3,7},{7,3},{8,12},{12,8},{9,1... | collective-permute-start | bytes 296 | tf_op jit(solution)/shard_map/ppermute | solution.py:427
  (6 other events, 5.3 us)
Sparse Core Ops, SparseCore 0:
  85.6 37.7 all-gather.3
  134.6 22.6 all-gather.5

commit v9 on v8

--- a/solution.py
+++ b/solution.py
@@ -96,8 +96,8 @@
     return (value - mean) * rstd, rstd
 
 
-def read_gain(w_ref):
-    tile = w_ref[0:16, LANES:CARRY].astype(F32)
+def read_gain(tile_ref, first=LANES):
+    tile = tile_ref[0:16, first : first + 128].astype(F32)
     return jnp.concatenate(
         [(tile[p : p + 1] + tile[3 + p : 4 + p]) + tile[6 + p : 7 + p] for p in range(3)], axis=1
     )
@@ -227,17 +227,21 @@
         whole = pltpu.make_async_copy(w_ref, whole_far, sem.at[1])
         whole.start()
     else:
-        nk, nbuf, pre, sem, w_ref = rest
+        nk, nbuf, pre, sem, w_ref, tile_ref = rest
         source = w_refs[0] if index is None else w_refs[0].at[index]
+        part = pltpu.make_async_copy(source.at[pl.ds(0, 16), pl.ds(LANES, 128)], tile_ref, sem.at[2])
+        part.start()
         coming = pltpu.make_async_copy(source, w_ref, sem.at[1])
         coming.start()
-        coming.wait()
+        part.wait()
     first_in = X_WIN[block][0]
     first_out, width_out = X_WIN[block + 1]
     first_s, width_s = S_WIN[block]
-    gain = read_gain(w_ref)
+    gain = read_gain(w_ref) if pieces > 1 else read_gain(tile_ref, 0)
     gain_ref[...] = gain
     norm_phase(block, xo_ref, xt_ref, gain, nbuf, nk)
+    if pieces == 1:
+        coming.wait()
     kept = pltpu.make_async_copy(nk, nk_far, sem.at[0])
     kept.start()
     conv_phase(block, nbuf, w_ref, pre)
@@ -330,11 +334,18 @@
     wg_ref[:, :CHANS] = jnp.where(spot == share, total / gain, first).astype(BF)
 
 
-def turn_kernel(dims, idx_ref, xo_ref, xt_ref, cot_ref, w_ref, q_ref, wg_ref, gain_ref,
-                nbuf, nk, pre, sbuf, sown, wq):
-    gain = read_gain(w_ref)
+def turn_kernel(dims, index, idx_ref, xo_ref, xt_ref, cot_ref, w_far, q_ref, wg_ref, gain_ref,
+                nbuf, nk, pre, sbuf, sown, wq, w_ref, tile_ref, sem):
+    source = w_far.at[index]
+    part = pltpu.make_async_copy(source.at[pl.ds(0, 16), pl.ds(LANES, 128)], tile_ref, sem.at[0])
+    part.start()
+    coming = pltpu.make_async_copy(source, w_ref, sem.at[1])
+    coming.start()
+    part.wait()
+    gain = read_gain(tile_ref, 0)
     gain_ref[...] = gain
     norm_phase(3, xo_ref, xt_ref, gain, nbuf, nk)
+    coming.wait()
     conv_phase(3, nbuf, w_ref, pre)
     n = R_TURN
 
@@ -445,15 +456,15 @@
     wide = wide.reshape(ns, nz * own_chans, CARRY)
 
 
-    first = from_chips(wide[0], "x", nx)
+    first, second = from_chips(wide[0], "x", nx), from_chips(wide[1], "x", nx)
 
     windows, wide = lax.optimization_barrier((windows, wide))
     recv = lax.all_to_all(windows, ("x", "zh"), 0, 0, tiled=True)
-    rest, first, recv = lax.optimization_barrier((wide[1:], first, recv))
-    pair = lax.all_gather(rest[:2], "x", axis=1, tiled=True)
-    last = lax.all_gather(rest[2], "x", axis=0, tiled=True)
-    weights, index = [first, [pair], [pair], [last]], [None, 0, 1, None]
     row_pieces = from_chips(recv, "slab", ny)
+    row_pieces, first, second = lax.optimization_barrier((row_pieces, first, second))
+    rest, _ = lax.optimization_barrier((wide[2:], second))
+    pair = lax.all_gather(rest, "x", axis=1, tiled=True)
+    weights, index = [first, second, [pair], [pair]], [None, None, 0, 1]
     x_own, cot_own = call(
         functools.partial(assemble_kernel, ny, rows),
         (shape((ROWS, XWIN, HALF), BF), shape((ROWS, CWIN, HALF), BF)),
@@ -484,9 +495,10 @@
                 pltpu.VMEM(nk_shape, BF),
                 pltpu.VMEM((ROWS + 2 * PAD, width, taps3), BF),
                 pltpu.VMEM((ROWS, width, HALF), F32),
-                pltpu.SemaphoreType.DMA((2,)),
+                pltpu.SemaphoreType.DMA((3,)),
+                pltpu.VMEM((HALF, CARRY), BF),
             ]
-            + [pltpu.VMEM((HALF, CARRY), BF)],
+            + [pltpu.VMEM((16, 128), BF)] * (not many),
             (idx, *halves[b], *weights[b]),
             (0,),
             () if many else (3,),
@@ -512,7 +524,7 @@
     width = X_WIN[4][1]
     sbuf_s, sown_s, wq_s = back_scratch(3)
     q, grads, gain_b = call(
-        functools.partial(turn_kernel, dims),
+        functools.partial(turn_kernel, dims, index[3]),
         (shape((2, ROWS, S_WIN[2][1], HALF), BF), wg_shape, gain_shape),
         [
             pltpu.VMEM((ROWS + 2 * PAD, width, taps3), BF),
@@ -521,9 +533,13 @@
             sbuf_s,
             sown_s,
             wq_s,
+            pltpu.VMEM((HALF, CARRY), BF),
+            pltpu.VMEM((16, 128), BF),
+            pltpu.SemaphoreType.DMA((2,)),
         ],
         (idx, *halves[3], cot_own, weights[3][0]),
         (0,),
+        (4,),
         micros=12,
     )
     gains.append(gain_b)

time: 289 us -> 284 us (0.983)
  waiting for transfers between devices: 105 us -> 95.5 us
  starting transfers between devices: 46.6 us -> 54.7 us
    ppermute x6 -> x9, waiting for transfers between devices: 39.6 us -> 18.9 us  [from_chips(): return [value] + [lax.ppermute(value, axis, move) for move in moves]]
    all_to_all x1, waiting for transfers between devices: 0.01 us -> 10 us  [local(): recv = lax.all_to_all(windows, ('x', 'zh'), 0, 0, tiled=True)]
    ppermute x6 -> x9, starting transfers between devices: 7.71 us -> 11.7 us  [from_chips(): return [value] + [lax.ppermute(value, axis, move) for move in moves]]
    unnamed x32 -> x30, local copies, waits for them, and re-layouts: 8.67 us -> 7.08 us
  transfers between devices with their start and end apart: 22 -> 24, of which waited for: 16 -> 15; matrix products, arithmetic and copies ran while one was open for 1% -> 1% of each run, Pallas kernels for 23% -> 19%
where the time goes in v9:
time: 284 us; the launch traced here: 283 us
  waiting for transfers between devices  95.5 us (34%)
  Pallas kernels  92.1 us (32%)
  starting transfers between devices  54.7 us (19%)
  between operations  14.2 us (5%)
  local copies, waits for them, and re-layouts  11.9 us (4%)
  blocking collectives  9.89 us (3%)
  other arithmetic  4.42 us (2%)
    pallas_call x11, Pallas kernels, call(): pl.pallas_call(kernel, out_shape=out_shape, in_specs=[sm if i in smem els...  92.1 us
    all_to_all x1, waiting for transfers between devices, local(): wide = lax.all_to_all(wide, ('section', 'zh'), 0, 0, tiled=True)  29.4 us
    ppermute x9, waiting for transfers between devices, from_chips(): return [value] + [lax.ppermute(value, axis, move) for move in moves]  18.9 us
    ppermute x8, waiting for transfers between devices, other(): return lax.ppermute(value, 'core', [(0, 1), (1, 0)])  13.8 us
    all_to_all x1, waiting for transfers between devices, local(): parts = lax.all_to_all(parts, ('section', 'zh'), 0, 0, tiled=True)  13.1 us
    ppermute x9, starting transfers between devices, from_chips(): return [value] + [lax.ppermute(value, axis, move) for move in moves]  11.7 us
    all_to_all x3, starting transfers between devices, reduced(): value = lax.all_to_all(value, 'x', 0, 0, tiled=True)  11 us
    all_to_all x3, waiting for transfers between devices, reduced(): value = lax.all_to_all(value, 'x', 0, 0, tiled=True)  10.3 us
  transfers between devices with their start and end apart: 24, of which 15 were waited for; matrix products, arithmetic and copies ran while one was open for 1% of the time, Pallas kernels for 19%

profile of v9, /device:TPU:33, one launch (start us, length us, event | category | flops | bytes accessed | tf_op | source)
XLA Modules:
  0.0 282.7 jit_solution(2363364969802097537)
XLA Ops:
  13.4 8.0 %all-to-all-start = ((bf16[8,24,3584]{2,1,0:T(8,128)(2,1)}), bf16[8,24,3584]{2,1,0:T(8,128)(2,1)S(1)}, u32[]{:S(2)}, u32[]{:S(2)}) async-start(bf16[8,24,3584]{2,1,0:T(8,128)(2,1)} %broadcast_in_dim.12), calls=%async_computation | async-start | bytes 2752512 | tf_op jit(solution)/shard_map/all_to_all | solution.py:455
  24.1 29.4 %all-to-all-done = bf16[8,24,3584]{2,1,0:T(8,128)(2,1)S(1)} async-done(((bf16[8,24,3584]{2,1,0:T(8,128)(2,1)}), bf16[8,24,3584]{2,1,0:T(8,128)(2,1)S(1)}, u32[]{:S(2)}, u32[]{:S(2)}) %all-to-all-start) | async-done | bytes 1376288 | tf_op jit(solution)/shard_map/all_to_all | solution.py:455
  53.5 6.7 %all-to-all-start.1 = ((bf16[8,8,24,128]{3,2,1,0:T(8,128)(2,1)}), bf16[8,8,24,128]{3,2,1,0:T(8,128)(2,1)S(1)}, u32[]{:S(2)}, u32[]{:S(2)}) async-start(bf16[8,8,24,128]{3,2,1,0:T(8,128)(2,1)} %shard_map.68), calls=%async_computation.1 | async-start | bytes 786432 | tf_op jit(solution)/shard_map/all_to_all | solution.py:462
  60.3 2.7 collective-permute-start.3
  66.2 10.0 %all-to-all-done.1.refs_0_ = bf16[8,8,24,128]{3,2,1,0:T(8,128)(2,1)S(1)} async-done(((bf16[8,8,24,128]{3,2,1,0:T(8,128)(2,1)}), bf16[8,8,24,128]{3,2,1,0:T(8,128)(2,1)S(1)}, u32[]{:S(2)}, u32[]{:S(2)}) %all-to-all-start.1) | async-done | bytes 393248 | tf_op jit(solution)/shard_map/all_to_all | solution.py:462
  76.3 2.7 collective-permute-start
  80.1 4.5 %collective-permute-done.5.rest_3_ = bf16[48,3584]{1,0:T(8,128)(2,1)} collective-permute-done((bf16[48,3584]{1,0:T(8,128)(2,1)S(1)}, bf16[48,3584]{1,0:T(8,128)(2,1)}, u32[]{:S(2)}, u32[]{:S(2)}) %collective-permute-start.5) | collective-permute-done | bytes 344096 | tf_op jit(solution)/shard_map/ppermute | solution.py:451
  89.6 3.7 %collective-permute-done.7.rest_2_ = bf16[48,3584]{1,0:T(8,128)(2,1)} collective-permute-done((bf16[48,3584]{1,0:T(8,128)(2,1)S(1)}, bf16[48,3584]{1,0:T(8,128)(2,1)}, u32[]{:S(2)}, u32[]{:S(2)}) %collective-permute-start.7) | collective-permute-done | bytes 344096 | tf_op jit(solution)/shard_map/ppermute | solution.py:451
  93.4 8.4 %collective-permute-done.8.rest_3_ = bf16[48,3584]{1,0:T(8,128)(2,1)} collective-permute-done((bf16[48,3584]{1,0:T(8,128)(2,1)S(1)}, bf16[48,3584]{1,0:T(8,128)(2,1)}, u32[]{:S(2)}, u32[]{:S(2)}) %collective-permute-start.8) | collective-permute-done | bytes 344096 | tf_op jit(solution)/shard_map/ppermute | solution.py:451
  101.8 4.9 %shard_map.70 = (bf16[32,80,192]{2,1,0:T(8,128)(2,1)}, bf16[32,48,192]{2,1,0:T(8,128)(2,1)}) custom-call(s32[4]{0:T(128)} %pad_add_fusion.idx_ref, bf16[8,8,24,128]{3,2,1,0:T(8,128)(2,1)} %copy-done.7, bf16[8,8,24,128]{3,2,1,0:T(8,128)(2,1)} %collective-permute-done.refs_1_, bf16[8,8,24,128]{3,2,1,0:T(8,128)(2,1)} %collective-permute-done.1.refs_2_, ...), custom_call_target="tpu_custom_call" | custom-call | flops 2000000000 | bytes 2000000 | tf_op jit(solution)/shard_map/pallas_call | solution.py:49
  109.1 2.9 %collective-permute-done.9.xt_ref = bf16[32,80,192]{2,1,0:T(8,128)(2,1)S(1)} collective-permute-done((bf16[32,80,192]{2,1,0:T(8,128)(2,1)}, bf16[32,80,192]{2,1,0:T(8,128)(2,1)S(1)}, u32[]{:S(2)}, u32[]{:S(2)}) %collective-permute-start.9) | collective-permute-done | bytes 983072 | tf_op jit(solution)/shard_map/ppermute | solution.py:438
  113.0 13.8 %shard_map.71 = (bf16[32,80,192]{2,1,0:T(8,128)(2,1)}, f32[32,16,192]{2,1,0:T(8,128)}, f32[1,384]{1,0:T(1,128)}, bf16[48,16,1152]{2,1,0:T(8,128)(2,1)}, bf16[192,3584]{1,0:T(8,128)(2,1)}) custom-call(s32[4]{0:T(128)} %pad_add_fusion.idx_ref, bf16[32,80,192]{2,1,0:T(8,128)(2,1)} %get-tuple-element.47.xo_ref, bf16[32,80,192]{2,1,0:T(8,128)(2,1)} %copy-done.3, ...), custom_call_target="tpu_custom_call" | custom-call | tf_op jit(solution)/shard_map/pallas_call | solution.py:49
  127.5 2.9 %collective-permute-done.10.xt_ref = bf16[32,80,192]{2,1,0:T(8,128)(2,1)S(1)} collective-permute-done((bf16[32,80,192]{2,1,0:T(8,128)(2,1)}, bf16[32,80,192]{2,1,0:T(8,128)(2,1)S(1)}, u32[]{:S(2)}, u32[]{:S(2)}) %collective-permute-start.10) | collective-permute-done | bytes 983072 | tf_op jit(solution)/shard_map/ppermute | solution.py:438
  131.5 14.2 %shard_map.72 = (bf16[32,80,192]{2,1,0:T(8,128)(2,1)}, f32[32,32,192]{2,1,0:T(8,128)}, f32[1,384]{1,0:T(1,128)}, bf16[48,16,1152]{2,1,0:T(8,128)(2,1)}, bf16[192,3584]{1,0:T(8,128)(2,1)}) custom-call(s32[4]{0:T(128)} %pad_add_fusion.idx_ref, bf16[32,80,192]{2,1,0:T(8,128)(2,1)} %get-tuple-element.52.xo_ref, bf16[32,80,192]{2,1,0:T(8,128)(2,1)} %copy-done, ...), custom_call_target="tpu_custom_call" | custom-call | tf_op jit(solution)/shard_map/pallas_call | solution.py:49
  146.1 2.9 %collective-permute-done.11.xt_ref = bf16[32,80,192]{2,1,0:T(8,128)(2,1)S(1)} collective-permute-done((bf16[32,80,192]{2,1,0:T(8,128)(2,1)}, bf16[32,80,192]{2,1,0:T(8,128)(2,1)S(1)}, u32[]{:S(2)}, u32[]{:S(2)}) %collective-permute-start.11) | collective-permute-done | bytes 983072 | tf_op jit(solution)/shard_map/ppermute | solution.py:438
  150.1 12.7 %shard_map.73 = (bf16[32,64,192]{2,1,0:T(8,128)(2,1)}, f32[32,32,192]{2,1,0:T(8,128)}, f32[1,384]{1,0:T(1,128)}, bf16[48,16,1152]{2,1,0:T(8,128)(2,1)}) custom-call(s32[4]{0:T(128)} %pad_add_fusion.idx_ref, bf16[32,80,192]{2,1,0:T(8,128)(2,1)} %get-tuple-element.57.xo_ref, bf16[32,80,192]{2,1,0:T(8,128)(2,1)} %copy-done.4, ...), custom_call_target="tpu_custom_call" | custom-call | tf_op jit(solution)/shard_map/pallas_call | solution.py:49
  163.2 2.5 collective-permute-done.12.xt_ref
  166.7 14.6 %shard_map.74 = (bf16[2,32,32,192]{3,2,1,0:T(8,128)(2,1)}, bf16[64,3456]{1,0:T(8,128)(2,1)}, f32[1,384]{1,0:T(1,128)}) custom-call(s32[4]{0:T(128)} %pad_add_fusion.idx_ref, bf16[32,64,192]{2,1,0:T(8,128)(2,1)} %get-tuple-element.60.xo_ref, bf16[32,64,192]{2,1,0:T(8,128)(2,1)} %copy-done.13, bf16[32,48,192]{2,1,0:T(8,128)(2,1)} %get-tuple-element.61.cot_ref.g_ref, ...), custom_call_target="tpu_custom_call" | custom-call | flops 12000000000 | bytes 12000000 | tf_op jit(solution)/shard_map/pallas_call | solution.py:49
  181.8 2.6 collective-permute-done.13.qr_ref
  185.3 9.8 %shard_map.75 = (bf16[2,32,32,192]{3,2,1,0:T(8,128)(2,1)}, bf16[32,32,192]{2,1,0:T(8,128)(2,1)}, bf16[64,3456]{1,0:T(8,128)(2,1)}) custom-call(s32[4]{0:T(128)} %pad_add_fusion.idx_ref, bf16[2,32,32,192]{3,2,1,0:T(8,128)(2,1)} %get-tuple-element.62.qm_ref, bf16[2,32,32,192]{3,2,1,0:T(8,128)(2,1)} %copy-done.14, ...), custom_call_target="tpu_custom_call" | custom-call | flops 8000000000 | bytes 8000000 | tf_op jit(solution)/shard_map/pallas_call | solution.py:49
  197.5 3.7 %all-to-all-start.4 = ((bf16[4,2,16,3456]{3,2,1,0:T(8,128)(2,1)}), bf16[4,2,16,3456]{3,2,1,0:T(8,128)(2,1)S(1)}, u32[]{:S(2)}, u32[]{:S(2)}) async-start(bf16[4,2,16,3456]{3,2,1,0:T(8,128)(2,1)} %pad_maximum_fusion), calls=%async_computation.4 | async-start | bytes 1769472 | tf_op jit(solution)/shard_map/all_to_all | solution.py:549
  202.2 8.2 %shard_map.76 = (bf16[2,32,16,192]{3,2,1,0:T(8,128)(2,1)}, bf16[32,32,192]{2,1,0:T(8,128)(2,1)}, bf16[64,3456]{1,0:T(8,128)(2,1)}) custom-call(s32[4]{0:T(128)} %pad_add_fusion.idx_ref, bf16[2,32,32,192]{3,2,1,0:T(8,128)(2,1)} %get-tuple-element.67.qm_ref, bf16[2,32,32,192]{3,2,1,0:T(8,128)(2,1)} %copy-done.12, ...), custom_call_target="tpu_custom_call" | custom-call | flops 8000000000 | bytes 8000000 | tf_op jit(solution)/shard_map/pallas_call | solution.py:49
  210.7 3.6 %all-to-all-done.4 = bf16[4,2,16,3456]{3,2,1,0:T(8,128)(2,1)S(1)} async-done(((bf16[4,2,16,3456]{3,2,1,0:T(8,128)(2,1)}), bf16[4,2,16,3456]{3,2,1,0:T(8,128)(2,1)S(1)}, u32[]{:S(2)}, u32[]{:S(2)}) %all-to-all-start.4) | async-done | bytes 884768 | tf_op jit(solution)/shard_map/all_to_all | solution.py:549
  214.3 3.5 %all-to-all-start.3 = ((bf16[4,1,16,3456]{3,2,1,0:T(8,128)(2,1)}), bf16[4,1,16,3456]{3,2,1,0:T(8,128)(2,1)S(1)}, u32[]{:S(2)}, u32[]{:S(2)}) async-start(bf16[4,1,16,3456]{3,2,1,0:T(8,128)(2,1)} %bitcast.41), calls=%async_computation.3 | async-start | bytes 884736 | tf_op jit(solution)/shard_map/all_to_all | solution.py:549
  218.6 6.1 %shard_map.77 = bf16[64,3456]{1,0:T(8,128)(2,1)} custom-call(s32[4]{0:T(128)} %pad_add_fusion.idx_ref, bf16[2,32,16,192]{3,2,1,0:T(8,128)(2,1)} %get-tuple-element.73.qm_ref, bf16[2,32,16,192]{3,2,1,0:T(8,128)(2,1)} %copy-done.5, bf16[32,80,192]{2,1,0:T(8,128)(2,1)} %get-tuple-element.52.xo_ref, bf16[32,80,192]{2,1,0:T(8,128)(2,1)} %copy-done, ...), custom_call_target="tpu_custom_call" | custom-call | flops 2000000000 | bytes 2000000 | tf_op jit(solution)/shard_map/pallas_call | solution.py:49
  225.1 3.8 %all-to-all-start.2 = ((bf16[4,1,16,3456]{3,2,1,0:T(8,128)(2,1)}), bf16[4,1,16,3456]{3,2,1,0:T(8,128)(2,1)S(1)}, u32[]{:S(2)}, u32[]{:S(2)}) async-start(bf16[4,1,16,3456]{3,2,1,0:T(8,128)(2,1)} %bitcast.30), calls=%async_computation.2 | async-start | bytes 884736 | tf_op jit(solution)/shard_map/all_to_all | solution.py:549
  229.1 6.3 %all-to-all-done.2 = bf16[4,1,16,3456]{3,2,1,0:T(8,128)(2,1)S(1)} async-done(((bf16[4,1,16,3456]{3,2,1,0:T(8,128)(2,1)}), bf16[4,1,16,3456]{3,2,1,0:T(8,128)(2,1)S(1)}, u32[]{:S(2)}, u32[]{:S(2)}) %all-to-all-start.2) | async-done | bytes 442400 | tf_op jit(solution)/shard_map/all_to_all | solution.py:549
  236.3 7.4 %all-to-all-start.5 = ((bf16[8,8,3456]{2,1,0:T(8,128)(2,1)}), bf16[8,8,3456]{2,1,0:T(8,128)(2,1)S(1)}, u32[]{:S(2)}, u32[]{:S(2)}) async-start(bf16[8,8,3456]{2,1,0:T(8,128)(2,1)} %bitcast.19), calls=%async_computation.5 | async-start | bytes 884736 | tf_op jit(solution)/shard_map/all_to_all | solution.py:590
  243.7 13.1 %all-to-all-done.5 = bf16[8,8,3456]{2,1,0:T(8,128)(2,1)S(1)} async-done(((bf16[8,8,3456]{2,1,0:T(8,128)(2,1)}), bf16[8,8,3456]{2,1,0:T(8,128)(2,1)S(1)}, u32[]{:S(2)}, u32[]{:S(2)}) %all-to-all-start.5) | async-done | bytes 442400 | tf_op jit(solution)/shard_map/all_to_all | solution.py:590
  256.8 9.9 %all_gather.7.all_ref = bf16[32,3456]{1,0:T(8,128)(2,1)S(1)} all-gather(bf16[8,3456]{1,0:T(8,128)(2,1)S(1)} %reduce_sum.66), channel_id=1, replica_groups=mesh['section'=4,'x'=4,'zh'=2,'core'=2,'slab'=4] {'slab'}, dimensions={0}, use_global_device_ids=true | all-gather | bytes 276480 | tf_op jit(solution)/shard_map/all_gather | solution.py:592
  266.8 5.0 %collective-permute-start.16 = (f32[24]{0:T(128)S(1)}, f32[24]{0:T(128)S(1)}, u32[]{:S(2)}, u32[]{:S(2)}) collective-permute-start(f32[24]{0:T(128)S(1)} %dynamic_slice.12), channel_id=1, source_target_pairs={{0,4},{4,0},{1,5},{5,1},{2,6},{6,2},{3,7},{7,3},{8,12},{12,8},{9,1... | collective-permute-start | bytes 296 | tf_op jit(solution)/shard_map/ppermute | solution.py:438
  271.9 3.4 %shard_map.78 = f32[9,24,384]{2,1,0:T(8,128)} custom-call(bf16[32,3456]{1,0:T(8,128)(2,1)} %copy-done.11, bf16[384,384]{1,0:T(8,128)(2,1)} %dynamic-slice_bitcast_fusion.perm_ref), custom_call_target="tpu_custom_call" | custom-call | flops 2000000000 | bytes 2000000 | tf_op jit(solution)/shard_map/pallas_call | solution.py:49
  (73 shorter events, 34.7 us)
Async XLA Ops:
  13.4 40.1 %all-to-all-start = ((bf16[8,24,3584]{2,1,0:T(8,128)(2,1)}), bf16[8,24,3584]{2,1,0:T(8,128)(2,1)S(1)}, u32[]{:S(2)}, u32[]{:S(2)}) async-start(bf16[8,24,3584]{2,1,0:T(8,128)(2,1)} %broadcast_in_dim.12), calls=%async_computation | async-start | bytes 2752512 | tf_op jit(solution)/shard_map/all_to_all | solution.py:455
  53.5 22.8 %all-to-all-start.1 = ((bf16[8,8,24,128]{3,2,1,0:T(8,128)(2,1)}), bf16[8,8,24,128]{3,2,1,0:T(8,128)(2,1)S(1)}, u32[]{:S(2)}, u32[]{:S(2)}) async-start(bf16[8,8,24,128]{3,2,1,0:T(8,128)(2,1)} %shard_map.68), calls=%async_computation.1 | async-start | bytes 786432 | tf_op jit(solution)/shard_map/all_to_all | solution.py:462
  60.2 88.9 %all-gather.2.cloned.1.call-start = ((), (), s32[]{:S(2)}) async-start(), calls=%async_computation.6 | async-start | bytes 3440640 | tf_op jit(solution)/shard_map/all_gather | solution.py:466
  60.3 46.5 %copy-start.1 = (bf16[2,24,3584]{2,1,0:T(8,128)(2,1)}, bf16[2,24,3584]{2,1,0:T(8,128)(2,1)S(1)}, u32[]{:S(2)}) copy-start(bf16[2,24,3584]{2,1,0:T(8,128)(2,1)S(1)} %get-tuple-element.82) | copy-start | bytes 1032196
  60.3 46.5 %copy-start.2 = (bf16[2,24,3584]{2,1,0:T(8,128)(2,1)}, bf16[2,24,3584]{2,1,0:T(8,128)(2,1)S(1)}, u32[]{:S(2)}) copy-start(bf16[2,24,3584]{2,1,0:T(8,128)(2,1)S(1)} %get-tuple-element.83) | copy-start | bytes 1032196
  60.3 18.7 %collective-permute-start.3 = (bf16[48,3584]{1,0:T(8,128)(2,1)S(1)}, bf16[48,3584]{1,0:T(8,128)(2,1)S(1)}, u32[]{:S(2)}, u32[]{:S(2)}) collective-permute-start(bf16[48,3584]{1,0:T(8,128)(2,1)S(1)} %bitcast.35), channel_id=1, source_target_pairs={{0,48},{16,0},{32,16},{48,32},{1,49},{17,1},{33,17},{49,33},{2,50}... | collective-permute-start | bytes 1032200 | tf_op jit(solution)/shard_map/ppermute | solution.py:451
  63.0 16.4 %collective-permute-start.4 = (bf16[48,3584]{1,0:T(8,128)(2,1)S(1)}, bf16[48,3584]{1,0:T(8,128)(2,1)S(1)}, u32[]{:S(2)}, u32[]{:S(2)}) collective-permute-start(bf16[48,3584]{1,0:T(8,128)(2,1)S(1)} %bitcast.36), channel_id=1, source_target_pairs={{0,32},{16,48},{32,0},{48,16},{1,33},{17,49},{33,1},{49,17},{2,34}... | collective-permute-start | bytes 1032200 | tf_op jit(solution)/shard_map/ppermute | solution.py:451
  63.6 21.0 %collective-permute-start.5 = (bf16[48,3584]{1,0:T(8,128)(2,1)S(1)}, bf16[48,3584]{1,0:T(8,128)(2,1)}, u32[]{:S(2)}, u32[]{:S(2)}) collective-permute-start(bf16[48,3584]{1,0:T(8,128)(2,1)S(1)} %bitcast.37), channel_id=1, source_target_pairs={{0,16},{16,32},{32,48},{48,0},{1,17},{17,33},{33,49},{49,1},{2,18}... | collective-permute-start | bytes 1032200 | tf_op jit(solution)/shard_map/ppermute | solution.py:451
  64.1 22.9 %collective-permute-start.6 = (bf16[48,3584]{1,0:T(8,128)(2,1)S(1)}, bf16[48,3584]{1,0:T(8,128)(2,1)S(1)}, u32[]{:S(2)}, u32[]{:S(2)}) collective-permute-start(bf16[48,3584]{1,0:T(8,128)(2,1)S(1)} %bitcast.31), channel_id=1, source_target_pairs={{0,48},{16,0},{32,16},{48,32},{1,49},{17,1},{33,17},{49,33},{2,50}... | collective-permute-start | bytes 1032200 | tf_op jit(solution)/shard_map/ppermute | solution.py:451
  76.3 25.6 %copy-start.7 = (bf16[8,8,24,128]{3,2,1,0:T(8,128)(2,1)}, bf16[8,8,24,128]{3,2,1,0:T(8,128)(2,1)S(1)}, u32[]{:S(2)}) copy-start(bf16[8,8,24,128]{3,2,1,0:T(8,128)(2,1)S(1)} %all-to-all-done.1.refs_0_) | copy-start | bytes 1179652
  76.3 25.5 %collective-permute-start = (bf16[8,8,24,128]{3,2,1,0:T(8,128)(2,1)S(1)}, bf16[8,8,24,128]{3,2,1,0:T(8,128)(2,1)}, u32[]{:S(2)}, u32[]{:S(2)}) collective-permute-start(bf16[8,8,24,128]{3,2,1,0:T(8,128)(2,1)S(1)} %all-to-all-done.1.refs_0_), channel_id=1, source_target_pairs={{0,3},{1,0},{2,1},{3,2},{4,7},{5,4},{6,5},{7,6},{8,11},{9,8},{10,9... | collective-permute-start | bytes 1179656 | tf_op jit(solution)/shard_map/ppermute | solution.py:451
  79.0 27.7 %copy-start.9 = (bf16[48,3584]{1,0:T(8,128)(2,1)}, bf16[48,3584]{1,0:T(8,128)(2,1)S(1)}, u32[]{:S(2)}) copy-start(bf16[48,3584]{1,0:T(8,128)(2,1)S(1)} %collective-permute-done.3.rest_1_) | copy-start | bytes 1032196
  79.0 22.8 %collective-permute-start.1 = (bf16[8,8,24,128]{3,2,1,0:T(8,128)(2,1)S(1)}, bf16[8,8,24,128]{3,2,1,0:T(8,128)(2,1)}, u32[]{:S(2)}, u32[]{:S(2)}) collective-permute-start(bf16[8,8,24,128]{3,2,1,0:T(8,128)(2,1)S(1)} %all-to-all-done.1.refs_0_), channel_id=1, source_target_pairs={{0,2},{1,3},{2,0},{3,1},{4,6},{5,7},{6,4},{7,5},{8,10},{9,11},{10,... | collective-permute-start | bytes 1179656 | tf_op jit(solution)/shard_map/ppermute | solution.py:451
  79.4 27.4 %copy-start.10 = (bf16[48,3584]{1,0:T(8,128)(2,1)}, bf16[48,3584]{1,0:T(8,128)(2,1)S(1)}, u32[]{:S(2)}) copy-start(bf16[48,3584]{1,0:T(8,128)(2,1)S(1)} %collective-permute-done.4.rest_2_) | copy-start | bytes 1032196
  79.4 22.4 %collective-permute-start.2 = (bf16[8,8,24,128]{3,2,1,0:T(8,128)(2,1)S(1)}, bf16[8,8,24,128]{3,2,1,0:T(8,128)(2,1)}, u32[]{:S(2)}, u32[]{:S(2)}) collective-permute-start(bf16[8,8,24,128]{3,2,1,0:T(8,128)(2,1)S(1)} %all-to-all-done.1.refs_0_), channel_id=1, source_target_pairs={{0,1},{1,2},{2,3},{3,0},{4,5},{5,6},{6,7},{7,4},{8,9},{9,10},{10,1... | collective-permute-start | bytes 1179656 | tf_op jit(solution)/shard_map/ppermute | solution.py:451
  84.5 8.8 %collective-permute-start.7 = (bf16[48,3584]{1,0:T(8,128)(2,1)S(1)}, bf16[48,3584]{1,0:T(8,128)(2,1)}, u32[]{:S(2)}, u32[]{:S(2)}) collective-permute-start(bf16[48,3584]{1,0:T(8,128)(2,1)S(1)} %bitcast.32), channel_id=1, source_target_pairs={{0,32},{16,48},{32,0},{48,16},{1,33},{17,49},{33,1},{49,17},{2,34}... | collective-permute-start | bytes 1032200 | tf_op jit(solution)/shard_map/ppermute | solution.py:451
  87.0 19.7 %copy-start.8 = (bf16[48,3584]{1,0:T(8,128)(2,1)}, bf16[48,3584]{1,0:T(8,128)(2,1)S(1)}, u32[]{:S(2)}) copy-start(bf16[48,3584]{1,0:T(8,128)(2,1)S(1)} %collective-permute-done.6.rest_1_) | copy-start | bytes 1032196
  87.0 14.8 %collective-permute-start.8 = (bf16[48,3584]{1,0:T(8,128)(2,1)S(1)}, bf16[48,3584]{1,0:T(8,128)(2,1)}, u32[]{:S(2)}, u32[]{:S(2)}) collective-permute-start(bf16[48,3584]{1,0:T(8,128)(2,1)S(1)} %bitcast.33), channel_id=1, source_target_pairs={{0,16},{16,32},{32,48},{48,0},{1,17},{17,33},{33,49},{49,1},{2,18}... | collective-permute-start | bytes 1032200 | tf_op jit(solution)/shard_map/ppermute | solution.py:451
  106.8 5.2 %collective-permute-start.9 = (bf16[32,80,192]{2,1,0:T(8,128)(2,1)}, bf16[32,80,192]{2,1,0:T(8,128)(2,1)S(1)}, u32[]{:S(2)}, u32[]{:S(2)}) collective-permute-start(bf16[32,80,192]{2,1,0:T(8,128)(2,1)} %get-tuple-element.47.xo_ref), channel_id=1, source_target_pairs={{0,4},{4,0},{1,5},{5,1},{2,6},{6,2},{3,7},{7,3},{8,12},{12,8},{9,1... | collective-permute-start | bytes 2949128 | tf_op jit(solution)/shard_map/ppermute | solution.py:438
  126.8 3.5 %collective-permute-start.10 = (bf16[32,80,192]{2,1,0:T(8,128)(2,1)}, bf16[32,80,192]{2,1,0:T(8,128)(2,1)S(1)}, u32[]{:S(2)}, u32[]{:S(2)}) collective-permute-start(bf16[32,80,192]{2,1,0:T(8,128)(2,1)} %get-tuple-element.52.xo_ref), channel_id=1, source_target_pairs={{0,4},{4,0},{1,5},{5,1},{2,6},{6,2},{3,7},{7,3},{8,12},{12,8},{9,1... | collective-permute-start | bytes 2949128 | tf_op jit(solution)/shard_map/ppermute | solution.py:438
  145.7 3.3 %collective-permute-start.11 = (bf16[32,80,192]{2,1,0:T(8,128)(2,1)}, bf16[32,80,192]{2,1,0:T(8,128)(2,1)S(1)}, u32[]{:S(2)}, u32[]{:S(2)}) collective-permute-start(bf16[32,80,192]{2,1,0:T(8,128)(2,1)} %get-tuple-element.57.xo_ref), channel_id=1, source_target_pairs={{0,4},{4,0},{1,5},{5,1},{2,6},{6,2},{3,7},{7,3},{8,12},{12,8},{9,1... | collective-permute-start | bytes 2949128 | tf_op jit(solution)/shard_map/ppermute | solution.py:438
  162.8 3.0 %collective-permute-start.12 = (bf16[32,64,192]{2,1,0:T(8,128)(2,1)}, bf16[32,64,192]{2,1,0:T(8,128)(2,1)S(1)}, u32[]{:S(2)}, u32[]{:S(2)}) collective-permute-start(bf16[32,64,192]{2,1,0:T(8,128)(2,1)} %get-tuple-element.60.xo_ref), channel_id=1, source_target_pairs={{0,4},{4,0},{1,5},{5,1},{2,6},{6,2},{3,7},{7,3},{8,12},{12,8},{9,1... | collective-permute-start | bytes 2359304 | tf_op jit(solution)/shard_map/ppermute | solution.py:438
  181.3 3.0 %collective-permute-start.13 = (bf16[2,32,32,192]{3,2,1,0:T(8,128)(2,1)}, bf16[2,32,32,192]{3,2,1,0:T(8,128)(2,1)S(1)}, u32[]{:S(2)}, u32[]{:S(2)}) collective-permute-start(bf16[2,32,32,192]{3,2,1,0:T(8,128)(2,1)} %get-tuple-element.62.qm_ref), channel_id=1, source_target_pairs={{0,4},{4,0},{1,5},{5,1},{2,6},{6,2},{3,7},{7,3},{8,12},{12,8},{9,1... | collective-permute-start | bytes 2359304 | tf_op jit(solution)/shard_map/ppermute | solution.py:438
  185.3 10.2 %copy-start.6 = (bf16[64,3456]{1,0:T(8,128)(2,1)S(1)}, bf16[64,3456]{1,0:T(8,128)(2,1)}, u32[]{:S(2)}) copy-start(bf16[64,3456]{1,0:T(8,128)(2,1)} %get-tuple-element.81) | copy-start | bytes 1327108
  195.1 6.2 %collective-permute-start.14 = (bf16[2,32,32,192]{3,2,1,0:T(8,128)(2,1)}, bf16[2,32,32,192]{3,2,1,0:T(8,128)(2,1)S(1)}, u32[]{:S(2)}, u32[]{:S(2)}) collective-permute-start(bf16[2,32,32,192]{3,2,1,0:T(8,128)(2,1)} %get-tuple-element.67.qm_ref), channel_id=1, source_target_pairs={{0,4},{4,0},{1,5},{5,1},{2,6},{6,2},{3,7},{7,3},{8,12},{12,8},{9,1... | collective-permute-start | bytes 2359304 | tf_op jit(solution)/shard_map/ppermute | solution.py:438
  197.5 16.8 %all-to-all-start.4 = ((bf16[4,2,16,3456]{3,2,1,0:T(8,128)(2,1)}), bf16[4,2,16,3456]{3,2,1,0:T(8,128)(2,1)S(1)}, u32[]{:S(2)}, u32[]{:S(2)}) async-start(bf16[4,2,16,3456]{3,2,1,0:T(8,128)(2,1)} %pad_maximum_fusion), calls=%async_computation.4 | async-start | bytes 1769472 | tf_op jit(solution)/shard_map/all_to_all | solution.py:549
  210.5 7.3 %collective-permute-start.15 = (bf16[2,32,16,192]{3,2,1,0:T(8,128)(2,1)}, bf16[2,32,16,192]{3,2,1,0:T(8,128)(2,1)S(1)}, u32[]{:S(2)}, u32[]{:S(2)}) collective-permute-start(bf16[2,32,16,192]{3,2,1,0:T(8,128)(2,1)} %get-tuple-element.73.qm_ref), channel_id=1, source_target_pairs={{0,4},{4,0},{1,5},{5,1},{2,6},{6,2},{3,7},{7,3},{8,12},{12,8},{9,1... | collective-permute-start | bytes 1179656 | tf_op jit(solution)/shard_map/ppermute | solution.py:438
  214.3 10.8 %all-to-all-start.3 = ((bf16[4,1,16,3456]{3,2,1,0:T(8,128)(2,1)}), bf16[4,1,16,3456]{3,2,1,0:T(8,128)(2,1)S(1)}, u32[]{:S(2)}, u32[]{:S(2)}) async-start(bf16[4,1,16,3456]{3,2,1,0:T(8,128)(2,1)} %bitcast.41), calls=%async_computation.3 | async-start | bytes 884736 | tf_op jit(solution)/shard_map/all_to_all | solution.py:549
  225.1 10.3 %all-to-all-start.2 = ((bf16[4,1,16,3456]{3,2,1,0:T(8,128)(2,1)}), bf16[4,1,16,3456]{3,2,1,0:T(8,128)(2,1)S(1)}, u32[]{:S(2)}, u32[]{:S(2)}) async-start(bf16[4,1,16,3456]{3,2,1,0:T(8,128)(2,1)} %bitcast.30), calls=%async_computation.2 | async-start | bytes 884736 | tf_op jit(solution)/shard_map/all_to_all | solution.py:549
  236.3 20.5 %all-to-all-start.5 = ((bf16[8,8,3456]{2,1,0:T(8,128)(2,1)}), bf16[8,8,3456]{2,1,0:T(8,128)(2,1)S(1)}, u32[]{:S(2)}, u32[]{:S(2)}) async-start(bf16[8,8,3456]{2,1,0:T(8,128)(2,1)} %bitcast.19), calls=%async_computation.5 | async-start | bytes 884736 | tf_op jit(solution)/shard_map/all_to_all | solution.py:590
  266.7 5.1 %copy-start.11 = (bf16[32,3456]{1,0:T(8,128)(2,1)}, bf16[32,3456]{1,0:T(8,128)(2,1)S(1)}, u32[]{:S(2)}) copy-start(bf16[32,3456]{1,0:T(8,128)(2,1)S(1)} %all_gather.7.all_ref) | copy-start | bytes 663556
  266.8 8.5 %collective-permute-start.16 = (f32[24]{0:T(128)S(1)}, f32[24]{0:T(128)S(1)}, u32[]{:S(2)}, u32[]{:S(2)}) collective-permute-start(f32[24]{0:T(128)S(1)} %dynamic_slice.12), channel_id=1, source_target_pairs={{0,4},{4,0},{1,5},{5,1},{2,6},{6,2},{3,7},{7,3},{8,12},{12,8},{9,1... | collective-permute-start | bytes 296 | tf_op jit(solution)/shard_map/ppermute | solution.py:438
  (7 other events, 7.1 us)
Sparse Core Ops, SparseCore 0:
  102.0 41.0 all-gather.1
